TPU v7x, 32 devices: a whole 2x2x4 slice. The times are simulated.
32 devices in a mesh: dp: 8 (over z, y), chan: 4 (over x, core).
Axes of the slice: x: 2, y: 2, z: 4, core: 2. Of those that a mesh axis runs over, the one named last changes fastest.
Arguments:
- feat_fine: bfloat16 [8, 128, 1600], P('dp', 'chan'), may hold values from -6 to 6
- feat_mid: bfloat16 [8, 256, 400], P('dp', 'chan'), may hold values from -6 to 6
- feat_coarse: bfloat16 [8, 512, 100], P('dp', 'chan'), may hold values from -6 to 6
- image_units: int32 [8], P('dp'), may hold values from 6 to 10, as said below
- stem_fine: bfloat16 [128, 128], P('chan'), may hold values from -0.5 to 0.5
- stem_mid: bfloat16 [128, 256], P('chan'), may hold values from -0.375 to 0.375
- stem_coarse: bfloat16 [128, 512], P('chan'), may hold values from -0.25 to 0.25
- conv_weights: bfloat16 [3, 4, 9, 128, 128], P(None, None, None, 'chan'), may hold values from -0.1875 to 0.1875
- norm_gains: float32 [3, 5, 128], P(None, None, 'chan'), may hold values from 0.1 to 1.9
- norm_shifts: float32 [3, 5, 128], P(None, None, 'chan'), may hold values from -3 to 3
- class_weights: bfloat16 [3, 80, 128], P(None, 'chan'), may hold values from -0.5 to 0.5
- class_bias: float32 [3, 80], P(None, 'chan'), may hold values from -3 to 3
- box_weights: bfloat16 [3, 5, 128], P(None, None, 'chan'), may hold values from -0.5 to 0.5
- box_bias: float32 [3, 5], replicated, may hold values from -3 to 3
- class_cot: bfloat16 [8, 80, 2100], P('dp', 'chan'), may hold values from -6 to 6
- box_cot: bfloat16 [8, 5, 2100], P('dp'), may hold values from -6 to 6
Outputs:
- class_out: bfloat16 [8, 80, 2100], P('dp', 'chan')
- box_out: bfloat16 [8, 5, 2100], P('dp')
- grad_fine: bfloat16 [8, 128, 1600], P('dp', 'chan')
- grad_mid: bfloat16 [8, 256, 400], P('dp', 'chan')
- grad_coarse: bfloat16 [8, 512, 100], P('dp', 'chan')
- grad_stem_fine: float32 [128, 128], P('chan')
- grad_stem_mid: float32 [128, 256], P('chan')
- grad_stem_coarse: float32 [128, 512], P('chan')
- grad_conv: float32 [3, 4, 9, 128, 128], P(None, None, None, 'chan')
- grad_gains: float32 [3, 5, 128], P(None, None, 'chan')
- grad_shifts: float32 [3, 5, 128], P(None, None, 'chan')
- grad_class_weights: float32 [3, 80, 128], P(None, 'chan')
- grad_class_bias: float32 [3, 80], P(None, 'chan')
- grad_box_weights: float32 [3, 5, 128], P(None, None, 'chan')
- grad_box_bias: float32 [3, 5], replicated
Inputs may be any that keep to these rules, and one draw needn't show every extreme that they name: `image_units`: each entry is 6, 8 or 10; both 6 and 10 occur in every draw.
All inputs are finite; a program needn't handle non-finite values.
Results may differ from a plain program's by a relative error of at most 0.024.
Values may be sent and summed in bfloat16 or wider, within the bound.
No kernel may reach another device: no remote copies, remote signals or barrier semaphores. Data moves between devices by JAX's collectives and lax.ppermute only.
A program may use at most 576 MiB of HBM per device.

v0:
```python
import math

import jax
import jax.numpy as jnp
from jax import lax
from jax.sharding import PartitionSpec as P

S_LARGE = 10


epsilon = 0.001
layout = ("NCHW", "OIHW", "NCHW")


def level_mask(image_units, level_id):
    edge_len = S_LARGE * 2 ** (2 - level_id)
    pixels = jnp.arange(edge_len * edge_len, dtype=jnp.int32)
    row_at = pixels // edge_len
    col_at = pixels % edge_len
    bounds = image_units * 2 ** (2 - level_id)
    inside = (row_at[None, :] < bounds[:, None]) & (col_at[None, :] < bounds[:, None])
    return inside.astype(jnp.float32)[:, None, :]


def split_joined(joined, members, rank_count):
    result = []
    offset = 0
    for member in members:
        length = member.shape[1] * member.shape[2]
        portion = joined[:, :, offset : offset + length]
        result.append(
            portion.reshape(member.shape[0], rank_count * member.shape[1], member.shape[2])
        )
        offset = offset + length
    return result


def share(members):
    images = members[0].shape[0]
    rank_count = lax.axis_size("chan")
    flattened = jnp.concatenate([member.reshape(images, -1) for member in members], axis=1)
    joined = lax.all_gather(flattened, "chan", axis=1, tiled=True).reshape(images, rank_count, -1)
    return split_joined(joined, members, rank_count)


def spread(partials):
    images = partials[0].shape[0]
    rank_count = lax.axis_size("chan")
    grouped = [partial_sum.reshape(images, rank_count, -1) for partial_sum in partials]
    flattened = jnp.concatenate(grouped, axis=2).reshape(images, -1)
    summed = lax.psum_scatter(
        flattened.astype(jnp.bfloat16), "chan", scatter_dimension=1, tiled=True
    ).astype(jnp.float32)
    result = []
    offset = 0
    for partial_sum in partials:
        own_rows = partial_sum.shape[1] // rank_count
        length = own_rows * partial_sum.shape[2]
        result.append(
            summed[:, offset : offset + length].reshape(images, own_rows, partial_sum.shape[2])
        )
        offset = offset + length
    return result


def box_total(partials):
    summed = lax.psum(jnp.concatenate(partials, axis=2), "chan")
    result = []
    offset = 0
    for partial_sum in partials:
        length = partial_sum.shape[2]
        result.append(summed[:, :, offset : offset + length])
        offset = offset + length
    return result


def norm_forward(outputs, masks, gains, shifts):
    first_sum = jnp.stack(
        [jnp.sum(output * valid_mask, axis=(0, 2)) for output, valid_mask in zip(outputs, masks)]
    )
    second = jnp.stack(
        [
            jnp.sum(output * output * valid_mask, axis=(0, 2))
            for output, valid_mask in zip(outputs, masks)
        ]
    )
    counts = jnp.stack([jnp.sum(valid_mask) for valid_mask in masks])
    first_sum, second, counts = lax.psum((first_sum, second, counts), "dp")
    actives = []
    kept = []
    for position in range(len(outputs)):
        center = first_sum[position] / counts[position]
        inv_std = lax.rsqrt(second[position] / counts[position] - center * center + epsilon)
        normed = (outputs[position] - center[None, :, None]) * inv_std[None, :, None]
        shifted = normed * gains[position][None, :, None] + shifts[position][None, :, None]
        actives.append((jax.nn.silu(shifted) * masks[position]).astype(jnp.bfloat16))
        kept.append((center, inv_std, counts[position]))
    return (actives, kept)


def norm_backward(grads, outputs, kept, masks, gains, shifts):
    pieces = []
    shift_sums = []
    gain_sums = []
    for position in range(len(outputs)):
        center, inv_std, total_count = kept[position]
        normed = (outputs[position] - center[None, :, None]) * inv_std[None, :, None]
        shifted = normed * gains[position][None, :, None] + shifts[position][None, :, None]
        sigmoid_v = jax.nn.sigmoid(shifted)
        slope_val = sigmoid_v * (1.0 + shifted * (1.0 - sigmoid_v))
        pre_grad = grads[position] * masks[position] * slope_val
        pieces.append((normed, pre_grad))
        shift_sums.append(jnp.sum(pre_grad, axis=(0, 2)))
        gain_sums.append(jnp.sum(pre_grad * normed, axis=(0, 2)))
    shift_total, gain_total = lax.psum((jnp.stack(shift_sums), jnp.stack(gain_sums)), "dp")
    results = []
    for position in range(len(outputs)):
        normed, pre_grad = pieces[position]
        center, inv_std, total_count = kept[position]
        factor = gains[position] * inv_std
        correction = (
            shift_total[position][None, :, None] + normed * gain_total[position][None, :, None]
        ) / total_count
        input_grad = masks[position] * factor[None, :, None] * (pre_grad - correction)
        results.append(input_grad.astype(jnp.bfloat16))
    return (results, gain_total, shift_total)


def conv_apply(gathered, weights):
    images, channels, pixels = gathered.shape
    edge_len = math.isqrt(pixels)
    planes = gathered.reshape(images, channels, edge_len, edge_len)
    kernel = weights.reshape(3, 3, weights.shape[1], weights.shape[2]).transpose(2, 3, 0, 1)
    output = lax.conv_general_dilated(
        planes,
        kernel,
        (1, 1),
        ((1, 1), (1, 1)),
        dimension_numbers=layout,
        preferred_element_type=jnp.float32,
    )
    return output.reshape(images, weights.shape[1], pixels)


def conv_input_grad(out_grad, weights):
    images, out_rows, pixels = out_grad.shape
    edge_len = math.isqrt(pixels)
    planes = out_grad.reshape(images, out_rows, edge_len, edge_len)
    kernel = weights.reshape(3, 3, weights.shape[1], weights.shape[2])[::-1, ::-1].transpose(
        3, 2, 0, 1
    )
    output = lax.conv_general_dilated(
        planes,
        kernel,
        (1, 1),
        ((1, 1), (1, 1)),
        dimension_numbers=layout,
        preferred_element_type=jnp.float32,
    )
    return output.reshape(images, weights.shape[2], pixels)


def conv_weight_grad(out_grad, gathered):
    images, channels, pixels = gathered.shape
    edge_len = math.isqrt(pixels)
    planes = gathered.reshape(images, channels, edge_len, edge_len)
    padded = jnp.pad(planes, ((0, 0), (0, 0), (1, 1), (1, 1)))
    terms = []
    for kernel_row in range(3):
        for kernel_col in range(3):
            shifted = padded[
                :, :, kernel_row : kernel_row + edge_len, kernel_col : kernel_col + edge_len
            ].reshape(images, channels, pixels)
            terms.append(
                jnp.einsum("nop,ncp->oc", out_grad, shifted, preferred_element_type=jnp.float32)
            )
    return jnp.stack(terms)


def apply_back(out_grad, weights, kind):
    if kind == "conv":
        return conv_input_grad(out_grad, weights)
    return jnp.einsum("oc,nop->ncp", weights, out_grad, preferred_element_type=jnp.float32)


def back_through(groups):
    partials = []
    for group in groups:
        total = None
        for term in group:
            value = apply_back(term[0], term[1], term[2])
            total = value if total is None else total + value
        partials.append(total)
    return spread(partials)


def shards(
    feat_fine,
    feat_mid,
    feat_coarse,
    image_units,
    stem_fine,
    stem_mid,
    stem_coarse,
    conv_weights,
    norm_gains,
    norm_shifts,
    class_weights,
    class_bias,
    box_weights,
    box_bias,
    class_cot,
    box_cot,
):
    features = [feat_fine, feat_mid, feat_coarse]
    stems = [stem_fine, stem_mid, stem_coarse]
    masks = [level_mask(image_units, level_id) for level_id in range(3)]
    starts = [0, feat_fine.shape[2], feat_fine.shape[2] + feat_mid.shape[2]]
    saved = {}

    def run_group(levels):
        count_lv = len(levels)
        group_masks = [masks[level_id] for level_id in levels]
        doubled = group_masks + group_masks

        def gains_of(layer_id):
            return [norm_gains[level_id, layer_id] for level_id in levels]

        def shifts_of(layer_id):
            return [norm_shifts[level_id, layer_id] for level_id in levels]

        level_inputs = [features[level_id] for level_id in levels]
        gathered_in = share(level_inputs)
        stem_out = [
            jnp.einsum(
                "oc,ncp->nop",
                stems[level_id],
                gathered_in[order_id],
                preferred_element_type=jnp.float32,
            )
            for order_id, level_id in enumerate(levels)
        ]
        stem_act, stem_kept = norm_forward(stem_out, group_masks, gains_of(0), shifts_of(0))
        gathered_stem = share(stem_act)
        first_out = [
            conv_apply(gathered_stem[order_id], conv_weights[level_id, 0])
            for order_id, level_id in enumerate(levels)
        ]
        first_out = first_out + [
            conv_apply(gathered_stem[order_id], conv_weights[level_id, 2])
            for order_id, level_id in enumerate(levels)
        ]
        first_act, first_kept = norm_forward(
            first_out, doubled, gains_of(1) + gains_of(3), shifts_of(1) + shifts_of(3)
        )
        gathered_first = share(first_act)
        second_out = [
            conv_apply(gathered_first[order_id], conv_weights[level_id, 1])
            for order_id, level_id in enumerate(levels)
        ]
        second_out = second_out + [
            conv_apply(gathered_first[count_lv + order_id], conv_weights[level_id, 3])
            for order_id, level_id in enumerate(levels)
        ]
        second_act, second_kept = norm_forward(
            second_out, doubled, gains_of(2) + gains_of(4), shifts_of(2) + shifts_of(4)
        )
        gathered_class = share(second_act[:count_lv])
        box_parts = [
            jnp.einsum(
                "kc,ncp->nkp",
                box_weights[level_id],
                second_act[count_lv + order_id],
                preferred_element_type=jnp.float32,
            )
            for order_id, level_id in enumerate(levels)
        ]
        box_full = box_total(box_parts)
        for order_id, level_id in enumerate(levels):
            valid_mask = group_masks[order_id]
            logits = jnp.einsum(
                "kc,ncp->nkp",
                class_weights[level_id],
                gathered_class[order_id],
                preferred_element_type=jnp.float32,
            )
            saved[level_id, "class"] = (
                (logits + class_bias[level_id][None, :, None]) * valid_mask
            ).astype(jnp.bfloat16)
            saved[level_id, "box"] = (
                (box_full[order_id] + box_bias[level_id][None, :, None]) * valid_mask
            ).astype(jnp.bfloat16)
        class_groups = []
        box_back = []
        for order_id, level_id in enumerate(levels):
            valid_mask = group_masks[order_id]
            pixels = valid_mask.shape[2]
            begin = starts[level_id]
            class_seed = (
                class_cot[:, :, begin : begin + pixels].astype(jnp.float32) * valid_mask
            ).astype(jnp.bfloat16)
            box_seed = (
                box_cot[:, :, begin : begin + pixels].astype(jnp.float32) * valid_mask
            ).astype(jnp.bfloat16)
            saved[level_id, "class_w"] = jnp.einsum(
                "nkp,ncp->kc",
                class_seed,
                gathered_class[order_id],
                preferred_element_type=jnp.float32,
            )
            saved[level_id, "class_b"] = jnp.sum(class_seed.astype(jnp.float32), axis=(0, 2))
            saved[level_id, "box_w"] = jnp.einsum(
                "nkp,ncp->kc",
                box_seed,
                second_act[count_lv + order_id],
                preferred_element_type=jnp.float32,
            )
            saved[level_id, "box_b"] = jnp.sum(box_seed.astype(jnp.float32), axis=(0, 2))
            class_groups.append([(class_seed, class_weights[level_id], "dense")])
            box_back.append(
                jnp.einsum(
                    "kc,nkp->ncp",
                    box_weights[level_id],
                    box_seed,
                    preferred_element_type=jnp.float32,
                )
            )
        second_grads = back_through(class_groups) + box_back
        second_dy, second_gain, second_shift = norm_backward(
            second_grads,
            second_out,
            second_kept,
            doubled,
            gains_of(2) + gains_of(4),
            shifts_of(2) + shifts_of(4),
        )
        first_groups = []
        for order_id, level_id in enumerate(levels):
            saved[level_id, 1] = conv_weight_grad(second_dy[order_id], gathered_first[order_id])
            saved[level_id, 3] = conv_weight_grad(
                second_dy[count_lv + order_id], gathered_first[count_lv + order_id]
            )
            first_groups.append([(second_dy[order_id], conv_weights[level_id, 1], "conv")])
        for order_id, level_id in enumerate(levels):
            first_groups.append(
                [(second_dy[count_lv + order_id], conv_weights[level_id, 3], "conv")]
            )
        first_grads = back_through(first_groups)
        first_dy, first_gain, first_shift = norm_backward(
            first_grads,
            first_out,
            first_kept,
            doubled,
            gains_of(1) + gains_of(3),
            shifts_of(1) + shifts_of(3),
        )
        stem_groups = []
        for order_id, level_id in enumerate(levels):
            saved[level_id, 0] = conv_weight_grad(first_dy[order_id], gathered_stem[order_id])
            saved[level_id, 2] = conv_weight_grad(
                first_dy[count_lv + order_id], gathered_stem[order_id]
            )
            stem_groups.append(
                [
                    (first_dy[order_id], conv_weights[level_id, 0], "conv"),
                    (first_dy[count_lv + order_id], conv_weights[level_id, 2], "conv"),
                ]
            )
        stem_grads = back_through(stem_groups)
        stem_dy, stem_gain, stem_shift = norm_backward(
            stem_grads, stem_out, stem_kept, group_masks, gains_of(0), shifts_of(0)
        )
        input_groups = []
        for order_id, level_id in enumerate(levels):
            saved[level_id, "stem"] = jnp.einsum(
                "nop,ncp->oc",
                stem_dy[order_id],
                gathered_in[order_id],
                preferred_element_type=jnp.float32,
            )
            input_groups.append([(stem_dy[order_id], stems[level_id], "dense")])
        input_grads = back_through(input_groups)
        for order_id, level_id in enumerate(levels):
            saved[level_id, "input"] = input_grads[order_id].astype(jnp.bfloat16)
            saved[level_id, "gains"] = jnp.stack(
                [
                    stem_gain[order_id],
                    first_gain[order_id],
                    second_gain[order_id],
                    first_gain[count_lv + order_id],
                    second_gain[count_lv + order_id],
                ]
            )
            saved[level_id, "shifts"] = jnp.stack(
                [
                    stem_shift[order_id],
                    first_shift[order_id],
                    second_shift[order_id],
                    first_shift[count_lv + order_id],
                    second_shift[count_lv + order_id],
                ]
            )

    for level_id in range(3):
        run_group([level_id])
    class_out = jnp.concatenate([saved[level_id, "class"] for level_id in range(3)], axis=2)
    box_out = jnp.concatenate([saved[level_id, "box"] for level_id in range(3)], axis=2)
    conv_grad = jnp.stack(
        [jnp.stack([saved[level_id, layer_id] for layer_id in range(4)]) for level_id in range(3)]
    )
    gains_grad = jnp.stack([saved[level_id, "gains"] for level_id in range(3)])
    shifts_grad = jnp.stack([saved[level_id, "shifts"] for level_id in range(3)])
    totals = lax.psum(
        (
            saved[0, "stem"],
            saved[1, "stem"],
            saved[2, "stem"],
            conv_grad,
            jnp.stack([saved[level_id, "class_w"] for level_id in range(3)]),
            jnp.stack([saved[level_id, "class_b"] for level_id in range(3)]),
            jnp.stack([saved[level_id, "box_w"] for level_id in range(3)]),
            jnp.stack([saved[level_id, "box_b"] for level_id in range(3)]),
        ),
        "dp",
    )
    return (
        class_out,
        box_out,
        saved[0, "input"],
        saved[1, "input"],
        saved[2, "input"],
        totals[0],
        totals[1],
        totals[2],
        totals[3],
        gains_grad,
        shifts_grad,
        totals[4],
        totals[5],
        totals[6],
        totals[7],
    )


def solution(mesh):
    placed = (
        P("dp", "chan", None),
        P("dp", "chan", None),
        P("dp", "chan", None),
        P("dp"),
        P("chan", None),
        P("chan", None),
        P("chan", None),
        P(None, None, None, "chan", None),
        P(None, None, "chan"),
        P(None, None, "chan"),
        P(None, "chan", None),
        P(None, "chan"),
        P(None, None, "chan"),
        P(),
        P("dp", "chan", None),
        P("dp", None, None),
    )
    return jax.shard_map(
        shards,
        mesh=mesh,
        in_specs=placed,
        out_specs=(
            P("dp", "chan", None),
            P("dp", None, None),
            P("dp", "chan", None),
            P("dp", "chan", None),
            P("dp", "chan", None),
            P("chan", None),
            P("chan", None),
            P("chan", None),
            P(None, None, None, "chan", None),
            P(None, None, "chan"),
            P(None, None, "chan"),
            P(None, "chan", None),
            P(None, "chan"),
            P(None, None, "chan"),
            P(),
        ),
        check_vma=False,
    )
```

profile of v0, /device:TPU:2, one launch (start us, length us, event | category | flops | bytes accessed | tf_op | source)
XLA Modules:
  0.0 3332.9 jit_solution(275381613143250082)
XLA Ops:
  12.9 14.6 convert_element_type.1035
  28.2 109.1 %convert_element_type.1031 = bf16[1,204800]{0,1:T(8,128)(2,1)} reshape(bf16[1,128,1600]{2,1,0:T(8,128)(2,1)S(1)} %copy.713) | data formatting | bytes 819200 | tf_op jit(solution)/shard_map/convert_element_type | solution.py:52
  138.8 9.1 all_gather.40
  149.9 11.7 all_gather.36
  161.6 8.5 reduce.41
  172.5 22.3 all-reduce.15
  197.5 5.6 all_gather.41
  209.9 9.2 all_gather.37
  219.1 8.5 reduce.42
  243.2 7.5 all_gather.44
  258.7 18.5 all-reduce.14
  284.4 9.1 all_gather.42
  317.4 22.7 all_gather.38
  340.0 17.0 reduce.43
  367.1 3.4 reshape.16075
  404.4 3.5 reshape_reshape.30
  409.1 3.4 reshape_reshape.31
  422.5 5.4 all_gather.45
  441.0 19.6 all-reduce.13
  470.9 6.0 all_gather.46
  499.0 3.7 fusion.516
  504.2 7.0 all_gather.43
  515.8 14.0 all_gather.39
  529.8 8.5 reduce.44
  551.0 5.5 pad_slice_fusion.16
  586.7 5.5 pad_slice_fusion.8
  621.9 5.5 pad_slice_fusion
  650.1 3.6 pad_slice_fusion.40
  673.9 3.6 pad_slice_fusion.32
  697.7 4.0 pad_slice_fusion.24
  780.8 3.3 copy.919
  785.9 9.7 copy.911
  797.6 17.9 all-reduce.12
  833.3 15.8 copy.950
  849.2 18.3 bitcast_bitcast_fusion.1
  884.0 61.1 %copy.948 = bf16[1,409600]{0,1:T(8,128)(2,1)} copy(bf16[1,409600]{1,0:T(2,128)(2,1)S(1)} %bitcast.1923) | data formatting | bytes 1638400
  945.2 70.0 %bitcast_bitcast_fusion = bf16[409600,1]{1,0:T(8,128)(2,1)} fusion(bf16[1,409600]{0,1:T(8,128)(2,1)} %copy.948), kind=kLoop, calls=%fused_computation | loop fusion | bytes 1638400
  1020.5 5.5 all_gather.47
  1039.9 13.7 all-reduce.17
  1069.4 6.3 copy.921
  1078.2 674.6 %reduce-scatter.39.cloned.1.call-done = bf16[102400,1]{1,0:T(8,128)(2,1)} async-done(((bf16[409600,1]{1,0:T(8,128)(2,1)}), bf16[102400,1]{1,0:T(8,128)(2,1)}) %reduce-scatter.39.cloned.1.call-update) | async-done | bytes 204816
  1752.8 18.6 copy.913
  1775.4 21.8 all-reduce.11
  1803.3 4.8 copy.952
  1808.1 6.0 bitcast_bitcast_fusion.2
  1820.1 10.2 convert_element_type.1037
  1835.4 4.1 add_multiply_fusion.1
  1847.2 39.8 %convert_element_type.1033 = bf16[1,204800]{0,1:T(8,128)(2,1)} reshape(bf16[1,128,40,40]{3,2,1,0:T(8,128)(2,1)S(1)} %copy.735) | data formatting | bytes 819200 | tf_op jit(solution)/shard_map/convert_element_type | solution.py:52
  1892.8 3.3 convert_reduce_fusion.1
  1916.3 90.6 %reduce-scatter.49.cloned.1.call-done = bf16[12800,1]{1,0:T(8,128)(2,1)} async-done(((bf16[51200,1]{1,0:T(8,128)(2,1)}), bf16[12800,1]{1,0:T(8,128)(2,1)}) %reduce-scatter.49.cloned.1.call-update) | async-done | bytes 25616
  2006.9 3.4 copy.923
  2010.8 355.7 %reduce-scatter.41.cloned.1.call-done = bf16[51200,1]{1,0:T(8,128)(2,1)} async-done(((bf16[204800,1]{1,0:T(8,128)(2,1)}), bf16[51200,1]{1,0:T(8,128)(2,1)}) %reduce-scatter.41.cloned.1.call-update) | async-done | bytes 102416
  2366.6 9.7 copy.915
  2377.4 22.1 all-reduce.10
  2403.9 3.7 convert_element_type.1041
  2417.9 28.0 convert_element_type.1038
  2449.0 109.3 %convert_element_type.1034 = bf16[1,204800]{0,1:T(8,128)(2,1)} reshape(bf16[1,128,1600]{2,1,0:T(8,128)(2,1)S(1)} %copy.736) | data formatting | bytes 819200 | tf_op jit(solution)/shard_map/convert_element_type | solution.py:52
  2559.9 8.0 convert_element_type.1042
  2577.3 90.1 %reduce-scatter.59.cloned.1.call-done = bf16[12800,1]{1,0:T(8,128)(2,1)} async-done(((bf16[51200,1]{1,0:T(8,128)(2,1)}), bf16[12800,1]{1,0:T(8,128)(2,1)}) %reduce-scatter.59.cloned.1.call-update) | async-done | bytes 25616
  2670.8 186.4 %reduce-scatter.51.cloned.1.call-done = bf16[25600,1]{1,0:T(8,128)(2,1)} async-done(((bf16[102400,1]{1,0:T(8,128)(2,1)}), bf16[25600,1]{1,0:T(8,128)(2,1)}) %reduce-scatter.51.cloned.1.call-update) | async-done | bytes 51216
  2857.2 4.6 bitcast_reduce_fusion.1
  2862.6 354.2 %reduce-scatter.43.cloned.1.call-done = bf16[51200,1]{1,0:T(8,128)(2,1)} async-done(((bf16[204800,1]{1,0:T(8,128)(2,1)}), bf16[51200,1]{1,0:T(8,128)(2,1)}) %reduce-scatter.43.cloned.1.call-update) | async-done | bytes 102416
  3216.8 6.7 bitcast_reduce_fusion
  3224.3 94.5 %all-reduce.23.cloned.1.call-done = (f32[32,512]{1,0:T(8,128)}, f32[3,4,9,32,128]{4,3,2,1,0:T(8,128)}) async-done(((f32[32,512]{1,0:T(8,128)}, f32[3,4,9,32,128]{4,3,2,1,0:T(8,128)}), (f32[32,512]{1,0:T(8,128)}, f32[3,4,9,32,128]{4,3,2,1,0:T(8,128)})) %all-reduce.23.cloned.1.call-update) | async-done | bytes 1835024 | tf_op jit(solution)/shard_map/psum | solution.py:413
  (2196 shorter events, 561.1 us)
Async XLA Ops:
  7.2 250.6 %copy-start = (bf16[32,512]{1,0:T(8,128)(2,1)S(1)}, bf16[32,512]{1,0:T(8,128)(2,1)}, u32[]{:S(2)}) copy-start(bf16[32,512]{1,0:T(8,128)(2,1)} %param.22) | copy-start | bytes 98308
  7.2 770.5 %reduce-scatter.53.cloned.1.call-start = ((), (), s32[]{:S(2)}) async-start(), calls=%async_computation.20 | async-start | bytes 4096000
  7.9 459.5 %copy-start.288 = (f32[100]{0:T(128)}, f32[100]{0:T(128)S(1)}, u32[]{:S(2)}) copy-start(f32[100]{0:T(128)S(1)} %and_convert_fusion) | copy-start | bytes 1204
  11.6 769.2 %reduce-scatter.45.cloned.1.call-start = ((), (), s32[]{:S(2)}) async-start(), calls=%async_computation.16 | async-start | bytes 16384000
  12.4 499.6 %copy-start.198 = (f32[400]{0:T(512)}, f32[400]{0:T(512)S(1)}, u32[]{:S(2)}) copy-start(f32[400]{0:T(512)S(1)} %fusion.508) | copy-start | bytes 4804
  27.5 758.3 %reduce-scatter.37.cloned.1.call-start = ((), (), s32[]{:S(2)}) async-start(), calls=%async_computation.12 | async-start | bytes 65536000
  137.3 932.2 %reduce-scatter.47.cloned.1.call-start = ((), (), s32[]{:S(2)}) async-start(), calls=%async_computation.17 | async-start | bytes 32768000
  138.6 162.3 %copy-start.161 = (f32[20,20]{0,1:T(8,128)}, f32[20,20]{0,1:T(8,128)S(1)}, u32[]{:S(2)}) copy-start(f32[20,20]{0,1:T(8,128)S(1)} %fusion.449) | copy-start | bytes 4804
  138.6 242.4 %copy-start.96 = (f32[40,40]{0,1:T(8,128)}, f32[40,40]{0,1:T(8,128)S(1)}, u32[]{:S(2)}) copy-start(f32[40,40]{0,1:T(8,128)S(1)} %fusion.420) | copy-start | bytes 19204
  170.5 34.1 %copy-start.21 = (bf16[128,1600]{1,0:T(8,128)(2,1)}, bf16[128,1600]{1,0:T(8,128)(2,1)S(1)}, u32[]{:S(2)}) copy-start(bf16[128,1600]{1,0:T(8,128)(2,1)S(1)} %reshape.15745) | copy-start | bytes 1228804
  171.2 25.5 copy-start.499
  171.2 38.3 %copy-start.495 = (f32[32]{0:T(128)}, f32[32]{0:T(128)S(1)}, u32[]{:S(2)}) copy-start(f32[32]{0:T(128)S(1)} %get-tuple-element.414) | copy-start | bytes 388
  171.9 25.5 copy-start.501
  171.9 37.7 %copy-start.497 = (f32[32]{0:T(128)}, f32[32]{0:T(128)S(1)}, u32[]{:S(2)}) copy-start(f32[32]{0:T(128)S(1)} %get-tuple-element.429) | copy-start | bytes 388
  172.2 25.3 copy-start.165
  172.5 37.1 %copy-start.32 = (f32[1,1600,32]{1,2,0:T(8,128)}, f32[1,1600,32]{1,2,0:T(8,128)S(1)}, u32[]{:S(2)}) copy-start(f32[1,1600,32]{1,2,0:T(8,128)S(1)} %get-tuple-element.528) | copy-start | bytes 614404
  206.0 26.6 copy-start.296
  206.0 30.5 copy-start.294
  207.3 74.5 %copy-start.51 = (f32[1,32,20,20]{1,2,3,0:T(8,128)}, f32[1,32,20,20]{1,2,3,0:T(8,128)S(1)}, u32[]{:S(2)}) copy-start(f32[1,32,20,20]{1,2,3,0:T(8,128)S(1)} %slice_bitcast_fusion.21) | copy-start | bytes 153604
  254.2 27.3 copy-start.185
  282.9 221.0 %copy-start.65 = (f32[1,12800]{1,0:T(1,128)}, f32[1,12800]{1,0:T(1,128)S(1)}, u32[]{:S(2)}) copy-start(f32[1,12800]{1,0:T(1,128)S(1)} %mul.7072) | copy-start | bytes 153604
  311.7 203.4 %copy-start.1 = (f32[1,51200]{1,0:T(1,128)}, f32[1,51200]{1,0:T(1,128)S(1)}, u32[]{:S(2)}) copy-start(f32[1,51200]{1,0:T(1,128)S(1)} %mul.7010) | copy-start | bytes 614404
  771.2 45.6 %copy-start.553 = (f32[32]{0:T(128)}, f32[32]{0:T(128)S(1)}, u32[]{:S(2)}) copy-start(f32[32]{0:T(128)S(1)} %fusion.515) | copy-start | bytes 388
  771.8 49.7 %copy-start.610 = (f32[32]{0:T(128)}, f32[32]{0:T(128)S(1)}, u32[]{:S(2)}) copy-start(f32[32]{0:T(128)S(1)} %fusion.518) | copy-start | bytes 388
  867.5 885.3 %reduce-scatter.39.cloned.1.call-start = ((), (), s32[]{:S(2)}) async-start(), calls=%async_computation.13 | async-start | bytes 131072000
  945.1 70.2 %copy-start.624 = (f32[2,32]{1,0:T(2,128)S(1)}, f32[2,32]{1,0:T(2,128)}, u32[]{:S(2)}) copy-start(f32[2,32]{1,0:T(2,128)} %get-tuple-element.180) | copy-start | bytes 772
  945.1 70.2 %copy-start.625 = (f32[2,32]{1,0:T(2,128)S(1)}, f32[2,32]{1,0:T(2,128)}, u32[]{:S(2)}) copy-start(f32[2,32]{1,0:T(2,128)} %get-tuple-element.181) | copy-start | bytes 772
  945.1 72.9 %copy-start.242 = (f32[1,32,10,10]{1,0,3,2:T(1,128)S(1)}, f32[1,32,10,10]{1,0,3,2:T(1,128)}, u32[]{:S(2)}) copy-start(f32[1,32,10,10]{1,0,3,2:T(1,128)} %copy-done.241) | copy-start | bytes 38404
  945.1 72.9 %copy-start.348 = (f32[10,10]{1,0:T(8,128)S(1)}, f32[10,10]{1,0:T(8,128)}, u32[]{:S(2)}) copy-start(f32[10,10]{1,0:T(8,128)} %copy-done.346) | copy-start | bytes 1204
  945.1 72.9 %copy-start.558 = (f32[32]{0:T(128)S(1)}, f32[32]{0:T(128)}, u32[]{:S(2)}) copy-start(f32[32]{0:T(128)} %get-tuple-element.401) | copy-start | bytes 388
  945.1 72.9 %copy-start.559 = (f32[32]{0:T(128)S(1)}, f32[32]{0:T(128)}, u32[]{:S(2)}) copy-start(f32[32]{0:T(128)} %get-tuple-element.416) | copy-start | bytes 388
  945.1 73.2 %copy-start.289 = (f32[100]{0:T(128)S(1)}, f32[100]{0:T(128)}, u32[]{:S(2)}) copy-start(f32[100]{0:T(128)} %copy-done.288) | copy-start | bytes 1204
  945.1 75.2 %copy-start.192 = (f32[1,3200]{1,0:T(1,128)S(1)}, f32[1,3200]{1,0:T(1,128)}, u32[]{:S(2)}) copy-start(f32[1,3200]{1,0:T(1,128)} %copy-done.191) | copy-start | bytes 38404
  945.1 75.2 %copy-start.280 = (f32[1,3200]{1,0:T(1,128)S(1)}, f32[1,3200]{1,0:T(1,128)}, u32[]{:S(2)}) copy-start(f32[1,3200]{1,0:T(1,128)} %reshape.15766) | copy-start | bytes 38404
  945.1 75.2 %copy-start.339 = (f32[1,3200]{1,0:T(1,128)S(1)}, f32[1,3200]{1,0:T(1,128)}, u32[]{:S(2)}) copy-start(f32[1,3200]{1,0:T(1,128)} %add.3346) | copy-start | bytes 38404
  945.1 75.2 %copy-start.340 = (f32[1,3200]{1,0:T(1,128)S(1)}, f32[1,3200]{1,0:T(1,128)}, u32[]{:S(2)}) copy-start(f32[1,3200]{1,0:T(1,128)} %mul.7157) | copy-start | bytes 38404
  945.1 82.0 %copy-start.522 = (f32[32]{0:T(128)S(1)}, f32[32]{0:T(128)}, u32[]{:S(2)}) copy-start(f32[32]{0:T(128)} %copy-done.521) | copy-start | bytes 388
  945.2 82.3 %copy-start.524 = (f32[32]{0:T(128)S(1)}, f32[32]{0:T(128)}, u32[]{:S(2)}) copy-start(f32[32]{0:T(128)} %copy-done.523) | copy-start | bytes 388
  1039.2 873.5 %reduce-scatter.55.cloned.1.call-start = ((), (), s32[]{:S(2)}) async-start(), calls=%async_computation.21 | async-start | bytes 8192000
  1774.5 23.9 copy-start.240
  1774.5 23.9 copy-start.305
  1814.1 192.8 %reduce-scatter.49.cloned.1.call-start = ((), (), s32[]{:S(2)}) async-start(), calls=%async_computation.18 | async-start | bytes 16384000
  1847.2 39.8 %copy-start.530 = (f32[32]{0:T(128)S(1)}, f32[32]{0:T(128)}, u32[]{:S(2)}) copy-start(f32[32]{0:T(128)} %copy-done.529) | copy-start | bytes 388
  1847.2 40.2 %copy-start.532 = (f32[32]{0:T(128)S(1)}, f32[32]{0:T(128)}, u32[]{:S(2)}) copy-start(f32[32]{0:T(128)} %copy-done.531) | copy-start | bytes 388
  1908.2 458.4 %reduce-scatter.41.cloned.1.call-start = ((), (), s32[]{:S(2)}) async-start(), calls=%async_computation.14 | async-start | bytes 65536000
  1909.3 536.7 %reduce-scatter.57.cloned.1.call-start = ((), (), s32[]{:S(2)}) async-start(), calls=%async_computation.22 | async-start | bytes 4096000
  2376.3 24.4 copy-start.238
  2376.3 24.4 copy-start.293
  2376.4 24.3 copy-start.350
  2376.4 24.3 copy-start.576
  2407.8 150.4 %all-reduce.21.cloned.1.call-start = ((), (), s32[]{:S(2)}) async-start(), calls=%async_computation.24 | async-start | bytes 206848 | tf_op jit(solution)/shard_map/psum | solution.py:115
  2417.9 29.7 copy-start.257
  2417.9 29.7 copy-start.538
  2417.9 29.7 copy-start.540
  2417.9 29.7 copy-start.542
  2417.9 29.7 copy-start.557
  2417.9 30.5 copy-start.345
  2448.4 219.0 %reduce-scatter.59.cloned.1.call-start = ((), (), s32[]{:S(2)}) async-start(), calls=%async_computation.23 | async-start | bytes 16384000
  2449.0 109.3 %copy-start.634 = (f32[32]{0:T(128)S(1)}, f32[32]{0:T(128)}, u32[]{:S(2)}) copy-start(f32[32]{0:T(128)} %get-tuple-element.213) | copy-start | bytes 388
  2568.0 289.2 %reduce-scatter.51.cloned.1.call-start = ((), (), s32[]{:S(2)}) async-start(), calls=%async_computation.19 | async-start | bytes 32768000
  2568.5 648.3 %reduce-scatter.43.cloned.1.call-start = ((), (), s32[]{:S(2)}) async-start(), calls=%async_computation.15 | async-start | bytes 65536000
  2569.3 749.5 %all-reduce.23.cloned.1.call-start = ((), (), s32[]{:S(2)}) async-start(), calls=%async_computation.25 | async-start | bytes 3670016 | tf_op jit(solution)/shard_map/psum | solution.py:413
  2862.6 456.2 %copy-start.372 = (f32[32,128]{1,0:T(8,128)S(1)}, f32[32,128]{1,0:T(8,128)}, u32[]{:S(2)}) copy-start(f32[32,128]{1,0:T(8,128)} %get-tuple-element.554) | copy-start | bytes 49156
  2862.6 456.8 %copy-start.351 = (f32[32,256]{1,0:T(8,128)S(1)}, f32[32,256]{1,0:T(8,128)}, u32[]{:S(2)}) copy-start(f32[32,256]{1,0:T(8,128)} %get-tuple-element.555) | copy-start | bytes 98308
  (592 other events, 3040.6 us)
Sparse Core Ops, SparseCore 0:
  11.7 38.8 reduce-scatter.52
  53.3 107.2 reduce-scatter.44
  163.4 375.9 reduce-scatter.36
  867.6 186.1 reduce-scatter.46
  1056.5 696.2 reduce-scatter.38
  1814.2 56.1 reduce-scatter.54
  1908.3 98.5 reduce-scatter.48
  2009.7 356.8 reduce-scatter.40
  2407.8 34.8 reduce-scatter.56
  2448.6 71.8 all-reduce.20
  2568.1 99.2 reduce-scatter.58
  2669.9 187.2 reduce-scatter.50
  2860.0 356.7 reduce-scatter.42
  3221.6 97.2 all-reduce.22
where the time goes:
time: 3350 us; the launch traced here: 3330 us
  waiting for transfers between devices  1850 us (55%)
  local copies, waits for them, and re-layouts  1010 us (30%)
  blocking collectives  249 us (7%)
  other arithmetic  128 us (4%)
  matrix products  77.9 us (2%)
    unnamed x26, waiting for transfers between devices  1750 us
    convert_element_type x22, local copies, waits for them, and re-layouts, spread(): flattened.astype(jnp.bfloat16)  330 us
    unnamed x1324, local copies, waits for them, and re-layouts  280 us
    all_gather x12, blocking collectives, share(): lax.all_gather(flattened, 'chan', axis=1, tiled=True)  113 us
    another operation x76, local copies, waits for them, and re-layouts  103 us
    psum x1, waiting for transfers between devices, shards(): lax.psum((saved[0, 'stem'], saved[1, 'stem'], saved[2, 'stem'], conv_grad...  94.5 us
    slice x33, local copies, waits for them, and re-layouts, conv_weight_grad(): padded[:, :, kernel_row:kernel_row + edge_len, kernel_col:kernel_col + ed...  92.5 us
    psum x4, blocking collectives, norm_forward(): first_sum, second, counts = lax.psum((first_sum, second, counts), 'dp')  78.3 us
  transfers between devices with their start and end apart: 14, of which 7 were waited for; matrix products, arithmetic and copies ran while one was open for 32% of the time, Pallas kernels for 0%

commit v1 on v0

v1 whole, which is shorter than its diff:
```python
import functools

import jax
import jax.numpy as jnp
from jax import lax
from jax.experimental import pallas as pl
from jax.experimental.pallas import tpu as pltpu
from jax.sharding import PartitionSpec as P

BF = jnp.bfloat16
F32 = jnp.float32
EPS = 0.001
ST = 48
ROWS = 40
PX = ST * ROWS
CR = 8
CH = CR * ST
NCH = ROWS // CR
SLOT = (0, 0, 0, 1, 1)
CUT = 24 * ST
CP = 1664
MID = 512
E0, E1, E2 = 40, 20, 10
WIDE = CP + 768
CLS = CP + 512
NT = (((1,), (1,)), ((), ()))
TN = (((0,), (0,)), ((), ()))


def dot(a, b, dims=(((1,), (0,)), ((), ()))):
    return lax.dot_general(a, b, dims, preferred_element_type=F32)


def limits(meta, slot):
    group, units = meta[0], meta[3]
    if slot == 0:
        edge = jnp.where(group == 0, 4 * units, 2 * units)
        return edge, edge
    return (
        jnp.where(group == 0, 4 * units, 24 + units),
        jnp.where(group == 0, 4 * units, units),
    )


def mask_of(meta, j):
    row_end, col_end = limits(meta, SLOT[j])
    row = lax.broadcasted_iota(jnp.int32, (CR, ST, 128), 0) + CR * j
    col = lax.broadcasted_iota(jnp.int32, (CR, ST, 128), 1)
    inside = (row < row_end) & (col < col_end)
    return jnp.where(inside, 1.0, 0.0).reshape(CH, 128)


def pick(meta, first, second):
    total = first + second
    return jnp.where(meta[0] == 0, total, first), jnp.where(meta[0] == 0, total, second)


def level_rows(meta, base, layer):
    fine = meta[0] == 0
    return base + layer + jnp.where(fine, 0, 5), base + layer + jnp.where(fine, 0, 10)


def norm_constants(meta, st, par, layer, cst):
    total = jnp.sum(st[...], axis=0)
    row = [total[i : i + 1] for i in range(6)]
    first = pick(meta, row[0], row[1])
    second = pick(meta, row[2], row[3])
    count = pick(meta, row[4], row[5])
    gain_at = level_rows(meta, 0, layer)
    shift_at = level_rows(meta, 16, layer)
    for s in range(2):
        rn = 1.0 / count[s]
        mean = first[s] * rn
        inv = lax.rsqrt(second[s] * rn - mean * mean + EPS)
        cst[s : s + 1] = mean
        cst[2 + s : 3 + s] = inv
        cst[4 + s : 5 + s] = par[pl.ds(gain_at[s], 1), :]
        cst[6 + s : 7 + s] = par[pl.ds(shift_at[s], 1), :]
        cst[8 + s : 9 + s] = rn
        cst[10 + s : 11 + s] = count[s]
    cst[12:16] = jnp.zeros((4, 128), F32)


def normed(cst, y, s):
    xhat = (y - cst[s : s + 1]) * cst[2 + s : 3 + s]
    return xhat, xhat * cst[4 + s : 5 + s] + cst[6 + s : 7 + s]


def sigmoid(z):
    return 0.5 * jnp.tanh(0.5 * z) + 0.5


def slope(z):
    s = sigmoid(z)
    return s * (1.0 + z * (1.0 - s))


def spread_out(st, rows):
    block = jnp.concatenate(rows + [jnp.zeros((8 - len(rows), 128), F32)], axis=0)
    st[...] = jnp.broadcast_to(block[None], st.shape)


def colsum(v):
    return jnp.sum(v, axis=0, keepdims=True)


def guard(field, shifts):
    field[0:8] = jnp.zeros((8, 128), F32)
    field[8 + PX : 16 + PX] = jnp.zeros((8, 128), F32)
    for k in range(3):
        shifts[k, 0:ST] = jnp.zeros((ST, 128), BF)
        shifts[k, ST + PX :] = jnp.zeros((ST, 128), BF)


def fill_shifts(field, shifts):
    for k in range(3):
        for j in range(NCH):
            at = 8 + CH * j + k - 1
            shifts[k, ST + CH * j : ST + CH * (j + 1)] = field[at : at + CH].astype(BF)


def taps(shifts, begin, size, back=False):
    parts = []
    for kr in range(3):
        for kc in range(3):
            k, r = (2 - kc, 1 - kr) if back else (kc, kr - 1)
            at = ST + begin + ST * r
            parts.append(shifts[k, at : at + size])
    return jnp.concatenate(parts, axis=1)


def slices_of(meta):
    c = meta[2]
    return (c, c ^ 2, c ^ 1, c ^ 3)


def at32(s, extra=0):
    return pl.ds(pl.multiple_of(32 * s + extra, 32), 32)


def weight_slot(meta, j):
    return jnp.where(meta[0] == 0, 0, SLOT[j])


def to_compact(meta, canvas, out):
    @pl.when(meta[0] == 0)
    def _():
        for r in range(E0):
            out[E0 * r : E0 * (r + 1)] = canvas[ST * r : ST * r + E0]

    @pl.when(meta[0] == 1)
    def _():
        for r in range(E1):
            out[E1 * r : E1 * (r + 1)] = canvas[ST * r : ST * r + E1]
        for r in range(E2):
            at = CUT + ST * r
            out[MID + E2 * r : MID + E2 * (r + 1)] = canvas[at : at + E2]


def to_canvas(meta, compact, out):
    @pl.when(meta[0] == 0)
    def _():
        for r in range(E0):
            out[ST * r : ST * r + E0] = compact[E0 * r : E0 * (r + 1)]

    @pl.when(meta[0] == 1)
    def _():
        for r in range(E1):
            out[ST * r : ST * r + E1] = compact[E1 * r : E1 * (r + 1)]
        for r in range(E2):
            at = CUT + ST * r
            out[at : at + E2] = compact[MID + E2 * r : MID + E2 * (r + 1)]


def load_inputs(meta, pieces, feat, stem):
    for s, u in zip(slices_of(meta), pieces):

        @pl.when(meta[0] == 0)
        def _():
            feat[at32(s), :] = u[:, 0:CP]
            stem[at32(s), 0:128] = u[:, CP : CP + 128]

        @pl.when(meta[0] == 1)
        def _():
            for i in range(2):
                at = pl.ds(pl.multiple_of(64 * s + 32 * i, 32), 32)
                feat[at, 0:MID] = u[:, MID * i : MID * (i + 1)]
            for i in range(4):
                at = pl.ds(pl.multiple_of(128 * s + 32 * i, 32), 32)
                feat[at, MID : MID + 128] = u[:, 1024 + 128 * i : 1152 + 128 * i]
            stem[at32(s), :] = u[:, CP : CP + 768]


def stem_kernel(meta, u0, u1, u2, u3, y, st, feat, stem, flat):
    load_inputs(meta, (u0, u1, u2, u3), feat, stem)
    y[...] = jnp.zeros((PX, 128), F32)

    @pl.when(meta[0] == 0)
    def _():
        flat[...] = dot(stem[:, 0:128], feat[0:128, :]).T

    @pl.when(meta[0] == 1)
    def _():
        flat[0:MID] = dot(stem[:, 0:256], feat[0:256, 0:MID]).T
        flat[MID : MID + 128] = dot(stem[:, 256:768], feat[0:512, MID : MID + 128]).T

    to_canvas(meta, flat, y)
    sums = [jnp.zeros((1, 128), F32) for _ in range(6)]
    for j in range(NCH):
        m = mask_of(meta, j)
        v = y[CH * j : CH * (j + 1)] * m
        s = SLOT[j]
        sums[s] += colsum(v)
        sums[2 + s] += colsum(v * v)
        sums[4 + s] += colsum(m)
    spread_out(st, sums)


def forward_kernel(first, meta, y, st, *refs):
    if first:
        p0, p1, p2, p3, cnt = refs[:5]
        refs = refs[5:]
    else:
        par, cnt = refs[:2]
        refs = refs[2:]
    w = refs[:4]
    act, out, st_out, cst = refs[4:8]
    refs = refs[8:]
    if first:
        par = refs[0]
        refs = refs[1:]
        par[...] = p0[...] + p1[...] + p2[...] + p3[...]
    field, shifts, weights = refs
    layer = 0 if first else 1 + 2 * meta[1]
    norm_constants(meta, st, par, layer, cst)
    guard(field, shifts)
    for j in range(NCH):
        rows = slice(CH * j, CH * (j + 1))
        _, z = normed(cst, y[rows], SLOT[j])
        v = z * sigmoid(z) * mask_of(meta, j)
        act[rows] = v.astype(BF)
        field[8 + CH * j : 8 + CH * (j + 1)] = v
    fill_shifts(field, shifts)
    for s, piece in zip(slices_of(meta), w):
        for slot in range(2):
            for t in range(9):
                weights[slot, at32(s), 128 * t : 128 * (t + 1)] = piece[slot, t]
    sums = [jnp.zeros((1, 128), F32) for _ in range(4)]
    for j in range(NCH):
        v = dot(taps(shifts, CH * j, CH), weights[weight_slot(meta, j)], NT)
        out[CH * j : CH * (j + 1)] = v
        v = v * mask_of(meta, j)
        s = SLOT[j]
        sums[s] += colsum(v)
        sums[2 + s] += colsum(v * v)
    spread_out(st_out, sums + [cnt[0:1], cnt[1:2]])


def heads_kernel(meta, y, st, par, k0, k1, k2, k3, logits, dz, st_out, cst, gw, cot, wp, x2, field, flat):
    norm_constants(meta, st, par, 2 + 2 * meta[1], cst)
    cot[...] = jnp.zeros((128, CP), BF)
    wp[...] = jnp.zeros((2, 128, 256), BF)

    @pl.when(meta[1] == 0)
    def _():
        for s, k in zip(slices_of(meta), (k0, k1, k2, k3)):
            cot[at32(s), :] = k[:, 0:CP]
            for slot in range(2):
                wp[slot, at32(s), :] = k[:, CP + 256 * slot : CP + 256 * (slot + 1)]

    @pl.when(meta[1] == 1)
    def _():
        cot[0:32, :] = k0[:, 0:CP]
        fine = meta[0] == 0
        for slot in range(2):
            rows = jnp.where(fine, par[32:37], par[37 + 5 * slot : 42 + 5 * slot])
            rows = jnp.concatenate([rows, jnp.zeros((27, 128), F32)], axis=0).astype(BF)
            wp[slot, 0:32, 0:128] = rows
            wp[slot, 0:32, 128:256] = k0[:, CP + 256 * slot + 128 : CP + 256 * (slot + 1)]

    for part in range(2):
        for j in range(NCH):
            m = mask_of(meta, j)
            if part == 0:
                _, z = normed(cst, y[CH * j : CH * (j + 1)], SLOT[j])
                m = z * sigmoid(z) * m
            field[CH * j : CH * (j + 1)] = m
        flat[...] = jnp.zeros((CP, 128), F32)
        to_compact(meta, field, flat)
        x2[:, 128 * part : 128 * (part + 1)] = flat[...].astype(BF)

    @pl.when(meta[0] == 0)
    def _():
        logits[...] = dot(wp[0], x2[...], NT).astype(BF)
        gw[0] = dot(cot[...], x2[...])
        gw[1] = jnp.zeros((128, 256), F32)
        flat[...] = dot(cot[...], wp[0, :, 0:128], TN)

    @pl.when(meta[0] == 1)
    def _():
        logits[...] = jnp.zeros((128, CP), BF)
        for slot, a, b in ((0, 0, MID), (1, MID, MID + 128)):
            logits[:, a:b] = dot(wp[slot], x2[a:b], NT).astype(BF)
            gw[slot] = dot(cot[:, a:b], x2[a:b])
            flat[a:b] = dot(cot[:, a:b], wp[slot, :, 0:128], TN)

    field[...] = jnp.zeros((PX, 128), F32)
    to_canvas(meta, flat, field)
    sums = [jnp.zeros((1, 128), F32) for _ in range(4)]
    for j in range(NCH):
        rows = slice(CH * j, CH * (j + 1))
        s = SLOT[j]
        xhat, z = normed(cst, y[rows], s)
        v = field[rows] * slope(z) * mask_of(meta, j)
        dz[rows] = v
        sums[s] += colsum(v)
        sums[2 + s] += colsum(v * xhat)
    spread_out(st_out, sums)


def grad_sums(meta, total, sums):
    shift = pick(meta, total[0:1], total[1:2])
    gain = pick(meta, total[2:3], total[3:4])
    sums[...] = jnp.concatenate(list(shift) + list(gain) + [jnp.zeros((4, 128), F32)], axis=0)


def input_grad(meta, dz, y, cst, sums, j):
    s = SLOT[j]
    xhat, _ = normed(cst, y[CH * j : CH * (j + 1)], s)
    factor = cst[4 + s : 5 + s] * cst[2 + s : 3 + s]
    mean = (sums[s : s + 1] + xhat * sums[2 + s : 3 + s]) * cst[8 + s : 9 + s]
    return mask_of(meta, j) * factor * (dz - mean)


def backward_kernel(last, meta, dz, y, cst, st, w0, w1, w2, w3, act, y_in, cst_in, *refs):
    grad, st_out, sums, wg, field, shifts, weights, dyt = refs
    grad_sums(meta, jnp.sum(st[...], axis=0), sums)
    guard(field, shifts)
    for j in range(NCH):
        rows = slice(CH * j, CH * (j + 1))
        v = input_grad(meta, dz[rows], y, cst, sums, j)
        field[8 + CH * j : 8 + CH * (j + 1)] = v
        dyt[:, rows] = v.T.astype(BF)
    fill_shifts(field, shifts)
    for s, piece in zip(slices_of(meta), (w0, w1, w2, w3)):
        for slot in range(2):
            for t in range(9):
                weights[slot, at32(s, 128 * t), :] = piece[slot, t]
    total = [jnp.zeros((1, 128), F32) for _ in range(4)]
    for j in range(NCH):
        rows = slice(CH * j, CH * (j + 1))
        s = SLOT[j]
        v = dot(taps(shifts, CH * j, CH, True), weights[weight_slot(meta, j)])
        xhat, z = normed(cst_in, y_in[rows], s)
        d = v * slope(z) * mask_of(meta, j)
        grad[rows] = v.astype(BF) if last else d
        total[s] += colsum(d)
        total[2 + s] += colsum(d * xhat)
    spread_out(st_out, total)
    for j in range(NCH):
        field[8 + CH * j : 8 + CH * (j + 1)] = act[CH * j : CH * (j + 1)].astype(F32)
    fill_shifts(field, shifts)
    for slot, a, b in ((0, 0, CUT), (1, CUT, PX)):
        v = dot(dyt[:, a:b], taps(shifts, a, b - a))
        for t in range(9):
            wg[slot, t] = v[:, 128 * t : 128 * (t + 1)]

    @pl.when(meta[0] == 0)
    def _():
        wg[0] = wg[0] + wg[1]


def final_kernel(meta, d0, d1, y, cst, st0, st1, u0, u1, u2, u3, own, other, gs, sums, feat, stem, field, flat, dyt, gf):
    load_inputs(meta, (u0, u1, u2, u3), feat, stem)
    grad_sums(meta, jnp.sum(st0[...] + st1[...], axis=0), sums)
    for j in range(NCH):
        rows = slice(CH * j, CH * (j + 1))
        _, z = normed(cst, y[rows], SLOT[j])
        v = (d0[rows].astype(F32) + d1[rows].astype(F32)) * slope(z) * mask_of(meta, j)
        field[rows] = input_grad(meta, v, y, cst, sums, j)
    flat[...] = jnp.zeros((CP, 128), F32)
    to_compact(meta, field, flat)
    dyt[...] = flat[...].T.astype(BF)
    c = meta[2]
    outs = ((own, c), (other, c ^ 2))

    @pl.when(meta[0] == 0)
    def _():
        gf[0:128, :] = dot(stem[:, 0:128], dyt[...], TN).astype(BF)
        gs[:, 0:128] = dot(dyt[...], feat[0:128, :], NT)
        gs[:, 128:768] = jnp.zeros((128, 640), F32)
        for out, s in outs:
            out[...] = gf[at32(s), :]

    @pl.when(meta[0] == 1)
    def _():
        gf[0:256, 0:MID] = dot(stem[:, 0:256], dyt[:, 0:MID], TN).astype(BF)
        gf[:, MID : MID + 128] = dot(stem[:, 256:768], dyt[:, MID : MID + 128], TN).astype(BF)
        gs[:, 0:256] = dot(dyt[:, 0:MID], feat[0:256, 0:MID], NT)
        gs[:, 256:768] = dot(dyt[:, MID : MID + 128], feat[:, MID : MID + 128], NT)
        for out, s in outs:
            out[...] = jnp.zeros((32, CP), BF)
            for i in range(2):
                at = pl.ds(pl.multiple_of(64 * s + 32 * i, 32), 32)
                out[:, MID * i : MID * (i + 1)] = gf[at, 0:MID]
            for i in range(4):
                at = pl.ds(pl.multiple_of(128 * s + 32 * i, 32), 32)
                out[:, 1024 + 128 * i : 1152 + 128 * i] = gf[at, MID : MID + 128]


def call(body, outs, scratch, args):
    specs = [pl.BlockSpec(memory_space=pltpu.SMEM)]
    specs += [pl.BlockSpec(memory_space=pltpu.VMEM)] * (len(args) - 1)
    return pl.pallas_call(
        body,
        out_shape=[jax.ShapeDtypeStruct(s, d) for s, d in outs],
        in_specs=specs,
        out_specs=[pl.BlockSpec(memory_space=pltpu.VMEM)] * len(outs),
        scratch_shapes=[pltpu.VMEM(s, d) for s, d in scratch],
        compiler_params=pltpu.CompilerParams(vmem_limit_bytes=56 * 2**20),
    )(*args)


def lanes(v, size):
    return jnp.pad(v, ((0, 0), (0, size - v.shape[1])))


def rows(v, size):
    return jnp.pad(v, ((0, size - v.shape[0]), (0, 0)))


def triple(v):
    high = lax.reduce_precision(v, 8, 7)
    mid = lax.reduce_precision(v - high, 8, 7)
    return jnp.stack([high, mid, v - high - mid], axis=1).astype(BF)


def shards(f0, f1, f2, units, s0, s1, s2, conv, gains, shifts, cw, cb, bw, bb, ccot, bcot):
    dp = lax.axis_size("dp")
    c = lax.axis_index("chan")
    group, branch = c // 2, c % 2
    fine = group == 0
    meta = jnp.stack([group, branch, c, units[0]]).astype(jnp.int32)

    def across(v):
        return lax.ppermute(v, "chan", [(i, i ^ 2) for i in range(4)])

    def beside(v, pairs=((0, 1), (1, 0), (2, 3), (3, 2))):
        return lax.ppermute(v, "chan", list(pairs))

    def exchange(st):
        return lax.all_to_all(st, "dp", 0, 0, tiled=True)

    def bring(keep, send):
        r = across(send)
        return keep, r, beside(keep), beside(r)

    f0, f1, f2 = f0[0], f1[0], f2[0]
    fine_pack = jnp.concatenate([lanes(f0, CP), lanes(s0, 768)], axis=1)
    f1p = lanes(f1, MID)
    f2p = lanes(f2, 128)
    rest_pack = jnp.concatenate(
        [f1p[:32], f1p[32:]] + [f2p[32 * i : 32 * (i + 1)] for i in range(4)] + [jnp.zeros((32, 128), BF), s1, s2], axis=1
    )
    u = bring(jnp.where(fine, fine_pack, rest_pack), jnp.where(fine, rest_pack, fine_pack))

    lane = lax.broadcasted_iota(jnp.int32, (48, 128), 1)
    small = jnp.concatenate(
        [rows(gains.reshape(15, 32), 16), rows(shifts.reshape(15, 32), 16), rows(bw.reshape(15, 32).astype(F32), 16)]
    )
    small = jnp.where(lane // 32 == c, jnp.tile(small, (1, 4)), 0.0)
    par = bring(small, small)

    def pred_pack(cot, first, w_first, b_first, second, w_second, b_second):
        if second is None:
            body = lanes(cot[:, :first], CP)
            w_second, b_second = w_first, b_first
        else:
            body = lanes(jnp.concatenate([lanes(cot[:, first : first + second], MID), cot[:, first + second :]], axis=1), CP)
        return rows(jnp.concatenate([body, w_first, lanes(triple(b_first), 128), w_second, lanes(triple(b_second), 128)], axis=1), 32)

    n0, n1 = f0.shape[1], f1.shape[1]
    fine_cls = pred_pack(ccot[0], n0, cw[0], cb[0], None, None, None)
    rest_cls = pred_pack(ccot[0], n0, cw[1], cb[1], n1, cw[2], cb[2])
    zero = jnp.zeros((5, 128), BF)
    fine_box = pred_pack(bcot[0], n0, zero, bb[0], None, None, None)
    rest_box = pred_pack(bcot[0], n0, zero, bb[1], n1, zero, bb[2])
    own_cls = jnp.where(fine, fine_cls, rest_cls)
    own_box = jnp.where(fine, fine_box, rest_box)
    r = across(jnp.where(fine, rest_cls, fine_cls))
    to_class = ((1, 0), (3, 2))
    pred = (jnp.where(branch == 0, own_cls, own_box), r, beside(own_cls, to_class), beside(r, to_class))

    def conv_pieces(layer):
        mine = lax.dynamic_slice_in_dim(conv[:, layer::2], group, 2, 0)
        theirs = lax.dynamic_slice_in_dim(conv[:, layer::2], 1 - group, 2, 0)
        r = across(theirs)

        def of(v, b):
            return lax.dynamic_index_in_dim(v, b, 1, keepdims=False)

        return of(mine, branch), of(r, branch), beside(of(mine, 1 - branch)), beside(of(r, 1 - branch))

    w1 = conv_pieces(0)
    w2 = conv_pieces(1)

    canvas = (PX, 128)
    stat = (dp, 8, 128)
    half = ((PX + 2 * ST), 128)
    padded = (PX + 16, 128)
    y0, st = call(
        stem_kernel,
        [(canvas, F32), (stat, F32)],
        [((512, CP), BF), ((128, 768), BF), ((CP, 128), F32)],
        (meta, *u),
    )
    cnt = st[0, 4:6]
    st = exchange(st)
    forward_outs = [(canvas, BF), (canvas, F32), (stat, F32), ((16, 128), F32)]
    forward_scratch = [(padded, F32), ((3, *half), BF), ((2, 128, 1152), BF)]
    act0, y1, st, cst0, par = call(
        functools.partial(forward_kernel, True),
        forward_outs + [((48, 128), F32)],
        forward_scratch,
        (meta, y0, st, *par, cnt, *w1),
    )
    st = exchange(st)
    act1, y2, st, cst1 = call(
        functools.partial(forward_kernel, False), forward_outs, forward_scratch, (meta, y1, st, par, cnt, *w2)
    )
    st = exchange(st)
    logits, dz2, st, cst2, gw = call(
        heads_kernel,
        [((128, CP), BF), (canvas, F32), (stat, F32), ((16, 128), F32), ((2, 128, 256), F32)],
        [((128, CP), BF), ((2, 128, 256), BF), ((CP, 256), BF), (canvas, F32), ((CP, 128), F32)],
        (meta, y2, st, par, *pred),
    )
    st = exchange(st)
    backward_scratch = [(padded, F32), ((3, *half), BF), ((2, 1152, 128), BF), ((128, PX), BF)]
    wg_shape = (2, 9, 128, 128)
    dz1, st, sums2, wg2 = call(
        functools.partial(backward_kernel, False),
        [(canvas, F32), (stat, F32), ((8, 128), F32), (wg_shape, F32)],
        backward_scratch,
        (meta, dz2, y2, cst2, st, *w2, act1, y1, cst1),
    )
    st = exchange(st)
    d0, st, sums1, wg1 = call(
        functools.partial(backward_kernel, True),
        [(canvas, BF), (stat, F32), ((8, 128), F32), (wg_shape, F32)],
        backward_scratch,
        (meta, dz1, y1, cst1, st, *w1, act0, y0, cst0),
    )
    d0_other = beside(d0)
    st = exchange(st)
    st_other = beside(st)
    own, other, gs, sums0 = call(
        final_kernel,
        [((32, CP), BF), ((32, CP), BF), ((128, 768), F32), ((8, 128), F32)],
        [((512, CP), BF), ((128, 768), BF), (canvas, F32), ((CP, 128), F32), ((128, CP), BF), ((512, CP), BF)],
        (meta, d0, d0_other, y0, cst0, st, st_other, *u),
    )

    received = across(other)
    g_fine = jnp.where(fine, own, received)
    g_rest = jnp.where(fine, received, own)
    grad_fine = g_fine[:, :n0]
    grad_mid = jnp.concatenate([g_rest[:, 0:n1], g_rest[:, MID : MID + n1]], axis=0)
    grad_coarse = jnp.concatenate([g_rest[:, 1024 + 128 * i : 1024 + 128 * i + f2.shape[1]] for i in range(4)], axis=0)

    blocks = logits.reshape(4, 32, CP)
    far = across(blocks)
    near = beside(blocks)
    far_near = beside(far)
    mine_cls = jnp.where(branch == 0, blocks, near)
    far_cls = jnp.where(branch == 0, far, far_near)
    mine_box = jnp.where(branch == 0, near, blocks)
    far_box = jnp.where(branch == 0, far_near, far)

    def assemble(mine, theirs):
        a = jnp.where(fine, mine, theirs)
        b = jnp.where(fine, theirs, mine)
        return jnp.concatenate([a[:, :n0], b[:, :n1], b[:, MID : MID + f2.shape[1]]], axis=1)

    def take(v, i):
        return lax.dynamic_index_in_dim(v, i, 0, keepdims=False)

    class_out = assemble(take(mine_cls, c)[: ccot.shape[1]], take(far_cls, c)[: ccot.shape[1]])
    box_out = assemble(mine_box[0, :5], far_box[0, :5])

    wg1, wg2, gw, gs = lax.psum((wg1, wg2, gw, gs), "dp")
    wg = jnp.stack([wg1, wg2]).reshape(2, 2, 9, 4, 32, 128).transpose(3, 0, 1, 2, 4, 5)
    wg = lax.all_to_all(wg, "chan", 0, 0, tiled=True)
    grad_conv = jnp.stack(
        [
            jnp.stack([wg[2 * g + b, k, slot] for b in range(2) for k in range(2)])
            for g, slot in ((0, 0), (1, 0), (1, 1))
        ]
    )
    gs = lax.all_to_all(gs.reshape(4, 32, 768), "chan", 0, 0, tiled=True)
    grad_s0 = gs[0, :, 0:128]
    grad_s1 = gs[2, :, 0:256]
    grad_s2 = gs[2, :, 256:768]
    gw = lax.all_gather(gw, "chan")
    gc = jnp.stack([gw[0, 0], gw[2, 0], gw[2, 1]])
    gb = jnp.stack([gw[1, 0], gw[3, 0], gw[3, 1]])
    gc = lax.dynamic_slice_in_dim(gc, 32 * c, 32, 1)[:, : cw.shape[1]]
    grad_cw, grad_cb = gc[:, :, :128], gc[:, :, 128]
    grad_bw = lax.dynamic_slice_in_dim(gb[:, :5], 32 * c, 32, 2)
    grad_bb = gb[:, :5, 128]
    norm = lax.all_gather(jnp.stack([sums0, sums1, sums2]), "chan")
    norm = lax.dynamic_slice_in_dim(norm, 32 * c, 32, 3)

    def norm_out(base):
        return jnp.stack(
            [
                jnp.stack([norm[2 * g, 0, base + s]] + [norm[2 * g + b, k, base + s] for b in range(2) for k in (1, 2)])
                for g, s in ((0, 0), (1, 0), (1, 1))
            ]
        )

    return (
        class_out[None],
        box_out[None],
        grad_fine[None],
        grad_mid[None],
        grad_coarse[None],
        grad_s0,
        grad_s1,
        grad_s2,
        grad_conv,
        norm_out(2),
        norm_out(0),
        grad_cw,
        grad_cb,
        grad_bw,
        grad_bb,
    )


def solution(mesh):
    placed = (
        P("dp", "chan", None),
        P("dp", "chan", None),
        P("dp", "chan", None),
        P("dp"),
        P("chan", None),
        P("chan", None),
        P("chan", None),
        P(None, None, None, "chan", None),
        P(None, None, "chan"),
        P(None, None, "chan"),
        P(None, "chan", None),
        P(None, "chan"),
        P(None, None, "chan"),
        P(),
        P("dp", "chan", None),
        P("dp", None, None),
    )
    return jax.shard_map(
        shards,
        mesh=mesh,
        in_specs=placed,
        out_specs=(
            P("dp", "chan", None),
            P("dp", None, None),
            P("dp", "chan", None),
            P("dp", "chan", None),
            P("dp", "chan", None),
            P("chan", None),
            P("chan", None),
            P("chan", None),
            P(None, None, None, "chan", None),
            P(None, None, "chan"),
            P(None, None, "chan"),
            P(None, "chan", None),
            P(None, "chan"),
            P(None, None, "chan"),
            P(),
        ),
        check_vma=False,
    )
```

time: 3350 us -> 319 us (0.10)
  waiting for transfers between devices: 1850 us -> 158 us
  local copies, waits for them, and re-layouts: 1010 us -> 26.9 us
  blocking collectives: 249 us -> 36.7 us
  other arithmetic: 128 us -> 11 us
  matrix products: 77.9 us -> 0 us
  starting transfers between devices: 0.8 us -> 35.1 us
    unnamed x26 -> x2, waiting for transfers between devices: 1750 us -> 0.1 us
    convert_element_type x46 -> x1, local copies, waits for them, and re-layouts: 334 us -> 0.02 us  [shards(): bw.reshape(15, 32).astype(F32)]
    unnamed x1324 -> x99, local copies, waits for them, and re-layouts: 280 us -> 12.4 us
    another operation x112 -> x16, local copies, waits for them, and re-layouts: 141 us -> 4.29 us  [the longest x2 2.25 us: shards(): jnp.stack([wg1, wg2]).reshape(2, 2, 9, 4, 32, 128)]
    psum x7 -> x0, blocking collectives: 136 us -> none  [the longest x4 78.3 us: norm_forward(): first_sum, second, counts = lax.psum((first_sum, second, counts), 'dp')]
    all_gather x12 -> x1, blocking collectives: 113 us -> 5.31 us  [shards(): norm = lax.all_gather(jnp.stack([sums0, sums1, sums2]), 'chan')]
    slice x57 -> x13, local copies, waits for them, and re-layouts: 106 us -> 1.7 us  [the longest x2 1.29 us: shards(): grad_cw, grad_cb = (gc[:, :, :128], gc[:, :, 128])]
    dot_general x135 -> x0, matrix products: 51.2 us -> none  [the longest x108 23.7 us: conv_weight_grad(): jnp.einsum('nop,ncp->oc', out_grad, shifted, preferred_element_type=jnp.f...]
  transfers between devices with their start and end apart: 14 -> 28, of which waited for: 7 -> 10; matrix products, arithmetic and copies ran while one was open for 32% -> 9% of each run, Pallas kernels for 0% -> 3%
where the time goes in v1:
time: 319 us; the launch traced here: 315 us
  waiting for transfers between devices  158 us (50%)
  blocking collectives  36.7 us (12%)
  starting transfers between devices  35.1 us (11%)
  Pallas kernels  31.6 us (10%)
  local copies, waits for them, and re-layouts  26.9 us (8%)
  between operations  15.4 us (5%)
  other arithmetic  11 us (3%)
    psum x1, waiting for transfers between devices, shards(): wg1, wg2, gw, gs = lax.psum((wg1, wg2, gw, gs), 'dp')  103 us
    pallas_call x7, Pallas kernels, call(): pl.pallas_call(body, out_shape=[jax.ShapeDtypeStruct(s, d) for s, d in ou...  31.6 us
    all_to_all x3, blocking collectives, exchange(): return lax.all_to_all(st, 'dp', 0, 0, tiled=True)  31.3 us
    ppermute x7, waiting for transfers between devices, across(): return lax.ppermute(v, 'chan', [(i, i ^ 2) for i in range(4)])  18.6 us
    all_to_all x1, waiting for transfers between devices, shards(): wg = lax.all_to_all(wg, 'chan', 0, 0, tiled=True)  17.1 us
    all_to_all x3, waiting for transfers between devices, exchange(): return lax.all_to_all(st, 'dp', 0, 0, tiled=True)  14.7 us
    all_to_all x3, starting transfers between devices, exchange(): return lax.all_to_all(st, 'dp', 0, 0, tiled=True)  13.7 us
    unnamed x99, local copies, waits for them, and re-layouts  12.4 us
  transfers between devices with their start and end apart: 28, of which 10 were waited for; matrix products, arithmetic and copies ran while one was open for 9% of the time, Pallas kernels for 3%

profile of v1, /device:TPU:2, one launch (start us, length us, event | category | flops | bytes accessed | tf_op | source)
XLA Modules:
  0.0 314.9 jit_solution(17340378600285093701)
XLA Ops:
  7.2 0.8 constant_dynamic-update-slice_fusion.8
  8.0 0.8 constant_dynamic-update-slice_fusion.7
  8.8 0.9 copy.74
  9.7 0.7 constant_dynamic-update-slice_fusion.1
  10.5 0.8 constant_dynamic-update-slice_fusion
  11.2 1.0 broadcast_select_fusion
  12.4 0.7 copy.76
  13.1 0.7 copy.75
  13.8 0.7 copy.77
  14.8 2.0 collective-permute-start.3
  17.1 2.0 collective-permute-start.9
  20.6 0.7 select_select_fusion
  21.3 0.7 dynamic-slice_bitcast_fusion.5
  22.0 0.7 dynamic-slice_bitcast_fusion.1
  24.2 2.7 collective-permute-done.6
  26.8 0.7 dynamic-slice_bitcast_fusion.4
  28.1 5.0 %collective-permute-done.9 = bf16[2,2,9,32,128]{4,3,2,1,0:T(8,128)(2,1)S(1)} collective-permute-done((bf16[2,2,9,32,128]{4,3,2,1,0:T(8,128)(2,1)S(1)}, bf16[2,2,9,32,128]{4,3,2,1,0:T(8,128)(2,1)S(1)}, u32[]{:S(2)}, u32[]{:S(2)}) %collective-permute-start.9) | collective-permute-done | bytes 294944 | tf_op jit(solution)/shard_map/ppermute | solution.py:446
  33.1 0.7 dynamic-slice_bitcast_fusion
  34.5 2.6 shard_map.271
  37.2 5.8 %all-to-all-start = ((f32[8,8,128]{2,1,0:T(8,128)}), f32[8,8,128]{2,1,0:T(8,128)S(1)}, u32[]{:S(2)}, u32[]{:S(2)}) async-start(f32[8,8,128]{2,1,0:T(8,128)} %get-tuple-element.44), calls=%async_computation | async-start | bytes 65536 | tf_op jit(solution)/shard_map/all_to_all | solution.py:452
  43.0 1.3 collective-permute-start.13
  44.3 1.3 collective-permute-start.14
  45.6 1.2 collective-permute-start.8
  46.9 1.2 slice_bitcast_fusion.21.refs_4_.refs_1_
  48.2 1.5 all-to-all-done.st
  50.3 4.1 %shard_map.272 = (bf16[1920,128]{1,0:T(8,128)(2,1)}, f32[1920,128]{1,0:T(8,128)}, f32[8,8,128]{2,1,0:T(8,128)}, f32[16,128]{1,0:T(8,128)}, f32[48,128]{1,0:T(8,128)}) custom-call(s32[4]{0:T(128)} %pad_add_fusion.meta, f32[1920,128]{1,0:T(8,128)} %get-tuple-element.43.y.y_in, f32[8,8,128]{2,1,0:T(8,128)} %copy-done.18, f32[48,128]{1,0:T(8,128)} %copy-done.22, ...), custom_call_target="tpu_custom_call" | custom-call | tf_op jit(solution)/shard_map/pallas_call | solution.py:414
  54.4 4.5 %all-to-all-start.1 = ((f32[8,8,128]{2,1,0:T(8,128)}), f32[8,8,128]{2,1,0:T(8,128)S(1)}, u32[]{:S(2)}, u32[]{:S(2)}) async-start(f32[8,8,128]{2,1,0:T(8,128)} %get-tuple-element.46), calls=%async_computation.1 | async-start | bytes 65536 | tf_op jit(solution)/shard_map/all_to_all | solution.py:452
  59.0 6.6 %all-to-all-done.1.st = f32[8,8,128]{2,1,0:T(8,128)S(1)} async-done(((f32[8,8,128]{2,1,0:T(8,128)}), f32[8,8,128]{2,1,0:T(8,128)S(1)}, u32[]{:S(2)}, u32[]{:S(2)}) %all-to-all-start.1) | async-done | bytes 32800 | tf_op jit(solution)/shard_map/all_to_all | solution.py:452
  66.2 4.0 %shard_map.273 = (bf16[1920,128]{1,0:T(8,128)(2,1)}, f32[1920,128]{1,0:T(8,128)}, f32[8,8,128]{2,1,0:T(8,128)}, f32[16,128]{1,0:T(8,128)}) custom-call(s32[4]{0:T(128)} %pad_add_fusion.meta, f32[1920,128]{1,0:T(8,128)} %get-tuple-element.45.y.y_in, f32[8,8,128]{2,1,0:T(8,128)} %copy-done.20, f32[48,128]{1,0:T(8,128)} %get-tuple-element.47.refs_0_.par, ...), custom_call_target="tpu_custom_call" | custom-call | tf_op jit(solution)/shard_map/pallas_call | solution.py:414
  70.2 3.3 %all-to-all-start.2 = ((f32[8,8,128]{2,1,0:T(8,128)}), f32[8,8,128]{2,1,0:T(8,128)S(1)}, u32[]{:S(2)}, u32[]{:S(2)}) async-start(f32[8,8,128]{2,1,0:T(8,128)} %get-tuple-element.49), calls=%async_computation.2 | async-start | bytes 65536 | tf_op jit(solution)/shard_map/all_to_all | solution.py:452
  73.7 6.5 %all-to-all-done.2.st = f32[8,8,128]{2,1,0:T(8,128)S(1)} async-done(((f32[8,8,128]{2,1,0:T(8,128)}), f32[8,8,128]{2,1,0:T(8,128)S(1)}, u32[]{:S(2)}, u32[]{:S(2)}) %all-to-all-start.2) | async-done | bytes 32800 | tf_op jit(solution)/shard_map/all_to_all | solution.py:452
  80.8 4.2 %shard_map.274 = (bf16[128,1664]{1,0:T(8,128)(2,1)}, f32[1920,128]{1,0:T(8,128)}, f32[8,8,128]{2,1,0:T(8,128)}, f32[16,128]{1,0:T(8,128)}, f32[2,128,256]{2,1,0:T(8,128)}) custom-call(s32[4]{0:T(128)} %pad_add_fusion.meta, f32[1920,128]{1,0:T(8,128)} %get-tuple-element.48.y, f32[8,8,128]{2,1,0:T(8,128)} %copy-done.19, ...), custom_call_target="tpu_custom_call" | custom-call | tf_op jit(solution)/shard_map/pallas_call | solution.py:414
  85.0 10.6 %all_to_all.40.st = f32[8,8,128]{2,1,0:T(8,128)} all-to-all(f32[8,8,128]{2,1,0:T(8,128)} %get-tuple-element.53), channel_id=1, replica_groups=mesh['dp'=8,'chan'=4] {'dp'}, dimensions={0} | all-to-all | bytes 65536 | tf_op jit(solution)/shard_map/all_to_all | solution.py:452
  95.7 6.3 %shard_map.275 = (f32[1920,128]{1,0:T(8,128)}, f32[8,8,128]{2,1,0:T(8,128)}, f32[8,128]{1,0:T(8,128)}, f32[2,9,128,128]{3,2,1,0:T(8,128)}) custom-call(s32[4]{0:T(128)} %pad_add_fusion.meta, f32[1920,128]{1,0:T(8,128)} %get-tuple-element.51.dz, f32[1920,128]{1,0:T(8,128)} %get-tuple-element.48.y, f32[16,128]{1,0:T(8,128)} %get-tuple-element.52.cst, ...), custom_call_target="tpu_custom_call" | custom-call | tf_op jit(solution)/shard_map/pallas_call | solution.py:414
  101.9 10.6 %all_to_all.41.st = f32[8,8,128]{2,1,0:T(8,128)} all-to-all(f32[8,8,128]{2,1,0:T(8,128)} %get-tuple-element.57), channel_id=1, replica_groups=mesh['dp'=8,'chan'=4] {'dp'}, dimensions={0} | all-to-all | bytes 65536 | tf_op jit(solution)/shard_map/all_to_all | solution.py:452
  112.5 6.2 %shard_map.276 = (bf16[1920,128]{1,0:T(8,128)(2,1)}, f32[8,8,128]{2,1,0:T(8,128)}, f32[8,128]{1,0:T(8,128)}, f32[2,9,128,128]{3,2,1,0:T(8,128)}) custom-call(s32[4]{0:T(128)} %pad_add_fusion.meta, f32[1920,128]{1,0:T(8,128)} %get-tuple-element.56.dz, f32[1920,128]{1,0:T(8,128)} %get-tuple-element.45.y.y_in, f32[16,128]{1,0:T(8,128)} %get-tuple-element.55.cst_in.cst, ...), custom_call_target="tpu_custom_call" | custom-call | tf_op jit(solution)/shard_map/pallas_call | solution.py:414
  118.7 10.1 %all_to_all.42.st0 = f32[8,8,128]{2,1,0:T(8,128)S(1)} all-to-all(f32[8,8,128]{2,1,0:T(8,128)} %get-tuple-element.61), channel_id=1, replica_groups=mesh['dp'=8,'chan'=4] {'dp'}, dimensions={0} | all-to-all | bytes 65536 | tf_op jit(solution)/shard_map/all_to_all | solution.py:452
  128.8 1.1 copy.90
  130.0 1.1 copy.89
  131.7 0.8 copy-done.12
  132.5 4.2 %shard_map.277 = (bf16[32,1664]{1,0:T(8,128)(2,1)}, bf16[32,1664]{1,0:T(8,128)(2,1)}, f32[128,768]{1,0:T(8,128)}, f32[8,128]{1,0:T(8,128)}) custom-call(s32[4]{0:T(128)} %pad_add_fusion.meta, bf16[1920,128]{1,0:T(8,128)(2,1)} %get-tuple-element.60.d0, bf16[1920,128]{1,0:T(8,128)(2,1)} %copy-done.12, f32[1920,128]{1,0:T(8,128)} %get-tuple-element.43.y.y_in, ...), custom_call_target="tpu_custom_call" | custom-call | tf_op jit(solution)/shard_map/pallas_call | solution.py:414
  136.8 0.9 copy-done.26
  137.7 1.2 collective-permute-start.16
  139.1 10.9 %collective-permute-done.16 = bf16[4,32,1664]{2,1,0:T(8,128)(2,1)} collective-permute-done((bf16[4,32,1664]{2,1,0:T(8,128)(2,1)S(1)}, bf16[4,32,1664]{2,1,0:T(8,128)(2,1)}, u32[]{:S(2)}, u32[]{:S(2)}) %collective-permute-start.16) | collective-permute-done | bytes 426016 | tf_op jit(solution)/shard_map/ppermute | solution.py:446
  150.0 1.2 collective-permute-start.20
  151.2 5.3 %all-gather = f32[12,8,128]{2,1,0:T(8,128)S(1)} all-gather(f32[3,8,128]{2,1,0:T(8,128)S(1)} %pad_maximum_fusion.3), channel_id=2, replica_groups=mesh['dp'=8,'chan'=4] {'chan'}, dimensions={0}, use_global_device_ids=true | all-gather | bytes 61440 | tf_op jit(solution)/shard_map/all_gather | solution.py:611
  158.1 0.7 fusion.3
  158.7 102.8 %all-reduce.24.cloned.1.call-done = (f32[4,32,768]{2,1,0:T(8,128)}, f32[1,2,9,4,32,128]{5,4,2,1,0,3:T(8,128)}, f32[1,2,9,4,32,128]{5,4,2,1,0,3:T(8,128)}, f32[1,2,128,256]{3,2,1,0:T(8,128)}) async-done(((f32[4,32,768]{2,1,0:T(8,128)}, f32[1,2,9,4,32,128]{5,4,2,1,0,3:T(8,128)}, f32[1,2,9,4,32,128]{5,4,2,1,0,3:T(8,128)}, f32[1,2,128,256]{3,2,1,0:T(8,128)}), (f32[4,32,768]{2,1,0:T(8,128)}, ...) | async-done | bytes 3014672 | tf_op jit(solution)/shard_map/psum | solution.py:591
  261.5 4.1 %all-to-all-start.6 = ((f32[4,32,768]{2,1,0:T(8,128)}), f32[4,32,768]{2,1,0:T(8,128)S(1)}, u32[]{:S(2)}, u32[]{:S(2)}) async-start(f32[4,32,768]{2,1,0:T(8,128)} %get-tuple-element.116), calls=%async_computation.6 | async-start | bytes 786432 | tf_op jit(solution)/shard_map/all_to_all | solution.py:600
  265.7 0.6 maximum_bitcast_fusion.4
  266.4 0.7 copy.91
  267.1 2.9 maximum_bitcast_fusion
  270.1 1.4 all-to-all-done.6
  271.4 5.3 %all-to-all-start.7 = ((f32[4,2,2,9,32,128]{5,4,3,2,1,0:T(8,128)}), f32[4,2,2,9,32,128]{5,4,3,2,1,0:T(8,128)S(1)}, u32[]{:S(2)}, u32[]{:S(2)}) async-start(f32[4,2,2,9,32,128]{5,4,3,2,1,0:T(8,128)} %maximum_bitcast_fusion), calls=%async_computation.7 | async-start | bytes 4718592 | tf_op jit(solution)/shard_map/all_to_all | solution.py:593
  276.7 1.0 select_bitcast_fusion
  277.7 0.8 select_bitcast_fusion.2
  278.5 0.7 concatenate.49
  279.3 0.7 concatenate.50
  281.8 3.6 %all-gather.3.cloned.1.call-done = f32[4,2,128,256]{3,2,1,0:T(8,128)} async-done(((f32[1,2,128,256]{3,2,1,0:T(8,128)}), f32[4,2,128,256]{3,2,1,0:T(8,128)}) %all-gather.3.cloned.1.call-update) | async-done | bytes 1048592 | tf_op jit(solution)/shard_map/all_gather | solution.py:604
  285.4 1.3 slice_bitcast_fusion.12
  288.0 0.7 fusion.15
  288.6 0.7 slice_reduce_fusion
  289.3 17.1 %all-to-all-done.7 = f32[4,2,2,9,32,128]{5,4,3,2,1,0:T(8,128)S(1)} async-done(((f32[4,2,2,9,32,128]{5,4,3,2,1,0:T(8,128)}), f32[4,2,2,9,32,128]{5,4,3,2,1,0:T(8,128)S(1)}, u32[]{:S(2)}, u32[]{:S(2)}) %all-to-all-start.7) | async-done | bytes 2359328 | tf_op jit(solution)/shard_map/all_to_all | solution.py:593
  306.7 1.4 pad_maximum_fusion
  (195 shorter events, 12.2 us)
Async XLA Ops:
  7.2 9.6 %copy-start.4 = (bf16[3,4,9,32,128]{4,3,2,1,0:T(8,128)(2,1)S(1)}, bf16[3,4,9,32,128]{4,3,2,1,0:T(8,128)(2,1)}, u32[]{:S(2)}) copy-start(bf16[3,4,9,32,128]{4,3,2,1,0:T(8,128)(2,1)} %param.23) | copy-start | bytes 2654212
  12.2 7.1 %copy-start = (bf16[32,2432]{1,0:T(8,128)(2,1)}, bf16[32,2432]{1,0:T(8,128)(2,1)S(1)}, u32[]{:S(2)}) copy-start(bf16[32,2432]{1,0:T(8,128)(2,1)S(1)} %get-tuple-element.155.u0) | copy-start | bytes 466948
  12.2 6.9 %copy-start.23 = (bf16[1,5,2100]{2,1,0:T(8,128)(2,1)S(1)}, bf16[1,5,2100]{2,1,0:T(8,128)(2,1)}, u32[]{:S(2)}) copy-start(bf16[1,5,2100]{2,1,0:T(8,128)(2,1)} %param.31) | copy-start | bytes 63004
  12.2 7.0 %copy-start.30 = (pred[1664]{0:T(1024)(128)(4,1)S(1)}, pred[1664]{0:T(1024)(128)(4,1)}, u32[]{:S(2)}) copy-start(pred[1664]{0:T(1024)(128)(4,1)} %constant.180.clone.1) | copy-start | bytes 4996
  12.2 7.0 %copy-start.21 = (bf16[1,20,2100]{2,1,0:T(8,128)(2,1)S(1)}, bf16[1,20,2100]{2,1,0:T(8,128)(2,1)}, u32[]{:S(2)}) copy-start(bf16[1,20,2100]{2,1,0:T(8,128)(2,1)} %param.30) | copy-start | bytes 252004
  12.2 11.7 %collective-permute-start = (bf16[32,2432]{1,0:T(8,128)(2,1)S(1)}, bf16[32,2432]{1,0:T(8,128)(2,1)S(1)}, u32[]{:S(2)}, u32[]{:S(2)}) collective-permute-start(bf16[32,2432]{1,0:T(8,128)(2,1)S(1)} %get-tuple-element.154), channel_id=1, source_target_pairs={{0,2},{1,3},{2,0},{3,1},{4,6},{5,7},{6,4},{7,5},{8,10},{9,11},{10,... | collective-permute-start | bytes 466952 | tf_op jit(solution)/shard_map/ppermute | solution.py:446
  12.3 15.2 %collective-permute-start.1 = (bf16[32,2432]{1,0:T(8,128)(2,1)S(1)}, bf16[32,2432]{1,0:T(8,128)(2,1)S(1)}, u32[]{:S(2)}, u32[]{:S(2)}) collective-permute-start(bf16[32,2432]{1,0:T(8,128)(2,1)S(1)} %get-tuple-element.155.u0), channel_id=1, source_target_pairs={{0,1},{1,0},{2,3},{3,2},{4,5},{5,4},{6,7},{7,6},{8,9},{9,8},{10,11... | collective-permute-start | bytes 466952 | tf_op jit(solution)/shard_map/ppermute | solution.py:449
  14.6 4.8 %copy-start.34 = (f32[3,5]{1,0:T(4,128)S(1)}, f32[3,5]{1,0:T(4,128)}, u32[]{:S(2)}) copy-start(f32[3,5]{1,0:T(4,128)} %param.29) | copy-start | bytes 184
  14.8 12.8 %copy-start.22 = (f32[48,128]{1,0:T(8,128)}, f32[48,128]{1,0:T(8,128)S(1)}, u32[]{:S(2)}) copy-start(f32[48,128]{1,0:T(8,128)S(1)} %fusion.10.refs_0_) | copy-start | bytes 73732
  14.8 9.2 %collective-permute-start.3 = (f32[48,128]{1,0:T(8,128)S(1)}, f32[48,128]{1,0:T(8,128)S(1)}, u32[]{:S(2)}, u32[]{:S(2)}) collective-permute-start(f32[48,128]{1,0:T(8,128)S(1)} %fusion.10.refs_0_), channel_id=1, source_target_pairs={{0,2},{1,3},{2,0},{3,1},{4,6},{5,7},{6,4},{7,5},{8,10},{9,11},{10,... | collective-permute-start | bytes 73736 | tf_op jit(solution)/shard_map/ppermute | solution.py:446
  16.8 3.3 %copy-start.35 = (f32[3,20]{1,0:T(4,128)S(1)}, f32[3,20]{1,0:T(4,128)}, u32[]{:S(2)}) copy-start(f32[3,20]{1,0:T(4,128)} %param.27) | copy-start | bytes 724
  16.8 3.7 %copy-start.25 = (bf16[3,20,128]{2,1,0:T(8,128)(2,1)S(1)}, bf16[3,20,128]{2,1,0:T(8,128)(2,1)}, u32[]{:S(2)}) copy-start(bf16[3,20,128]{2,1,0:T(8,128)(2,1)} %param.26) | copy-start | bytes 46084
  16.9 9.9 %collective-permute-start.6 = (bf16[2,2,9,32,128]{4,3,2,1,0:T(8,128)(2,1)S(1)}, bf16[2,2,9,32,128]{4,3,2,1,0:T(8,128)(2,1)S(1)}, u32[]{:S(2)}, u32[]{:S(2)}) collective-permute-start(bf16[2,2,9,32,128]{4,3,2,1,0:T(8,128)(2,1)S(1)} %constant_dynamic-slice_fusion.17), channel_id=1, source_target_pairs={{0,2},{1,3},{2,0},{3,1},{4,6},{5,7},{6,4},{7,5},{8,10},{9,11},{10,... | collective-permute-start | bytes 884744 | tf_op jit(solution)/shard_map/ppermute | solution.py:446
  17.1 16.1 %collective-permute-start.9 = (bf16[2,2,9,32,128]{4,3,2,1,0:T(8,128)(2,1)S(1)}, bf16[2,2,9,32,128]{4,3,2,1,0:T(8,128)(2,1)S(1)}, u32[]{:S(2)}, u32[]{:S(2)}) collective-permute-start(bf16[2,2,9,32,128]{4,3,2,1,0:T(8,128)(2,1)S(1)} %constant_dynamic-slice_fusion.16), channel_id=1, source_target_pairs={{0,2},{1,3},{2,0},{3,1},{4,6},{5,7},{6,4},{7,5},{8,10},{9,11},{10,... | collective-permute-start | bytes 884744 | tf_op jit(solution)/shard_map/ppermute | solution.py:446
  24.0 25.7 %copy-start.27 = (f32[48,128]{1,0:T(8,128)}, f32[48,128]{1,0:T(8,128)S(1)}, u32[]{:S(2)}) copy-start(f32[48,128]{1,0:T(8,128)S(1)} %collective-permute-done.3.refs_1_) | copy-start | bytes 73732
  24.0 22.9 %collective-permute-start.7 = (bf16[2,9,32,128]{3,2,1,0:T(8,128)(2,1)S(1)}, bf16[2,9,32,128]{3,2,1,0:T(8,128)(2,1)S(1)}, u32[]{:S(2)}, u32[]{:S(2)}) collective-permute-start(bf16[2,9,32,128]{3,2,1,0:T(8,128)(2,1)S(1)} %get-tuple-element.148), channel_id=1, source_target_pairs={{0,1},{1,0},{2,3},{3,2},{4,5},{5,4},{6,7},{7,6},{8,9},{9,8},{10,11... | collective-permute-start | bytes 442376 | tf_op jit(solution)/shard_map/ppermute | solution.py:449
  24.0 10.4 %copy-start.5 = (bf16[32,2432]{1,0:T(8,128)(2,1)}, bf16[32,2432]{1,0:T(8,128)(2,1)S(1)}, u32[]{:S(2)}) copy-start(bf16[32,2432]{1,0:T(8,128)(2,1)S(1)} %collective-permute-done.u1) | copy-start | bytes 466948
  24.0 20.3 %collective-permute-start.12 = (bf16[32,2176]{1,0:T(8,128)(2,1)S(1)}, bf16[32,2176]{1,0:T(8,128)(2,1)S(1)}, u32[]{:S(2)}, u32[]{:S(2)}) collective-permute-start(bf16[32,2176]{1,0:T(8,128)(2,1)S(1)} %get-tuple-element.156), channel_id=1, source_target_pairs={{0,2},{1,3},{2,0},{3,1},{4,6},{5,7},{6,4},{7,5},{8,10},{9,11},{10,... | collective-permute-start | bytes 417800 | tf_op jit(solution)/shard_map/ppermute | solution.py:446
  26.8 7.0 %collective-permute-start.2 = (bf16[32,2432]{1,0:T(8,128)(2,1)S(1)}, bf16[32,2432]{1,0:T(8,128)(2,1)S(1)}, u32[]{:S(2)}, u32[]{:S(2)}) collective-permute-start(bf16[32,2432]{1,0:T(8,128)(2,1)S(1)} %collective-permute-done.u1), channel_id=1, source_target_pairs={{0,1},{1,0},{2,3},{3,2},{4,5},{5,4},{6,7},{7,6},{8,9},{9,8},{10,11... | collective-permute-start | bytes 466952 | tf_op jit(solution)/shard_map/ppermute | solution.py:449
  27.5 6.8 %copy-start.6 = (bf16[32,2432]{1,0:T(8,128)(2,1)}, bf16[32,2432]{1,0:T(8,128)(2,1)S(1)}, u32[]{:S(2)}) copy-start(bf16[32,2432]{1,0:T(8,128)(2,1)S(1)} %collective-permute-done.1.u2) | copy-start | bytes 466948
  27.5 15.4 %collective-permute-start.4 = (f32[48,128]{1,0:T(8,128)S(1)}, f32[48,128]{1,0:T(8,128)S(1)}, u32[]{:S(2)}, u32[]{:S(2)}) collective-permute-start(f32[48,128]{1,0:T(8,128)S(1)} %fusion.10.refs_0_), channel_id=1, source_target_pairs={{0,1},{1,0},{2,3},{3,2},{4,5},{5,4},{6,7},{7,6},{8,9},{9,8},{10,11... | collective-permute-start | bytes 73736 | tf_op jit(solution)/shard_map/ppermute | solution.py:449
  33.1 12.5 %collective-permute-start.5 = (f32[48,128]{1,0:T(8,128)S(1)}, f32[48,128]{1,0:T(8,128)S(1)}, u32[]{:S(2)}, u32[]{:S(2)}) collective-permute-start(f32[48,128]{1,0:T(8,128)S(1)} %collective-permute-done.3.refs_1_), channel_id=1, source_target_pairs={{0,1},{1,0},{2,3},{3,2},{4,5},{5,4},{6,7},{7,6},{8,9},{9,8},{10,11... | collective-permute-start | bytes 73736 | tf_op jit(solution)/shard_map/ppermute | solution.py:449
  33.8 0.7 copy-start.7
  33.8 25.1 %collective-permute-start.10 = (bf16[2,9,32,128]{3,2,1,0:T(8,128)(2,1)S(1)}, bf16[2,9,32,128]{3,2,1,0:T(8,128)(2,1)S(1)}, u32[]{:S(2)}, u32[]{:S(2)}) collective-permute-start(bf16[2,9,32,128]{3,2,1,0:T(8,128)(2,1)S(1)} %get-tuple-element.146), channel_id=1, source_target_pairs={{0,1},{1,0},{2,3},{3,2},{4,5},{5,4},{6,7},{7,6},{8,9},{9,8},{10,11... | collective-permute-start | bytes 442376 | tf_op jit(solution)/shard_map/ppermute | solution.py:449
  37.2 12.5 %all-to-all-start = ((f32[8,8,128]{2,1,0:T(8,128)}), f32[8,8,128]{2,1,0:T(8,128)S(1)}, u32[]{:S(2)}, u32[]{:S(2)}) async-start(f32[8,8,128]{2,1,0:T(8,128)} %get-tuple-element.44), calls=%async_computation | async-start | bytes 65536 | tf_op jit(solution)/shard_map/all_to_all | solution.py:452
  43.0 6.7 %copy-start.28 = (f32[48,128]{1,0:T(8,128)}, f32[48,128]{1,0:T(8,128)S(1)}, u32[]{:S(2)}) copy-start(f32[48,128]{1,0:T(8,128)S(1)} %collective-permute-done.4.refs_2_) | copy-start | bytes 73732
  43.0 30.6 %collective-permute-start.13 = (bf16[32,2176]{1,0:T(8,128)(2,1)S(1)}, bf16[32,2176]{1,0:T(8,128)(2,1)S(1)}, u32[]{:S(2)}, u32[]{:S(2)}) collective-permute-start(bf16[32,2176]{1,0:T(8,128)(2,1)S(1)} %get-tuple-element.121), channel_id=1, source_target_pairs={{1,0},{3,2},{5,4},{7,6},{9,8},{11,10},{13,12},{15,14},{17,16},{19,... | collective-permute-start | bytes 417800 | tf_op jit(solution)/shard_map/ppermute | solution.py:449
  44.3 35.9 %copy-start.14 = (bf16[32,2176]{1,0:T(8,128)(2,1)}, bf16[32,2176]{1,0:T(8,128)(2,1)S(1)}, u32[]{:S(2)}) copy-start(bf16[32,2176]{1,0:T(8,128)(2,1)S(1)} %collective-permute-done.12.k1) | copy-start | bytes 417796
  44.3 29.3 %collective-permute-start.14 = (bf16[32,2176]{1,0:T(8,128)(2,1)S(1)}, bf16[32,2176]{1,0:T(8,128)(2,1)S(1)}, u32[]{:S(2)}, u32[]{:S(2)}) collective-permute-start(bf16[32,2176]{1,0:T(8,128)(2,1)S(1)} %collective-permute-done.12.k1), channel_id=1, source_target_pairs={{1,0},{3,2},{5,4},{7,6},{9,8},{11,10},{13,12},{15,14},{17,16},{19,... | collective-permute-start | bytes 417800 | tf_op jit(solution)/shard_map/ppermute | solution.py:449
  45.6 4.1 %copy-start.29 = (f32[48,128]{1,0:T(8,128)}, f32[48,128]{1,0:T(8,128)S(1)}, u32[]{:S(2)}) copy-start(f32[48,128]{1,0:T(8,128)S(1)} %collective-permute-done.5.refs_3_) | copy-start | bytes 73732
  45.6 4.0 %collective-permute-start.8 = (bf16[2,9,32,128]{3,2,1,0:T(8,128)(2,1)S(1)}, bf16[2,9,32,128]{3,2,1,0:T(8,128)(2,1)S(1)}, u32[]{:S(2)}, u32[]{:S(2)}) collective-permute-start(bf16[2,9,32,128]{3,2,1,0:T(8,128)(2,1)S(1)} %get-tuple-element.152), channel_id=1, source_target_pairs={{0,1},{1,0},{2,3},{3,2},{4,5},{5,4},{6,7},{7,6},{8,9},{9,8},{10,11... | collective-permute-start | bytes 442376 | tf_op jit(solution)/shard_map/ppermute | solution.py:449
  46.8 2.9 copy-start.8
  46.8 12.1 %collective-permute-start.11 = (bf16[2,9,32,128]{3,2,1,0:T(8,128)(2,1)S(1)}, bf16[2,9,32,128]{3,2,1,0:T(8,128)(2,1)S(1)}, u32[]{:S(2)}, u32[]{:S(2)}) collective-permute-start(bf16[2,9,32,128]{3,2,1,0:T(8,128)(2,1)S(1)} %get-tuple-element.150), channel_id=1, source_target_pairs={{0,1},{1,0},{2,3},{3,2},{4,5},{5,4},{6,7},{7,6},{8,9},{9,8},{10,11... | collective-permute-start | bytes 442376 | tf_op jit(solution)/shard_map/ppermute | solution.py:449
  49.7 0.6 copy-start.18
  49.7 0.7 copy-start.10
  54.4 11.2 %all-to-all-start.1 = ((f32[8,8,128]{2,1,0:T(8,128)}), f32[8,8,128]{2,1,0:T(8,128)S(1)}, u32[]{:S(2)}, u32[]{:S(2)}) async-start(f32[8,8,128]{2,1,0:T(8,128)} %get-tuple-element.46), calls=%async_computation.1 | async-start | bytes 65536 | tf_op jit(solution)/shard_map/all_to_all | solution.py:452
  58.9 6.7 %copy-start.9 = (bf16[2,9,32,128]{3,2,1,0:T(8,128)(2,1)}, bf16[2,9,32,128]{3,2,1,0:T(8,128)(2,1)S(1)}, u32[]{:S(2)}) copy-start(bf16[2,9,32,128]{3,2,1,0:T(8,128)(2,1)S(1)} %collective-permute-done.10.refs_4_.w2) | copy-start | bytes 442372
  59.0 6.7 %copy-start.11 = (bf16[2,9,32,128]{3,2,1,0:T(8,128)(2,1)}, bf16[2,9,32,128]{3,2,1,0:T(8,128)(2,1)S(1)}, u32[]{:S(2)}) copy-start(bf16[2,9,32,128]{3,2,1,0:T(8,128)(2,1)S(1)} %collective-permute-done.11.refs_5_.w3) | copy-start | bytes 442372
  65.6 0.6 copy-start.20
  70.2 10.0 %all-to-all-start.2 = ((f32[8,8,128]{2,1,0:T(8,128)}), f32[8,8,128]{2,1,0:T(8,128)S(1)}, u32[]{:S(2)}, u32[]{:S(2)}) async-start(f32[8,8,128]{2,1,0:T(8,128)} %get-tuple-element.49), calls=%async_computation.2 | async-start | bytes 65536 | tf_op jit(solution)/shard_map/all_to_all | solution.py:452
  73.6 188.0 %all-reduce.24.cloned.1.call-start = ((), (), s32[]{:S(2)}) async-start(), calls=%async_computation.9 | async-start | bytes 6029312 | tf_op jit(solution)/shard_map/psum | solution.py:591
  73.6 6.6 %copy-start.15 = (bf16[32,2176]{1,0:T(8,128)(2,1)}, bf16[32,2176]{1,0:T(8,128)(2,1)S(1)}, u32[]{:S(2)}) copy-start(bf16[32,2176]{1,0:T(8,128)(2,1)S(1)} %collective-permute-done.13.k2) | copy-start | bytes 417796
  73.7 6.6 %copy-start.16 = (bf16[32,2176]{1,0:T(8,128)(2,1)}, bf16[32,2176]{1,0:T(8,128)(2,1)S(1)}, u32[]{:S(2)}) copy-start(bf16[32,2176]{1,0:T(8,128)(2,1)S(1)} %collective-permute-done.14.k3) | copy-start | bytes 417796
  112.5 16.3 %copy-start.1 = (f32[2,9,128,128]{3,2,1,0:T(8,128)S(1)}, f32[2,9,128,128]{3,2,1,0:T(8,128)}, u32[]{:S(2)}) copy-start(f32[2,9,128,128]{3,2,1,0:T(8,128)} %get-tuple-element.66) | copy-start | bytes 3538948
  118.7 11.2 %copy-start.2 = (f32[2,9,128,128]{3,2,1,0:T(8,128)S(1)}, f32[2,9,128,128]{3,2,1,0:T(8,128)}, u32[]{:S(2)}) copy-start(f32[2,9,128,128]{3,2,1,0:T(8,128)} %get-tuple-element.65) | copy-start | bytes 3538948
  118.7 12.4 %collective-permute-start.18 = (bf16[1920,128]{1,0:T(8,128)(2,1)}, bf16[1920,128]{1,0:T(8,128)(2,1)S(1)}, u32[]{:S(2)}, u32[]{:S(2)}) collective-permute-start(bf16[1920,128]{1,0:T(8,128)(2,1)} %get-tuple-element.60.d0), channel_id=1, source_target_pairs={{0,1},{1,0},{2,3},{3,2},{4,5},{5,4},{6,7},{7,6},{8,9},{9,8},{10,11... | collective-permute-start | bytes 1474568 | tf_op jit(solution)/shard_map/ppermute | solution.py:449
  128.8 2.3 copy-start.17
  128.8 2.3 collective-permute-start.19
  131.1 0.6 copy-start.24
  131.7 0.8 copy-start.12
  136.7 1.0 copy-start.26
  136.7 13.3 %copy-start.36 = (bf16[32,1664]{1,0:T(8,128)(2,1)S(1)}, bf16[32,1664]{1,0:T(8,128)(2,1)}, u32[]{:S(2)}) copy-start(bf16[32,1664]{1,0:T(8,128)(2,1)} %get-tuple-element.63) | copy-start | bytes 319492
  136.7 14.5 %copy-start.31 = (f32[8,128]{1,0:T(8,128)S(1)}, f32[8,128]{1,0:T(8,128)}, u32[]{:S(2)}) copy-start(f32[8,128]{1,0:T(8,128)} %get-tuple-element.69) | copy-start | bytes 12292
  136.7 14.5 %copy-start.32 = (f32[8,128]{1,0:T(8,128)S(1)}, f32[8,128]{1,0:T(8,128)}, u32[]{:S(2)}) copy-start(f32[8,128]{1,0:T(8,128)} %get-tuple-element.68) | copy-start | bytes 12292
  136.7 14.5 %copy-start.33 = (f32[8,128]{1,0:T(8,128)S(1)}, f32[8,128]{1,0:T(8,128)}, u32[]{:S(2)}) copy-start(f32[8,128]{1,0:T(8,128)} %get-tuple-element.67) | copy-start | bytes 12292
  136.7 21.3 %copy-start.13 = (bf16[32,1664]{1,0:T(8,128)(2,1)S(1)}, bf16[32,1664]{1,0:T(8,128)(2,1)}, u32[]{:S(2)}) copy-start(bf16[32,1664]{1,0:T(8,128)(2,1)} %get-tuple-element.62) | copy-start | bytes 319492
  137.7 12.3 %collective-permute-start.16 = (bf16[4,32,1664]{2,1,0:T(8,128)(2,1)S(1)}, bf16[4,32,1664]{2,1,0:T(8,128)(2,1)}, u32[]{:S(2)}, u32[]{:S(2)}) collective-permute-start(bf16[4,32,1664]{2,1,0:T(8,128)(2,1)S(1)} %bitcast.227), channel_id=1, source_target_pairs={{0,2},{1,3},{2,0},{3,1},{4,6},{5,7},{6,4},{7,5},{8,10},{9,11},{10,... | collective-permute-start | bytes 1277960 | tf_op jit(solution)/shard_map/ppermute | solution.py:446
  138.9 137.8 %collective-permute-start.15 = (bf16[4,32,1664]{2,1,0:T(8,128)(2,1)S(1)}, bf16[4,32,1664]{2,1,0:T(8,128)(2,1)}, u32[]{:S(2)}, u32[]{:S(2)}) collective-permute-start(bf16[4,32,1664]{2,1,0:T(8,128)(2,1)S(1)} %bitcast.228), channel_id=1, source_target_pairs={{0,1},{1,0},{2,3},{3,2},{4,5},{5,4},{6,7},{7,6},{8,9},{9,8},{10,11... | collective-permute-start | bytes 1277960 | tf_op jit(solution)/shard_map/ppermute | solution.py:449
  150.0 126.7 %collective-permute-start.17 = (bf16[4,32,1664]{2,1,0:T(8,128)(2,1)}, bf16[4,32,1664]{2,1,0:T(8,128)(2,1)}, u32[]{:S(2)}, u32[]{:S(2)}) collective-permute-start(bf16[4,32,1664]{2,1,0:T(8,128)(2,1)} %collective-permute-done.16), channel_id=1, source_target_pairs={{0,1},{1,0},{2,3},{3,2},{4,5},{5,4},{6,7},{7,6},{8,9},{9,8},{10,11... | collective-permute-start | bytes 1277960 | tf_op jit(solution)/shard_map/ppermute | solution.py:449
  150.0 8.0 %collective-permute-start.20 = (bf16[32,1664]{1,0:T(8,128)(2,1)S(1)}, bf16[32,1664]{1,0:T(8,128)(2,1)S(1)}, u32[]{:S(2)}, u32[]{:S(2)}) collective-permute-start(bf16[32,1664]{1,0:T(8,128)(2,1)S(1)} %copy-done.36), channel_id=1, source_target_pairs={{0,2},{1,3},{2,0},{3,1},{4,6},{5,7},{6,4},{7,5},{8,10},{9,11},{10,... | collective-permute-start | bytes 319496 | tf_op jit(solution)/shard_map/ppermute | solution.py:446
  261.5 5.6 %copy-start.3 = (f32[1,2,9,4,32,128]{5,4,2,1,0,3:T(8,128)S(1)}, f32[1,2,9,4,32,128]{5,4,2,1,0,3:T(8,128)}, u32[]{:S(2)}) copy-start(f32[1,2,9,4,32,128]{5,4,2,1,0,3:T(8,128)} %get-tuple-element.117) | copy-start | bytes 3538948
  261.5 9.9 %all-to-all-start.6 = ((f32[4,32,768]{2,1,0:T(8,128)}), f32[4,32,768]{2,1,0:T(8,128)S(1)}, u32[]{:S(2)}, u32[]{:S(2)}) async-start(f32[4,32,768]{2,1,0:T(8,128)} %get-tuple-element.116), calls=%async_computation.6 | async-start | bytes 786432 | tf_op jit(solution)/shard_map/all_to_all | solution.py:600
  265.7 19.7 %all-gather.3.cloned.1.call-start = ((), (), s32[]{:S(2)}) async-start(), calls=%async_computation.8 | async-start | bytes 1310720 | tf_op jit(solution)/shard_map/all_gather | solution.py:604
  271.4 34.9 %all-to-all-start.7 = ((f32[4,2,2,9,32,128]{5,4,3,2,1,0:T(8,128)}), f32[4,2,2,9,32,128]{5,4,3,2,1,0:T(8,128)S(1)}, u32[]{:S(2)}, u32[]{:S(2)}) async-start(f32[4,2,2,9,32,128]{5,4,3,2,1,0:T(8,128)} %maximum_bitcast_fusion), calls=%async_computation.7 | async-start | bytes 4718592 | tf_op jit(solution)/shard_map/all_to_all | solution.py:593
  (1 other events, 0.6 us)
Sparse Core Ops, SparseCore 0:
  136.9 124.6 all-reduce.23
  268.1 17.2 all-gather.2

commit v2 on v1

v2 whole, which is shorter than its diff:
```python
import functools

import jax
import jax.numpy as jnp
from jax import lax
from jax.experimental import pallas as pl
from jax.experimental.pallas import tpu as pltpu
from jax.sharding import PartitionSpec as P

BF = jnp.bfloat16
F32 = jnp.float32
EPS = 0.001
ST = 48
ROWS = 40
PX = ST * ROWS
CR = 8
CH = CR * ST
NCH = ROWS // CR
SLOT = (0, 0, 0, 1, 1)
CUT = 24 * ST
CP = 1664
MID = 512
E0, E1, E2 = 40, 20, 10
STEM = 1536
PAR = STEM + 768
WIDE = PAR + 256
CLS = CP + 512
VMEM = 12 * 2**20
WHOLE = 56 * 2**20
OWNER = (0, 2, 1, 3)
NT = (((1,), (1,)), ((), ()))
TN = (((0,), (0,)), ((), ()))


def dot(a, b, dims=(((1,), (0,)), ((), ()))):
    return lax.dot_general(a, b, dims, preferred_element_type=F32)


def limits(meta, slot):
    group, units = meta[0], meta[3]
    if slot == 0:
        edge = jnp.where(group == 0, 4 * units, 2 * units)
        return edge, edge
    return (
        jnp.where(group == 0, 4 * units, 24 + units),
        jnp.where(group == 0, 4 * units, units),
    )


def mask_of(meta, j):
    row_end, col_end = limits(meta, SLOT[j])
    row = lax.broadcasted_iota(jnp.int32, (CR, ST, 128), 0) + CR * j
    col = lax.broadcasted_iota(jnp.int32, (CR, ST, 128), 1)
    inside = (row < row_end) & (col < col_end)
    return jnp.where(inside, 1.0, 0.0).reshape(CH, 128)


def pick(meta, first, second):
    total = first + second
    return jnp.where(meta[0] == 0, total, first), jnp.where(meta[0] == 0, total, second)


def level_rows(meta, base, layer):
    fine = meta[0] == 0
    at = base + 3 * layer
    return at + jnp.where(fine, 0, 1), at + jnp.where(fine, 0, 2)


def norm_constants(meta, st, par, layer, cst):
    total = jnp.sum(st[...], axis=0)
    row = [total[i : i + 1] for i in range(6)]
    first = pick(meta, row[0], row[1])
    second = pick(meta, row[2], row[3])
    count = pick(meta, row[4], row[5])
    gain_at = level_rows(meta, 0, layer)
    shift_at = level_rows(meta, 16, layer)
    for s in range(2):
        rn = 1.0 / count[s]
        mean = first[s] * rn
        inv = lax.rsqrt(second[s] * rn - mean * mean + EPS)
        cst[s : s + 1] = mean
        cst[2 + s : 3 + s] = inv
        cst[4 + s : 5 + s] = par[pl.ds(gain_at[s], 1), :]
        cst[6 + s : 7 + s] = par[pl.ds(shift_at[s], 1), :]
        cst[8 + s : 9 + s] = rn
        cst[10 + s : 11 + s] = count[s]
    cst[12:16] = jnp.zeros((4, 128), F32)


def normed(cst, y, s):
    xhat = (y - cst[s : s + 1]) * cst[2 + s : 3 + s]
    return xhat, xhat * cst[4 + s : 5 + s] + cst[6 + s : 7 + s]


def sigmoid(z):
    return 0.5 * jnp.tanh(0.5 * z) + 0.5


def slope(z):
    s = sigmoid(z)
    return s * (1.0 + z * (1.0 - s))


def spread_out(st, rows):
    block = jnp.concatenate(rows + [jnp.zeros((8 - len(rows), 128), F32)], axis=0)
    st[...] = jnp.broadcast_to(block[None], st.shape)


def colsum(v):
    return jnp.sum(v, axis=0, keepdims=True)


def guard(field, shifts):
    field[0:8] = jnp.zeros((8, 128), F32)
    field[8 + PX : 16 + PX] = jnp.zeros((8, 128), F32)
    for k in range(3):
        shifts[k, 0:ST] = jnp.zeros((ST, 128), BF)
        shifts[k, ST + PX :] = jnp.zeros((ST, 128), BF)


def fill_shifts(field, shifts):
    for k in range(3):
        for j in range(NCH):
            at = 8 + CH * j + k - 1
            shifts[k, ST + CH * j : ST + CH * (j + 1)] = field[at : at + CH].astype(BF)


def taps(shifts, begin, size, back=False):
    parts = []
    for kr in range(3):
        for kc in range(3):
            k, r = (2 - kc, 1 - kr) if back else (kc, kr - 1)
            at = ST + begin + ST * r
            parts.append(shifts[k, at : at + size])
    return jnp.concatenate(parts, axis=1)


def slices_of(meta):
    c = meta[2]
    return (c, c ^ 2, c ^ 1, c ^ 3)


def at32(s, extra=0):
    return pl.ds(pl.multiple_of(32 * s + extra, 32), 32)


def weight_slot(meta, j):
    return jnp.where(meta[0] == 0, 0, SLOT[j])


def to_compact(meta, canvas, out):
    @pl.when(meta[0] == 0)
    def _():
        for r in range(E0):
            out[E0 * r : E0 * (r + 1)] = canvas[ST * r : ST * r + E0]

    @pl.when(meta[0] == 1)
    def _():
        for r in range(E1):
            out[E1 * r : E1 * (r + 1)] = canvas[ST * r : ST * r + E1]
        for r in range(E2):
            at = CUT + ST * r
            out[MID + E2 * r : MID + E2 * (r + 1)] = canvas[at : at + E2]


def to_canvas(meta, compact, out):
    @pl.when(meta[0] == 0)
    def _():
        for r in range(E0):
            out[ST * r : ST * r + E0] = compact[E0 * r : E0 * (r + 1)]

    @pl.when(meta[0] == 1)
    def _():
        for r in range(E1):
            out[ST * r : ST * r + E1] = compact[E1 * r : E1 * (r + 1)]
        for r in range(E2):
            at = CUT + ST * r
            out[at : at + E2] = compact[MID + E2 * r : MID + E2 * (r + 1)]


def load_inputs(meta, pieces, feat, stem):
    for s, u in zip(slices_of(meta), pieces):

        @pl.when(meta[0] == 0)
        def _():
            feat[at32(s), :] = u[:, 0:CP]
            stem[at32(s), 0:128] = u[:, CP : CP + 128]

        @pl.when(meta[0] == 1)
        def _():
            for i in range(2):
                at = pl.ds(pl.multiple_of(64 * s + 32 * i, 32), 32)
                feat[at, 0:MID] = u[:, MID * i : MID * (i + 1)]
            for i in range(4):
                at = pl.ds(pl.multiple_of(128 * s + 32 * i, 32), 32)
                feat[at, MID : MID + 128] = u[:, 1024 + 128 * i : 1152 + 128 * i]
            stem[at32(s), :] = u[:, STEM:PAR]


def stem_kernel(meta, u0, u1, u2, u3, y, st, cnt, par, feat, stem, flat):
    load_inputs(meta, (u0, u1, u2, u3), feat, stem)
    lane = lax.broadcasted_iota(jnp.int32, (32, 128), 1) // 32
    for i in range(2):
        total = jnp.zeros((32, 128), F32)
        for s, u in zip(slices_of(meta), (u0, u1, u2, u3)):
            v = u[:, PAR + 128 * i : PAR + 128 * (i + 1)].astype(F32)
            v = v[:, 0:32] + v[:, 32:64] + v[:, 64:96]
            total = jnp.where(lane == s, jnp.concatenate([v] * 4, axis=1), total)
        par[32 * i : 32 * (i + 1)] = total
    y[...] = jnp.zeros((PX, 128), F32)

    @pl.when(meta[0] == 0)
    def _():
        flat[...] = dot(stem[:, 0:128], feat[0:128, :]).T

    @pl.when(meta[0] == 1)
    def _():
        flat[0:MID] = dot(stem[:, 0:256], feat[0:256, 0:MID]).T
        flat[MID : MID + 128] = dot(stem[:, 256:768], feat[0:512, MID : MID + 128]).T

    to_canvas(meta, flat, y)
    sums = [jnp.zeros((1, 128), F32) for _ in range(6)]
    for j in range(NCH):
        m = mask_of(meta, j)
        v = y[CH * j : CH * (j + 1)] * m
        s = SLOT[j]
        sums[s] += colsum(v)
        sums[2 + s] += colsum(v * v)
        sums[4 + s] += colsum(m)
    spread_out(st, sums)
    cnt[...] = jnp.concatenate(sums[4:6] + [jnp.zeros((6, 128), F32)], axis=0)


def forward_kernel(first, meta, y, st, cnt, w, *refs):
    par, act, out, st_out, cst, field, shifts = refs
    layer = 0 if first else 1 + 2 * meta[1]
    norm_constants(meta, st, par, layer, cst)
    guard(field, shifts)
    for j in range(NCH):
        rows = slice(CH * j, CH * (j + 1))
        _, z = normed(cst, y[rows], SLOT[j])
        v = z * sigmoid(z) * mask_of(meta, j)
        act[rows] = v.astype(BF)
        field[8 + CH * j : 8 + CH * (j + 1)] = v
    fill_shifts(field, shifts)
    sums = [jnp.zeros((1, 128), F32) for _ in range(4)]
    for j in range(NCH):
        v = dot(taps(shifts, CH * j, CH), w[weight_slot(meta, j)], NT)
        out[CH * j : CH * (j + 1)] = v
        v = v * mask_of(meta, j)
        s = SLOT[j]
        sums[s] += colsum(v)
        sums[2 + s] += colsum(v * v)
    spread_out(st_out, sums + [cnt[0:1], cnt[1:2]])


def weight_kernel(layer, meta, mine, near, far, cross, flat, tall):
    group, branch, c = meta[0], meta[1], meta[2]
    conv = 2 * branch + layer
    for slot in range(2):
        level = group + slot
        for t in range(9):
            for s, piece in (
                (c, mine[level, conv, t]),
                (c ^ 1, near[level, conv, t]),
                (c ^ 2, far[slot, branch, t]),
                (c ^ 3, cross[slot, branch, t]),
            ):
                flat[slot, at32(s), 128 * t : 128 * (t + 1)] = piece
                tall[slot, at32(s, 128 * t), :] = piece


def heads_kernel(meta, y, st, par, k0, k1, k2, k3, box_pack, dz, st_out, cst, x2, cot, wp, field, flat):
    norm_constants(meta, st, par, 2 + 2 * meta[1], cst)
    cot[...] = jnp.zeros((128, CP), BF)
    wp[...] = jnp.zeros((2, 128, 256), BF)

    @pl.when(meta[1] == 0)
    def _():
        for s, k in zip(slices_of(meta), (k0, k1, k2, k3)):
            cot[at32(s), :] = k[:, 0:CP]
            for slot in range(2):
                wp[slot, at32(s), :] = k[:, CP + 256 * slot : CP + 256 * (slot + 1)]

    @pl.when(meta[1] == 1)
    def _():
        cot[0:32, :] = box_pack[:, 0:CP]
        fine = meta[0] == 0
        for slot in range(2):
            row = lax.broadcasted_iota(jnp.int32, (32, 128), 0)
            box = jnp.zeros((32, 128), F32)
            for i in range(5):
                at = 32 + 3 * i
                line = jnp.where(fine, par[at : at + 1], par[at + 1 + slot : at + 2 + slot])
                box = jnp.where(row == i, line, box)
            wp[slot, 0:32, 0:128] = box.astype(BF)
            wp[slot, 0:32, 128:256] = box_pack[:, CP + 256 * slot + 128 : CP + 256 * (slot + 1)]

    for part in range(2):
        for j in range(NCH):
            m = mask_of(meta, j)
            if part == 0:
                _, z = normed(cst, y[CH * j : CH * (j + 1)], SLOT[j])
                m = z * sigmoid(z) * m
            field[CH * j : CH * (j + 1)] = m
        flat[...] = jnp.zeros((CP, 128), F32)
        to_compact(meta, field, flat)
        x2[:, 128 * part : 128 * (part + 1)] = flat[...].astype(BF)

    @pl.when(meta[0] == 0)
    def _():
        flat[...] = dot(cot[...], wp[0, :, 0:128], TN)

    @pl.when(meta[0] == 1)
    def _():
        for slot, a, b in ((0, 0, MID), (1, MID, MID + 128)):
            flat[a:b] = dot(cot[:, a:b], wp[slot, :, 0:128], TN)

    field[...] = jnp.zeros((PX, 128), F32)
    to_canvas(meta, flat, field)
    sums = [jnp.zeros((1, 128), F32) for _ in range(4)]
    for j in range(NCH):
        rows = slice(CH * j, CH * (j + 1))
        s = SLOT[j]
        xhat, z = normed(cst, y[rows], s)
        v = field[rows] * slope(z) * mask_of(meta, j)
        dz[rows] = v
        sums[s] += colsum(v)
        sums[2 + s] += colsum(v * xhat)
    spread_out(st_out, sums)


def logits_kernel(meta, x2, cot, wp, gw, mine, far, logits):
    def store(slot, v):
        bias = v[:, 128:256]

        @pl.when(meta[1] == 0)
        def _():
            gw_block(gw, slot, v[:, 0:128])

        @pl.when(meta[1] == 1)
        def _():
            gw_block(gw, slot, v[:, 0:128].T)

        return bias

    def finish(first, second):
        lane = lax.broadcasted_iota(jnp.int32, (128, 128), 1)
        cls = jnp.where(lane == 0, first, jnp.where(lane == 1, second, 0.0))
        a, b = first.T, second.T
        box = jnp.where((lane >= 7) & (lane < 12), pltpu.roll(b, 7, 1), 0.0)
        box = jnp.where((lane >= 2) & (lane < 7), pltpu.roll(a, 2, 1), box)
        gw_block(gw, 2, jnp.where(meta[1] == 0, cls, box))

    @pl.when(meta[0] == 0)
    def _():
        logits[...] = dot(wp[0], x2[...], NT).astype(BF)
        first = store(0, dot(cot[...], x2[...]))
        gw_block(gw, 1, jnp.zeros((128, 128), F32))
        finish(first, jnp.zeros((128, 128), F32))

    @pl.when(meta[0] == 1)
    def _():
        logits[...] = jnp.zeros((128, CP), BF)
        bias = []
        for slot, a, b in ((0, 0, MID), (1, MID, MID + 128)):
            logits[:, a:b] = dot(wp[slot], x2[a:b], NT).astype(BF)
            bias.append(store(slot, dot(cot[:, a:b], x2[a:b])))
        finish(*bias)

    for out, group in ((mine, meta[0]), (far, 1 - meta[0])):
        for i in range(2):
            out[i] = logits[at32(jnp.where(meta[1] == 0, 2 * group + i, 0)), :]


def gw_block(gw, i, v):
    for j in range(8):
        gw[j, i] = v[16 * j : 16 * (j + 1)].astype(BF)


def grad_sums(meta, total, sums):
    shift = pick(meta, total[0:1], total[1:2])
    gain = pick(meta, total[2:3], total[3:4])
    sums[...] = jnp.concatenate(list(shift) + list(gain) + [jnp.zeros((4, 128), F32)], axis=0)


def input_grad(meta, dz, y, cst, sums, j):
    s = SLOT[j]
    xhat, _ = normed(cst, y[CH * j : CH * (j + 1)], s)
    factor = cst[4 + s : 5 + s] * cst[2 + s : 3 + s]
    mean = (sums[s : s + 1] + xhat * sums[2 + s : 3 + s]) * cst[8 + s : 9 + s]
    return mask_of(meta, j) * factor * (dz - mean)


def out_grad(meta, dz, y, cst, st, sums, field, dyt):
    grad_sums(meta, jnp.sum(st[...], axis=0), sums)
    for j in range(NCH):
        rows = slice(CH * j, CH * (j + 1))
        v = input_grad(meta, dz[rows], y, cst, sums, j)
        field[8 + CH * j : 8 + CH * (j + 1)] = v
        dyt[:, rows] = v.T.astype(BF)


def conv_back(meta, last, w, y_in, cst_in, shifts, grad, st_out):
    total = [jnp.zeros((1, 128), F32) for _ in range(4)]
    for j in range(NCH):
        rows = slice(CH * j, CH * (j + 1))
        s = SLOT[j]
        v = dot(taps(shifts, CH * j, CH, True), w[weight_slot(meta, j)])
        xhat, z = normed(cst_in, y_in[rows], s)
        d = v * slope(z) * mask_of(meta, j)
        grad[rows] = v.astype(BF) if last else d
        total[s] += colsum(d)
        total[2 + s] += colsum(d * xhat)
    spread_out(st_out, total)
    return total


def as_parts(rows):
    v = jnp.concatenate(rows, axis=0)
    high = v.astype(BF).astype(F32)
    mid = (v - high).astype(BF).astype(F32)
    return jnp.concatenate([high, mid, v - high - mid, jnp.zeros((4, 128), F32)], axis=0).astype(BF)


def from_parts(block):
    v = block.astype(F32)
    return v[0:4] + v[4:8] + v[8:12]


def place_of(direct, j):
    return 2 * OWNER[j // 2] + j % 2 if direct else j


def weight_grad(direct, meta, dyt, act, field, shifts, wg):
    for j in range(NCH):
        field[8 + CH * j : 8 + CH * (j + 1)] = act[CH * j : CH * (j + 1)].astype(F32)
    fill_shifts(field, shifts)

    def store(slot, v):
        for t in range(9):
            for j in range(8):
                block = v[16 * j : 16 * (j + 1), 128 * t : 128 * (t + 1)].astype(BF)
                wg[place_of(direct, j), 9 * slot + t] = block

    @pl.when(meta[0] == 0)
    def _():
        store(0, dot(dyt[...], taps(shifts, 0, PX)))
        store(1, jnp.zeros((128, 1152), F32))

    @pl.when(meta[0] == 1)
    def _():
        store(0, dot(dyt[:, 0:CUT], taps(shifts, 0, CUT)))
        store(1, dot(dyt[:, CUT:PX], taps(shifts, CUT, PX - CUT)))


def second_back_kernel(direct, meta, dz, y, cst, st, w, act, y_in, cst_in, gw, grad, st_out, sums, wg, field, shifts, dyt):
    guard(field, shifts)
    out_grad(meta, dz, y, cst, st, sums, field, dyt)
    fill_shifts(field, shifts)
    block = as_parts(conv_back(meta, False, w, y_in, cst_in, shifts, grad, st_out))
    weight_grad(direct, meta, dyt, act, field, shifts, wg)
    for j in range(8):
        for i in range(3):
            wg[place_of(direct, j), 18 + i] = gw[j, i]
        wg[j, 21] = block


def first_back_kernel(direct, meta, dz, y, cst, st, w, act, y_in, cst_in, grad, st_out, sums, wg, field, shifts, dyt):
    guard(field, shifts)
    out_grad(meta, dz, y, cst, st, sums, field, dyt)
    fill_shifts(field, shifts)
    block = as_parts(conv_back(meta, True, w, y_in, cst_in, shifts, grad, st_out))
    weight_grad(direct, meta, dyt, act, field, shifts, wg)
    for j in range(8):
        wg[j, 18] = block


def final_kernel(direct, meta, d0, d1, y, cst, st0, st1, sums1, sums2, u0, u1, u2, u3, own, other, gs, norm, *scratch):
    sums, feat, stem, field, flat, dyt, gf, blocks = scratch
    load_inputs(meta, (u0, u1, u2, u3), feat, stem)
    grad_sums(meta, jnp.sum(st0[...] + st1[...], axis=0), sums)
    for j in range(NCH):
        rows = slice(CH * j, CH * (j + 1))
        _, z = normed(cst, y[rows], SLOT[j])
        v = (d0[rows].astype(F32) + d1[rows].astype(F32)) * slope(z) * mask_of(meta, j)
        field[rows] = input_grad(meta, v, y, cst, sums, j)
    flat[...] = jnp.zeros((CP, 128), F32)
    to_compact(meta, field, flat)
    dyt[...] = flat[...].T.astype(BF)
    c = meta[2]
    outs = ((own, c), (other, c ^ 2))

    @pl.when(meta[0] == 0)
    def _():
        gf[0:128, :] = dot(stem[:, 0:128], dyt[...], TN).astype(BF)
        blocks[0] = dot(dyt[...], feat[0:128, :], NT).astype(BF)
        for i in range(1, 6):
            blocks[i] = jnp.zeros((128, 128), BF)
        for out, s in outs:
            out[...] = gf[at32(s), :]

    @pl.when(meta[0] == 1)
    def _():
        gf[0:256, 0:MID] = dot(stem[:, 0:256], dyt[:, 0:MID], TN).astype(BF)
        gf[:, MID : MID + 128] = dot(stem[:, 256:768], dyt[:, MID : MID + 128], TN).astype(BF)
        for i in range(2):
            blocks[i] = dot(dyt[:, 0:MID], feat[128 * i : 128 * (i + 1), 0:MID], NT).astype(BF)
        for i in range(4):
            rows = slice(128 * i, 128 * (i + 1))
            blocks[2 + i] = dot(dyt[:, MID : MID + 128], feat[rows, MID : MID + 128], NT).astype(BF)
        for out, s in outs:
            out[...] = jnp.zeros((32, CP), BF)
            for i in range(2):
                at = pl.ds(pl.multiple_of(64 * s + 32 * i, 32), 32)
                out[:, MID * i : MID * (i + 1)] = gf[at, 0:MID]
            for i in range(4):
                at = pl.ds(pl.multiple_of(128 * s + 32 * i, 32), 32)
                out[:, 1024 + 128 * i : 1152 + 128 * i] = gf[at, MID : MID + 128]

    for i in range(3):
        block = blocks[3 * meta[1] + i]
        for j in range(8):
            gs[place_of(direct, j), i] = block[16 * j : 16 * (j + 1)]
    rest = jnp.zeros((4, 128), F32)
    norm[0] = jnp.concatenate([sums[0:4], sums1[0:4], sums2[0:4], rest], axis=0).astype(BF)


def sum_kernel(meta, got, total, st):
    n = total.shape[0]
    v = got[0].astype(F32)
    rows = from_parts(got[0, n])
    for d in range(1, got.shape[0]):
        v += got[d].astype(F32)
        rows += from_parts(got[d, n])
    total[...] = v[0:n].astype(BF)
    st[0] = jnp.concatenate([rows, jnp.zeros((4, 128), F32)], axis=0)


def source(meta, k):
    c = meta[4] ^ (k % 4)
    return c >> 1, c & 1, meta[5] ^ (k // 4)


def at16(h):
    return pl.ds(pl.multiple_of(16 * h, 16), 16)


def conv_out(meta, half, parts, out, room, sems):
    for k in range(4):
        group, branch, _ = source(meta, k)
        r = parts[k]
        for slot in range(2):

            @pl.when(group >= slot)
            def _():
                level = jnp.where(group == 0, 0, 1 + slot)
                for layer in range(2):
                    for t in range(9):
                        room[layer, level, branch, t] = r[18 * layer + 9 * slot + t].astype(F32)

    h = meta[5] ^ half
    copies = []
    for layer in range(2):
        for level in range(3):
            for branch in range(2):
                to = out.at[level, 2 * branch + layer, :, at16(h), :]
                copy = pltpu.make_async_copy(room.at[layer, level, branch], to, sems.at[layer, level, branch])
                copy.start()
                copies.append(copy)
    return copies


def near_out_kernel(meta, *refs):
    parts, (out, room, sems) = refs[:4], refs[4:]
    for copy in conv_out(meta, 0, parts, out, room, sems):
        copy.wait()


def far_out_kernel(meta, *refs):
    parts, (_, out, gcw, gcb, gbw, gbb, s0, s1, s2, gains, shifts, room, sems) = refs[:8], refs[8:]
    copies = conv_out(meta, 1, parts[4:], out, room, sems)
    c = meta[2]
    for k in range(8):
        group, branch, h = source(meta, k)
        r = parts[k]
        for group_id in range(2):
            slots = range(1 + group_id)

            @pl.when((group == group_id) & (branch == 0))
            def _():
                turned = r[38].astype(F32).T
                for half in range(2):
                    size = (16, 4)[half]

                    @pl.when(h == half)
                    def _():
                        for slot in slots:
                            level = group_id + slot
                            gcw[level, 16 * half : 16 * half + size, :] = r[36 + slot].astype(F32)[0:size]
                            gcb[level : level + 1, 16 * half : 16 * half + size] = turned[slot : slot + 1, 0:size]

            @pl.when((group == group_id) & (branch == 1))
            def _():
                bias = r[38, 0:16].astype(F32)
                for slot in slots:
                    level = group_id + slot
                    gbb[level : level + 1, :] = bias[0:1, 2 + 5 * slot : 7 + 5 * slot]
                    turned = r[36 + slot].astype(F32).T
                    for half in range(2):

                        @pl.when(h == half)
                        def _():
                            for i in range(5):
                                gbw[i, level : level + 1, 16 * half : 16 * half + 16] = turned[i : i + 1, 0:16]

        @pl.when((group == 0) & (branch == 0))
        def _():
            s0[at16(h), :] = r[39].astype(F32)

        @pl.when((group == 1) & (branch == 0))
        def _():
            for i in range(2):
                s1[at16(h), 128 * i : 128 * (i + 1)] = r[39 + i].astype(F32)
            s2[at16(h), 0:128] = r[41].astype(F32)

        @pl.when((group == 1) & (branch == 1))
        def _():
            for i in range(3):
                s2[at16(h), 128 * (i + 1) : 128 * (i + 2)] = r[39 + i].astype(F32)

    for k in range(4):
        group, branch, _ = source(meta, k)
        v = parts[k][42].astype(F32)
        mine = v[:, 0:32]
        for i in range(1, 4):
            mine = jnp.where(c == i, v[:, 32 * i : 32 * (i + 1)], mine)
        for layer in range(3):
            at = 0 if layer == 0 else layer + 2 * branch
            base = 4 * layer

            @pl.when(group == 0)
            def _():
                shifts[at, 0:1, :] = mine[base : base + 1]
                gains[at, 0:1, :] = mine[base + 2 : base + 3]

            @pl.when(group == 1)
            def _():
                shifts[at, 1:3, :] = mine[base : base + 2]
                gains[at, 1:3, :] = mine[base + 2 : base + 4]

    for copy in copies:
        copy.wait()


def class_out_kernel(sizes, meta, mine, near, far, far_near, class_out, box_out):
    n0, n1, n2 = sizes
    group, branch = meta[0], meta[1]

    def store(fine, rest):
        for out, src in ((class_out, 0), (box_out, 1)):
            n = out.shape[0]
            a, b = fine[src][0:n], rest[src][0:n]
            out[:, 0:n0] = a[:, 0:n0]
            out[:, n0 : n0 + n1] = b[:, 0:n1]
            out[:, n0 + n1 : n0 + n1 + n2] = b[:, MID : MID + n2]

    for b in range(2):

        @pl.when((group == 0) & (branch == b))
        def _():
            here, there = (mine, near), (far, far_near)
            store((here[b][b], here[1 - b][0]), (there[b][b], there[1 - b][0]))

        @pl.when((group == 1) & (branch == b))
        def _():
            here, there = (mine, near), (far, far_near)
            store((there[b][b], there[1 - b][0]), (here[b][b], here[1 - b][0]))


def feature_out_kernel(meta, own, received, fine, mid, coarse):
    def store(a, b):
        n1, n2 = mid.shape[1], coarse.shape[0]
        fine[...] = a[:, 0 : fine.shape[1]]
        for i in range(2):
            mid[32 * i : 32 * (i + 1), :] = b[:, MID * i : MID * i + n1]
        v = jnp.concatenate([b[:, 1024 + 128 * i : 1152 + 128 * i] for i in range(4)], axis=0)
        coarse[...] = v.astype(F32).T[0:n2].astype(BF)

    @pl.when(meta[0] == 0)
    def _():
        store(own, received)

    @pl.when(meta[0] == 1)
    def _():
        store(received, own)


def pack_kernel(f0, f1, f2, s0, s1, s2, gains, shifts, box, own, send, small):
    group = lax.axis_index("chan") // 2

    def fine(out):
        out[:, 0 : f0.shape[1]] = f0[...]
        out[:, f0.shape[1] : CP] = jnp.zeros((32, CP - f0.shape[1]), BF)
        out[:, CP : CP + 128] = s0[...]
        out[:, CP + 128 : PAR] = jnp.zeros((32, PAR - CP - 128), BF)

    def rest(out):
        n1, n2 = f1.shape[1], f2.shape[0]
        for i in range(2):
            out[:, MID * i : MID * i + n1] = f1[32 * i : 32 * (i + 1), :]
            out[:, MID * i + n1 : MID * (i + 1)] = jnp.zeros((32, MID - n1), BF)
        v = jnp.concatenate([f2[...].astype(F32), jnp.zeros((128 - n2, 128), F32)], axis=0).T.astype(BF)
        for i in range(4):
            out[:, 1024 + 128 * i : 1152 + 128 * i] = v[32 * i : 32 * (i + 1)]
        out[:, STEM : STEM + 256] = s1[...]
        out[:, STEM + 256 : PAR] = s2[...]

    @pl.when(group == 0)
    def _():
        fine(own)
        rest(send)

    @pl.when(group == 1)
    def _():
        rest(own)
        fine(send)

    small[...] = jnp.zeros((64, 32), F32)
    for base, v in ((0, gains), (16, shifts), (32, box)):
        for k in range(5):
            small[base + 3 * k : base + 3 * k + 3] = v[k].astype(F32)
    for i in range(2):
        v = small[32 * i : 32 * (i + 1)]
        high = v.astype(BF).astype(F32)
        mid = (v - high).astype(BF).astype(F32)
        block = jnp.concatenate([high, mid, v - high - mid, jnp.zeros((32, 32), F32)], axis=1).astype(BF)
        for out in (own, send):
            out[:, PAR + 128 * i : PAR + 128 * (i + 1)] = block


def pred_kernel(sizes, meta, ccot, cw, cb, bcot, bb, own, send, box):
    n0, n1, n2 = sizes
    lane = lax.broadcasted_iota(jnp.int32, (32, 128), 1)

    def biases(b, level):
        block = jnp.concatenate([b[...], jnp.zeros((3, 128 - b.shape[1]), F32)], axis=1)
        block = jnp.concatenate([block, jnp.zeros((5, 128), F32)], axis=0)
        col = block.T[0:32, level : level + 1]
        high = col.astype(BF).astype(F32)
        mid = (col - high).astype(BF).astype(F32)
        low = col - high - mid
        v = jnp.where(lane == 0, high, jnp.where(lane == 1, mid, jnp.where(lane == 2, low, 0.0)))
        return v.astype(BF)

    def fill(out, cot, b, fine, weights):
        n = cot.shape[0]
        out[...] = jnp.zeros((32, CLS), BF)
        if fine:
            out[0:n, 0:n0] = cot[:, 0:n0]
        else:
            out[0:n, 0:n1] = cot[:, n0 : n0 + n1]
            out[0:n, MID : MID + n2] = cot[:, n0 + n1 : n0 + n1 + n2]
        for slot in range(2):
            level = 0 if fine else 1 + slot
            at = CP + 256 * slot
            if weights:
                out[0:n, at : at + 128] = cw[level]
            out[:, at + 128 : at + 256] = biases(b, level)

    for group in range(2):

        @pl.when(meta[0] == group)
        def _():
            fill(own, ccot, cb, group == 0, True)
            fill(box, bcot, bb, group == 0, False)

        @pl.when(meta[0] != group)
        def _():
            fill(send, ccot, cb, group == 0, True)


def call(body, outs, scratch, args, last=False, limit=VMEM):
    place = jax.ShapeDtypeStruct if last else pltpu.VMEM
    specs = [pl.BlockSpec(memory_space=pltpu.SMEM if a.dtype == jnp.int32 else pltpu.VMEM) for a in args]
    return pl.pallas_call(
        body,
        out_shape=[place(s, d) for s, d in outs],
        in_specs=specs,
        out_specs=[pl.BlockSpec(memory_space=pltpu.VMEM)] * len(outs),
        scratch_shapes=[pltpu.VMEM(s, d) for s, d in scratch],
        compiler_params=pltpu.CompilerParams(vmem_limit_bytes=limit),
        cost_estimate=pl.CostEstimate(flops=10**6, bytes_accessed=10**4, transcendentals=0),
    )(*args)


def shards(f0, f1, f2, units, s0, s1, s2, conv, gains, shifts, cw, cb, bw, bb, ccot, bcot):
    dp = lax.axis_size("dp")
    c = lax.axis_index("chan")
    group, branch = c // 2, c % 2
    fine = group == 0
    direct = dp == 8
    place = lax.axis_index("dp") if direct else 0
    meta = jnp.stack([group, branch, c, units[0], place // 2, place % 2]).astype(jnp.int32)
    n0, n1, n2 = f0.shape[2], f1.shape[2], f2.shape[2]

    def across(v):
        return lax.ppermute(v, "chan", [(i, i ^ 2) for i in range(4)])

    def beside(v, pairs=((0, 1), (1, 0), (2, 3), (3, 2))):
        return lax.ppermute(v, "chan", list(pairs))

    def exchange(st, *hold):
        st, *hold = lax.optimization_barrier((st, *hold))
        st = lax.all_to_all(st, "dp", 0, 0, tiled=True)
        return lax.optimization_barrier((st, *hold)) if hold else st

    def add_up(st, between=None):
        if not direct:
            st = exchange(st)
            return (st, between(st)[1]) if between else st
        st = st[:1]
        for k in (2, 4):
            st = st + lax.ppermute(st, "dp", [(i, i ^ k) for i in range(8)])
        if between:
            st, got = between(st)
        st = st + lax.ppermute(st, "dp", [(i, i ^ 1) for i in range(8)])
        return (st, got) if between else st

    def after(v, *others):
        return lax.optimization_barrier((v, *others))[0]

    def over_z(v):
        if not direct:
            return v
        parts = []
        for k in range(4):
            pairs = [
                (8 * z + 4 * y + i, 8 * (i ^ k) + 4 * y + OWNER[z]) for z in range(4) for y in range(2) for i in range(4)
            ]
            parts.append(lax.ppermute(v, ("dp", "chan"), pairs))
        return parts

    def everywhere(parts, joined):
        if direct:
            parts = [jnp.stack(parts)] if joined else parts
            return parts + [over_y(p) for p in parts]
        v = lax.all_to_all(parts.reshape(4, 2, *parts.shape[1:]), "chan", 0, 0, tiled=True)
        return [v[:, 0], v[:, 1]] if joined else [v[k % 4, k // 4] for k in range(8)]

    def joined(*parts):
        return jnp.concatenate(parts, axis=-3)

    def over_y(v):
        return lax.ppermute(v, "dp", [(i, i ^ 1) for i in range(8)])

    def reduce(v, st=None):
        if not direct:
            v = lax.optimization_barrier(lax.psum(v.astype(F32), "dp")).astype(BF)
            return (v[:, :-1], exchange(st)) if st is not None else v
        v = exchange(v)
        if st is None:
            return jnp.sum(v.astype(F32), axis=0).astype(BF)
        return call(sum_kernel, [((v.shape[1] - 1, 16, 128), BF), ((1, 8, 128), F32)], [], (meta, v))

    own, send = call(
        pack_kernel,
        [((32, WIDE), BF), ((32, WIDE), BF)],
        [((64, 32), F32)],
        (f0[0], f1[0], f2[0].T, s0, s1, s2, gains.transpose(1, 0, 2), shifts.transpose(1, 0, 2), bw.transpose(1, 0, 2)),
        limit=WHOLE,
    )
    far_u = across(send)
    own_pred, send_pred, box_pred = call(
        functools.partial(pred_kernel, (n0, n1, n2)),
        [((32, CLS), BF)] * 3,
        [],
        (meta, ccot[0], cw, cb, bcot[0], after(bb, own)),
        limit=WHOLE,
    )
    u = (after(own, send_pred), far_u, beside(own), beside(far_u))
    near = beside(conv)
    far_pred = across(send_pred)
    to_class = ((1, 0), (3, 2))
    near_pred, cross_pred = beside(own_pred, to_class), beside(far_pred, to_class)

    def weights_of(layer, far):
        return call(
            functools.partial(weight_kernel, layer),
            [((2, 128, 1152), BF), ((2, 1152, 128), BF)],
            [],
            (meta, conv, near, far, beside(far)),
        )

    canvas = (PX, 128)
    stat = (dp, 8, 128)
    moved = [((PX + 16, 128), F32), ((3, PX + 2 * ST, 128), BF)]
    y0, st, cnt, par = call(
        stem_kernel,
        [(canvas, F32), (stat, F32), ((8, 128), F32), ((64, 128), F32)],
        [((512, CP), BF), ((128, 768), BF), ((CP, 128), F32)],
        (meta, *u),
    )
    far1, far2 = (
        across(after(lax.dynamic_slice_in_dim(conv[:, layer::2], 1 - group, 2, 0), cnt, far_pred)) for layer in range(2)
    )
    st, far1 = add_up(st, lambda v: (after(v, near_pred, cross_pred), after(far1, v)))
    w1, w1_tall = weights_of(0, far1)
    forward_outs = [(canvas, BF), (canvas, F32), (stat, F32), ((16, 128), F32)]
    act0, y1, st, cst0 = call(functools.partial(forward_kernel, True), forward_outs, moved, (meta, y0, st, cnt, w1, par))
    w2, w2_tall = weights_of(1, after(far2, act0))
    pred = (own_pred, far_pred, near_pred, cross_pred, box_pred)
    st, w2, w2_tall, *pred = exchange(st, w2, w2_tall, *pred)
    act1, y2, st, cst1 = call(
        functools.partial(forward_kernel, False), forward_outs, moved, (meta, y1, st, cnt, w2, par)
    )
    st = exchange(st)
    dz2, st, cst2, x2, cot, wp = call(
        heads_kernel,
        [(canvas, F32), (stat, F32), ((16, 128), F32), ((CP, 256), BF), ((128, CP), BF), ((2, 128, 256), BF)],
        [(canvas, F32), ((CP, 128), F32)],
        (meta, y2, st, par, *pred),
    )
    st = exchange(st)
    gw, mine, far = call(
        logits_kernel,
        [((8, 3, 16, 128), BF), ((2, 32, CP), BF), ((2, 32, CP), BF)],
        [((128, CP), BF)],
        (meta, x2, cot, after(wp, st)),
    )
    far = across(far)
    near = beside(mine)
    back_scratch = moved + [((128, PX), BF)]
    dz1, st, sums2, wg2 = call(
        functools.partial(second_back_kernel, direct),
        [(canvas, F32), (stat, F32), ((8, 128), F32), ((8, 22, 16, 128), BF)],
        back_scratch,
        (meta, dz2, y2, cst2, st, w2_tall, act1, y1, cst1, gw),
    )
    wg2, near, far = lax.optimization_barrier((wg2, near, far))
    sum2, st = reduce(wg2, st)
    far = after(far, st)
    far_near = beside(far)
    d0, st, sums1, wg1 = call(
        functools.partial(first_back_kernel, direct),
        [(canvas, BF), (stat, F32), ((8, 128), F32), ((8, 19, 16, 128), BF)],
        back_scratch,
        (meta, dz1, y1, cst1, st, w1_tall, act0, y0, cst0),
    )
    d0_other = beside(d0)
    wg1, d0_other, far_near = lax.optimization_barrier((wg1, d0_other, far_near))
    sum1, st = reduce(wg1, st)
    st_other = beside(st)
    own, other, gs, norm = call(
        functools.partial(final_kernel, direct),
        [((32, CP), BF), ((32, CP), BF), ((8, 3, 16, 128), BF), ((1, 16, 128), BF)],
        [
            ((8, 128), F32),
            ((512, CP), BF),
            ((128, 768), BF),
            (canvas, F32),
            ((CP, 128), F32),
            ((128, CP), BF),
            ((512, CP), BF),
            ((6, 128, 128), BF),
        ],
        (meta, d0, d0_other, y0, cst0, st, st_other, sums1, sums2, *u),
    )
    received = across(other)
    gs = reduce(gs)
    norm = norm if direct else jnp.broadcast_to(norm[None], (8, *norm.shape))
    grads = everywhere(over_z(joined(sum1, sum2, gs, norm)), False)

    box_rows, class_rows = bcot.shape[1], ccot.shape[1]
    class_out, box_out = call(
        functools.partial(class_out_kernel, (n0, n1, n2)),
        [((class_rows, n0 + n1 + n2), BF), ((box_rows, n0 + n1 + n2), BF)],
        [],
        (meta, mine, near, far, far_near),
        True,
    )
    grad_fine, grad_mid, grad_coarse = call(
        feature_out_kernel, [(f0.shape[1:], BF), (f1.shape[1:], BF), ((n2, f2.shape[1]), BF)], [], (meta, own, received), True
    )

    any_space = pl.BlockSpec(memory_space=pl.ANY)
    vmem = pl.BlockSpec(memory_space=pltpu.VMEM)
    smem = pl.BlockSpec(memory_space=pltpu.SMEM)
    room = [pltpu.VMEM((2, 3, 2, conv.shape[2], 16, 128), F32), pltpu.SemaphoreType.DMA((2, 3, 2))]
    params = pltpu.CompilerParams(vmem_limit_bytes=VMEM)
    grad_conv = pl.pallas_call(
        near_out_kernel,
        out_shape=jax.ShapeDtypeStruct(conv.shape, F32),
        in_specs=[smem] + [vmem] * 4,
        out_specs=any_space,
        scratch_shapes=room,
        compiler_params=params,
    )(meta, *grads[:4])
    shapes = [conv.shape, cw.shape, cb.shape, (5, 3, 32), bb.shape, s0.shape, s1.shape, s2.shape, (5, 3, 32), (5, 3, 32)]
    grad_conv, grad_cw, grad_cb, grad_bw, grad_bb, grad_s0, grad_s1, grad_s2, grad_gains, grad_shifts = pl.pallas_call(
        far_out_kernel,
        out_shape=[jax.ShapeDtypeStruct(s, F32) for s in shapes],
        in_specs=[smem] + [vmem] * 8 + [any_space],
        out_specs=[any_space] + [vmem] * 9,
        scratch_shapes=room,
        input_output_aliases={9: 0},
        compiler_params=params,
    )(meta, *grads, grad_conv)
    return (
        class_out[None],
        box_out[None],
        grad_fine[None],
        grad_mid[None],
        grad_coarse.T[None],
        grad_s0,
        grad_s1,
        grad_s2,
        grad_conv,
        grad_gains.transpose(1, 0, 2),
        grad_shifts.transpose(1, 0, 2),
        grad_cw,
        grad_cb,
        grad_bw.transpose(1, 0, 2),
        grad_bb,
    )


def solution(mesh):
    placed = (
        P("dp", "chan", None),
        P("dp", "chan", None),
        P("dp", "chan", None),
        P("dp"),
        P("chan", None),
        P("chan", None),
        P("chan", None),
        P(None, None, None, "chan", None),
        P(None, None, "chan"),
        P(None, None, "chan"),
        P(None, "chan", None),
        P(None, "chan"),
        P(None, None, "chan"),
        P(),
        P("dp", "chan", None),
        P("dp", None, None),
    )
    return jax.shard_map(
        shards,
        mesh=mesh,
        in_specs=placed,
        out_specs=(
            P("dp", "chan", None),
            P("dp", None, None),
            P("dp", "chan", None),
            P("dp", "chan", None),
            P("dp", "chan", None),
            P("chan", None),
            P("chan", None),
            P("chan", None),
            P(None, None, None, "chan", None),
            P(None, None, "chan"),
            P(None, None, "chan"),
            P(None, "chan", None),
            P(None, "chan"),
            P(None, None, "chan"),
            P(),
        ),
        check_vma=False,
    )
```

time: 319 us -> 180 us (0.56)
  the two profiles are of different devices: /device:TPU:2 before, /device:TPU:9 now
where the time goes in v2:
time: 180 us
  blocking collectives  73.7 us (41%)
  starting transfers between devices  37.4 us (21%)
  Pallas kernels  34.3 us (19%)
  waiting for transfers between devices  28.8 us (16%)
  local copies, waits for them, and re-layouts  3.63 us (2%)
    all_to_all x6, blocking collectives, exchange(): st = lax.all_to_all(st, 'dp', 0, 0, tiled=True)  73.7 us
    pallas_call x16, Pallas kernels, call(): pl.pallas_call(body, out_shape=[place(s, d) for s, d in outs], in_specs=s...  28.3 us
    ppermute x11, starting transfers between devices, beside(): return lax.ppermute(v, 'chan', list(pairs))  15.8 us
    ppermute x4, starting transfers between devices, over_z(): parts.append(lax.ppermute(v, ('dp', 'chan'), pairs))  11.3 us
    ppermute x4, waiting for transfers between devices, over_z(): parts.append(lax.ppermute(v, ('dp', 'chan'), pairs))  9.58 us
    ppermute x11, waiting for transfers between devices, beside(): return lax.ppermute(v, 'chan', list(pairs))  4.8 us
    ppermute x4, waiting for transfers between devices, over_y(): return lax.ppermute(v, 'dp', [(i, i ^ 1) for i in range(8)])  4.66 us
    ppermute x6, waiting for transfers between devices, across(): return lax.ppermute(v, 'chan', [(i, i ^ 2) for i in range(4)])  4.6 us
  transfers between devices with their start and end apart: 28, of which 13 were waited for; matrix products, arithmetic and copies ran while one was open for 2% of the time, Pallas kernels for 8%

profile of v2, /device:TPU:9, one launch (start us, length us, event | category | flops | bytes accessed | tf_op | source)
XLA Modules:
  0.0 179.5 jit_solution(14342521751555064776)
XLA Ops:
  0.6 1.2 shard_map.271
  1.8 1.3 collective-permute-start
  3.1 1.0 collective-permute-start.1
  4.7 0.6 stack.23.meta
  5.3 1.3 shard_map.272
  6.7 0.3 collective-permute-start.6
  7.3 1.2 collective-permute-start.2
  8.5 2.0 %fusion = (bf16[3,2,9,32,128]{4,3,2,1,0:T(8,128)(2,1)S(1)}, bf16[3,2,9,32,128]{4,3,2,1,0:T(8,128)(2,1)}) fusion(bf16[3,4,9,32,128]{4,3,2,1,0:T(8,128)(2,1)} %mine.3), kind=kLoop, calls=%fused_computation.4 | loop fusion | bytes 1769472 | tf_op jit(solution)/shard_map/slice | solution.py:905
  10.5 1.0 constant_dynamic-slice_fusion
  11.6 1.7 shard_map.273
  13.3 1.1 collective-permute-start.10
  14.6 2.6 %collective-permute-done.3 = f32[1,8,128]{2,1,0:T(8,128)S(1)} collective-permute-done((f32[1,8,128]{2,1,0:T(8,128)S(1)}, f32[1,8,128]{2,1,0:T(8,128)S(1)}, u32[]{:S(2)}, u32[]{:S(2)}) %collective-permute-start.3) | collective-permute-done | bytes 4128 | tf_op jit(solution)/shard_map/ppermute | solution.py:824
  17.2 2.3 %collective-permute-start.4 = (f32[1,8,128]{2,1,0:T(8,128)S(1)}, f32[1,8,128]{2,1,0:T(8,128)S(1)}, u32[]{:S(2)}, u32[]{:S(2)}) collective-permute-start(f32[1,8,128]{2,1,0:T(8,128)S(1)} %slice_add_fusion), channel_id=1, source_target_pairs={{0,16},{4,20},{8,24},{12,28},{16,0},{20,4},{24,8},{28,12},{1,17},{... | collective-permute-start | bytes 12296 | tf_op jit(solution)/shard_map/ppermute | solution.py:824
  19.5 1.0 collective-permute-done.4
  20.5 1.4 collective-permute-done.10.far
  22.0 0.8 collective-permute-start.11
  22.8 1.0 collective-permute-start.12
  23.8 2.2 %collective-permute-start.5 = (bf16[32,2176]{1,0:T(8,128)(2,1)S(1)}, bf16[32,2176]{1,0:T(8,128)(2,1)S(1)}, u32[]{:S(2)}, u32[]{:S(2)}) collective-permute-start(bf16[32,2176]{1,0:T(8,128)(2,1)S(1)} %get-tuple-element.139.k0), channel_id=1, source_target_pairs={{1,0},{3,2},{5,4},{7,6},{9,8},{11,10},{13,12},{15,14},{17,16},{19,... | collective-permute-start | bytes 417800 | tf_op jit(solution)/shard_map/ppermute | solution.py:811
  26.0 1.3 collective-permute-start.7
  27.3 1.0 collective-permute-done.7.k3
  28.3 1.2 collective-permute-start.8
  29.5 1.5 collective-permute-done.8
  31.1 0.7 shard_map.274
  31.8 2.1 %shard_map.275 = (bf16[1920,128]{1,0:T(8,128)(2,1)S(1)}, f32[1920,128]{1,0:T(8,128)S(1)}, f32[8,8,128]{2,1,0:T(8,128)S(1)}, f32[16,128]{1,0:T(8,128)S(1)}) custom-call(s32[6]{0:T(128)S(1)} %copy-done.1, f32[1920,128]{1,0:T(8,128)S(1)} %get-tuple-element.110.y.y_in, f32[1,8,128]{2,1,0:T(8,128)S(1)} %add.27.st, f32[8,128]{1,0:T(8,128)S(1)} %get-tuple-element.114.cnt, ...), custom_call_target="tpu_custom_call" | custom-call | flops 1000000 | bytes 10000 | tf_op jit(solution)/shard_map/pallas_call | solution.py:786
  34.0 1.3 collective-permute-start.13
  35.3 1.2 collective-permute-done.13.cross
  36.5 0.7 shard_map.276
  37.2 9.7 %all_to_all.30.st = f32[8,8,128]{2,1,0:T(8,128)S(1)} all-to-all(f32[8,8,128]{2,1,0:T(8,128)S(1)} %get-tuple-element.127), channel_id=1, replica_groups=mesh['dp'=8,'chan'=4] {'dp'}, dimensions={0} | all-to-all | bytes 65536 | tf_op jit(solution)/shard_map/all_to_all | solution.py:815
  46.9 2.1 %shard_map.277 = (bf16[1920,128]{1,0:T(8,128)(2,1)S(1)}, f32[1920,128]{1,0:T(8,128)S(1)}, f32[8,8,128]{2,1,0:T(8,128)S(1)}, f32[16,128]{1,0:T(8,128)S(1)}) custom-call(s32[6]{0:T(128)S(1)} %copy-done.1, f32[1920,128]{1,0:T(8,128)S(1)} %get-tuple-element.119.y.y_in, f32[8,8,128]{2,1,0:T(8,128)S(1)} %all_to_all.30.st, f32[8,128]{1,0:T(8,128)S(1)} %get-tuple-element.114.cnt, ...), custom_call_target="tpu_custom_call" | custom-call | flops 1000000 | bytes 10000 | tf_op jit(solution)/shard_map/pallas_call | solution.py:786
  49.1 7.9 %all_to_all.31.st = f32[8,8,128]{2,1,0:T(8,128)S(1)} all-to-all(f32[8,8,128]{2,1,0:T(8,128)S(1)} %get-tuple-element.138), channel_id=1, replica_groups=mesh['dp'=8,'chan'=4] {'dp'}, dimensions={0} | all-to-all | bytes 65536 | tf_op jit(solution)/shard_map/all_to_all | solution.py:815
  57.0 2.4 %shard_map.278 = (f32[1920,128]{1,0:T(8,128)S(1)}, f32[8,8,128]{2,1,0:T(8,128)S(1)}, f32[16,128]{1,0:T(8,128)S(1)}, bf16[1664,256]{1,0:T(8,128)(2,1)S(1)}, bf16[...) custom-call(s32[6]{0:T(128)S(1)} %copy-done.1, f32[1920,128]{1,0:T(8,128)S(1)} %get-tuple-element.137.y, ...), custom_call_target="tpu_custom_call" | custom-call | flops 1000000 | bytes 10000 | tf_op jit(solution)/shard_map/pallas_call | solution.py:786
  59.4 7.9 %all_to_all.32.st = f32[8,8,128]{2,1,0:T(8,128)S(1)} all-to-all(f32[8,8,128]{2,1,0:T(8,128)S(1)} %get-tuple-element.147), channel_id=1, replica_groups=mesh['dp'=8,'chan'=4] {'dp'}, dimensions={0} | all-to-all | bytes 65536 | tf_op jit(solution)/shard_map/all_to_all | solution.py:815
  67.3 1.4 shard_map.279
  68.7 0.5 collective-permute-start.15
  69.2 4.2 %collective-permute-start.14 = (bf16[2,32,1664]{2,1,0:T(8,128)(2,1)S(1)}, bf16[2,32,1664]{2,1,0:T(8,128)(2,1)S(1)}, u32[]{:S(2)}, u32[]{:S(2)}) collective-permute-start(bf16[2,32,1664]{2,1,0:T(8,128)(2,1)S(1)} %get-tuple-element.149.mine), channel_id=1, source_target_pairs={{0,1},{1,0},{2,3},{3,2},{4,5},{5,4},{6,7},{7,6},{8,9},{9,8},{10,11... | collective-permute-start | bytes 638984 | tf_op jit(solution)/shard_map/ppermute | solution.py:811
  73.4 4.3 %shard_map.280 = (f32[1920,128]{1,0:T(8,128)S(1)}, f32[8,8,128]{2,1,0:T(8,128)}, f32[8,128]{1,0:T(8,128)S(1)}, bf16[8,22,16,128]{3,2,1,0:T(8,128)(2,1)S(1)}) custom-call(s32[6]{0:T(128)S(1)} %copy-done.1, f32[1920,128]{1,0:T(8,128)S(1)} %get-tuple-element.150.dz, f32[1920,128]{1,0:T(8,128)S(1)} %get-tuple-element.137.y, ...), custom_call_target="tpu_custom_call" | custom-call | flops 1000000 | bytes 10000 | tf_op jit(solution)/shard_map/pallas_call | solution.py:786
  77.7 21.0 %all_to_all.33.got = bf16[8,22,16,128]{3,2,1,0:T(8,128)(2,1)S(1)} all-to-all(bf16[8,22,16,128]{3,2,1,0:T(8,128)(2,1)S(1)} %get-tuple-element.160), channel_id=1, replica_groups=mesh['dp'=8,'chan'=4] {'dp'}, dimensions={0} | all-to-all | bytes 1441792 | tf_op jit(solution)/shard_map/all_to_all | solution.py:815
  98.7 0.6 shard_map.281
  99.3 4.1 %shard_map.282 = (bf16[1920,128]{1,0:T(8,128)(2,1)S(1)}, f32[8,8,128]{2,1,0:T(8,128)}, f32[8,128]{1,0:T(8,128)S(1)}, bf16[8,19,16,128]{3,2,1,0:T(8,128)(2,1)S(1)}) custom-call(s32[6]{0:T(128)S(1)} %copy-done.1, f32[1920,128]{1,0:T(8,128)S(1)} %get-tuple-element.163.dz, f32[1920,128]{1,0:T(8,128)S(1)} %get-tuple-element.119.y.y_in, ...), custom_call_target="tpu_custom_call" | custom-call | flops 1000000 | bytes 10000 | tf_op jit(solution)/shard_map/pallas_call | solution.py:786
  103.5 1.9 %collective-permute-start.16 = (bf16[1920,128]{1,0:T(8,128)(2,1)S(1)}, bf16[1920,128]{1,0:T(8,128)(2,1)S(1)}, u32[]{:S(2)}, u32[]{:S(2)}) collective-permute-start(bf16[1920,128]{1,0:T(8,128)(2,1)S(1)} %get-tuple-element.167.d0), channel_id=1, source_target_pairs={{0,1},{1,0},{2,3},{3,2},{4,5},{5,4},{6,7},{7,6},{8,9},{9,8},{10,11... | collective-permute-start | bytes 1474568 | tf_op jit(solution)/shard_map/ppermute | solution.py:811
  105.3 1.8 collective-permute-done.17.far_near
  107.1 19.3 %all_to_all.34.got = bf16[8,19,16,128]{3,2,1,0:T(8,128)(2,1)S(1)} all-to-all(bf16[8,19,16,128]{3,2,1,0:T(8,128)(2,1)S(1)} %get-tuple-element.172), channel_id=1, replica_groups=mesh['dp'=8,'chan'=4] {'dp'}, dimensions={0} | all-to-all | bytes 1245184 | tf_op jit(solution)/shard_map/all_to_all | solution.py:815
  126.4 0.6 shard_map.284
  127.0 1.6 collective-permute-start.18
  128.6 0.8 collective-permute-done.18.st1
  129.5 2.2 %shard_map.285 = (bf16[32,1664]{1,0:T(8,128)(2,1)S(1)}, bf16[32,1664]{1,0:T(8,128)(2,1)S(1)}, bf16[8,3,16,128]{3,2,1,0:T(8,128)(2,1)S(1)}, bf16[1,16,128]{2,1,0:T(8,128)(2,1)S(1)}) custom-call(s32[6]{0:T(128)S(1)} %copy-done.1, bf16[1920,128]{1,0:T(8,128)(2,1)S(1)} %get-tuple-element.167.d0, bf16[1920,128]{1,0:T(8,128)(2,1)S(1)} %collective-permute-done.16.d1, ...), custom_call_target="tpu_custom_call" | custom-call | flops 1000000 | bytes 10000 | tf_op jit(solution)/shard_map/pallas_call | solution.py:786
  131.7 7.9 %all_to_all.35 = bf16[8,3,16,128]{3,2,1,0:T(8,128)(2,1)S(1)} all-to-all(bf16[8,3,16,128]{3,2,1,0:T(8,128)(2,1)S(1)} %get-tuple-element.183), channel_id=1, replica_groups=mesh['dp'=8,'chan'=4] {'dp'}, dimensions={0} | all-to-all | bytes 196608 | tf_op jit(solution)/shard_map/all_to_all | solution.py:815
  139.7 5.1 %collective-permute-start.23 = (bf16[43,16,128]{2,1,0:T(8,128)(2,1)S(1)}, bf16[43,16,128]{2,1,0:T(8,128)(2,1)S(1)}, u32[]{:S(2)}, u32[]{:S(2)}) collective-permute-start(bf16[43,16,128]{2,1,0:T(8,128)(2,1)S(1)} %pad_maximum_fusion), channel_id=1, source_target_pairs={{0,24},{1,16},{2,8},{3,0},{4,28},{5,20},{6,12},{7,4},{8,26},{9,18}... | collective-permute-start | bytes 528392 | tf_op jit(solution)/shard_map/ppermute | solution.py:841
  144.8 0.4 collective-permute-start.22
  145.2 1.8 collective-permute-start.21
  147.0 4.0 %collective-permute-start.20 = (bf16[43,16,128]{2,1,0:T(8,128)(2,1)S(1)}, bf16[43,16,128]{2,1,0:T(8,128)(2,1)S(1)}, u32[]{:S(2)}, u32[]{:S(2)}) collective-permute-start(bf16[43,16,128]{2,1,0:T(8,128)(2,1)S(1)} %pad_maximum_fusion), channel_id=1, source_target_pairs={{0,0},{1,8},{2,16},{3,24},{4,4},{5,12},{6,20},{7,28},{8,2},{9,10},... | collective-permute-start | bytes 528392 | tf_op jit(solution)/shard_map/ppermute | solution.py:841
  151.0 6.1 %collective-permute-done.23.refs_3_ = bf16[43,16,128]{2,1,0:T(8,128)(2,1)S(1)} collective-permute-done((bf16[43,16,128]{2,1,0:T(8,128)(2,1)S(1)}, bf16[43,16,128]{2,1,0:T(8,128)(2,1)S(1)}, u32[]{:S(2)}, u32[]{:S(2)}) %collective-permute-start.23) | collective-permute-done | bytes 176160 | tf_op jit(solution)/shard_map/ppermute | solution.py:841
  157.1 0.6 collective-permute-start.27
  157.7 3.4 %collective-permute-done.22.refs_2_ = bf16[43,16,128]{2,1,0:T(8,128)(2,1)S(1)} collective-permute-done((bf16[43,16,128]{2,1,0:T(8,128)(2,1)S(1)}, bf16[43,16,128]{2,1,0:T(8,128)(2,1)S(1)}, u32[]{:S(2)}, u32[]{:S(2)}) %collective-permute-start.22) | collective-permute-done | bytes 176160 | tf_op jit(solution)/shard_map/ppermute | solution.py:841
  161.1 0.3 collective-permute-start.26
  161.5 1.1 collective-permute-start.25
  162.6 0.3 collective-permute-start.24
  162.9 1.3 shard_map.283
  164.2 3.1 %collective-permute-done.19.received = bf16[32,1664]{1,0:T(8,128)(2,1)S(1)} collective-permute-done((bf16[32,1664]{1,0:T(8,128)(2,1)S(1)}, bf16[32,1664]{1,0:T(8,128)(2,1)S(1)}, u32[]{:S(2)}, u32[]{:S(2)}) %collective-permute-start.19) | collective-permute-done | bytes 106528 | tf_op jit(solution)/shard_map/ppermute | solution.py:808
  167.4 1.3 shard_map.286
  168.7 1.7 shard_map.287.refs_8_
  170.4 0.9 collective-permute-done.25.refs_5_
  171.3 3.8 %collective-permute-done.24.refs_4_ = bf16[43,16,128]{2,1,0:T(8,128)(2,1)S(1)} collective-permute-done((bf16[43,16,128]{2,1,0:T(8,128)(2,1)S(1)}, bf16[43,16,128]{2,1,0:T(8,128)(2,1)S(1)}, u32[]{:S(2)}, u32[]{:S(2)}) %collective-permute-start.24) | collective-permute-done | bytes 176160 | tf_op jit(solution)/shard_map/ppermute | solution.py:855
  175.0 4.3 %shard_map.288 = (f32[3,4,9,32,128]{4,3,2,1,0:T(8,128)}, f32[3,20,128]{2,1,0:T(8,128)}, f32[3,20]{1,0:T(4,128)}, f32[5,3,32]{2,1,0:T(4,128)}, f32[3,5]{1,0:T(4,1...) custom-call(s32[6]{0:T(128)S(1)} %copy-done.1, ...), custom_call_target="tpu_custom_call", output_to_operand_aliasing={{0}: (9, {})} | custom-call | tf_op jit(solution)/shard_map/pallas_call | solution.py:1000
  (29 shorter events, 0.6 us)
Async XLA Ops:
  1.8 5.4 %collective-permute-start = (bf16[32,2560]{1,0:T(8,128)(2,1)S(1)}, bf16[32,2560]{1,0:T(8,128)(2,1)S(1)}, u32[]{:S(2)}, u32[]{:S(2)}) collective-permute-start(bf16[32,2560]{1,0:T(8,128)(2,1)S(1)} %get-tuple-element.109), channel_id=1, source_target_pairs={{0,2},{1,3},{2,0},{3,1},{4,6},{5,7},{6,4},{7,5},{8,10},{9,11},{10,... | collective-permute-start | bytes 491528 | tf_op jit(solution)/shard_map/ppermute | solution.py:808
  3.1 8.4 %collective-permute-start.1 = (bf16[32,2560]{1,0:T(8,128)(2,1)S(1)}, bf16[32,2560]{1,0:T(8,128)(2,1)S(1)}, u32[]{:S(2)}, u32[]{:S(2)}) collective-permute-start(bf16[32,2560]{1,0:T(8,128)(2,1)S(1)} %get-tuple-element.108.u0), channel_id=1, source_target_pairs={{0,1},{1,0},{2,3},{3,2},{4,5},{5,4},{6,7},{7,6},{8,9},{9,8},{10,11... | collective-permute-start | bytes 491528 | tf_op jit(solution)/shard_map/ppermute | solution.py:811
  5.3 6.2 %copy-start.1 = (s32[6]{0:T(128)S(1)}, s32[6]{0:T(128)}, u32[]{:S(2)}) copy-start(s32[6]{0:T(128)} %stack.23.meta) | copy-start | bytes 76
  6.7 24.4 %copy-start = (bf16[3,4,9,32,128]{4,3,2,1,0:T(8,128)(2,1)S(1)}, bf16[3,4,9,32,128]{4,3,2,1,0:T(8,128)(2,1)}, u32[]{:S(2)}) copy-start(bf16[3,4,9,32,128]{4,3,2,1,0:T(8,128)(2,1)} %mine.3) | copy-start | bytes 2654212
  6.7 6.6 %collective-permute-start.6 = (bf16[32,2176]{1,0:T(8,128)(2,1)S(1)}, bf16[32,2176]{1,0:T(8,128)(2,1)S(1)}, u32[]{:S(2)}, u32[]{:S(2)}) collective-permute-start(bf16[32,2176]{1,0:T(8,128)(2,1)S(1)} %get-tuple-element.107), channel_id=1, source_target_pairs={{0,2},{1,3},{2,0},{3,1},{4,6},{5,7},{6,4},{7,5},{8,10},{9,11},{10,... | collective-permute-start | bytes 417800 | tf_op jit(solution)/shard_map/ppermute | solution.py:808
  7.0 24.1 %collective-permute-start.9 = (bf16[3,4,9,32,128]{4,3,2,1,0:T(8,128)(2,1)}, bf16[3,4,9,32,128]{4,3,2,1,0:T(8,128)(2,1)S(1)}, u32[]{:S(2)}, u32[]{:S(2)}) collective-permute-start(bf16[3,4,9,32,128]{4,3,2,1,0:T(8,128)(2,1)} %mine.3), channel_id=1, source_target_pairs={{0,1},{1,0},{2,3},{3,2},{4,5},{5,4},{6,7},{7,6},{8,9},{9,8},{10,11... | collective-permute-start | bytes 2654216 | tf_op jit(solution)/shard_map/ppermute | solution.py:811
  7.3 4.3 %collective-permute-start.2 = (bf16[32,2560]{1,0:T(8,128)(2,1)S(1)}, bf16[32,2560]{1,0:T(8,128)(2,1)S(1)}, u32[]{:S(2)}, u32[]{:S(2)}) collective-permute-start(bf16[32,2560]{1,0:T(8,128)(2,1)S(1)} %collective-permute-done.u1), channel_id=1, source_target_pairs={{0,1},{1,0},{2,3},{3,2},{4,5},{5,4},{6,7},{7,6},{8,9},{9,8},{10,11... | collective-permute-start | bytes 491528 | tf_op jit(solution)/shard_map/ppermute | solution.py:811
  13.3 8.7 %collective-permute-start.10 = (bf16[2,2,9,32,128]{4,3,2,1,0:T(8,128)(2,1)S(1)}, bf16[2,2,9,32,128]{4,3,2,1,0:T(8,128)(2,1)S(1)}, u32[]{:S(2)}, u32[]{:S(2)}) collective-permute-start(bf16[2,2,9,32,128]{4,3,2,1,0:T(8,128)(2,1)S(1)} %get-tuple-element.115), channel_id=1, source_target_pairs={{0,2},{1,3},{2,0},{3,1},{4,6},{5,7},{6,4},{7,5},{8,10},{9,11},{10,... | collective-permute-start | bytes 884744 | tf_op jit(solution)/shard_map/ppermute | solution.py:808
  14.4 2.8 %collective-permute-start.3 = (f32[1,8,128]{2,1,0:T(8,128)S(1)}, f32[1,8,128]{2,1,0:T(8,128)S(1)}, u32[]{:S(2)}, u32[]{:S(2)}) collective-permute-start(f32[1,8,128]{2,1,0:T(8,128)S(1)} %slice.9), channel_id=1, source_target_pairs={{0,8},{4,12},{8,0},{12,4},{16,24},{20,28},{24,16},{28,20},{1,9},{5... | collective-permute-start | bytes 12296 | tf_op jit(solution)/shard_map/ppermute | solution.py:824
  17.2 3.4 %collective-permute-start.4 = (f32[1,8,128]{2,1,0:T(8,128)S(1)}, f32[1,8,128]{2,1,0:T(8,128)S(1)}, u32[]{:S(2)}, u32[]{:S(2)}) collective-permute-start(f32[1,8,128]{2,1,0:T(8,128)S(1)} %slice_add_fusion), channel_id=1, source_target_pairs={{0,16},{4,20},{8,24},{12,28},{16,0},{20,4},{24,8},{28,12},{1,17},{... | collective-permute-start | bytes 12296 | tf_op jit(solution)/shard_map/ppermute | solution.py:824
  22.0 9.1 %collective-permute-start.11 = (bf16[2,2,9,32,128]{4,3,2,1,0:T(8,128)(2,1)S(1)}, bf16[2,2,9,32,128]{4,3,2,1,0:T(8,128)(2,1)S(1)}, u32[]{:S(2)}, u32[]{:S(2)}) collective-permute-start(bf16[2,2,9,32,128]{4,3,2,1,0:T(8,128)(2,1)S(1)} %collective-permute-done.10.far), channel_id=1, source_target_pairs={{0,1},{1,0},{2,3},{3,2},{4,5},{5,4},{6,7},{7,6},{8,9},{9,8},{10,11... | collective-permute-start | bytes 884744 | tf_op jit(solution)/shard_map/ppermute | solution.py:811
  22.8 11.1 %collective-permute-start.12 = (bf16[2,2,9,32,128]{4,3,2,1,0:T(8,128)(2,1)S(1)}, bf16[2,2,9,32,128]{4,3,2,1,0:T(8,128)(2,1)S(1)}, u32[]{:S(2)}, u32[]{:S(2)}) collective-permute-start(bf16[2,2,9,32,128]{4,3,2,1,0:T(8,128)(2,1)S(1)} %get-tuple-element.121), channel_id=1, source_target_pairs={{0,2},{1,3},{2,0},{3,1},{4,6},{5,7},{6,4},{7,5},{8,10},{9,11},{10,... | collective-permute-start | bytes 884744 | tf_op jit(solution)/shard_map/ppermute | solution.py:808
  23.8 3.5 %collective-permute-start.5 = (bf16[32,2176]{1,0:T(8,128)(2,1)S(1)}, bf16[32,2176]{1,0:T(8,128)(2,1)S(1)}, u32[]{:S(2)}, u32[]{:S(2)}) collective-permute-start(bf16[32,2176]{1,0:T(8,128)(2,1)S(1)} %get-tuple-element.139.k0), channel_id=1, source_target_pairs={{1,0},{3,2},{5,4},{7,6},{9,8},{11,10},{13,12},{15,14},{17,16},{19,... | collective-permute-start | bytes 417800 | tf_op jit(solution)/shard_map/ppermute | solution.py:811
  26.0 2.3 %collective-permute-start.7 = (bf16[32,2176]{1,0:T(8,128)(2,1)S(1)}, bf16[32,2176]{1,0:T(8,128)(2,1)S(1)}, u32[]{:S(2)}, u32[]{:S(2)}) collective-permute-start(bf16[32,2176]{1,0:T(8,128)(2,1)S(1)} %collective-permute-done.6.k1), channel_id=1, source_target_pairs={{1,0},{3,2},{5,4},{7,6},{9,8},{11,10},{13,12},{15,14},{17,16},{19,... | collective-permute-start | bytes 417800 | tf_op jit(solution)/shard_map/ppermute | solution.py:811
  28.3 2.8 %collective-permute-start.8 = (f32[1,8,128]{2,1,0:T(8,128)S(1)}, f32[1,8,128]{2,1,0:T(8,128)S(1)}, u32[]{:S(2)}, u32[]{:S(2)}) collective-permute-start(f32[1,8,128]{2,1,0:T(8,128)S(1)} %add.26), channel_id=1, source_target_pairs={{0,4},{4,0},{8,12},{12,8},{16,20},{20,16},{24,28},{28,24},{1,5},{5... | collective-permute-start | bytes 12296 | tf_op jit(solution)/shard_map/ppermute | solution.py:827
  34.0 2.5 %collective-permute-start.13 = (bf16[2,2,9,32,128]{4,3,2,1,0:T(8,128)(2,1)S(1)}, bf16[2,2,9,32,128]{4,3,2,1,0:T(8,128)(2,1)S(1)}, u32[]{:S(2)}, u32[]{:S(2)}) collective-permute-start(bf16[2,2,9,32,128]{4,3,2,1,0:T(8,128)(2,1)S(1)} %collective-permute-done.12.far), channel_id=1, source_target_pairs={{0,1},{1,0},{2,3},{3,2},{4,5},{5,4},{6,7},{7,6},{8,9},{9,8},{10,11... | collective-permute-start | bytes 884744 | tf_op jit(solution)/shard_map/ppermute | solution.py:811
  68.7 9.0 %collective-permute-start.15 = (bf16[2,32,1664]{2,1,0:T(8,128)(2,1)S(1)}, bf16[2,32,1664]{2,1,0:T(8,128)(2,1)S(1)}, u32[]{:S(2)}, u32[]{:S(2)}) collective-permute-start(bf16[2,32,1664]{2,1,0:T(8,128)(2,1)S(1)} %get-tuple-element.157), channel_id=1, source_target_pairs={{0,2},{1,3},{2,0},{3,1},{4,6},{5,7},{6,4},{7,5},{8,10},{9,11},{10,... | collective-permute-start | bytes 638984 | tf_op jit(solution)/shard_map/ppermute | solution.py:808
  69.2 8.5 %collective-permute-start.14 = (bf16[2,32,1664]{2,1,0:T(8,128)(2,1)S(1)}, bf16[2,32,1664]{2,1,0:T(8,128)(2,1)S(1)}, u32[]{:S(2)}, u32[]{:S(2)}) collective-permute-start(bf16[2,32,1664]{2,1,0:T(8,128)(2,1)S(1)} %get-tuple-element.149.mine), channel_id=1, source_target_pairs={{0,1},{1,0},{2,3},{3,2},{4,5},{5,4},{6,7},{7,6},{8,9},{9,8},{10,11... | collective-permute-start | bytes 638984 | tf_op jit(solution)/shard_map/ppermute | solution.py:811
  103.5 3.7 %collective-permute-start.16 = (bf16[1920,128]{1,0:T(8,128)(2,1)S(1)}, bf16[1920,128]{1,0:T(8,128)(2,1)S(1)}, u32[]{:S(2)}, u32[]{:S(2)}) collective-permute-start(bf16[1920,128]{1,0:T(8,128)(2,1)S(1)} %get-tuple-element.167.d0), channel_id=1, source_target_pairs={{0,1},{1,0},{2,3},{3,2},{4,5},{5,4},{6,7},{7,6},{8,9},{9,8},{10,11... | collective-permute-start | bytes 1474568 | tf_op jit(solution)/shard_map/ppermute | solution.py:811
  105.3 1.8 collective-permute-start.17
  127.0 2.4 %collective-permute-start.18 = (f32[1,8,128]{2,1,0:T(8,128)S(1)}, f32[1,8,128]{2,1,0:T(8,128)S(1)}, u32[]{:S(2)}, u32[]{:S(2)}) collective-permute-start(f32[1,8,128]{2,1,0:T(8,128)S(1)} %get-tuple-element.173.st0), channel_id=1, source_target_pairs={{0,1},{1,0},{2,3},{3,2},{4,5},{5,4},{6,7},{7,6},{8,9},{9,8},{10,11... | collective-permute-start | bytes 12296 | tf_op jit(solution)/shard_map/ppermute | solution.py:811
  139.7 17.4 %collective-permute-start.23 = (bf16[43,16,128]{2,1,0:T(8,128)(2,1)S(1)}, bf16[43,16,128]{2,1,0:T(8,128)(2,1)S(1)}, u32[]{:S(2)}, u32[]{:S(2)}) collective-permute-start(bf16[43,16,128]{2,1,0:T(8,128)(2,1)S(1)} %pad_maximum_fusion), channel_id=1, source_target_pairs={{0,24},{1,16},{2,8},{3,0},{4,28},{5,20},{6,12},{7,4},{8,26},{9,18}... | collective-permute-start | bytes 528392 | tf_op jit(solution)/shard_map/ppermute | solution.py:841
  144.8 16.3 %collective-permute-start.22 = (bf16[43,16,128]{2,1,0:T(8,128)(2,1)S(1)}, bf16[43,16,128]{2,1,0:T(8,128)(2,1)S(1)}, u32[]{:S(2)}, u32[]{:S(2)}) collective-permute-start(bf16[43,16,128]{2,1,0:T(8,128)(2,1)S(1)} %pad_maximum_fusion), channel_id=1, source_target_pairs={{0,16},{1,24},{2,0},{3,8},{4,20},{5,28},{6,4},{7,12},{8,18},{9,26}... | collective-permute-start | bytes 528392 | tf_op jit(solution)/shard_map/ppermute | solution.py:841
  145.2 16.3 %collective-permute-start.21 = (bf16[43,16,128]{2,1,0:T(8,128)(2,1)S(1)}, bf16[43,16,128]{2,1,0:T(8,128)(2,1)S(1)}, u32[]{:S(2)}, u32[]{:S(2)}) collective-permute-start(bf16[43,16,128]{2,1,0:T(8,128)(2,1)S(1)} %pad_maximum_fusion), channel_id=1, source_target_pairs={{0,8},{1,0},{2,24},{3,16},{4,12},{5,4},{6,28},{7,20},{8,10},{9,2},... | collective-permute-start | bytes 528392 | tf_op jit(solution)/shard_map/ppermute | solution.py:841
  147.0 15.6 %collective-permute-start.20 = (bf16[43,16,128]{2,1,0:T(8,128)(2,1)S(1)}, bf16[43,16,128]{2,1,0:T(8,128)(2,1)S(1)}, u32[]{:S(2)}, u32[]{:S(2)}) collective-permute-start(bf16[43,16,128]{2,1,0:T(8,128)(2,1)S(1)} %pad_maximum_fusion), channel_id=1, source_target_pairs={{0,0},{1,8},{2,16},{3,24},{4,4},{5,12},{6,20},{7,28},{8,2},{9,10},... | collective-permute-start | bytes 528392 | tf_op jit(solution)/shard_map/ppermute | solution.py:841
  157.1 13.3 %collective-permute-start.27 = (bf16[43,16,128]{2,1,0:T(8,128)(2,1)S(1)}, bf16[43,16,128]{2,1,0:T(8,128)(2,1)S(1)}, u32[]{:S(2)}, u32[]{:S(2)}) collective-permute-start(bf16[43,16,128]{2,1,0:T(8,128)(2,1)S(1)} %collective-permute-done.23.refs_3_), channel_id=1, source_target_pairs={{0,4},{4,0},{8,12},{12,8},{16,20},{20,16},{24,28},{28,24},{1,5},{5... | collective-permute-start | bytes 528392 | tf_op jit(solution)/shard_map/ppermute | solution.py:855
  161.1 9.3 %collective-permute-start.26 = (bf16[43,16,128]{2,1,0:T(8,128)(2,1)S(1)}, bf16[43,16,128]{2,1,0:T(8,128)(2,1)S(1)}, u32[]{:S(2)}, u32[]{:S(2)}) collective-permute-start(bf16[43,16,128]{2,1,0:T(8,128)(2,1)S(1)} %collective-permute-done.22.refs_2_), channel_id=1, source_target_pairs={{0,4},{4,0},{8,12},{12,8},{16,20},{20,16},{24,28},{28,24},{1,5},{5... | collective-permute-start | bytes 528392 | tf_op jit(solution)/shard_map/ppermute | solution.py:855
  161.5 9.8 %collective-permute-start.25 = (bf16[43,16,128]{2,1,0:T(8,128)(2,1)S(1)}, bf16[43,16,128]{2,1,0:T(8,128)(2,1)S(1)}, u32[]{:S(2)}, u32[]{:S(2)}) collective-permute-start(bf16[43,16,128]{2,1,0:T(8,128)(2,1)S(1)} %collective-permute-done.21.refs_1_), channel_id=1, source_target_pairs={{0,4},{4,0},{8,12},{12,8},{16,20},{20,16},{24,28},{28,24},{1,5},{5... | collective-permute-start | bytes 528392 | tf_op jit(solution)/shard_map/ppermute | solution.py:855
  162.6 12.5 %collective-permute-start.24 = (bf16[43,16,128]{2,1,0:T(8,128)(2,1)S(1)}, bf16[43,16,128]{2,1,0:T(8,128)(2,1)S(1)}, u32[]{:S(2)}, u32[]{:S(2)}) collective-permute-start(bf16[43,16,128]{2,1,0:T(8,128)(2,1)S(1)} %collective-permute-done.20.refs_0_), channel_id=1, source_target_pairs={{0,4},{4,0},{8,12},{12,8},{16,20},{20,16},{24,28},{28,24},{1,5},{5... | collective-permute-start | bytes 528392 | tf_op jit(solution)/shard_map/ppermute | solution.py:855
  162.9 4.4 %collective-permute-start.19 = (bf16[32,1664]{1,0:T(8,128)(2,1)S(1)}, bf16[32,1664]{1,0:T(8,128)(2,1)S(1)}, u32[]{:S(2)}, u32[]{:S(2)}) collective-permute-start(bf16[32,1664]{1,0:T(8,128)(2,1)S(1)} %get-tuple-element.177), channel_id=1, source_target_pairs={{0,2},{1,3},{2,0},{3,1},{4,6},{5,7},{6,4},{7,5},{8,10},{9,11},{10,... | collective-permute-start | bytes 319496 | tf_op jit(solution)/shard_map/ppermute | solution.py:808

commit v3 on v2

--- a/solution.py
+++ b/solution.py
@@ -24,7 +24,8 @@
 STEM = 1536
 PAR = STEM + 768
 WIDE = PAR + 256
-CLS = CP + 512
+CLS = CP // 128 + 4
+TAPS = 36
 VMEM = 12 * 2**20
 WHOLE = 56 * 2**20
 OWNER = (0, 2, 1, 3)
@@ -263,8 +264,8 @@
             for s, piece in (
                 (c, mine[level, conv, t]),
                 (c ^ 1, near[level, conv, t]),
-                (c ^ 2, far[slot, branch, t]),
-                (c ^ 3, cross[slot, branch, t]),
+                (c ^ 2, far[9 * (2 * slot + branch) + t]),
+                (c ^ 3, cross[9 * (2 * slot + branch) + t]),
             ):
                 flat[slot, at32(s), 128 * t : 128 * (t + 1)] = piece
                 tall[slot, at32(s, 128 * t), :] = piece
@@ -275,16 +276,21 @@
     cot[...] = jnp.zeros((128, CP), BF)
     wp[...] = jnp.zeros((2, 128, 256), BF)
 
+    pixels = CP // 128
+
     @pl.when(meta[1] == 0)
     def _():
-        for s, k in zip(slices_of(meta), (k0, k1, k2, k3)):
-            cot[at32(s), :] = k[:, 0:CP]
+        for s, k, base in zip(slices_of(meta), (k0, k1, k2, k3), (0, TAPS, 0, TAPS)):
+            for i in range(pixels):
+                cot[at32(s), 128 * i : 128 * (i + 1)] = k[base + i]
             for slot in range(2):
-                wp[slot, at32(s), :] = k[:, CP + 256 * slot : CP + 256 * (slot + 1)]
+                for i in range(2):
+                    wp[slot, at32(s), 128 * i : 128 * (i + 1)] = k[base + pixels + 2 * slot + i]
 
     @pl.when(meta[1] == 1)
     def _():
-        cot[0:32, :] = box_pack[:, 0:CP]
+        for i in range(pixels):
+            cot[0:32, 128 * i : 128 * (i + 1)] = box_pack[i]
         fine = meta[0] == 0
         for slot in range(2):
             row = lax.broadcasted_iota(jnp.int32, (32, 128), 0)
@@ -294,7 +300,7 @@
                 line = jnp.where(fine, par[at : at + 1], par[at + 1 + slot : at + 2 + slot])
                 box = jnp.where(row == i, line, box)
             wp[slot, 0:32, 0:128] = box.astype(BF)
-            wp[slot, 0:32, 128:256] = box_pack[:, CP + 256 * slot + 128 : CP + 256 * (slot + 1)]
+            wp[slot, 0:32, 128:256] = box_pack[pixels + 2 * slot + 1]
 
     for part in range(2):
         for j in range(NCH):
@@ -378,6 +384,16 @@
         gw[j, i] = v[16 * j : 16 * (j + 1)].astype(BF)
 
 
+def stat_total(st):
+    if st.dtype == F32:
+        return jnp.sum(st[...], axis=0)
+    n = st.shape[1] - 1
+    rows = from_parts(st[0, n])
+    for d in range(1, st.shape[0]):
+        rows += from_parts(st[d, n])
+    return rows
+
+
 def grad_sums(meta, total, sums):
     shift = pick(meta, total[0:1], total[1:2])
     gain = pick(meta, total[2:3], total[3:4])
@@ -393,7 +409,7 @@
 
 
 def out_grad(meta, dz, y, cst, st, sums, field, dyt):
-    grad_sums(meta, jnp.sum(st[...], axis=0), sums)
+    grad_sums(meta, stat_total(st), sums)
     for j in range(NCH):
         rows = slice(CH * j, CH * (j + 1))
         v = input_grad(meta, dz[rows], y, cst, sums, j)
@@ -476,10 +492,10 @@
         wg[j, 18] = block
 
 
-def final_kernel(direct, meta, d0, d1, y, cst, st0, st1, sums1, sums2, u0, u1, u2, u3, own, other, gs, norm, *scratch):
+def final_kernel(direct, meta, d0, d1, y, cst, st, sums1, sums2, u0, u1, u2, u3, own, other, gs, norm, *scratch):
     sums, feat, stem, field, flat, dyt, gf, blocks = scratch
     load_inputs(meta, (u0, u1, u2, u3), feat, stem)
-    grad_sums(meta, jnp.sum(st0[...] + st1[...], axis=0), sums)
+    grad_sums(meta, stat_total(st), sums)
     for j in range(NCH):
         rows = slice(CH * j, CH * (j + 1))
         _, z = normed(cst, y[rows], SLOT[j])
@@ -526,15 +542,41 @@
     norm[0] = jnp.concatenate([sums[0:4], sums1[0:4], sums2[0:4], rest], axis=0).astype(BF)
 
 
-def sum_kernel(meta, got, total, st):
-    n = total.shape[0]
-    v = got[0].astype(F32)
-    rows = from_parts(got[0, n])
-    for d in range(1, got.shape[0]):
-        v += got[d].astype(F32)
-        rows += from_parts(got[d, n])
-    total[...] = v[0:n].astype(BF)
-    st[0] = jnp.concatenate([rows, jnp.zeros((4, 128), F32)], axis=0)
+def patch_kernel(wg, other, out):
+    n = wg.shape[1] - 1
+    block = as_parts([from_parts(wg[0, n]) + other[0, 0:4]])
+    for j in range(8):
+        out[j, n] = block
+
+
+def summed(v, begin, end):
+    total = v[0, begin:end].astype(F32)
+    for d in range(1, v.shape[0]):
+        total += v[d, begin:end].astype(F32)
+    return total.astype(BF)
+
+
+def sum_kernel(meta, second, total, extra):
+    total[0:9] = summed(second, 0, 9)
+    total[9:12] = summed(second, 18, 21)
+    extra[...] = summed(second, 9, 18)
+
+
+def join_kernel(meta, first, total, extra, gs, norm, out):
+    out[0:9] = summed(first, 0, 9)
+    out[9:18] = total[0:9]
+    out[27:30] = total[9:12]
+
+    @pl.when(meta[0] == 0)
+    def _():
+        out[18:27] = extra[...]
+
+    @pl.when(meta[0] == 1)
+    def _():
+        out[18:27] = summed(first, 9, 18)
+
+    out[30:33] = summed(gs, 0, 3)
+    out[33:34] = norm[...]
 
 
 def source(meta, k):
@@ -550,14 +592,11 @@
     for k in range(4):
         group, branch, _ = source(meta, k)
         r = parts[k]
-        for slot in range(2):
-
-            @pl.when(group >= slot)
-            def _():
-                level = jnp.where(group == 0, 0, 1 + slot)
-                for layer in range(2):
-                    for t in range(9):
-                        room[layer, level, branch, t] = r[18 * layer + 9 * slot + t].astype(F32)
+        for i in range(3):
+            layer = i if i < 2 else 1 - group
+            level = group if i < 2 else 2
+            for t in range(9):
+                room[layer, level, branch, t] = r[9 * i + t].astype(F32)
 
     h = meta[5] ^ half
     copies = []
@@ -571,67 +610,73 @@
     return copies
 
 
-def near_out_kernel(meta, *refs):
-    parts, (out, room, sems) = refs[:4], refs[4:]
-    for copy in conv_out(meta, 0, parts, out, room, sems):
-        copy.wait()
-
-
-def far_out_kernel(meta, *refs):
-    parts, (_, out, gcw, gcb, gbw, gbb, s0, s1, s2, gains, shifts, room, sems) = refs[:8], refs[8:]
-    copies = conv_out(meta, 1, parts[4:], out, room, sems)
-    c = meta[2]
-    for k in range(8):
-        group, branch, h = source(meta, k)
+def row_outs(meta, half, parts, gcw, gcb, gbw, s0, s1, s2):
+    h = meta[5] ^ half
+    for k in range(4):
+        group, branch, _ = source(meta, k)
         r = parts[k]
         for group_id in range(2):
             slots = range(1 + group_id)
 
             @pl.when((group == group_id) & (branch == 0))
             def _():
-                turned = r[38].astype(F32).T
-                for half in range(2):
-                    size = (16, 4)[half]
-
-                    @pl.when(h == half)
+                turned = r[29].astype(F32).T
+                for half_id in range(2):
+                    size = (16, 4)[half_id]
+
+                    @pl.when(h == half_id)
                     def _():
                         for slot in slots:
                             level = group_id + slot
-                            gcw[level, 16 * half : 16 * half + size, :] = r[36 + slot].astype(F32)[0:size]
-                            gcb[level : level + 1, 16 * half : 16 * half + size] = turned[slot : slot + 1, 0:size]
+                            gcw[level, 16 * half_id : 16 * half_id + size, :] = r[27 + slot].astype(F32)[0:size]
+                            gcb[level : level + 1, 16 * half_id : 16 * half_id + size] = turned[slot : slot + 1, 0:size]
 
             @pl.when((group == group_id) & (branch == 1))
             def _():
-                bias = r[38, 0:16].astype(F32)
                 for slot in slots:
-                    level = group_id + slot
-                    gbb[level : level + 1, :] = bias[0:1, 2 + 5 * slot : 7 + 5 * slot]
-                    turned = r[36 + slot].astype(F32).T
-                    for half in range(2):
-
-                        @pl.when(h == half)
+                    turned = r[27 + slot].astype(F32).T
+                    for half_id in range(2):
+
+                        @pl.when(h == half_id)
                         def _():
                             for i in range(5):
-                                gbw[i, level : level + 1, 16 * half : 16 * half + 16] = turned[i : i + 1, 0:16]
+                                at = 16 * half_id
+                                gbw[i, group_id + slot : group_id + slot + 1, at : at + 16] = turned[i : i + 1, 0:16]
 
         @pl.when((group == 0) & (branch == 0))
         def _():
-            s0[at16(h), :] = r[39].astype(F32)
+            s0[at16(h), :] = r[30].astype(F32)
 
         @pl.when((group == 1) & (branch == 0))
         def _():
             for i in range(2):
-                s1[at16(h), 128 * i : 128 * (i + 1)] = r[39 + i].astype(F32)
-            s2[at16(h), 0:128] = r[41].astype(F32)
+                s1[at16(h), 128 * i : 128 * (i + 1)] = r[30 + i].astype(F32)
+            s2[at16(h), 0:128] = r[32].astype(F32)
 
         @pl.when((group == 1) & (branch == 1))
         def _():
             for i in range(3):
-                s2[at16(h), 128 * (i + 1) : 128 * (i + 2)] = r[39 + i].astype(F32)
-
+                s2[at16(h), 128 * (i + 1) : 128 * (i + 2)] = r[30 + i].astype(F32)
+
+
+def near_out_kernel(meta, *refs):
+    parts, (out, gcw, gcb, gbw, s0, s1, s2, gbb, gains, shifts, room, sems) = refs[:4], refs[4:]
+    copies = conv_out(meta, 0, parts, out, room, sems)
+    row_outs(meta, 0, parts, gcw, gcb, gbw, s0, s1, s2)
+    c = meta[2]
     for k in range(4):
         group, branch, _ = source(meta, k)
-        v = parts[k][42].astype(F32)
+        r = parts[k]
+        for group_id in range(2):
+
+            @pl.when((group == group_id) & (branch == 1))
+            def _():
+                bias = r[29].astype(F32)
+                for slot in range(1 + group_id):
+                    level = group_id + slot
+                    gbb[level : level + 1, :] = bias[0:1, 2 + 5 * slot : 7 + 5 * slot]
+
+        v = r[33].astype(F32)
         mine = v[:, 0:32]
         for i in range(1, 4):
             mine = jnp.where(c == i, v[:, 32 * i : 32 * (i + 1)], mine)
@@ -649,6 +694,17 @@
                 shifts[at, 1:3, :] = mine[base : base + 2]
                 gains[at, 1:3, :] = mine[base + 2 : base + 4]
 
+    for copy in copies:
+        copy.wait()
+
+
+def far_out_kernel(meta, *refs):
+    parts, earlier, (out, gcw, gcb, gbw, s0, s1, s2, room, sems) = refs[:4], refs[5:11], refs[11:]
+    copies = conv_out(meta, 1, parts, out, room, sems)
+    outs = (gcw, gcb, gbw, s0, s1, s2)
+    for old, new in zip(earlier, outs):
+        new[...] = old[...]
+    row_outs(meta, 1, parts, *outs)
     for copy in copies:
         copy.wait()
 
@@ -739,8 +795,17 @@
             out[:, PAR + 128 * i : PAR + 128 * (i + 1)] = block
 
 
-def pred_kernel(sizes, meta, ccot, cw, cb, bcot, bb, own, send, box):
+def pred_kernel(sizes, meta, ccot, cw, cb, bcot, bb, conv, own, box, first, second, room, sems):
     n0, n1, n2 = sizes
+    copies = []
+    for layer, out in enumerate((first, second)):
+        for slot in range(2):
+            for branch in range(2):
+                taken = conv.at[1 - meta[0] + slot, 2 * branch + layer]
+                to = out.at[pl.ds(9 * (2 * slot + branch), 9)]
+                copy = pltpu.make_async_copy(taken, to, sems.at[layer, slot, branch])
+                copy.start()
+                copies.append(copy)
     lane = lax.broadcasted_iota(jnp.int32, (32, 128), 1)
 
     def biases(b, level):
@@ -753,44 +818,56 @@
         v = jnp.where(lane == 0, high, jnp.where(lane == 1, mid, jnp.where(lane == 2, low, 0.0)))
         return v.astype(BF)
 
-    def fill(out, cot, b, fine, weights):
+    def fill(out, base, cot, b, fine, weights):
         n = cot.shape[0]
-        out[...] = jnp.zeros((32, CLS), BF)
+        room[...] = jnp.zeros((32, CP), BF)
         if fine:
-            out[0:n, 0:n0] = cot[:, 0:n0]
+            room[0:n, 0:n0] = cot[:, 0:n0]
         else:
-            out[0:n, 0:n1] = cot[:, n0 : n0 + n1]
-            out[0:n, MID : MID + n2] = cot[:, n0 + n1 : n0 + n1 + n2]
+            room[0:n, 0:n1] = cot[:, n0 : n0 + n1]
+            room[0:n, MID : MID + n2] = cot[:, n0 + n1 : n0 + n1 + n2]
+        for i in range(CP // 128):
+            out[base + i] = room[:, 128 * i : 128 * (i + 1)]
         for slot in range(2):
             level = 0 if fine else 1 + slot
-            at = CP + 256 * slot
+            at = base + CP // 128 + 2 * slot
+            out[at] = jnp.zeros((32, 128), BF)
             if weights:
-                out[0:n, at : at + 128] = cw[level]
-            out[:, at + 128 : at + 256] = biases(b, level)
+                out[at, 0:n] = cw[level]
+            out[at + 1] = biases(b, level)
 
     for group in range(2):
 
         @pl.when(meta[0] == group)
         def _():
-            fill(own, ccot, cb, group == 0, True)
-            fill(box, bcot, bb, group == 0, False)
+            fill(own, 0, ccot, cb, group == 0, True)
+            fill(box, 0, bcot, bb, group == 0, False)
 
         @pl.when(meta[0] != group)
         def _():
-            fill(send, ccot, cb, group == 0, True)
-
-
-def call(body, outs, scratch, args, last=False, limit=VMEM):
+            fill(second, TAPS, ccot, cb, group == 0, True)
+
+    for copy in copies:
+        copy.wait()
+
+
+def call(body, outs, scratch, args, last=False, limit=VMEM, in_place=(), aliases={}, flops=10**6):
     place = jax.ShapeDtypeStruct if last else pltpu.VMEM
-    specs = [pl.BlockSpec(memory_space=pltpu.SMEM if a.dtype == jnp.int32 else pltpu.VMEM) for a in args]
+
+    def space(i, dtype):
+        if i in in_place:
+            return pl.BlockSpec(memory_space=pl.ANY)
+        return pl.BlockSpec(memory_space=pltpu.SMEM if dtype == jnp.int32 else pltpu.VMEM)
+
     return pl.pallas_call(
         body,
         out_shape=[place(s, d) for s, d in outs],
-        in_specs=specs,
-        out_specs=[pl.BlockSpec(memory_space=pltpu.VMEM)] * len(outs),
-        scratch_shapes=[pltpu.VMEM(s, d) for s, d in scratch],
+        in_specs=[space(i, a.dtype) for i, a in enumerate(args)],
+        out_specs=[space(len(args) + i, d) for i, (_, d) in enumerate(outs)],
+        scratch_shapes=[s if callable(getattr(s, "get_ref_aval", None)) else pltpu.VMEM(*s) for s in scratch],
+        input_output_aliases=aliases,
         compiler_params=pltpu.CompilerParams(vmem_limit_bytes=limit),
-        cost_estimate=pl.CostEstimate(flops=10**6, bytes_accessed=10**4, transcendentals=0),
+        cost_estimate=pl.CostEstimate(flops=flops, bytes_accessed=10**4, transcendentals=0),
     )(*args)
 
 
@@ -841,12 +918,11 @@
             parts.append(lax.ppermute(v, ("dp", "chan"), pairs))
         return parts
 
-    def everywhere(parts, joined):
+    def everywhere(parts):
         if direct:
-            parts = [jnp.stack(parts)] if joined else parts
             return parts + [over_y(p) for p in parts]
         v = lax.all_to_all(parts.reshape(4, 2, *parts.shape[1:]), "chan", 0, 0, tiled=True)
-        return [v[:, 0], v[:, 1]] if joined else [v[k % 4, k // 4] for k in range(8)]
+        return [v[k % 4, k // 4] for k in range(8)]
 
     def joined(*parts):
         return jnp.concatenate(parts, axis=-3)
@@ -854,14 +930,8 @@
     def over_y(v):
         return lax.ppermute(v, "dp", [(i, i ^ 1) for i in range(8)])
 
-    def reduce(v, st=None):
-        if not direct:
-            v = lax.optimization_barrier(lax.psum(v.astype(F32), "dp")).astype(BF)
-            return (v[:, :-1], exchange(st)) if st is not None else v
-        v = exchange(v)
-        if st is None:
-            return jnp.sum(v.astype(F32), axis=0).astype(BF)
-        return call(sum_kernel, [((v.shape[1] - 1, 16, 128), BF), ((1, 8, 128), F32)], [], (meta, v))
+    def reduce(v):
+        return lax.optimization_barrier(lax.psum(v.astype(F32), "dp")).astype(BF)
 
     own, send = call(
         pack_kernel,
@@ -871,25 +941,27 @@
         limit=WHOLE,
     )
     far_u = across(send)
-    own_pred, send_pred, box_pred = call(
+    own_pred, box_pred, send1, send2 = call(
         functools.partial(pred_kernel, (n0, n1, n2)),
-        [((32, CLS), BF)] * 3,
-        [],
-        (meta, ccot[0], cw, cb, bcot[0], after(bb, own)),
+        [((CLS, 32, 128), BF)] * 2 + [((TAPS, 32, 128), BF), ((TAPS + CLS, 32, 128), BF)],
+        [((32, CP), BF), pltpu.SemaphoreType.DMA((2, 2, 2))],
+        (meta, ccot[0], cw, cb, bcot[0], after(bb, own), conv),
         limit=WHOLE,
-    )
-    u = (after(own, send_pred), far_u, beside(own), beside(far_u))
-    near = beside(conv)
-    far_pred = across(send_pred)
+        in_place=(6,),
+        flops=2 * 10**9,
+    )
+    near = beside(after(conv, own))
+    far_u = after(far_u, near, send2)
+    u = (own, far_u, beside(own), beside(far_u))
     to_class = ((1, 0), (3, 2))
-    near_pred, cross_pred = beside(own_pred, to_class), beside(far_pred, to_class)
-
-    def weights_of(layer, far):
+    near_pred = beside(own_pred, to_class)
+
+    def weights_of(layer, far, cross):
         return call(
             functools.partial(weight_kernel, layer),
             [((2, 128, 1152), BF), ((2, 1152, 128), BF)],
             [],
-            (meta, conv, near, far, beside(far)),
+            (meta, conv, near, far, cross),
         )
 
     canvas = (PX, 128)
@@ -901,16 +973,17 @@
         [((512, CP), BF), ((128, 768), BF), ((CP, 128), F32)],
         (meta, *u),
     )
-    far1, far2 = (
-        across(after(lax.dynamic_slice_in_dim(conv[:, layer::2], 1 - group, 2, 0), cnt, far_pred)) for layer in range(2)
-    )
-    st, far1 = add_up(st, lambda v: (after(v, near_pred, cross_pred), after(far1, v)))
-    w1, w1_tall = weights_of(0, far1)
+    far1 = across(after(send1, far_u))
+    st, near_pred = exchange(st, near_pred)
+    far1 = after(far1, st)
+    far2 = across(after(send2, far1))
+    w1, w1_tall = weights_of(0, far1, beside(far1))
     forward_outs = [(canvas, BF), (canvas, F32), (stat, F32), ((16, 128), F32)]
     act0, y1, st, cst0 = call(functools.partial(forward_kernel, True), forward_outs, moved, (meta, y0, st, cnt, w1, par))
-    w2, w2_tall = weights_of(1, after(far2, act0))
-    pred = (own_pred, far_pred, near_pred, cross_pred, box_pred)
-    st, w2, w2_tall, *pred = exchange(st, w2, w2_tall, *pred)
+    st = exchange(st)
+    far2 = after(far2, st)
+    cross2 = beside(far2)
+    w2, w2_tall = weights_of(1, far2, cross2)
     act1, y2, st, cst1 = call(
         functools.partial(forward_kernel, False), forward_outs, moved, (meta, y1, st, cnt, w2, par)
     )
@@ -919,7 +992,7 @@
         heads_kernel,
         [(canvas, F32), (stat, F32), ((16, 128), F32), ((CP, 256), BF), ((128, CP), BF), ((2, 128, 256), BF)],
         [(canvas, F32), ((CP, 128), F32)],
-        (meta, y2, st, par, *pred),
+        (meta, y2, st, par, own_pred, far2, near_pred, cross2, box_pred),
     )
     st = exchange(st)
     gw, mine, far = call(
@@ -938,7 +1011,8 @@
         (meta, dz2, y2, cst2, st, w2_tall, act1, y1, cst1, gw),
     )
     wg2, near, far = lax.optimization_barrier((wg2, near, far))
-    sum2, st = reduce(wg2, st)
+    got2 = exchange(wg2) if direct else reduce(wg2)
+    st = got2 if direct else exchange(st)
     far = after(far, st)
     far_near = beside(far)
     d0, st, sums1, wg1 = call(
@@ -948,9 +1022,17 @@
         (meta, dz1, y1, cst1, st, w1_tall, act0, y0, cst0),
     )
     d0_other = beside(d0)
-    wg1, d0_other, far_near = lax.optimization_barrier((wg1, d0_other, far_near))
-    sum1, st = reduce(wg1, st)
-    st_other = beside(st)
+    st_other = beside(st[:1])
+    if direct:
+        (wg1,) = call(patch_kernel, [(wg1.shape, BF)], [], (wg1, st_other), aliases={0: 0})
+        total, extra = call(sum_kernel, [((12, 16, 128), BF), ((9, 16, 128), BF)], [], (meta, after(got2, d0)))
+        extra = lax.ppermute(extra, "chan", [(2, 0), (3, 1)])
+        wg1 = after(wg1, total)
+        wg1, d0_other, far_near = lax.optimization_barrier((wg1, d0_other, far_near))
+        got1 = st = exchange(wg1)
+    else:
+        got1 = reduce(wg1)
+        st = exchange(st + st_other)
     own, other, gs, norm = call(
         functools.partial(final_kernel, direct),
         [((32, CP), BF), ((32, CP), BF), ((8, 3, 16, 128), BF), ((1, 16, 128), BF)],
@@ -964,13 +1046,26 @@
             ((512, CP), BF),
             ((6, 128, 128), BF),
         ],
-        (meta, d0, d0_other, y0, cst0, st, st_other, sums1, sums2, *u),
+        (meta, d0, d0_other, y0, cst0, st, sums1, sums2, *u),
     )
     received = across(other)
-    gs = reduce(gs)
-    norm = norm if direct else jnp.broadcast_to(norm[None], (8, *norm.shape))
-    grads = everywhere(over_z(joined(sum1, sum2, gs, norm)), False)
-
+    if direct:
+        gs, extra, received = lax.optimization_barrier((exchange(gs), extra, received))
+        (grads,) = call(join_kernel, [((34, 16, 128), BF)], [], (meta, got1, total, extra, gs, norm))
+    else:
+        extra = lax.ppermute(got2[:, 9:18], "chan", [(2, 0), (3, 1)])
+        third = jnp.where(fine, extra, got1[:, 9:18])
+        norm = jnp.broadcast_to(norm[None], (8, *norm.shape))
+        grads = joined(got1[:, :9], got2[:, :9], third, got2[:, 18:21], reduce(gs), norm)
+    grads = everywhere(over_z(grads))
+
+    room = [((2, 3, 2, conv.shape[2], 16, 128), F32), pltpu.SemaphoreType.DMA((2, 3, 2))]
+    rows = [(cw.shape, F32), (cb.shape, F32), ((5, 3, 32), F32), (s0.shape, F32), (s1.shape, F32), (s2.shape, F32)]
+    wholes = [(bb.shape, F32), ((5, 3, 32), F32), ((5, 3, 32), F32)]
+    grad_conv, *half, grad_bb, grad_gains, grad_shifts = call(
+        near_out_kernel, [(conv.shape, F32)] + rows + wholes, room, (meta, *grads[:4]), True, in_place=(5,)
+    )
+    mine, own = after((mine, own), *half)
     box_rows, class_rows = bcot.shape[1], ccot.shape[1]
     class_out, box_out = call(
         functools.partial(class_out_kernel, (n0, n1, n2)),
@@ -983,29 +1078,15 @@
         feature_out_kernel, [(f0.shape[1:], BF), (f1.shape[1:], BF), ((n2, f2.shape[1]), BF)], [], (meta, own, received), True
     )
 
-    any_space = pl.BlockSpec(memory_space=pl.ANY)
-    vmem = pl.BlockSpec(memory_space=pltpu.VMEM)
-    smem = pl.BlockSpec(memory_space=pltpu.SMEM)
-    room = [pltpu.VMEM((2, 3, 2, conv.shape[2], 16, 128), F32), pltpu.SemaphoreType.DMA((2, 3, 2))]
-    params = pltpu.CompilerParams(vmem_limit_bytes=VMEM)
-    grad_conv = pl.pallas_call(
-        near_out_kernel,
-        out_shape=jax.ShapeDtypeStruct(conv.shape, F32),
-        in_specs=[smem] + [vmem] * 4,
-        out_specs=any_space,
-        scratch_shapes=room,
-        compiler_params=params,
-    )(meta, *grads[:4])
-    shapes = [conv.shape, cw.shape, cb.shape, (5, 3, 32), bb.shape, s0.shape, s1.shape, s2.shape, (5, 3, 32), (5, 3, 32)]
-    grad_conv, grad_cw, grad_cb, grad_bw, grad_bb, grad_s0, grad_s1, grad_s2, grad_gains, grad_shifts = pl.pallas_call(
+    grad_conv, grad_cw, grad_cb, grad_bw, grad_s0, grad_s1, grad_s2 = call(
         far_out_kernel,
-        out_shape=[jax.ShapeDtypeStruct(s, F32) for s in shapes],
-        in_specs=[smem] + [vmem] * 8 + [any_space],
-        out_specs=[any_space] + [vmem] * 9,
-        scratch_shapes=room,
-        input_output_aliases={9: 0},
-        compiler_params=params,
-    )(meta, *grads, grad_conv)
+        [(conv.shape, F32)] + rows,
+        room,
+        (meta, *grads[4:], grad_conv, *half),
+        True,
+        in_place=(5, 12),
+        aliases={5: 0},
+    )
     return (
         class_out[None],
         box_out[None],

time: 180 us -> 166 us (0.922)
  the two profiles are of different devices: /device:TPU:9 before, /device:TPU:2 now
where the time goes in v3:
time: 166 us; the launch traced here: 164 us
  blocking collectives  81.8 us (49%)
  Pallas kernels  34.9 us (21%)
  starting transfers between devices  27.4 us (17%)
  waiting for transfers between devices  17.4 us (10%)
  between operations  1.7 us (1%)
    all_to_all x6, blocking collectives, exchange(): st = lax.all_to_all(st, 'dp', 0, 0, tiled=True)  81.8 us
    pallas_call x19, Pallas kernels, call(): pl.pallas_call(body, out_shape=[place(s, d) for s, d in outs], in_specs=[...  34.9 us
    ppermute x4, starting transfers between devices, over_z(): parts.append(lax.ppermute(v, ('dp', 'chan'), pairs))  8.76 us
    ppermute x4, starting transfers between devices, over_y(): return lax.ppermute(v, 'dp', [(i, i ^ 1) for i in range(8)])  6.21 us
    ppermute x4, waiting for transfers between devices, over_z(): parts.append(lax.ppermute(v, ('dp', 'chan'), pairs))  5.82 us
    ppermute x10, waiting for transfers between devices, beside(): return lax.ppermute(v, 'chan', list(pairs))  4.68 us
    ppermute x5, starting transfers between devices, across(): return lax.ppermute(v, 'chan', [(i, i ^ 2) for i in range(4)])  3.93 us
    ppermute x5, waiting for transfers between devices, across(): return lax.ppermute(v, 'chan', [(i, i ^ 2) for i in range(4)])  3.8 us
  transfers between devices with their start and end apart: 25, of which 11 were waited for; matrix products, arithmetic and copies ran while one was open for 0% of the time, Pallas kernels for 11%

profile of v3, /device:TPU:2, one launch (start us, length us, event | category | flops | bytes accessed | tf_op | source)
XLA Modules:
  0.0 163.8 jit_solution(15965526566168758756)
XLA Ops:
  0.6 1.2 shard_map.271
  1.8 0.1 collective-permute-start.1
  1.9 0.1 collective-permute-start
  2.7 0.6 stack.23.meta
  3.3 2.2 %shard_map.272 = (bf16[17,32,128]{2,1,0:T(8,128)(2,1)S(1)}, bf16[17,32,128]{2,1,0:T(8,128)(2,1)S(1)}, bf16[36,32,128]{2,1,0:T(8,128)(2,1)S(1)}, bf16[53,32,128]{2,1,0:T(8,128)(2,1)S(1)}) custom-call(s32[6]{0:T(128)} %stack.23.meta, bf16[20,2100]{1,0:T(8,128)(2,1)} %bitcast.32, bf16[3,20,128]{2,1,0:T(8,128)(2,1)} %cw.1, f32[3,20]{1,0:T(4,128)} %cb.1, ...), custom_call_target="tpu_custom_call" | custom-call | flops 2000000000 | bytes 10000 | tf_op jit(solution)/shard_map/pallas_call | solution.py:862
  5.5 3.0 %collective-permute-done.u1 = bf16[32,2560]{1,0:T(8,128)(2,1)S(1)} collective-permute-done((bf16[32,2560]{1,0:T(8,128)(2,1)S(1)}, bf16[32,2560]{1,0:T(8,128)(2,1)S(1)}, u32[]{:S(2)}, u32[]{:S(2)}) %collective-permute-start) | collective-permute-done | bytes 163872 | tf_op jit(solution)/shard_map/ppermute | solution.py:885
  8.5 0.3 collective-permute-start.5
  8.8 0.5 collective-permute-start.3
  9.3 1.3 collective-permute-start.4
  10.6 0.0 collective-permute-done.2.u2
  10.6 0.0 collective-permute-done.3.u3
  10.6 1.6 shard_map.273
  12.2 0.4 collective-permute-done.4.k2
  12.6 12.6 %all_to_all.35.st = f32[8,8,128]{2,1,0:T(8,128)S(1)} all-to-all(f32[8,8,128]{2,1,0:T(8,128)S(1)} %get-tuple-element.116), channel_id=1, replica_groups=mesh['dp'=8,'chan'=4] {'dp'}, dimensions={0} | all-to-all | bytes 65536 | tf_op jit(solution)/shard_map/all_to_all | solution.py:892
  25.1 0.0 collective-permute-done.5.far
  25.1 1.5 collective-permute-start.7
  26.6 1.6 collective-permute-done.6.cross
  28.2 0.7 shard_map.274
  29.0 2.2 %shard_map.275 = (bf16[1920,128]{1,0:T(8,128)(2,1)S(1)}, f32[1920,128]{1,0:T(8,128)S(1)}, f32[8,8,128]{2,1,0:T(8,128)S(1)}, f32[16,128]{1,0:T(8,128)S(1)}) custom-call(s32[6]{0:T(128)S(1)} %copy-done.1, f32[1920,128]{1,0:T(8,128)S(1)} %get-tuple-element.113.y.y_in, f32[8,8,128]{2,1,0:T(8,128)S(1)} %all_to_all.35.st, f32[8,128]{1,0:T(8,128)S(1)} %get-tuple-element.119.cnt, ...), custom_call_target="tpu_custom_call" | custom-call | flops 1000000 | bytes 10000 | tf_op jit(solution)/shard_map/pallas_call | solution.py:862
  31.1 9.1 %all_to_all.36.st = f32[8,8,128]{2,1,0:T(8,128)S(1)} all-to-all(f32[8,8,128]{2,1,0:T(8,128)S(1)} %get-tuple-element.126), channel_id=1, replica_groups=mesh['dp'=8,'chan'=4] {'dp'}, dimensions={0} | all-to-all | bytes 65536 | tf_op jit(solution)/shard_map/all_to_all | solution.py:892
  40.2 1.8 %collective-permute-done.8.cross.k3 = bf16[53,32,128]{2,1,0:T(8,128)(2,1)S(1)} collective-permute-done((bf16[53,32,128]{2,1,0:T(8,128)(2,1)S(1)}, bf16[53,32,128]{2,1,0:T(8,128)(2,1)S(1)}, u32[]{:S(2)}, u32[]{:S(2)}) %collective-permute-start.8) | collective-permute-done | bytes 434208 | tf_op jit(solution)/shard_map/ppermute | solution.py:888
  42.0 0.7 shard_map.276
  42.7 2.1 %shard_map.277 = (bf16[1920,128]{1,0:T(8,128)(2,1)S(1)}, f32[1920,128]{1,0:T(8,128)S(1)}, f32[8,8,128]{2,1,0:T(8,128)S(1)}, f32[16,128]{1,0:T(8,128)S(1)}) custom-call(s32[6]{0:T(128)S(1)} %copy-done.1, f32[1920,128]{1,0:T(8,128)S(1)} %get-tuple-element.125.y.y_in, f32[8,8,128]{2,1,0:T(8,128)S(1)} %all_to_all.36.st, f32[8,128]{1,0:T(8,128)S(1)} %get-tuple-element.119.cnt, ...), custom_call_target="tpu_custom_call" | custom-call | flops 1000000 | bytes 10000 | tf_op jit(solution)/shard_map/pallas_call | solution.py:862
  44.9 9.1 %all_to_all.37.st = f32[8,8,128]{2,1,0:T(8,128)S(1)} all-to-all(f32[8,8,128]{2,1,0:T(8,128)S(1)} %get-tuple-element.131), channel_id=1, replica_groups=mesh['dp'=8,'chan'=4] {'dp'}, dimensions={0} | all-to-all | bytes 65536 | tf_op jit(solution)/shard_map/all_to_all | solution.py:892
  53.9 2.3 %shard_map.278 = (f32[1920,128]{1,0:T(8,128)S(1)}, f32[8,8,128]{2,1,0:T(8,128)S(1)}, f32[16,128]{1,0:T(8,128)S(1)}, bf16[1664,256]{1,0:T(8,128)(2,1)S(1)}, bf16[...) custom-call(s32[6]{0:T(128)S(1)} %copy-done.1, f32[1920,128]{1,0:T(8,128)S(1)} %get-tuple-element.130.y, ...), custom_call_target="tpu_custom_call" | custom-call | flops 1000000 | bytes 10000 | tf_op jit(solution)/shard_map/pallas_call | solution.py:862
  56.2 9.1 %all_to_all.38.st = f32[8,8,128]{2,1,0:T(8,128)S(1)} all-to-all(f32[8,8,128]{2,1,0:T(8,128)S(1)} %get-tuple-element.137), channel_id=1, replica_groups=mesh['dp'=8,'chan'=4] {'dp'}, dimensions={0} | all-to-all | bytes 65536 | tf_op jit(solution)/shard_map/all_to_all | solution.py:892
  65.3 1.3 shard_map.279
  66.6 0.8 collective-permute-start.10
  67.4 0.0 collective-permute-start.9
  67.4 4.3 %shard_map.280 = (f32[1920,128]{1,0:T(8,128)S(1)}, f32[8,8,128]{2,1,0:T(8,128)}, f32[8,128]{1,0:T(8,128)S(1)}, bf16[8,22,16,128]{3,2,1,0:T(8,128)(2,1)S(1)}) custom-call(s32[6]{0:T(128)S(1)} %copy-done.1, f32[1920,128]{1,0:T(8,128)S(1)} %get-tuple-element.140.dz, f32[1920,128]{1,0:T(8,128)S(1)} %get-tuple-element.130.y, ...), custom_call_target="tpu_custom_call" | custom-call | flops 1000000 | bytes 10000 | tf_op jit(solution)/shard_map/pallas_call | solution.py:862
  71.7 0.8 collective-permute-done.10.far
  72.5 0.0 collective-permute-done.9.near
  72.5 21.4 %all_to_all.39.st.second = bf16[8,22,16,128]{3,2,1,0:T(8,128)(2,1)S(1)} all-to-all(bf16[8,22,16,128]{3,2,1,0:T(8,128)(2,1)S(1)} %get-tuple-element.149), channel_id=1, replica_groups=mesh['dp'=8,'chan'=4] {'dp'}, dimensions={0} | all-to-all | bytes 1441792 | tf_op jit(solution)/shard_map/all_to_all | solution.py:892
  93.9 3.6 %shard_map.281 = (bf16[1920,128]{1,0:T(8,128)(2,1)S(1)}, f32[8,8,128]{2,1,0:T(8,128)S(1)}, f32[8,128]{1,0:T(8,128)S(1)}, bf16[8,19,16,128]{3,2,1,0:T(8,128)(2,1)S(1)}) custom-call(s32[6]{0:T(128)S(1)} %copy-done.1, f32[1920,128]{1,0:T(8,128)S(1)} %get-tuple-element.146.dz, f32[1920,128]{1,0:T(8,128)S(1)} %get-tuple-element.125.y.y_in, ...), custom_call_target="tpu_custom_call" | custom-call | flops 1000000 | bytes 10000 | tf_op jit(solution)/shard_map/pallas_call | solution.py:862
  97.5 0.1 collective-permute-start.12
  97.5 0.5 collective-permute-start.13
  98.0 0.1 collective-permute-start.11
  98.1 0.6 shard_map.283
  98.7 0.9 collective-permute-done.11.other
  99.7 0.0 collective-permute-done.13.far_near
  99.7 0.0 collective-permute-done.12.d1
  99.7 20.7 %all_to_all.40.st.first = bf16[8,19,16,128]{3,2,1,0:T(8,128)(2,1)S(1)} all-to-all(bf16[8,19,16,128]{3,2,1,0:T(8,128)(2,1)S(1)} %shard_map.282), channel_id=1, replica_groups=mesh['dp'=8,'chan'=4] {'dp'}, dimensions={0} | all-to-all | bytes 1245184 | tf_op jit(solution)/shard_map/all_to_all | solution.py:892
  120.4 2.9 %shard_map.284 = (bf16[32,1664]{1,0:T(8,128)(2,1)S(1)}, bf16[32,1664]{1,0:T(8,128)(2,1)S(1)}, bf16[8,3,16,128]{3,2,1,0:T(8,128)(2,1)}, bf16[1,16,128]{2,1,0:T(8,128)(2,1)S(1)}) custom-call(s32[6]{0:T(128)S(1)} %copy-done.1, bf16[1920,128]{1,0:T(8,128)(2,1)S(1)} %get-tuple-element.153.d0, bf16[1920,128]{1,0:T(8,128)(2,1)S(1)} %collective-permute-done.12.d1, ...), custom_call_target="tpu_custom_call" | custom-call | flops 1000000 | bytes 10000 | tf_op jit(solution)/shard_map/pallas_call | solution.py:862
  123.3 3.4 %all-to-all-start.6 = ((bf16[8,3,16,128]{3,2,1,0:T(8,128)(2,1)}), bf16[8,3,16,128]{3,2,1,0:T(8,128)(2,1)S(1)}, u32[]{:S(2)}, u32[]{:S(2)}) async-start(bf16[8,3,16,128]{3,2,1,0:T(8,128)(2,1)} %get-tuple-element.166), calls=%async_computation.6 | async-start | bytes 196608 | tf_op jit(solution)/shard_map/all_to_all | solution.py:892
  126.7 1.3 collective-permute-start.15
  128.0 2.7 %collective-permute-start.14 = (bf16[9,16,128]{2,1,0:T(8,128)(2,1)S(1)}, bf16[9,16,128]{2,1,0:T(8,128)(2,1)S(1)}, u32[]{:S(2)}, u32[]{:S(2)}) collective-permute-start(bf16[9,16,128]{2,1,0:T(8,128)(2,1)S(1)} %get-tuple-element.167), channel_id=1, source_target_pairs={{2,0},{3,1},{6,4},{7,5},{10,8},{11,9},{14,12},{15,13},{18,16},{19,... | collective-permute-start | bytes 110600 | tf_op jit(solution)/shard_map/ppermute | solution.py:1029
  130.7 1.6 collective-permute-done.14.extra
  132.3 0.0 collective-permute-done.15.received
  132.3 1.4 all-to-all-done.6.gs
  133.8 0.6 shard_map.285
  134.4 4.1 %collective-permute-start.19 = (bf16[34,16,128]{2,1,0:T(8,128)(2,1)S(1)}, bf16[34,16,128]{2,1,0:T(8,128)(2,1)S(1)}, u32[]{:S(2)}, u32[]{:S(2)}) collective-permute-start(bf16[34,16,128]{2,1,0:T(8,128)(2,1)S(1)} %shard_map.285), channel_id=1, source_target_pairs={{0,24},{1,16},{2,8},{3,0},{4,28},{5,20},{6,12},{7,4},{8,26},{9,18}... | collective-permute-start | bytes 417800 | tf_op jit(solution)/shard_map/ppermute | solution.py:918
  138.5 2.4 %collective-permute-start.18 = (bf16[34,16,128]{2,1,0:T(8,128)(2,1)S(1)}, bf16[34,16,128]{2,1,0:T(8,128)(2,1)S(1)}, u32[]{:S(2)}, u32[]{:S(2)}) collective-permute-start(bf16[34,16,128]{2,1,0:T(8,128)(2,1)S(1)} %shard_map.285), channel_id=1, source_target_pairs={{0,16},{1,24},{2,0},{3,8},{4,20},{5,28},{6,4},{7,12},{8,18},{9,26}... | collective-permute-start | bytes 417800 | tf_op jit(solution)/shard_map/ppermute | solution.py:918
  140.9 2.3 %collective-permute-start.16 = (bf16[34,16,128]{2,1,0:T(8,128)(2,1)S(1)}, bf16[34,16,128]{2,1,0:T(8,128)(2,1)S(1)}, u32[]{:S(2)}, u32[]{:S(2)}) collective-permute-start(bf16[34,16,128]{2,1,0:T(8,128)(2,1)S(1)} %shard_map.285), channel_id=1, source_target_pairs={{0,0},{1,8},{2,16},{3,24},{4,4},{5,12},{6,20},{7,28},{8,2},{9,10},... | collective-permute-start | bytes 417800 | tf_op jit(solution)/shard_map/ppermute | solution.py:918
  143.2 1.5 collective-permute-start.23
  144.7 0.1 collective-permute-done.18.refs_2_
  144.9 1.7 %collective-permute-start.22 = (bf16[34,16,128]{2,1,0:T(8,128)(2,1)S(1)}, bf16[34,16,128]{2,1,0:T(8,128)(2,1)S(1)}, u32[]{:S(2)}, u32[]{:S(2)}) collective-permute-start(bf16[34,16,128]{2,1,0:T(8,128)(2,1)S(1)} %collective-permute-done.18.refs_2_), channel_id=1, source_target_pairs={{0,4},{4,0},{8,12},{12,8},{16,20},{20,16},{24,28},{28,24},{1,5},{5... | collective-permute-start | bytes 417800 | tf_op jit(solution)/shard_map/ppermute | solution.py:931
  146.6 4.0 %collective-permute-done.17.refs_1_ = bf16[34,16,128]{2,1,0:T(8,128)(2,1)S(1)} collective-permute-done((bf16[34,16,128]{2,1,0:T(8,128)(2,1)S(1)}, bf16[34,16,128]{2,1,0:T(8,128)(2,1)S(1)}, u32[]{:S(2)}, u32[]{:S(2)}) %collective-permute-start.17) | collective-permute-done | bytes 139296 | tf_op jit(solution)/shard_map/ppermute | solution.py:918
  150.6 1.5 collective-permute-start.21
  152.0 1.7 %collective-permute-done.16.refs_0_ = bf16[34,16,128]{2,1,0:T(8,128)(2,1)S(1)} collective-permute-done((bf16[34,16,128]{2,1,0:T(8,128)(2,1)S(1)}, bf16[34,16,128]{2,1,0:T(8,128)(2,1)S(1)}, u32[]{:S(2)}, u32[]{:S(2)}) %collective-permute-start.16) | collective-permute-done | bytes 139296 | tf_op jit(solution)/shard_map/ppermute | solution.py:918
  153.8 1.5 collective-permute-start.20
  155.2 3.5 %shard_map.286 = (f32[3,4,9,32,128]{4,3,2,1,0:T(8,128)}, f32[3,20,128]{2,1,0:T(8,128)S(1)}, f32[3,20]{1,0:T(4,128)S(1)}, f32[5,3,32]{2,1,0:T(4,128)S(1)}, f32[32...) custom-call(s32[6]{0:T(128)S(1)} %copy-done.1, ...), custom_call_target="tpu_custom_call" | custom-call | flops 1000000 | bytes 10000 | tf_op jit(solution)/shard_map/pallas_call | solution.py:862
  158.7 1.3 shard_map.288
  160.1 1.3 shard_map.287
  161.4 2.3 %shard_map.289 = (f32[3,4,9,32,128]{4,3,2,1,0:T(8,128)}, f32[3,20,128]{2,1,0:T(8,128)}, f32[3,20]{1,0:T(4,128)}, f32[5,3,32]{2,1,0:T(4,128)}, f32[32,128]{1,0:T(...) custom-call(s32[6]{0:T(128)S(1)} %copy-done.1, ...), custom_call_target="tpu_custom_call", output_to_operand_aliasing={{0}: (5, {})} | custom-call | flops 1000000 | bytes 10000 | tf_op jit(solution)/shard_map/pallas_call | solution.py:862
  (17 shorter events, 0.1 us)
Async XLA Ops:
  1.8 6.7 %collective-permute-start.1 = (bf16[3,4,9,32,128]{4,3,2,1,0:T(8,128)(2,1)}, bf16[3,4,9,32,128]{4,3,2,1,0:T(8,128)(2,1)S(1)}, u32[]{:S(2)}, u32[]{:S(2)}) collective-permute-start(bf16[3,4,9,32,128]{4,3,2,1,0:T(8,128)(2,1)} %mine.3), channel_id=1, source_target_pairs={{0,1},{1,0},{2,3},{3,2},{4,5},{5,4},{6,7},{7,6},{8,9},{9,8},{10,11... | collective-permute-start | bytes 2654216 | tf_op jit(solution)/shard_map/ppermute | solution.py:888
  1.9 6.6 %collective-permute-start = (bf16[32,2560]{1,0:T(8,128)(2,1)S(1)}, bf16[32,2560]{1,0:T(8,128)(2,1)S(1)}, u32[]{:S(2)}, u32[]{:S(2)}) collective-permute-start(bf16[32,2560]{1,0:T(8,128)(2,1)S(1)} %get-tuple-element.108), channel_id=1, source_target_pairs={{0,2},{1,3},{2,0},{3,1},{4,6},{5,7},{6,4},{7,5},{8,10},{9,11},{10,... | collective-permute-start | bytes 491528 | tf_op jit(solution)/shard_map/ppermute | solution.py:885
  3.3 7.3 %copy-start.1 = (s32[6]{0:T(128)S(1)}, s32[6]{0:T(128)}, u32[]{:S(2)}) copy-start(s32[6]{0:T(128)} %stack.23.meta) | copy-start | bytes 76
  3.3 24.9 %copy-start = (bf16[3,4,9,32,128]{4,3,2,1,0:T(8,128)(2,1)S(1)}, bf16[3,4,9,32,128]{4,3,2,1,0:T(8,128)(2,1)}, u32[]{:S(2)}) copy-start(bf16[3,4,9,32,128]{4,3,2,1,0:T(8,128)(2,1)} %mine.3) | copy-start | bytes 2654212
  8.5 16.6 %collective-permute-start.5 = (bf16[36,32,128]{2,1,0:T(8,128)(2,1)S(1)}, bf16[36,32,128]{2,1,0:T(8,128)(2,1)S(1)}, u32[]{:S(2)}, u32[]{:S(2)}) collective-permute-start(bf16[36,32,128]{2,1,0:T(8,128)(2,1)S(1)} %get-tuple-element.121), channel_id=1, source_target_pairs={{0,2},{1,3},{2,0},{3,1},{4,6},{5,7},{6,4},{7,5},{8,10},{9,11},{10,... | collective-permute-start | bytes 884744 | tf_op jit(solution)/shard_map/ppermute | solution.py:885
  8.8 1.8 %collective-permute-start.2 = (bf16[32,2560]{1,0:T(8,128)(2,1)S(1)}, bf16[32,2560]{1,0:T(8,128)(2,1)S(1)}, u32[]{:S(2)}, u32[]{:S(2)}) collective-permute-start(bf16[32,2560]{1,0:T(8,128)(2,1)S(1)} %get-tuple-element.107.u0), channel_id=1, source_target_pairs={{0,1},{1,0},{2,3},{3,2},{4,5},{5,4},{6,7},{7,6},{8,9},{9,8},{10,11... | collective-permute-start | bytes 491528 | tf_op jit(solution)/shard_map/ppermute | solution.py:888
  8.8 1.8 %collective-permute-start.3 = (bf16[32,2560]{1,0:T(8,128)(2,1)S(1)}, bf16[32,2560]{1,0:T(8,128)(2,1)S(1)}, u32[]{:S(2)}, u32[]{:S(2)}) collective-permute-start(bf16[32,2560]{1,0:T(8,128)(2,1)S(1)} %collective-permute-done.u1), channel_id=1, source_target_pairs={{0,1},{1,0},{2,3},{3,2},{4,5},{5,4},{6,7},{7,6},{8,9},{9,8},{10,11... | collective-permute-start | bytes 491528 | tf_op jit(solution)/shard_map/ppermute | solution.py:888
  9.3 3.2 %collective-permute-start.4 = (bf16[17,32,128]{2,1,0:T(8,128)(2,1)S(1)}, bf16[17,32,128]{2,1,0:T(8,128)(2,1)S(1)}, u32[]{:S(2)}, u32[]{:S(2)}) collective-permute-start(bf16[17,32,128]{2,1,0:T(8,128)(2,1)S(1)} %get-tuple-element.115.k0), channel_id=1, source_target_pairs={{1,0},{3,2},{5,4},{7,6},{9,8},{11,10},{13,12},{15,14},{17,16},{19,... | collective-permute-start | bytes 417800 | tf_op jit(solution)/shard_map/ppermute | solution.py:888
  25.1 15.0 %collective-permute-start.7 = (bf16[53,32,128]{2,1,0:T(8,128)(2,1)S(1)}, bf16[53,32,128]{2,1,0:T(8,128)(2,1)S(1)}, u32[]{:S(2)}, u32[]{:S(2)}) collective-permute-start(bf16[53,32,128]{2,1,0:T(8,128)(2,1)S(1)} %get-tuple-element.127), channel_id=1, source_target_pairs={{0,2},{1,3},{2,0},{3,1},{4,6},{5,7},{6,4},{7,5},{8,10},{9,11},{10,... | collective-permute-start | bytes 1302536 | tf_op jit(solution)/shard_map/ppermute | solution.py:885
  26.6 1.6 collective-permute-start.6
  40.2 1.8 %collective-permute-start.8 = (bf16[53,32,128]{2,1,0:T(8,128)(2,1)S(1)}, bf16[53,32,128]{2,1,0:T(8,128)(2,1)S(1)}, u32[]{:S(2)}, u32[]{:S(2)}) collective-permute-start(bf16[53,32,128]{2,1,0:T(8,128)(2,1)S(1)} %collective-permute-done.7.far.k1), channel_id=1, source_target_pairs={{0,1},{1,0},{2,3},{3,2},{4,5},{5,4},{6,7},{7,6},{8,9},{9,8},{10,11... | collective-permute-start | bytes 1302536 | tf_op jit(solution)/shard_map/ppermute | solution.py:888
  66.6 5.9 %collective-permute-start.10 = (bf16[2,32,1664]{2,1,0:T(8,128)(2,1)S(1)}, bf16[2,32,1664]{2,1,0:T(8,128)(2,1)S(1)}, u32[]{:S(2)}, u32[]{:S(2)}) collective-permute-start(bf16[2,32,1664]{2,1,0:T(8,128)(2,1)S(1)} %get-tuple-element.148), channel_id=1, source_target_pairs={{0,2},{1,3},{2,0},{3,1},{4,6},{5,7},{6,4},{7,5},{8,10},{9,11},{10,... | collective-permute-start | bytes 638984 | tf_op jit(solution)/shard_map/ppermute | solution.py:885
  67.4 5.1 %collective-permute-start.9 = (bf16[2,32,1664]{2,1,0:T(8,128)(2,1)S(1)}, bf16[2,32,1664]{2,1,0:T(8,128)(2,1)S(1)}, u32[]{:S(2)}, u32[]{:S(2)}) collective-permute-start(bf16[2,32,1664]{2,1,0:T(8,128)(2,1)S(1)} %get-tuple-element.178.mine), channel_id=1, source_target_pairs={{0,1},{1,0},{2,3},{3,2},{4,5},{5,4},{6,7},{7,6},{8,9},{9,8},{10,11... | collective-permute-start | bytes 638984 | tf_op jit(solution)/shard_map/ppermute | solution.py:888
  97.5 2.3 %collective-permute-start.12 = (bf16[1920,128]{1,0:T(8,128)(2,1)S(1)}, bf16[1920,128]{1,0:T(8,128)(2,1)S(1)}, u32[]{:S(2)}, u32[]{:S(2)}) collective-permute-start(bf16[1920,128]{1,0:T(8,128)(2,1)S(1)} %get-tuple-element.153.d0), channel_id=1, source_target_pairs={{0,1},{1,0},{2,3},{3,2},{4,5},{5,4},{6,7},{7,6},{8,9},{9,8},{10,11... | collective-permute-start | bytes 1474568 | tf_op jit(solution)/shard_map/ppermute | solution.py:888
  97.5 2.2 %collective-permute-start.13 = (bf16[2,32,1664]{2,1,0:T(8,128)(2,1)S(1)}, bf16[2,32,1664]{2,1,0:T(8,128)(2,1)S(1)}, u32[]{:S(2)}, u32[]{:S(2)}) collective-permute-start(bf16[2,32,1664]{2,1,0:T(8,128)(2,1)S(1)} %collective-permute-done.10.far), channel_id=1, source_target_pairs={{0,1},{1,0},{2,3},{3,2},{4,5},{5,4},{6,7},{7,6},{8,9},{9,8},{10,11... | collective-permute-start | bytes 638984 | tf_op jit(solution)/shard_map/ppermute | solution.py:888
  98.0 1.7 %collective-permute-start.11 = (f32[1,8,128]{2,1,0:T(8,128)S(1)}, f32[1,8,128]{2,1,0:T(8,128)S(1)}, u32[]{:S(2)}, u32[]{:S(2)}) collective-permute-start(f32[1,8,128]{2,1,0:T(8,128)S(1)} %slice.3), channel_id=1, source_target_pairs={{0,1},{1,0},{2,3},{3,2},{4,5},{5,4},{6,7},{7,6},{8,9},{9,8},{10,11... | collective-permute-start | bytes 12296 | tf_op jit(solution)/shard_map/ppermute | solution.py:888
  123.3 10.4 %all-to-all-start.6 = ((bf16[8,3,16,128]{3,2,1,0:T(8,128)(2,1)}), bf16[8,3,16,128]{3,2,1,0:T(8,128)(2,1)S(1)}, u32[]{:S(2)}, u32[]{:S(2)}) async-start(bf16[8,3,16,128]{3,2,1,0:T(8,128)(2,1)} %get-tuple-element.166), calls=%async_computation.6 | async-start | bytes 196608 | tf_op jit(solution)/shard_map/all_to_all | solution.py:892
  126.7 5.6 %collective-permute-start.15 = (bf16[32,1664]{1,0:T(8,128)(2,1)S(1)}, bf16[32,1664]{1,0:T(8,128)(2,1)S(1)}, u32[]{:S(2)}, u32[]{:S(2)}) collective-permute-start(bf16[32,1664]{1,0:T(8,128)(2,1)S(1)} %get-tuple-element.168), channel_id=1, source_target_pairs={{0,2},{1,3},{2,0},{3,1},{4,6},{5,7},{6,4},{7,5},{8,10},{9,11},{10,... | collective-permute-start | bytes 319496 | tf_op jit(solution)/shard_map/ppermute | solution.py:885
  128.0 4.3 %collective-permute-start.14 = (bf16[9,16,128]{2,1,0:T(8,128)(2,1)S(1)}, bf16[9,16,128]{2,1,0:T(8,128)(2,1)S(1)}, u32[]{:S(2)}, u32[]{:S(2)}) collective-permute-start(bf16[9,16,128]{2,1,0:T(8,128)(2,1)S(1)} %get-tuple-element.167), channel_id=1, source_target_pairs={{2,0},{3,1},{6,4},{7,5},{10,8},{11,9},{14,12},{15,13},{18,16},{19,... | collective-permute-start | bytes 110600 | tf_op jit(solution)/shard_map/ppermute | solution.py:1029
  134.4 8.8 %collective-permute-start.19 = (bf16[34,16,128]{2,1,0:T(8,128)(2,1)S(1)}, bf16[34,16,128]{2,1,0:T(8,128)(2,1)S(1)}, u32[]{:S(2)}, u32[]{:S(2)}) collective-permute-start(bf16[34,16,128]{2,1,0:T(8,128)(2,1)S(1)} %shard_map.285), channel_id=1, source_target_pairs={{0,24},{1,16},{2,8},{3,0},{4,28},{5,20},{6,12},{7,4},{8,26},{9,18}... | collective-permute-start | bytes 417800 | tf_op jit(solution)/shard_map/ppermute | solution.py:918
  138.5 6.4 %collective-permute-start.18 = (bf16[34,16,128]{2,1,0:T(8,128)(2,1)S(1)}, bf16[34,16,128]{2,1,0:T(8,128)(2,1)S(1)}, u32[]{:S(2)}, u32[]{:S(2)}) collective-permute-start(bf16[34,16,128]{2,1,0:T(8,128)(2,1)S(1)} %shard_map.285), channel_id=1, source_target_pairs={{0,16},{1,24},{2,0},{3,8},{4,20},{5,28},{6,4},{7,12},{8,18},{9,26}... | collective-permute-start | bytes 417800 | tf_op jit(solution)/shard_map/ppermute | solution.py:918
  140.9 9.6 %collective-permute-start.17 = (bf16[34,16,128]{2,1,0:T(8,128)(2,1)S(1)}, bf16[34,16,128]{2,1,0:T(8,128)(2,1)S(1)}, u32[]{:S(2)}, u32[]{:S(2)}) collective-permute-start(bf16[34,16,128]{2,1,0:T(8,128)(2,1)S(1)} %shard_map.285), channel_id=1, source_target_pairs={{0,8},{1,0},{2,24},{3,16},{4,12},{5,4},{6,28},{7,20},{8,10},{9,2},... | collective-permute-start | bytes 417800 | tf_op jit(solution)/shard_map/ppermute | solution.py:918
  140.9 12.8 %collective-permute-start.16 = (bf16[34,16,128]{2,1,0:T(8,128)(2,1)S(1)}, bf16[34,16,128]{2,1,0:T(8,128)(2,1)S(1)}, u32[]{:S(2)}, u32[]{:S(2)}) collective-permute-start(bf16[34,16,128]{2,1,0:T(8,128)(2,1)S(1)} %shard_map.285), channel_id=1, source_target_pairs={{0,0},{1,8},{2,16},{3,24},{4,4},{5,12},{6,20},{7,28},{8,2},{9,10},... | collective-permute-start | bytes 417800 | tf_op jit(solution)/shard_map/ppermute | solution.py:918
  143.2 18.2 %collective-permute-start.23 = (bf16[34,16,128]{2,1,0:T(8,128)(2,1)S(1)}, bf16[34,16,128]{2,1,0:T(8,128)(2,1)S(1)}, u32[]{:S(2)}, u32[]{:S(2)}) collective-permute-start(bf16[34,16,128]{2,1,0:T(8,128)(2,1)S(1)} %collective-permute-done.19.refs_3_), channel_id=1, source_target_pairs={{0,4},{4,0},{8,12},{12,8},{16,20},{20,16},{24,28},{28,24},{1,5},{5... | collective-permute-start | bytes 417800 | tf_op jit(solution)/shard_map/ppermute | solution.py:931
  144.9 16.5 %collective-permute-start.22 = (bf16[34,16,128]{2,1,0:T(8,128)(2,1)S(1)}, bf16[34,16,128]{2,1,0:T(8,128)(2,1)S(1)}, u32[]{:S(2)}, u32[]{:S(2)}) collective-permute-start(bf16[34,16,128]{2,1,0:T(8,128)(2,1)S(1)} %collective-permute-done.18.refs_2_), channel_id=1, source_target_pairs={{0,4},{4,0},{8,12},{12,8},{16,20},{20,16},{24,28},{28,24},{1,5},{5... | collective-permute-start | bytes 417800 | tf_op jit(solution)/shard_map/ppermute | solution.py:931
  150.6 10.8 %collective-permute-start.21 = (bf16[34,16,128]{2,1,0:T(8,128)(2,1)S(1)}, bf16[34,16,128]{2,1,0:T(8,128)(2,1)S(1)}, u32[]{:S(2)}, u32[]{:S(2)}) collective-permute-start(bf16[34,16,128]{2,1,0:T(8,128)(2,1)S(1)} %collective-permute-done.17.refs_1_), channel_id=1, source_target_pairs={{0,4},{4,0},{8,12},{12,8},{16,20},{20,16},{24,28},{28,24},{1,5},{5... | collective-permute-start | bytes 417800 | tf_op jit(solution)/shard_map/ppermute | solution.py:931
  153.8 7.6 %collective-permute-start.20 = (bf16[34,16,128]{2,1,0:T(8,128)(2,1)S(1)}, bf16[34,16,128]{2,1,0:T(8,128)(2,1)S(1)}, u32[]{:S(2)}, u32[]{:S(2)}) collective-permute-start(bf16[34,16,128]{2,1,0:T(8,128)(2,1)S(1)} %collective-permute-done.16.refs_0_), channel_id=1, source_target_pairs={{0,4},{4,0},{8,12},{12,8},{16,20},{20,16},{24,28},{28,24},{1,5},{5... | collective-permute-start | bytes 417800 | tf_op jit(solution)/shard_map/ppermute | solution.py:931

commit v4 on v3

--- a/solution.py
+++ b/solution.py
@@ -25,10 +25,10 @@
 PAR = STEM + 768
 WIDE = PAR + 256
 CLS = CP // 128 + 4
-TAPS = 36
+TAPS = 18
+SENT = 50
 VMEM = 12 * 2**20
 WHOLE = 56 * 2**20
-OWNER = (0, 2, 1, 3)
 NT = (((1,), (1,)), ((), ()))
 TN = (((0,), (0,)), ((), ()))
 
@@ -264,8 +264,8 @@
             for s, piece in (
                 (c, mine[level, conv, t]),
                 (c ^ 1, near[level, conv, t]),
-                (c ^ 2, far[9 * (2 * slot + branch) + t]),
-                (c ^ 3, cross[9 * (2 * slot + branch) + t]),
+                (c ^ 2, far[9 * slot + t]),
+                (c ^ 3, cross[9 * slot + t]),
             ):
                 flat[slot, at32(s), 128 * t : 128 * (t + 1)] = piece
                 tall[slot, at32(s, 128 * t), :] = piece
@@ -336,7 +336,7 @@
     spread_out(st_out, sums)
 
 
-def logits_kernel(meta, x2, cot, wp, gw, mine, far, logits):
+def logits_kernel(meta, x2, cot, wp, gw, mine, near, far, cross, logits):
     def store(slot, v):
         bias = v[:, 128:256]
 
@@ -374,9 +374,8 @@
             bias.append(store(slot, dot(cot[:, a:b], x2[a:b])))
         finish(*bias)
 
-    for out, group in ((mine, meta[0]), (far, 1 - meta[0])):
-        for i in range(2):
-            out[i] = logits[at32(jnp.where(meta[1] == 0, 2 * group + i, 0)), :]
+    for out, c in ((mine, 0), (near, 1), (far, 2), (cross, 3)):
+        out[...] = logits[at32(jnp.where(meta[1] == 0, meta[2] ^ c, 0)), :]
 
 
 def gw_block(gw, i, v):
@@ -444,11 +443,7 @@
     return v[0:4] + v[4:8] + v[8:12]
 
 
-def place_of(direct, j):
-    return 2 * OWNER[j // 2] + j % 2 if direct else j
-
-
-def weight_grad(direct, meta, dyt, act, field, shifts, wg):
+def weight_grad(meta, dyt, act, field, shifts, wg):
     for j in range(NCH):
         field[8 + CH * j : 8 + CH * (j + 1)] = act[CH * j : CH * (j + 1)].astype(F32)
     fill_shifts(field, shifts)
@@ -457,7 +452,7 @@
         for t in range(9):
             for j in range(8):
                 block = v[16 * j : 16 * (j + 1), 128 * t : 128 * (t + 1)].astype(BF)
-                wg[place_of(direct, j), 9 * slot + t] = block
+                wg[j, 9 * slot + t] = block
 
     @pl.when(meta[0] == 0)
     def _():
@@ -470,30 +465,30 @@
         store(1, dot(dyt[:, CUT:PX], taps(shifts, CUT, PX - CUT)))
 
 
-def second_back_kernel(direct, meta, dz, y, cst, st, w, act, y_in, cst_in, gw, grad, st_out, sums, wg, field, shifts, dyt):
+def second_back_kernel(meta, dz, y, cst, st, w, act, y_in, cst_in, gw, grad, st_out, sums, wg, field, shifts, dyt):
     guard(field, shifts)
     out_grad(meta, dz, y, cst, st, sums, field, dyt)
     fill_shifts(field, shifts)
     block = as_parts(conv_back(meta, False, w, y_in, cst_in, shifts, grad, st_out))
-    weight_grad(direct, meta, dyt, act, field, shifts, wg)
+    weight_grad(meta, dyt, act, field, shifts, wg)
     for j in range(8):
         for i in range(3):
-            wg[place_of(direct, j), 18 + i] = gw[j, i]
+            wg[j, 18 + i] = gw[j, i]
         wg[j, 21] = block
 
 
-def first_back_kernel(direct, meta, dz, y, cst, st, w, act, y_in, cst_in, grad, st_out, sums, wg, field, shifts, dyt):
+def first_back_kernel(meta, dz, y, cst, st, w, act, y_in, cst_in, grad, st_out, sums, wg, field, shifts, dyt):
     guard(field, shifts)
     out_grad(meta, dz, y, cst, st, sums, field, dyt)
     fill_shifts(field, shifts)
     block = as_parts(conv_back(meta, True, w, y_in, cst_in, shifts, grad, st_out))
-    weight_grad(direct, meta, dyt, act, field, shifts, wg)
+    weight_grad(meta, dyt, act, field, shifts, wg)
     for j in range(8):
         wg[j, 18] = block
 
 
-def final_kernel(direct, meta, d0, d1, y, cst, st, sums1, sums2, u0, u1, u2, u3, own, other, gs, norm, *scratch):
-    sums, feat, stem, field, flat, dyt, gf, blocks = scratch
+def final_kernel(meta, d0, d1, y, cst, st, sums1, sums2, u0, u1, u2, u3, extra, own, send, gs, norm, *scratch):
+    sums, feat, stem, field, flat, dyt, gf, blocks, other = scratch
     load_inputs(meta, (u0, u1, u2, u3), feat, stem)
     grad_sums(meta, stat_total(st), sums)
     for j in range(NCH):
@@ -534,10 +529,14 @@
                 at = pl.ds(pl.multiple_of(128 * s + 32 * i, 32), 32)
                 out[:, 1024 + 128 * i : 1152 + 128 * i] = gf[at, MID : MID + 128]
 
+    for i in range(CP // 128):
+        for h in range(2):
+            send[2 * i + h] = other[16 * h : 16 * (h + 1), 128 * i : 128 * (i + 1)]
+    send[2 * (CP // 128) : 2 * (CP // 128) + 9] = extra[...]
     for i in range(3):
         block = blocks[3 * meta[1] + i]
         for j in range(8):
-            gs[place_of(direct, j), i] = block[16 * j : 16 * (j + 1)]
+            gs[j, i] = block[16 * j : 16 * (j + 1)]
     rest = jnp.zeros((4, 128), F32)
     norm[0] = jnp.concatenate([sums[0:4], sums1[0:4], sums2[0:4], rest], axis=0).astype(BF)
 
@@ -569,7 +568,7 @@
 
     @pl.when(meta[0] == 0)
     def _():
-        out[18:27] = extra[...]
+        out[18:27] = extra[2 * (CP // 128) : 2 * (CP // 128) + 9]
 
     @pl.when(meta[0] == 1)
     def _():
@@ -709,32 +708,31 @@
         copy.wait()
 
 
-def class_out_kernel(sizes, meta, mine, near, far, far_near, class_out, box_out):
+def class_out_kernel(sizes, meta, mine, near, far, cross, class_out, box_out):
     n0, n1, n2 = sizes
-    group, branch = meta[0], meta[1]
-
-    def store(fine, rest):
-        for out, src in ((class_out, 0), (box_out, 1)):
-            n = out.shape[0]
-            a, b = fine[src][0:n], rest[src][0:n]
-            out[:, 0:n0] = a[:, 0:n0]
-            out[:, n0 : n0 + n1] = b[:, 0:n1]
-            out[:, n0 + n1 : n0 + n1 + n2] = b[:, MID : MID + n2]
-
-    for b in range(2):
-
-        @pl.when((group == 0) & (branch == b))
-        def _():
-            here, there = (mine, near), (far, far_near)
-            store((here[b][b], here[1 - b][0]), (there[b][b], there[1 - b][0]))
-
-        @pl.when((group == 1) & (branch == b))
-        def _():
-            here, there = (mine, near), (far, far_near)
-            store((there[b][b], there[1 - b][0]), (here[b][b], here[1 - b][0]))
-
-
-def feature_out_kernel(meta, own, received, fine, mid, coarse):
+
+    def store(out, fine, rest):
+        n = out.shape[0]
+        out[:, 0:n0] = fine[0:n, 0:n0]
+        out[:, n0 : n0 + n1] = rest[0:n, 0:n1]
+        out[:, n0 + n1 : n0 + n1 + n2] = rest[0:n, MID : MID + n2]
+
+    for group in range(2):
+        for branch in range(2):
+
+            @pl.when((meta[0] == group) & (meta[1] == branch))
+            def _():
+                here, there = (mine, near), (far, cross)
+                for i, out in enumerate((class_out, box_out)):
+                    pair = (here[branch ^ i], there[branch ^ i])
+                    store(out, pair[group], pair[1 - group])
+
+
+def feature_out_kernel(meta, own, received, fine, mid, coarse, other):
+    for i in range(CP // 128):
+        for h in range(2):
+            other[16 * h : 16 * (h + 1), 128 * i : 128 * (i + 1)] = received[2 * i + h]
+
     def store(a, b):
         n1, n2 = mid.shape[1], coarse.shape[0]
         fine[...] = a[:, 0 : fine.shape[1]]
@@ -745,11 +743,11 @@
 
     @pl.when(meta[0] == 0)
     def _():
-        store(own, received)
+        store(own, other)
 
     @pl.when(meta[0] == 1)
     def _():
-        store(received, own)
+        store(other, own)
 
 
 def pack_kernel(f0, f1, f2, s0, s1, s2, gains, shifts, box, own, send, small):
@@ -795,15 +793,14 @@
             out[:, PAR + 128 * i : PAR + 128 * (i + 1)] = block
 
 
-def pred_kernel(sizes, meta, ccot, cw, cb, bcot, bb, conv, own, box, first, second, room, sems):
+def pred_kernel(sizes, meta, ccot, cw, cb, bcot, bb, conv, own, box, first, first_cross, second, second_cross, room, sems):
     n0, n1, n2 = sizes
     copies = []
-    for layer, out in enumerate((first, second)):
-        for slot in range(2):
-            for branch in range(2):
-                taken = conv.at[1 - meta[0] + slot, 2 * branch + layer]
-                to = out.at[pl.ds(9 * (2 * slot + branch), 9)]
-                copy = pltpu.make_async_copy(taken, to, sems.at[layer, slot, branch])
+    for layer, outs in enumerate(((first, first_cross), (second, second_cross))):
+        for i, out in enumerate(outs):
+            for slot in range(2):
+                taken = conv.at[1 - meta[0] + slot, 2 * (meta[1] ^ i) + layer]
+                copy = pltpu.make_async_copy(taken, out.at[pl.ds(9 * slot, 9)], sems.at[layer, i, slot])
                 copy.start()
                 copies.append(copy)
     lane = lax.broadcasted_iota(jnp.int32, (32, 128), 1)
@@ -846,6 +843,7 @@
         @pl.when(meta[0] != group)
         def _():
             fill(second, TAPS, ccot, cb, group == 0, True)
+            second_cross[TAPS:] = second[TAPS:]
 
     for copy in copies:
         copy.wait()
@@ -884,6 +882,9 @@
     def across(v):
         return lax.ppermute(v, "chan", [(i, i ^ 2) for i in range(4)])
 
+    def diagonal(v):
+        return lax.ppermute(v, "chan", [(i, i ^ 3) for i in range(4)])
+
     def beside(v, pairs=((0, 1), (1, 0), (2, 3), (3, 2))):
         return lax.ppermute(v, "chan", list(pairs))
 
@@ -891,18 +892,6 @@
         st, *hold = lax.optimization_barrier((st, *hold))
         st = lax.all_to_all(st, "dp", 0, 0, tiled=True)
         return lax.optimization_barrier((st, *hold)) if hold else st
-
-    def add_up(st, between=None):
-        if not direct:
-            st = exchange(st)
-            return (st, between(st)[1]) if between else st
-        st = st[:1]
-        for k in (2, 4):
-            st = st + lax.ppermute(st, "dp", [(i, i ^ k) for i in range(8)])
-        if between:
-            st, got = between(st)
-        st = st + lax.ppermute(st, "dp", [(i, i ^ 1) for i in range(8)])
-        return (st, got) if between else st
 
     def after(v, *others):
         return lax.optimization_barrier((v, *others))[0]
@@ -913,7 +902,7 @@
         parts = []
         for k in range(4):
             pairs = [
-                (8 * z + 4 * y + i, 8 * (i ^ k) + 4 * y + OWNER[z]) for z in range(4) for y in range(2) for i in range(4)
+                (8 * z + 4 * y + i, 8 * (i ^ k) + 4 * y + z) for z in range(4) for y in range(2) for i in range(4)
             ]
             parts.append(lax.ppermute(v, ("dp", "chan"), pairs))
         return parts
@@ -941,9 +930,9 @@
         limit=WHOLE,
     )
     far_u = across(send)
-    own_pred, box_pred, send1, send2 = call(
+    own_pred, box_pred, send1, send1_cross, send2, send2_cross = call(
         functools.partial(pred_kernel, (n0, n1, n2)),
-        [((CLS, 32, 128), BF)] * 2 + [((TAPS, 32, 128), BF), ((TAPS + CLS, 32, 128), BF)],
+        [((CLS, 32, 128), BF)] * 2 + [((TAPS, 32, 128), BF)] * 2 + [((TAPS + CLS, 32, 128), BF)] * 2,
         [((32, CP), BF), pltpu.SemaphoreType.DMA((2, 2, 2))],
         (meta, ccot[0], cw, cb, bcot[0], after(bb, own), conv),
         limit=WHOLE,
@@ -973,16 +962,15 @@
         [((512, CP), BF), ((128, 768), BF), ((CP, 128), F32)],
         (meta, *u),
     )
-    far1 = across(after(send1, far_u))
+    far1, cross1 = across(after(send1, far_u)), diagonal(after(send1_cross, far_u))
     st, near_pred = exchange(st, near_pred)
-    far1 = after(far1, st)
-    far2 = across(after(send2, far1))
-    w1, w1_tall = weights_of(0, far1, beside(far1))
+    far1, cross1 = after((far1, cross1), st)
+    far2, cross2 = across(after(send2, far1)), diagonal(after(send2_cross, cross1))
+    w1, w1_tall = weights_of(0, far1, cross1)
     forward_outs = [(canvas, BF), (canvas, F32), (stat, F32), ((16, 128), F32)]
     act0, y1, st, cst0 = call(functools.partial(forward_kernel, True), forward_outs, moved, (meta, y0, st, cnt, w1, par))
     st = exchange(st)
-    far2 = after(far2, st)
-    cross2 = beside(far2)
+    far2, cross2 = after((far2, cross2), st)
     w2, w2_tall = weights_of(1, far2, cross2)
     act1, y2, st, cst1 = call(
         functools.partial(forward_kernel, False), forward_outs, moved, (meta, y1, st, cnt, w2, par)
@@ -994,48 +982,43 @@
         [(canvas, F32), ((CP, 128), F32)],
         (meta, y2, st, par, own_pred, far2, near_pred, cross2, box_pred),
     )
-    st = exchange(st)
-    gw, mine, far = call(
-        logits_kernel,
-        [((8, 3, 16, 128), BF), ((2, 32, CP), BF), ((2, 32, CP), BF)],
-        [((128, CP), BF)],
-        (meta, x2, cot, after(wp, st)),
-    )
-    far = across(far)
-    near = beside(mine)
+    gw, mine, near, far, cross = call(
+        logits_kernel, [((8, 3, 16, 128), BF)] + [((32, CP), BF)] * 4, [((128, CP), BF)], (meta, x2, cot, wp)
+    )
+    near, far, cross = beside(near), across(far), diagonal(cross)
+    st = exchange(after(st, gw))
+    st, near, far, cross = lax.optimization_barrier((st, near, far, cross))
     back_scratch = moved + [((128, PX), BF)]
     dz1, st, sums2, wg2 = call(
-        functools.partial(second_back_kernel, direct),
+        second_back_kernel,
         [(canvas, F32), (stat, F32), ((8, 128), F32), ((8, 22, 16, 128), BF)],
         back_scratch,
         (meta, dz2, y2, cst2, st, w2_tall, act1, y1, cst1, gw),
     )
-    wg2, near, far = lax.optimization_barrier((wg2, near, far))
     got2 = exchange(wg2) if direct else reduce(wg2)
     st = got2 if direct else exchange(st)
-    far = after(far, st)
-    far_near = beside(far)
     d0, st, sums1, wg1 = call(
-        functools.partial(first_back_kernel, direct),
+        first_back_kernel,
         [(canvas, BF), (stat, F32), ((8, 128), F32), ((8, 19, 16, 128), BF)],
         back_scratch,
         (meta, dz1, y1, cst1, st, w1_tall, act0, y0, cst0),
+        flops=6 * 10**9,
     )
     d0_other = beside(d0)
     st_other = beside(st[:1])
     if direct:
         (wg1,) = call(patch_kernel, [(wg1.shape, BF)], [], (wg1, st_other), aliases={0: 0})
         total, extra = call(sum_kernel, [((12, 16, 128), BF), ((9, 16, 128), BF)], [], (meta, after(got2, d0)))
-        extra = lax.ppermute(extra, "chan", [(2, 0), (3, 1)])
-        wg1 = after(wg1, total)
-        wg1, d0_other, far_near = lax.optimization_barrier((wg1, d0_other, far_near))
+        wg1, d0_other, total = lax.optimization_barrier((wg1, d0_other, total))
         got1 = st = exchange(wg1)
     else:
         got1 = reduce(wg1)
         st = exchange(st + st_other)
-    own, other, gs, norm = call(
-        functools.partial(final_kernel, direct),
-        [((32, CP), BF), ((32, CP), BF), ((8, 3, 16, 128), BF), ((1, 16, 128), BF)],
+    if not direct:
+        extra = jnp.zeros((9, 16, 128), BF)
+    own, send, gs, norm = call(
+        final_kernel,
+        [((32, CP), BF), ((SENT, 16, 128), BF), ((8, 3, 16, 128), BF), ((1, 16, 128), BF)],
         [
             ((8, 128), F32),
             ((512, CP), BF),
@@ -1045,13 +1028,14 @@
             ((128, CP), BF),
             ((512, CP), BF),
             ((6, 128, 128), BF),
+            ((32, CP), BF),
         ],
-        (meta, d0, d0_other, y0, cst0, st, sums1, sums2, *u),
-    )
-    received = across(other)
+        (meta, d0, d0_other, y0, cst0, st, sums1, sums2, *u, extra),
+    )
+    received = across(send)
     if direct:
-        gs, extra, received = lax.optimization_barrier((exchange(gs), extra, received))
-        (grads,) = call(join_kernel, [((34, 16, 128), BF)], [], (meta, got1, total, extra, gs, norm))
+        gs, received = lax.optimization_barrier((exchange(gs), received))
+        (grads,) = call(join_kernel, [((34, 16, 128), BF)], [], (meta, got1, total, received, gs, norm))
     else:
         extra = lax.ppermute(got2[:, 9:18], "chan", [(2, 0), (3, 1)])
         third = jnp.where(fine, extra, got1[:, 9:18])
@@ -1071,11 +1055,15 @@
         functools.partial(class_out_kernel, (n0, n1, n2)),
         [((class_rows, n0 + n1 + n2), BF), ((box_rows, n0 + n1 + n2), BF)],
         [],
-        (meta, mine, near, far, far_near),
+        (meta, mine, near, far, cross),
         True,
     )
     grad_fine, grad_mid, grad_coarse = call(
-        feature_out_kernel, [(f0.shape[1:], BF), (f1.shape[1:], BF), ((n2, f2.shape[1]), BF)], [], (meta, own, received), True
+        feature_out_kernel,
+        [(f0.shape[1:], BF), (f1.shape[1:], BF), ((n2, f2.shape[1]), BF)],
+        [((32, CP), BF)],
+        (meta, own, received),
+        True,
     )
 
     grad_conv, grad_cw, grad_cb, grad_bw, grad_s0, grad_s1, grad_s2 = call(

time: 166 us -> 161 us (0.970)
  blocking collectives: 81.8 us -> 91 us
  starting transfers between devices: 27.4 us -> 19.6 us
  waiting for transfers between devices: 17.4 us -> 12.4 us
    all_to_all x6 -> x7, blocking collectives: 81.8 us -> 91 us  [exchange(): st = lax.all_to_all(st, 'dp', 0, 0, tiled=True)]
    ppermute x10 -> x7, waiting for transfers between devices: 4.68 us -> 0.74 us  [beside(): return lax.ppermute(v, 'chan', list(pairs))]
    ppermute x4, starting transfers between devices: 6.21 us -> 2.63 us  [over_y(): return lax.ppermute(v, 'dp', [(i, i ^ 1) for i in range(8)])]
    all_to_all x1 -> x0, starting transfers between devices: 3.36 us -> none  [exchange(): st = lax.all_to_all(st, 'dp', 0, 0, tiled=True)]
    ppermute x4, waiting for transfers between devices: 5.82 us -> 7.94 us  [over_z(): parts.append(lax.ppermute(v, ('dp', 'chan'), pairs))]
    ppermute x4, starting transfers between devices: 8.76 us -> 6.97 us  [over_z(): parts.append(lax.ppermute(v, ('dp', 'chan'), pairs))]
  transfers between devices with their start and end apart: 25 -> 23, of which waited for: 11 -> 6; matrix products, arithmetic and copies ran while one was open for 0% -> 0% of each run, Pallas kernels for 11% -> 8%
where the time goes in v4:
time: 161 us; the launch traced here: 159 us
  blocking collectives  91 us (57%)
  Pallas kernels  34.3 us (21%)
  starting transfers between devices  19.6 us (12%)
  waiting for transfers between devices  12.4 us (8%)
  between operations  1.67 us (1%)
    all_to_all x7, blocking collectives, exchange(): st = lax.all_to_all(st, 'dp', 0, 0, tiled=True)  91 us
    pallas_call x19, Pallas kernels, call(): pl.pallas_call(body, out_shape=[place(s, d) for s, d in outs], in_specs=[...  34.3 us
    ppermute x4, waiting for transfers between devices, over_z(): parts.append(lax.ppermute(v, ('dp', 'chan'), pairs))  7.94 us
    ppermute x4, starting transfers between devices, over_z(): parts.append(lax.ppermute(v, ('dp', 'chan'), pairs))  6.97 us
    ppermute x5, starting transfers between devices, across(): return lax.ppermute(v, 'chan', [(i, i ^ 2) for i in range(4)])  5.27 us
    ppermute x5, waiting for transfers between devices, across(): return lax.ppermute(v, 'chan', [(i, i ^ 2) for i in range(4)])  3.66 us
  transfers between devices with their start and end apart: 23, of which 6 were waited for; matrix products, arithmetic and copies ran while one was open for 0% of the time, Pallas kernels for 8%

profile of v4, /device:TPU:2, one launch (start us, length us, event | category | flops | bytes accessed | tf_op | source)
XLA Modules:
  0.0 159.5 jit_solution(13655791463754212939)
XLA Ops:
  0.6 1.2 shard_map.271
  1.8 0.1 collective-permute-start.1
  1.9 0.5 collective-permute-start.2
  2.4 0.0 collective-permute-start
  3.1 0.6 stack.23.meta
  3.7 2.2 %shard_map.272 = (bf16[17,32,128]{2,1,0:T(8,128)(2,1)S(1)}, bf16[17,32,128]{2,1,0:T(8,128)(2,1)S(1)}, bf16[18,32,128]{2,1,0:T(8,128)(2,1)S(1)}, bf16[18,32,128]{...) custom-call(s32[6]{0:T(128)} %stack.23.meta, bf16[20,2100]{1,0:T(8,128)(2,1)} %bitcast.32, ...), custom_call_target="tpu_custom_call" | custom-call | flops 2000000000 | bytes 10000 | tf_op jit(solution)/shard_map/pallas_call | solution.py:860
  5.9 2.7 %collective-permute-done.u1 = bf16[32,2560]{1,0:T(8,128)(2,1)S(1)} collective-permute-done((bf16[32,2560]{1,0:T(8,128)(2,1)S(1)}, bf16[32,2560]{1,0:T(8,128)(2,1)S(1)}, u32[]{:S(2)}, u32[]{:S(2)}) %collective-permute-start) | collective-permute-done | bytes 163872 | tf_op jit(solution)/shard_map/ppermute | solution.py:883
  8.6 0.0 collective-permute-done.1.near
  8.6 0.0 collective-permute-start.3
  8.6 1.3 collective-permute-start.4
  9.9 0.3 collective-permute-start.5
  10.3 2.2 %collective-permute-start.6 = (bf16[18,32,128]{2,1,0:T(8,128)(2,1)S(1)}, bf16[18,32,128]{2,1,0:T(8,128)(2,1)S(1)}, u32[]{:S(2)}, u32[]{:S(2)}) collective-permute-start(bf16[18,32,128]{2,1,0:T(8,128)(2,1)S(1)} %get-tuple-element.129), channel_id=1, source_target_pairs={{0,3},{1,2},{2,1},{3,0},{4,7},{5,6},{6,5},{7,4},{8,11},{9,10},{10,... | collective-permute-start | bytes 442376 | tf_op jit(solution)/shard_map/ppermute | solution.py:886
  12.5 0.0 collective-permute-done.2.u2
  12.5 0.0 collective-permute-done.3.u3
  12.5 1.6 shard_map.273
  14.0 0.0 collective-permute-done.4.k2
  14.0 12.3 %all_to_all.35.st = f32[8,8,128]{2,1,0:T(8,128)S(1)} all-to-all(f32[8,8,128]{2,1,0:T(8,128)S(1)} %get-tuple-element.122), channel_id=1, replica_groups=mesh['dp'=8,'chan'=4] {'dp'}, dimensions={0} | all-to-all | bytes 65536 | tf_op jit(solution)/shard_map/all_to_all | solution.py:893
  26.4 0.7 collective-permute-start.7
  27.1 0.7 shard_map.274
  27.9 2.2 %shard_map.275 = (bf16[1920,128]{1,0:T(8,128)(2,1)S(1)}, f32[1920,128]{1,0:T(8,128)S(1)}, f32[8,8,128]{2,1,0:T(8,128)S(1)}, f32[16,128]{1,0:T(8,128)S(1)}) custom-call(s32[6]{0:T(128)S(1)} %copy-done.1, f32[1920,128]{1,0:T(8,128)S(1)} %get-tuple-element.119.y.y_in, f32[8,8,128]{2,1,0:T(8,128)S(1)} %all_to_all.35.st, f32[8,128]{1,0:T(8,128)S(1)} %get-tuple-element.125.cnt, ...), custom_call_target="tpu_custom_call" | custom-call | flops 1000000 | bytes 10000 | tf_op jit(solution)/shard_map/pallas_call | solution.py:860
  30.0 9.1 %all_to_all.36.st = f32[8,8,128]{2,1,0:T(8,128)S(1)} all-to-all(f32[8,8,128]{2,1,0:T(8,128)S(1)} %get-tuple-element.135), channel_id=1, replica_groups=mesh['dp'=8,'chan'=4] {'dp'}, dimensions={0} | all-to-all | bytes 65536 | tf_op jit(solution)/shard_map/all_to_all | solution.py:893
  39.2 1.0 collective-permute-done.7.far.k1
  40.1 0.7 shard_map.276
  40.9 2.2 %shard_map.277 = (bf16[1920,128]{1,0:T(8,128)(2,1)S(1)}, f32[1920,128]{1,0:T(8,128)S(1)}, f32[8,8,128]{2,1,0:T(8,128)S(1)}, f32[16,128]{1,0:T(8,128)S(1)}) custom-call(s32[6]{0:T(128)S(1)} %copy-done.1, f32[1920,128]{1,0:T(8,128)S(1)} %get-tuple-element.134.y.y_in, f32[8,8,128]{2,1,0:T(8,128)S(1)} %all_to_all.36.st, f32[8,128]{1,0:T(8,128)S(1)} %get-tuple-element.125.cnt, ...), custom_call_target="tpu_custom_call" | custom-call | flops 1000000 | bytes 10000 | tf_op jit(solution)/shard_map/pallas_call | solution.py:860
  43.0 9.1 %all_to_all.37.st = f32[8,8,128]{2,1,0:T(8,128)S(1)} all-to-all(f32[8,8,128]{2,1,0:T(8,128)S(1)} %get-tuple-element.143), channel_id=1, replica_groups=mesh['dp'=8,'chan'=4] {'dp'}, dimensions={0} | all-to-all | bytes 65536 | tf_op jit(solution)/shard_map/all_to_all | solution.py:893
  52.1 2.3 %shard_map.278 = (f32[1920,128]{1,0:T(8,128)S(1)}, f32[8,8,128]{2,1,0:T(8,128)S(1)}, f32[16,128]{1,0:T(8,128)S(1)}, bf16[1664,256]{1,0:T(8,128)(2,1)S(1)}, bf16[...) custom-call(s32[6]{0:T(128)S(1)} %copy-done.1, f32[1920,128]{1,0:T(8,128)S(1)} %get-tuple-element.142.y, ...), custom_call_target="tpu_custom_call" | custom-call | flops 1000000 | bytes 10000 | tf_op jit(solution)/shard_map/pallas_call | solution.py:860
  54.4 1.3 shard_map.279
  55.7 0.1 collective-permute-start.9
  55.8 2.2 %collective-permute-start.10 = (bf16[32,1664]{1,0:T(8,128)(2,1)S(1)}, bf16[32,1664]{1,0:T(8,128)(2,1)S(1)}, u32[]{:S(2)}, u32[]{:S(2)}) collective-permute-start(bf16[32,1664]{1,0:T(8,128)(2,1)S(1)} %get-tuple-element.156), channel_id=1, source_target_pairs={{0,2},{1,3},{2,0},{3,1},{4,6},{5,7},{6,4},{7,5},{8,10},{9,11},{10,... | collective-permute-start | bytes 319496 | tf_op jit(solution)/shard_map/ppermute | solution.py:883
  58.0 0.1 collective-permute-start.11
  58.1 9.0 %all_to_all.38.st = f32[8,8,128]{2,1,0:T(8,128)S(1)} all-to-all(f32[8,8,128]{2,1,0:T(8,128)S(1)} %get-tuple-element.154), channel_id=1, replica_groups=mesh['dp'=8,'chan'=4] {'dp'}, dimensions={0} | all-to-all | bytes 65536 | tf_op jit(solution)/shard_map/all_to_all | solution.py:893
  67.1 0.0 collective-permute-done.9.near
  67.1 0.0 collective-permute-done.10.far
  67.1 0.0 collective-permute-done.11.cross
  67.1 4.3 %shard_map.280 = (f32[1920,128]{1,0:T(8,128)S(1)}, f32[8,8,128]{2,1,0:T(8,128)}, f32[8,128]{1,0:T(8,128)S(1)}, bf16[8,22,16,128]{3,2,1,0:T(8,128)(2,1)S(1)}) custom-call(s32[6]{0:T(128)S(1)} %copy-done.1, f32[1920,128]{1,0:T(8,128)S(1)} %get-tuple-element.150.dz, f32[1920,128]{1,0:T(8,128)S(1)} %get-tuple-element.142.y, ...), custom_call_target="tpu_custom_call" | custom-call | flops 1000000 | bytes 10000 | tf_op jit(solution)/shard_map/pallas_call | solution.py:860
  71.4 20.7 %all_to_all.39.st.second = bf16[8,22,16,128]{3,2,1,0:T(8,128)(2,1)S(1)} all-to-all(bf16[8,22,16,128]{3,2,1,0:T(8,128)(2,1)S(1)} %get-tuple-element.163), channel_id=1, replica_groups=mesh['dp'=8,'chan'=4] {'dp'}, dimensions={0} | all-to-all | bytes 1441792 | tf_op jit(solution)/shard_map/all_to_all | solution.py:893
  92.1 3.6 %shard_map.281 = (bf16[1920,128]{1,0:T(8,128)(2,1)S(1)}, f32[8,8,128]{2,1,0:T(8,128)S(1)}, f32[8,128]{1,0:T(8,128)S(1)}, bf16[8,19,16,128]{3,2,1,0:T(8,128)(2,1)S(1)}) custom-call(s32[6]{0:T(128)S(1)} %copy-done.1, f32[1920,128]{1,0:T(8,128)S(1)} %get-tuple-element.162.dz, f32[1920,128]{1,0:T(8,128)S(1)} %get-tuple-element.134.y.y_in, ...), custom_call_target="tpu_custom_call" | custom-call | flops 6000000000 | bytes 10000 | tf_op jit(solution)/shard_map/pallas_call | solution.py:860
  95.7 0.1 collective-permute-start.13
  95.8 0.5 collective-permute-start.12
  96.3 0.6 shard_map.283
  96.9 0.7 collective-permute-done.12.other
  97.7 0.0 collective-permute-done.13.d1
  97.7 20.7 %all_to_all.40.st.first = bf16[8,19,16,128]{3,2,1,0:T(8,128)(2,1)S(1)} all-to-all(bf16[8,19,16,128]{3,2,1,0:T(8,128)(2,1)S(1)} %shard_map.282), channel_id=1, replica_groups=mesh['dp'=8,'chan'=4] {'dp'}, dimensions={0} | all-to-all | bytes 1245184 | tf_op jit(solution)/shard_map/all_to_all | solution.py:893
  118.4 2.3 %shard_map.284 = (bf16[32,1664]{1,0:T(8,128)(2,1)S(1)}, bf16[50,16,128]{2,1,0:T(8,128)(2,1)S(1)}, bf16[8,3,16,128]{3,2,1,0:T(8,128)(2,1)S(1)}, bf16[1,16,128]{2,1,0:T(8,128)(2,1)S(1)}) custom-call(s32[6]{0:T(128)S(1)} %copy-done.1, bf16[1920,128]{1,0:T(8,128)(2,1)S(1)} %get-tuple-element.167.d0, bf16[1920,128]{1,0:T(8,128)(2,1)S(1)} %collective-permute-done.13.d1, ...), custom_call_target="tpu_custom_call" | custom-call | flops 1000000 | bytes 10000 | tf_op jit(solution)/shard_map/pallas_call | solution.py:860
  120.6 1.9 %collective-permute-start.14 = (bf16[50,16,128]{2,1,0:T(8,128)(2,1)S(1)}, bf16[50,16,128]{2,1,0:T(8,128)(2,1)S(1)}, u32[]{:S(2)}, u32[]{:S(2)}) collective-permute-start(bf16[50,16,128]{2,1,0:T(8,128)(2,1)S(1)} %get-tuple-element.180), channel_id=1, source_target_pairs={{0,2},{1,3},{2,0},{3,1},{4,6},{5,7},{6,4},{7,5},{8,10},{9,11},{10,... | collective-permute-start | bytes 614408 | tf_op jit(solution)/shard_map/ppermute | solution.py:883
  122.6 10.0 %all_to_all.41.gs = bf16[8,3,16,128]{3,2,1,0:T(8,128)(2,1)S(1)} all-to-all(bf16[8,3,16,128]{3,2,1,0:T(8,128)(2,1)S(1)} %get-tuple-element.179), channel_id=1, replica_groups=mesh['dp'=8,'chan'=4] {'dp'}, dimensions={0} | all-to-all | bytes 196608 | tf_op jit(solution)/shard_map/all_to_all | solution.py:893
  132.6 0.6 shard_map.285
  133.2 0.1 collective-permute-start.18
  133.3 0.7 collective-permute-start.17
  134.0 4.3 %collective-permute-start.16 = (bf16[34,16,128]{2,1,0:T(8,128)(2,1)S(1)}, bf16[34,16,128]{2,1,0:T(8,128)(2,1)S(1)}, u32[]{:S(2)}, u32[]{:S(2)}) collective-permute-start(bf16[34,16,128]{2,1,0:T(8,128)(2,1)S(1)} %shard_map.285), channel_id=1, source_target_pairs={{0,8},{1,0},{2,24},{3,16},{4,12},{5,4},{6,28},{7,20},{8,9},{9,1},{... | collective-permute-start | bytes 417800 | tf_op jit(solution)/shard_map/ppermute | solution.py:907
  138.3 1.9 %collective-permute-start.15 = (bf16[34,16,128]{2,1,0:T(8,128)(2,1)S(1)}, bf16[34,16,128]{2,1,0:T(8,128)(2,1)S(1)}, u32[]{:S(2)}, u32[]{:S(2)}) collective-permute-start(bf16[34,16,128]{2,1,0:T(8,128)(2,1)S(1)} %shard_map.285), channel_id=1, source_target_pairs={{0,0},{1,8},{2,16},{3,24},{4,4},{5,12},{6,20},{7,28},{8,1},{9,9},{... | collective-permute-start | bytes 417800 | tf_op jit(solution)/shard_map/ppermute | solution.py:907
  140.2 4.2 %collective-permute-done.18.refs_3_ = bf16[34,16,128]{2,1,0:T(8,128)(2,1)S(1)} collective-permute-done((bf16[34,16,128]{2,1,0:T(8,128)(2,1)S(1)}, bf16[34,16,128]{2,1,0:T(8,128)(2,1)S(1)}, u32[]{:S(2)}, u32[]{:S(2)}) %collective-permute-start.18) | collective-permute-done | bytes 139296 | tf_op jit(solution)/shard_map/ppermute | solution.py:907
  144.4 0.5 collective-permute-start.22
  145.0 2.3 %collective-permute-done.17.refs_2_ = bf16[34,16,128]{2,1,0:T(8,128)(2,1)S(1)} collective-permute-done((bf16[34,16,128]{2,1,0:T(8,128)(2,1)S(1)}, bf16[34,16,128]{2,1,0:T(8,128)(2,1)S(1)}, u32[]{:S(2)}, u32[]{:S(2)}) %collective-permute-start.17) | collective-permute-done | bytes 139296 | tf_op jit(solution)/shard_map/ppermute | solution.py:907
  147.3 0.7 collective-permute-start.21
  148.0 0.0 collective-permute-done.16.refs_1_
  148.0 1.3 collective-permute-start.20
  149.3 1.4 collective-permute-done.15.refs_0_
  150.7 0.1 collective-permute-start.19
  150.8 3.5 %shard_map.286 = (f32[3,4,9,32,128]{4,3,2,1,0:T(8,128)}, f32[3,20,128]{2,1,0:T(8,128)S(1)}, f32[3,20]{1,0:T(4,128)S(1)}, f32[5,3,32]{2,1,0:T(4,128)S(1)}, f32[32...) custom-call(s32[6]{0:T(128)S(1)} %copy-done.1, ...), custom_call_target="tpu_custom_call" | custom-call | flops 1000000 | bytes 10000 | tf_op jit(solution)/shard_map/pallas_call | solution.py:860
  154.3 1.3 shard_map.288
  155.7 1.3 shard_map.287
  157.0 0.0 collective-permute-done.19.refs_0_
  157.0 2.3 %shard_map.289 = (f32[3,4,9,32,128]{4,3,2,1,0:T(8,128)}, f32[3,20,128]{2,1,0:T(8,128)}, f32[3,20]{1,0:T(4,128)}, f32[5,3,32]{2,1,0:T(4,128)}, f32[32,128]{1,0:T(...) custom-call(s32[6]{0:T(128)S(1)} %copy-done.1, ...), custom_call_target="tpu_custom_call", output_to_operand_aliasing={{0}: (5, {})} | custom-call | flops 1000000 | bytes 10000 | tf_op jit(solution)/shard_map/pallas_call | solution.py:860
  (14 shorter events, 0.0 us)
Async XLA Ops:
  1.8 6.8 %collective-permute-start.1 = (bf16[3,4,9,32,128]{4,3,2,1,0:T(8,128)(2,1)}, bf16[3,4,9,32,128]{4,3,2,1,0:T(8,128)(2,1)S(1)}, u32[]{:S(2)}, u32[]{:S(2)}) collective-permute-start(bf16[3,4,9,32,128]{4,3,2,1,0:T(8,128)(2,1)} %mine.3), channel_id=1, source_target_pairs={{0,1},{1,0},{2,3},{3,2},{4,5},{5,4},{6,7},{7,6},{8,9},{9,8},{10,11... | collective-permute-start | bytes 2654216 | tf_op jit(solution)/shard_map/ppermute | solution.py:889
  1.9 10.5 %collective-permute-start.2 = (bf16[32,2560]{1,0:T(8,128)(2,1)S(1)}, bf16[32,2560]{1,0:T(8,128)(2,1)S(1)}, u32[]{:S(2)}, u32[]{:S(2)}) collective-permute-start(bf16[32,2560]{1,0:T(8,128)(2,1)S(1)} %get-tuple-element.113.u0), channel_id=1, source_target_pairs={{0,1},{1,0},{2,3},{3,2},{4,5},{5,4},{6,7},{7,6},{8,9},{9,8},{10,11... | collective-permute-start | bytes 491528 | tf_op jit(solution)/shard_map/ppermute | solution.py:889
  2.4 6.2 %collective-permute-start = (bf16[32,2560]{1,0:T(8,128)(2,1)S(1)}, bf16[32,2560]{1,0:T(8,128)(2,1)S(1)}, u32[]{:S(2)}, u32[]{:S(2)}) collective-permute-start(bf16[32,2560]{1,0:T(8,128)(2,1)S(1)} %get-tuple-element.114), channel_id=1, source_target_pairs={{0,2},{1,3},{2,0},{3,1},{4,6},{5,7},{6,4},{7,5},{8,10},{9,11},{10,... | collective-permute-start | bytes 491528 | tf_op jit(solution)/shard_map/ppermute | solution.py:883
  3.7 8.8 %copy-start.1 = (s32[6]{0:T(128)S(1)}, s32[6]{0:T(128)}, u32[]{:S(2)}) copy-start(s32[6]{0:T(128)} %stack.23.meta) | copy-start | bytes 76
  3.7 23.4 %copy-start = (bf16[3,4,9,32,128]{4,3,2,1,0:T(8,128)(2,1)S(1)}, bf16[3,4,9,32,128]{4,3,2,1,0:T(8,128)(2,1)}, u32[]{:S(2)}) copy-start(bf16[3,4,9,32,128]{4,3,2,1,0:T(8,128)(2,1)} %mine.3) | copy-start | bytes 2654212
  8.6 3.8 %collective-permute-start.3 = (bf16[32,2560]{1,0:T(8,128)(2,1)S(1)}, bf16[32,2560]{1,0:T(8,128)(2,1)S(1)}, u32[]{:S(2)}, u32[]{:S(2)}) collective-permute-start(bf16[32,2560]{1,0:T(8,128)(2,1)S(1)} %collective-permute-done.u1), channel_id=1, source_target_pairs={{0,1},{1,0},{2,3},{3,2},{4,5},{5,4},{6,7},{7,6},{8,9},{9,8},{10,11... | collective-permute-start | bytes 491528 | tf_op jit(solution)/shard_map/ppermute | solution.py:889
  8.6 5.4 %collective-permute-start.4 = (bf16[17,32,128]{2,1,0:T(8,128)(2,1)S(1)}, bf16[17,32,128]{2,1,0:T(8,128)(2,1)S(1)}, u32[]{:S(2)}, u32[]{:S(2)}) collective-permute-start(bf16[17,32,128]{2,1,0:T(8,128)(2,1)S(1)} %get-tuple-element.121.k0), channel_id=1, source_target_pairs={{1,0},{3,2},{5,4},{7,6},{9,8},{11,10},{13,12},{15,14},{17,16},{19,... | collective-permute-start | bytes 417800 | tf_op jit(solution)/shard_map/ppermute | solution.py:889
  9.9 16.4 %collective-permute-start.5 = (bf16[18,32,128]{2,1,0:T(8,128)(2,1)S(1)}, bf16[18,32,128]{2,1,0:T(8,128)(2,1)S(1)}, u32[]{:S(2)}, u32[]{:S(2)}) collective-permute-start(bf16[18,32,128]{2,1,0:T(8,128)(2,1)S(1)} %get-tuple-element.127), channel_id=1, source_target_pairs={{0,2},{1,3},{2,0},{3,1},{4,6},{5,7},{6,4},{7,5},{8,10},{9,11},{10,... | collective-permute-start | bytes 442376 | tf_op jit(solution)/shard_map/ppermute | solution.py:883
  10.3 16.1 %collective-permute-start.6 = (bf16[18,32,128]{2,1,0:T(8,128)(2,1)S(1)}, bf16[18,32,128]{2,1,0:T(8,128)(2,1)S(1)}, u32[]{:S(2)}, u32[]{:S(2)}) collective-permute-start(bf16[18,32,128]{2,1,0:T(8,128)(2,1)S(1)} %get-tuple-element.129), channel_id=1, source_target_pairs={{0,3},{1,2},{2,1},{3,0},{4,7},{5,6},{6,5},{7,4},{8,11},{9,10},{10,... | collective-permute-start | bytes 442376 | tf_op jit(solution)/shard_map/ppermute | solution.py:886
  26.4 12.8 %collective-permute-start.8 = (bf16[35,32,128]{2,1,0:T(8,128)(2,1)S(1)}, bf16[35,32,128]{2,1,0:T(8,128)(2,1)S(1)}, u32[]{:S(2)}, u32[]{:S(2)}) collective-permute-start(bf16[35,32,128]{2,1,0:T(8,128)(2,1)S(1)} %get-tuple-element.138), channel_id=1, source_target_pairs={{0,3},{1,2},{2,1},{3,0},{4,7},{5,6},{6,5},{7,4},{8,11},{9,10},{10,... | collective-permute-start | bytes 860168 | tf_op jit(solution)/shard_map/ppermute | solution.py:886
  26.4 13.8 %collective-permute-start.7 = (bf16[35,32,128]{2,1,0:T(8,128)(2,1)S(1)}, bf16[35,32,128]{2,1,0:T(8,128)(2,1)S(1)}, u32[]{:S(2)}, u32[]{:S(2)}) collective-permute-start(bf16[35,32,128]{2,1,0:T(8,128)(2,1)S(1)} %get-tuple-element.136), channel_id=1, source_target_pairs={{0,2},{1,3},{2,0},{3,1},{4,6},{5,7},{6,4},{7,5},{8,10},{9,11},{10,... | collective-permute-start | bytes 860168 | tf_op jit(solution)/shard_map/ppermute | solution.py:883
  55.7 11.4 %collective-permute-start.9 = (bf16[32,1664]{1,0:T(8,128)(2,1)S(1)}, bf16[32,1664]{1,0:T(8,128)(2,1)S(1)}, u32[]{:S(2)}, u32[]{:S(2)}) collective-permute-start(bf16[32,1664]{1,0:T(8,128)(2,1)S(1)} %get-tuple-element.155), channel_id=1, source_target_pairs={{0,1},{1,0},{2,3},{3,2},{4,5},{5,4},{6,7},{7,6},{8,9},{9,8},{10,11... | collective-permute-start | bytes 319496 | tf_op jit(solution)/shard_map/ppermute | solution.py:889
  55.8 11.4 %collective-permute-start.10 = (bf16[32,1664]{1,0:T(8,128)(2,1)S(1)}, bf16[32,1664]{1,0:T(8,128)(2,1)S(1)}, u32[]{:S(2)}, u32[]{:S(2)}) collective-permute-start(bf16[32,1664]{1,0:T(8,128)(2,1)S(1)} %get-tuple-element.156), channel_id=1, source_target_pairs={{0,2},{1,3},{2,0},{3,1},{4,6},{5,7},{6,4},{7,5},{8,10},{9,11},{10,... | collective-permute-start | bytes 319496 | tf_op jit(solution)/shard_map/ppermute | solution.py:883
  58.0 9.1 %collective-permute-start.11 = (bf16[32,1664]{1,0:T(8,128)(2,1)S(1)}, bf16[32,1664]{1,0:T(8,128)(2,1)S(1)}, u32[]{:S(2)}, u32[]{:S(2)}) collective-permute-start(bf16[32,1664]{1,0:T(8,128)(2,1)S(1)} %get-tuple-element.157), channel_id=1, source_target_pairs={{0,3},{1,2},{2,1},{3,0},{4,7},{5,6},{6,5},{7,4},{8,11},{9,10},{10,... | collective-permute-start | bytes 319496 | tf_op jit(solution)/shard_map/ppermute | solution.py:886
  95.7 2.0 %collective-permute-start.13 = (bf16[1920,128]{1,0:T(8,128)(2,1)S(1)}, bf16[1920,128]{1,0:T(8,128)(2,1)S(1)}, u32[]{:S(2)}, u32[]{:S(2)}) collective-permute-start(bf16[1920,128]{1,0:T(8,128)(2,1)S(1)} %get-tuple-element.167.d0), channel_id=1, source_target_pairs={{0,1},{1,0},{2,3},{3,2},{4,5},{5,4},{6,7},{7,6},{8,9},{9,8},{10,11... | collective-permute-start | bytes 1474568 | tf_op jit(solution)/shard_map/ppermute | solution.py:889
  95.8 1.8 %collective-permute-start.12 = (f32[1,8,128]{2,1,0:T(8,128)S(1)}, f32[1,8,128]{2,1,0:T(8,128)S(1)}, u32[]{:S(2)}, u32[]{:S(2)}) collective-permute-start(f32[1,8,128]{2,1,0:T(8,128)S(1)} %slice.3), channel_id=1, source_target_pairs={{0,1},{1,0},{2,3},{3,2},{4,5},{5,4},{6,7},{7,6},{8,9},{9,8},{10,11... | collective-permute-start | bytes 12296 | tf_op jit(solution)/shard_map/ppermute | solution.py:889
  120.6 12.0 %collective-permute-start.14 = (bf16[50,16,128]{2,1,0:T(8,128)(2,1)S(1)}, bf16[50,16,128]{2,1,0:T(8,128)(2,1)S(1)}, u32[]{:S(2)}, u32[]{:S(2)}) collective-permute-start(bf16[50,16,128]{2,1,0:T(8,128)(2,1)S(1)} %get-tuple-element.180), channel_id=1, source_target_pairs={{0,2},{1,3},{2,0},{3,1},{4,6},{5,7},{6,4},{7,5},{8,10},{9,11},{10,... | collective-permute-start | bytes 614408 | tf_op jit(solution)/shard_map/ppermute | solution.py:883
  133.2 11.2 %collective-permute-start.18 = (bf16[34,16,128]{2,1,0:T(8,128)(2,1)S(1)}, bf16[34,16,128]{2,1,0:T(8,128)(2,1)S(1)}, u32[]{:S(2)}, u32[]{:S(2)}) collective-permute-start(bf16[34,16,128]{2,1,0:T(8,128)(2,1)S(1)} %shard_map.285), channel_id=1, source_target_pairs={{0,24},{1,16},{2,8},{3,0},{4,28},{5,20},{6,12},{7,4},{8,25},{9,17}... | collective-permute-start | bytes 417800 | tf_op jit(solution)/shard_map/ppermute | solution.py:907
  133.3 13.9 %collective-permute-start.17 = (bf16[34,16,128]{2,1,0:T(8,128)(2,1)S(1)}, bf16[34,16,128]{2,1,0:T(8,128)(2,1)S(1)}, u32[]{:S(2)}, u32[]{:S(2)}) collective-permute-start(bf16[34,16,128]{2,1,0:T(8,128)(2,1)S(1)} %shard_map.285), channel_id=1, source_target_pairs={{0,16},{1,24},{2,0},{3,8},{4,20},{5,28},{6,4},{7,12},{8,17},{9,25}... | collective-permute-start | bytes 417800 | tf_op jit(solution)/shard_map/ppermute | solution.py:907
  134.0 14.0 %collective-permute-start.16 = (bf16[34,16,128]{2,1,0:T(8,128)(2,1)S(1)}, bf16[34,16,128]{2,1,0:T(8,128)(2,1)S(1)}, u32[]{:S(2)}, u32[]{:S(2)}) collective-permute-start(bf16[34,16,128]{2,1,0:T(8,128)(2,1)S(1)} %shard_map.285), channel_id=1, source_target_pairs={{0,8},{1,0},{2,24},{3,16},{4,12},{5,4},{6,28},{7,20},{8,9},{9,1},{... | collective-permute-start | bytes 417800 | tf_op jit(solution)/shard_map/ppermute | solution.py:907
  138.3 12.4 %collective-permute-start.15 = (bf16[34,16,128]{2,1,0:T(8,128)(2,1)S(1)}, bf16[34,16,128]{2,1,0:T(8,128)(2,1)S(1)}, u32[]{:S(2)}, u32[]{:S(2)}) collective-permute-start(bf16[34,16,128]{2,1,0:T(8,128)(2,1)S(1)} %shard_map.285), channel_id=1, source_target_pairs={{0,0},{1,8},{2,16},{3,24},{4,4},{5,12},{6,20},{7,28},{8,1},{9,9},{... | collective-permute-start | bytes 417800 | tf_op jit(solution)/shard_map/ppermute | solution.py:907
  144.4 12.5 %collective-permute-start.22 = (bf16[34,16,128]{2,1,0:T(8,128)(2,1)S(1)}, bf16[34,16,128]{2,1,0:T(8,128)(2,1)S(1)}, u32[]{:S(2)}, u32[]{:S(2)}) collective-permute-start(bf16[34,16,128]{2,1,0:T(8,128)(2,1)S(1)} %collective-permute-done.18.refs_3_), channel_id=1, source_target_pairs={{0,4},{4,0},{8,12},{12,8},{16,20},{20,16},{24,28},{28,24},{1,5},{5... | collective-permute-start | bytes 417800 | tf_op jit(solution)/shard_map/ppermute | solution.py:920
  147.3 9.7 %collective-permute-start.21 = (bf16[34,16,128]{2,1,0:T(8,128)(2,1)S(1)}, bf16[34,16,128]{2,1,0:T(8,128)(2,1)S(1)}, u32[]{:S(2)}, u32[]{:S(2)}) collective-permute-start(bf16[34,16,128]{2,1,0:T(8,128)(2,1)S(1)} %collective-permute-done.17.refs_2_), channel_id=1, source_target_pairs={{0,4},{4,0},{8,12},{12,8},{16,20},{20,16},{24,28},{28,24},{1,5},{5... | collective-permute-start | bytes 417800 | tf_op jit(solution)/shard_map/ppermute | solution.py:920
  148.0 9.0 %collective-permute-start.20 = (bf16[34,16,128]{2,1,0:T(8,128)(2,1)S(1)}, bf16[34,16,128]{2,1,0:T(8,128)(2,1)S(1)}, u32[]{:S(2)}, u32[]{:S(2)}) collective-permute-start(bf16[34,16,128]{2,1,0:T(8,128)(2,1)S(1)} %collective-permute-done.16.refs_1_), channel_id=1, source_target_pairs={{0,4},{4,0},{8,12},{12,8},{16,20},{20,16},{24,28},{28,24},{1,5},{5... | collective-permute-start | bytes 417800 | tf_op jit(solution)/shard_map/ppermute | solution.py:920
  150.7 6.3 %collective-permute-start.19 = (bf16[34,16,128]{2,1,0:T(8,128)(2,1)S(1)}, bf16[34,16,128]{2,1,0:T(8,128)(2,1)S(1)}, u32[]{:S(2)}, u32[]{:S(2)}) collective-permute-start(bf16[34,16,128]{2,1,0:T(8,128)(2,1)S(1)} %collective-permute-done.15.refs_0_), channel_id=1, source_target_pairs={{0,4},{4,0},{8,12},{12,8},{16,20},{20,16},{24,28},{28,24},{1,5},{5... | collective-permute-start | bytes 417800 | tf_op jit(solution)/shard_map/ppermute | solution.py:920

commit v5 on v4

--- a/solution.py
+++ b/solution.py
@@ -26,7 +26,7 @@
 WIDE = PAR + 256
 CLS = CP // 128 + 4
 TAPS = 18
-SENT = 50
+SENT = 2 * (CP // 128) + 9
 VMEM = 12 * 2**20
 WHOLE = 56 * 2**20
 NT = (((1,), (1,)), ((), ()))
@@ -383,16 +383,6 @@
         gw[j, i] = v[16 * j : 16 * (j + 1)].astype(BF)
 
 
-def stat_total(st):
-    if st.dtype == F32:
-        return jnp.sum(st[...], axis=0)
-    n = st.shape[1] - 1
-    rows = from_parts(st[0, n])
-    for d in range(1, st.shape[0]):
-        rows += from_parts(st[d, n])
-    return rows
-
-
 def grad_sums(meta, total, sums):
     shift = pick(meta, total[0:1], total[1:2])
     gain = pick(meta, total[2:3], total[3:4])
@@ -408,7 +398,7 @@
 
 
 def out_grad(meta, dz, y, cst, st, sums, field, dyt):
-    grad_sums(meta, stat_total(st), sums)
+    grad_sums(meta, jnp.sum(st[...], axis=0), sums)
     for j in range(NCH):
         rows = slice(CH * j, CH * (j + 1))
         v = input_grad(meta, dz[rows], y, cst, sums, j)
@@ -428,19 +418,6 @@
         total[s] += colsum(d)
         total[2 + s] += colsum(d * xhat)
     spread_out(st_out, total)
-    return total
-
-
-def as_parts(rows):
-    v = jnp.concatenate(rows, axis=0)
-    high = v.astype(BF).astype(F32)
-    mid = (v - high).astype(BF).astype(F32)
-    return jnp.concatenate([high, mid, v - high - mid, jnp.zeros((4, 128), F32)], axis=0).astype(BF)
-
-
-def from_parts(block):
-    v = block.astype(F32)
-    return v[0:4] + v[4:8] + v[8:12]
 
 
 def weight_grad(meta, dyt, act, field, shifts, wg):
@@ -465,32 +442,36 @@
         store(1, dot(dyt[:, CUT:PX], taps(shifts, CUT, PX - CUT)))
 
 
-def second_back_kernel(meta, dz, y, cst, st, w, act, y_in, cst_in, gw, grad, st_out, sums, wg, field, shifts, dyt):
+def part_out(meta, wg, send):
+    for z in range(4):
+        send[z] = wg[2 * z + 1 - meta[5]]
+
+
+def second_back_kernel(meta, dz, y, cst, st, w, act, y_in, cst_in, gw, grad, st_out, sums, wg, send, field, shifts, dyt):
     guard(field, shifts)
     out_grad(meta, dz, y, cst, st, sums, field, dyt)
     fill_shifts(field, shifts)
-    block = as_parts(conv_back(meta, False, w, y_in, cst_in, shifts, grad, st_out))
+    conv_back(meta, False, w, y_in, cst_in, shifts, grad, st_out)
     weight_grad(meta, dyt, act, field, shifts, wg)
     for j in range(8):
         for i in range(3):
             wg[j, 18 + i] = gw[j, i]
-        wg[j, 21] = block
-
-
-def first_back_kernel(meta, dz, y, cst, st, w, act, y_in, cst_in, grad, st_out, sums, wg, field, shifts, dyt):
+    part_out(meta, wg, send)
+
+
+def first_back_kernel(meta, dz, y, cst, st, w, act, y_in, cst_in, grad, st_out, sums, wg, send, field, shifts, dyt):
     guard(field, shifts)
     out_grad(meta, dz, y, cst, st, sums, field, dyt)
     fill_shifts(field, shifts)
-    block = as_parts(conv_back(meta, True, w, y_in, cst_in, shifts, grad, st_out))
+    conv_back(meta, True, w, y_in, cst_in, shifts, grad, st_out)
     weight_grad(meta, dyt, act, field, shifts, wg)
-    for j in range(8):
-        wg[j, 18] = block
-
-
-def final_kernel(meta, d0, d1, y, cst, st, sums1, sums2, u0, u1, u2, u3, extra, own, send, gs, norm, *scratch):
+    part_out(meta, wg, send)
+
+
+def final_kernel(meta, d0, d1, y, cst, st, sums1, sums2, u0, u1, u2, u3, extra, own, send, gs, gs_send, norm, *scratch):
     sums, feat, stem, field, flat, dyt, gf, blocks, other = scratch
     load_inputs(meta, (u0, u1, u2, u3), feat, stem)
-    grad_sums(meta, stat_total(st), sums)
+    grad_sums(meta, jnp.sum(st[...], axis=0), sums)
     for j in range(NCH):
         rows = slice(CH * j, CH * (j + 1))
         _, z = normed(cst, y[rows], SLOT[j])
@@ -537,44 +518,56 @@
         block = blocks[3 * meta[1] + i]
         for j in range(8):
             gs[j, i] = block[16 * j : 16 * (j + 1)]
+    part_out(meta, gs, gs_send)
     rest = jnp.zeros((4, 128), F32)
     norm[0] = jnp.concatenate([sums[0:4], sums1[0:4], sums2[0:4], rest], axis=0).astype(BF)
 
 
-def patch_kernel(wg, other, out):
-    n = wg.shape[1] - 1
-    block = as_parts([from_parts(wg[0, n]) + other[0, 0:4]])
-    for j in range(8):
-        out[j, n] = block
-
-
-def summed(v, begin, end):
-    total = v[0, begin:end].astype(F32)
-    for d in range(1, v.shape[0]):
-        total += v[d, begin:end].astype(F32)
+def total_kernel(st, out):
+    out[0] = jnp.sum(st[...], axis=0)
+
+
+def add_kernel(count, meta, *refs):
+    kept, got, outs = refs[:count], refs[count : 2 * count], refs[2 * count :]
+    for k, out in enumerate(outs):
+        z = meta[4] ^ k
+        at = 0
+        for a, b in zip(kept, got):
+            n = a.shape[1]
+            out[at : at + n] = (a[2 * z + meta[5]].astype(F32) + b[z].astype(F32)).astype(out.dtype)
+            at += n
+
+
+def summed(refs, begin, end):
+    total = refs[0][begin:end].astype(F32)
+    for r in refs[1:]:
+        total += r[begin:end].astype(F32)
     return total.astype(BF)
 
 
-def sum_kernel(meta, second, total, extra):
-    total[0:9] = summed(second, 0, 9)
-    total[9:12] = summed(second, 18, 21)
-    extra[...] = summed(second, 9, 18)
-
-
-def join_kernel(meta, first, total, extra, gs, norm, out):
-    out[0:9] = summed(first, 0, 9)
+def sum_kernel(meta, *refs):
+    parts, (total, extra) = refs[:4], refs[4:]
+    total[0:9] = summed(parts, 0, 9)
+    total[9:12] = summed(parts, 18, 21)
+    extra[...] = summed(parts, 9, 18)
+
+
+def join_kernel(meta, *refs):
+    parts, (total, received, norm, out) = refs[:4], refs[4:]
+    out[0:9] = summed(parts, 0, 9)
     out[9:18] = total[0:9]
     out[27:30] = total[9:12]
 
     @pl.when(meta[0] == 0)
     def _():
-        out[18:27] = extra[2 * (CP // 128) : 2 * (CP // 128) + 9]
+        at = 2 * (CP // 128)
+        out[18:27] = received[at : at + 9]
 
     @pl.when(meta[0] == 1)
     def _():
-        out[18:27] = summed(first, 9, 18)
-
-    out[30:33] = summed(gs, 0, 3)
+        out[18:27] = summed(parts, 9, 18)
+
+    out[30:33] = summed(parts, 18, 21)
     out[33:34] = norm[...]
 
 
@@ -919,6 +912,12 @@
     def over_y(v):
         return lax.ppermute(v, "dp", [(i, i ^ 1) for i in range(8)])
 
+    def along_z(kept, got):
+        shape = (sum(v.shape[1] for v in kept), 16, 128)
+        outs = [(shape, F32)] + [(shape, BF)] * 3
+        own, *rest = call(functools.partial(add_kernel, len(kept)), outs, [], (meta, *kept, *got))
+        return [own] + [lax.ppermute(v, "dp", [(i, i ^ (2 * k + 2)) for i in range(8)]) for k, v in enumerate(rest)]
+
     def reduce(v):
         return lax.optimization_barrier(lax.psum(v.astype(F32), "dp")).astype(BF)
 
@@ -989,36 +988,35 @@
     st = exchange(after(st, gw))
     st, near, far, cross = lax.optimization_barrier((st, near, far, cross))
     back_scratch = moved + [((128, PX), BF)]
-    dz1, st, sums2, wg2 = call(
+    dz1, st, sums2, wg2, send2 = call(
         second_back_kernel,
-        [(canvas, F32), (stat, F32), ((8, 128), F32), ((8, 22, 16, 128), BF)],
+        [(canvas, F32), (stat, F32), ((8, 128), F32), ((8, 21, 16, 128), BF), ((4, 21, 16, 128), BF)],
         back_scratch,
         (meta, dz2, y2, cst2, st, w2_tall, act1, y1, cst1, gw),
     )
-    got2 = exchange(wg2) if direct else reduce(wg2)
-    st = got2 if direct else exchange(st)
-    d0, st, sums1, wg1 = call(
+    got2 = over_y(send2) if direct else reduce(wg2)
+    st, got2 = lax.optimization_barrier((exchange(after(st, send2)), got2))
+    d0, st, sums1, wg1, send1 = call(
         first_back_kernel,
-        [(canvas, BF), (stat, F32), ((8, 128), F32), ((8, 19, 16, 128), BF)],
+        [(canvas, BF), (stat, F32), ((8, 128), F32), ((8, 18, 16, 128), BF), ((4, 18, 16, 128), BF)],
         back_scratch,
         (meta, dz1, y1, cst1, st, w1_tall, act0, y0, cst0),
-        flops=6 * 10**9,
-    )
-    d0_other = beside(d0)
-    st_other = beside(st[:1])
+    )
+    got1 = over_y(send1) if direct else reduce(wg1)
+    d0_other, st_other = beside(d0), beside(st)
+    st = st + st_other
     if direct:
-        (wg1,) = call(patch_kernel, [(wg1.shape, BF)], [], (wg1, st_other), aliases={0: 0})
-        total, extra = call(sum_kernel, [((12, 16, 128), BF), ((9, 16, 128), BF)], [], (meta, after(got2, d0)))
-        wg1, d0_other, total = lax.optimization_barrier((wg1, d0_other, total))
-        got1 = st = exchange(wg1)
+        parts2 = along_z([wg2], [after(got2, d0)])
+        st = after(st, d0_other, *parts2[:1])
+        (st,) = call(total_kernel, [((1, 8, 128), F32)], [], (exchange(st),))
+        st, got1, *parts2 = lax.optimization_barrier((st, got1, *parts2))
+        total, extra = call(sum_kernel, [((12, 16, 128), BF), ((9, 16, 128), BF)], [], (meta, *parts2))
     else:
-        got1 = reduce(wg1)
-        st = exchange(st + st_other)
-    if not direct:
+        st = exchange(st)
         extra = jnp.zeros((9, 16, 128), BF)
-    own, send, gs, norm = call(
+    own, send, gs, gs_send, norm = call(
         final_kernel,
-        [((32, CP), BF), ((SENT, 16, 128), BF), ((8, 3, 16, 128), BF), ((1, 16, 128), BF)],
+        [((32, CP), BF), ((SENT, 16, 128), BF), ((8, 3, 16, 128), BF), ((4, 3, 16, 128), BF), ((1, 16, 128), BF)],
         [
             ((8, 128), F32),
             ((512, CP), BF),
@@ -1034,8 +1032,8 @@
     )
     received = across(send)
     if direct:
-        gs, received = lax.optimization_barrier((exchange(gs), received))
-        (grads,) = call(join_kernel, [((34, 16, 128), BF)], [], (meta, got1, total, received, gs, norm))
+        parts1 = along_z([wg1, gs], [got1, over_y(gs_send)])
+        (grads,) = call(join_kernel, [((34, 16, 128), BF)], [], (meta, *parts1, total, received, norm))
     else:
         extra = lax.ppermute(got2[:, 9:18], "chan", [(2, 0), (3, 1)])
         third = jnp.where(fine, extra, got1[:, 9:18])

time: 161 us -> 147 us (0.913)
  blocking collectives: 91 us -> 58.2 us
  starting transfers between devices: 19.6 us -> 33 us
  waiting for transfers between devices: 12.4 us -> 16.9 us
    all_to_all x7 -> x6, blocking collectives: 91 us -> 58.2 us  [exchange(): st = lax.all_to_all(st, 'dp', 0, 0, tiled=True)]
    ppermute x0 -> x6, starting transfers between devices: none -> 8.9 us  [along_z(): lax.ppermute(v, 'dp', [(i, i ^ 2 * k + 2) for i in range(8)])]
    ppermute x4 -> x7, waiting for transfers between devices: 0.01 us -> 3.63 us  [over_y(): return lax.ppermute(v, 'dp', [(i, i ^ 1) for i in range(8)])]
    ppermute x0 -> x6, waiting for transfers between devices: none -> 3.59 us  [along_z(): lax.ppermute(v, 'dp', [(i, i ^ 2 * k + 2) for i in range(8)])]
    ppermute x4 -> x7, starting transfers between devices: 2.63 us -> 5.62 us  [over_y(): return lax.ppermute(v, 'dp', [(i, i ^ 1) for i in range(8)])]
    ppermute x4, starting transfers between devices: 6.97 us -> 9 us  [over_z(): parts.append(lax.ppermute(v, ('dp', 'chan'), pairs))]
    ppermute x4, waiting for transfers between devices: 7.94 us -> 5.96 us  [over_z(): parts.append(lax.ppermute(v, ('dp', 'chan'), pairs))]
    pallas_call x19 -> x21, Pallas kernels: 34.3 us -> 34.8 us  [call(): pl.pallas_call(body, out_shape=[place(s, d) for s, d in outs], in_specs=[...]
  transfers between devices with their start and end apart: 23 -> 32, of which waited for: 6 -> 10; matrix products, arithmetic and copies ran while one was open for 0% -> 0% of each run, Pallas kernels for 8% -> 10%
where the time goes in v5:
time: 147 us; the launch traced here: 145 us
  blocking collectives  58.2 us (40%)
  Pallas kernels  34.8 us (24%)
  starting transfers between devices  33 us (22%)
  waiting for transfers between devices  16.9 us (11%)
  between operations  1.7 us (1%)
    all_to_all x6, blocking collectives, exchange(): st = lax.all_to_all(st, 'dp', 0, 0, tiled=True)  58.2 us
    pallas_call x21, Pallas kernels, call(): pl.pallas_call(body, out_shape=[place(s, d) for s, d in outs], in_specs=[...  34.8 us
    ppermute x4, starting transfers between devices, over_z(): parts.append(lax.ppermute(v, ('dp', 'chan'), pairs))  9 us
    ppermute x6, starting transfers between devices, along_z(): lax.ppermute(v, 'dp', [(i, i ^ 2 * k + 2) for i in range(8)])  8.9 us
    ppermute x4, waiting for transfers between devices, over_z(): parts.append(lax.ppermute(v, ('dp', 'chan'), pairs))  5.96 us
    ppermute x7, starting transfers between devices, over_y(): return lax.ppermute(v, 'dp', [(i, i ^ 1) for i in range(8)])  5.62 us
    ppermute x5, starting transfers between devices, across(): return lax.ppermute(v, 'chan', [(i, i ^ 2) for i in range(4)])  5.08 us
    ppermute x5, waiting for transfers between devices, across(): return lax.ppermute(v, 'chan', [(i, i ^ 2) for i in range(4)])  3.66 us
  transfers between devices with their start and end apart: 32, of which 10 were waited for; matrix products, arithmetic and copies ran while one was open for 0% of the time, Pallas kernels for 10%

profile of v5, /device:TPU:2, one launch (start us, length us, event | category | flops | bytes accessed | tf_op | source)
XLA Modules:
  0.0 145.2 jit_solution(17035465447487113244)
XLA Ops:
  0.6 1.2 shard_map.271
  1.8 0.1 collective-permute-start.1
  1.9 0.5 collective-permute-start.2
  3.1 0.6 stack.23.meta
  3.7 2.2 %shard_map.272 = (bf16[17,32,128]{2,1,0:T(8,128)(2,1)S(1)}, bf16[17,32,128]{2,1,0:T(8,128)(2,1)S(1)}, bf16[18,32,128]{2,1,0:T(8,128)(2,1)S(1)}, bf16[18,32,128]{...) custom-call(s32[6]{0:T(128)} %stack.23.meta, bf16[20,2100]{1,0:T(8,128)(2,1)} %bitcast.32, ...), custom_call_target="tpu_custom_call" | custom-call | flops 2000000000 | bytes 10000 | tf_op jit(solution)/shard_map/pallas_call | solution.py:853
  5.9 2.7 %collective-permute-done.u1 = bf16[32,2560]{1,0:T(8,128)(2,1)S(1)} collective-permute-done((bf16[32,2560]{1,0:T(8,128)(2,1)S(1)}, bf16[32,2560]{1,0:T(8,128)(2,1)S(1)}, u32[]{:S(2)}, u32[]{:S(2)}) %collective-permute-start) | collective-permute-done | bytes 163872 | tf_op jit(solution)/shard_map/ppermute | solution.py:876
  8.6 1.3 collective-permute-start.4
  9.9 0.3 collective-permute-start.5
  10.3 2.2 %collective-permute-start.6 = (bf16[18,32,128]{2,1,0:T(8,128)(2,1)S(1)}, bf16[18,32,128]{2,1,0:T(8,128)(2,1)S(1)}, u32[]{:S(2)}, u32[]{:S(2)}) collective-permute-start(bf16[18,32,128]{2,1,0:T(8,128)(2,1)S(1)} %get-tuple-element.146), channel_id=1, source_target_pairs={{0,3},{1,2},{2,1},{3,0},{4,7},{5,6},{6,5},{7,4},{8,11},{9,10},{10,... | collective-permute-start | bytes 442376 | tf_op jit(solution)/shard_map/ppermute | solution.py:879
  12.5 1.6 %shard_map.273 = (f32[1920,128]{1,0:T(8,128)S(1)}, f32[8,8,128]{2,1,0:T(8,128)S(1)}, f32[8,128]{1,0:T(8,128)S(1)}, f32[64,128]{1,0:T(8,128)S(1)}) custom-call(s32[6]{0:T(128)S(1)} %copy-done.1, bf16[32,2560]{1,0:T(8,128)(2,1)S(1)} %get-tuple-element.130.u0, bf16[32,2560]{1,0:T(8,128)(2,1)S(1)} %collective-permute-done.u1, ...), custom_call_target="tpu_custom_call" | custom-call | flops 1000000 | bytes 10000 | tf_op jit(solution)/shard_map/pallas_call | solution.py:853
  14.0 12.3 %all_to_all.30.st = f32[8,8,128]{2,1,0:T(8,128)S(1)} all-to-all(f32[8,8,128]{2,1,0:T(8,128)S(1)} %get-tuple-element.139), channel_id=1, replica_groups=mesh['dp'=8,'chan'=4] {'dp'}, dimensions={0} | all-to-all | bytes 65536 | tf_op jit(solution)/shard_map/all_to_all | solution.py:886
  26.4 0.7 collective-permute-start.7
  27.1 0.7 shard_map.274
  27.9 2.2 %shard_map.275 = (bf16[1920,128]{1,0:T(8,128)(2,1)S(1)}, f32[1920,128]{1,0:T(8,128)S(1)}, f32[8,8,128]{2,1,0:T(8,128)S(1)}, f32[16,128]{1,0:T(8,128)S(1)}) custom-call(s32[6]{0:T(128)S(1)} %copy-done.1, f32[1920,128]{1,0:T(8,128)S(1)} %get-tuple-element.136.y.y_in, f32[8,8,128]{2,1,0:T(8,128)S(1)} %all_to_all.30.st, f32[8,128]{1,0:T(8,128)S(1)} %get-tuple-element.142.cnt, ...), custom_call_target="tpu_custom_call" | custom-call | flops 1000000 | bytes 10000 | tf_op jit(solution)/shard_map/pallas_call | solution.py:853
  30.0 9.1 %all_to_all.31.st = f32[8,8,128]{2,1,0:T(8,128)S(1)} all-to-all(f32[8,8,128]{2,1,0:T(8,128)S(1)} %get-tuple-element.152), channel_id=1, replica_groups=mesh['dp'=8,'chan'=4] {'dp'}, dimensions={0} | all-to-all | bytes 65536 | tf_op jit(solution)/shard_map/all_to_all | solution.py:886
  39.1 1.0 collective-permute-done.7.far.k1
  40.1 0.7 shard_map.276
  40.9 2.2 %shard_map.277 = (bf16[1920,128]{1,0:T(8,128)(2,1)S(1)}, f32[1920,128]{1,0:T(8,128)S(1)}, f32[8,8,128]{2,1,0:T(8,128)S(1)}, f32[16,128]{1,0:T(8,128)S(1)}) custom-call(s32[6]{0:T(128)S(1)} %copy-done.1, f32[1920,128]{1,0:T(8,128)S(1)} %get-tuple-element.151.y.y_in, f32[8,8,128]{2,1,0:T(8,128)S(1)} %all_to_all.31.st, f32[8,128]{1,0:T(8,128)S(1)} %get-tuple-element.142.cnt, ...), custom_call_target="tpu_custom_call" | custom-call | flops 1000000 | bytes 10000 | tf_op jit(solution)/shard_map/pallas_call | solution.py:853
  43.0 9.1 %all_to_all.32.st = f32[8,8,128]{2,1,0:T(8,128)S(1)} all-to-all(f32[8,8,128]{2,1,0:T(8,128)S(1)} %get-tuple-element.160), channel_id=1, replica_groups=mesh['dp'=8,'chan'=4] {'dp'}, dimensions={0} | all-to-all | bytes 65536 | tf_op jit(solution)/shard_map/all_to_all | solution.py:886
  52.1 2.3 %shard_map.278 = (f32[1920,128]{1,0:T(8,128)S(1)}, f32[8,8,128]{2,1,0:T(8,128)S(1)}, f32[16,128]{1,0:T(8,128)S(1)}, bf16[1664,256]{1,0:T(8,128)(2,1)S(1)}, bf16[...) custom-call(s32[6]{0:T(128)S(1)} %copy-done.1, f32[1920,128]{1,0:T(8,128)S(1)} %get-tuple-element.159.y, ...), custom_call_target="tpu_custom_call" | custom-call | flops 1000000 | bytes 10000 | tf_op jit(solution)/shard_map/pallas_call | solution.py:853
  54.4 1.3 shard_map.279
  55.7 0.1 collective-permute-start.9
  55.8 2.2 %collective-permute-start.10 = (bf16[32,1664]{1,0:T(8,128)(2,1)S(1)}, bf16[32,1664]{1,0:T(8,128)(2,1)S(1)}, u32[]{:S(2)}, u32[]{:S(2)}) collective-permute-start(bf16[32,1664]{1,0:T(8,128)(2,1)S(1)} %get-tuple-element.173), channel_id=1, source_target_pairs={{0,2},{1,3},{2,0},{3,1},{4,6},{5,7},{6,4},{7,5},{8,10},{9,11},{10,... | collective-permute-start | bytes 319496 | tf_op jit(solution)/shard_map/ppermute | solution.py:876
  58.1 9.0 %all_to_all.33.st = f32[8,8,128]{2,1,0:T(8,128)S(1)} all-to-all(f32[8,8,128]{2,1,0:T(8,128)S(1)} %get-tuple-element.171), channel_id=1, replica_groups=mesh['dp'=8,'chan'=4] {'dp'}, dimensions={0} | all-to-all | bytes 65536 | tf_op jit(solution)/shard_map/all_to_all | solution.py:886
  67.1 3.7 %shard_map.280 = (f32[1920,128]{1,0:T(8,128)S(1)}, f32[8,8,128]{2,1,0:T(8,128)S(1)}, f32[8,128]{1,0:T(8,128)S(1)}, bf16[8,21,16,128]{3,2,1,0:T(8,128)(2,1)S(1)}, bf16[4,21,16,128]{3,2,1,0:T(8,128)(2,1)S(1)}) custom-call(s32[6]{0:T(128)S(1)} %copy-done.1, f32[1920,128]{1,0:T(8,128)S(1)} %get-tuple-element.167.dz, f32[1920,128]{1,0:T(8,128)S(1)} %get-tuple-element.159.y, ...), custom_call_target="tpu_custom_call" | custom-call | flops 1000000 | bytes 10000 | tf_op jit(solution)/shard_map/pallas_call | solution.py:853
  70.8 0.5 collective-permute-start.12
  71.4 9.3 %all_to_all.34.st = f32[8,8,128]{2,1,0:T(8,128)S(1)} all-to-all(f32[8,8,128]{2,1,0:T(8,128)S(1)} %get-tuple-element.182), channel_id=1, replica_groups=mesh['dp'=8,'chan'=4] {'dp'}, dimensions={0} | all-to-all | bytes 65536 | tf_op jit(solution)/shard_map/all_to_all | solution.py:886
  80.7 3.5 %shard_map.281 = (bf16[1920,128]{1,0:T(8,128)(2,1)S(1)}, f32[8,8,128]{2,1,0:T(8,128)S(1)}, f32[8,128]{1,0:T(8,128)S(1)}, bf16[8,18,16,128]{3,2,1,0:T(8,128)(2,1)S(1)}, bf16[4,18,16,128]{3,2,1,0:T(8,128)(2,1)S(1)}) custom-call(s32[6]{0:T(128)S(1)} %copy-done.1, f32[1920,128]{1,0:T(8,128)S(1)} %get-tuple-element.179.dz, ...), custom_call_target="tpu_custom_call" | custom-call | flops 1000000 | bytes 10000 | tf_op jit(solution)/shard_map/pallas_call | solution.py:853
  84.2 0.1 collective-permute-start.13
  84.3 0.5 collective-permute-start.15
  84.9 0.2 collective-permute-start.14
  85.0 0.6 shard_map.282
  85.7 0.8 collective-permute-start.16
  86.4 0.6 collective-permute-start.17
  87.1 3.0 %collective-permute-start.18 = (bf16[21,16,128]{2,1,0:T(8,128)(2,1)S(1)}, bf16[21,16,128]{2,1,0:T(8,128)(2,1)S(1)}, u32[]{:S(2)}, u32[]{:S(2)}) collective-permute-start(bf16[21,16,128]{2,1,0:T(8,128)(2,1)S(1)} %get-tuple-element.197), channel_id=1, source_target_pairs={{0,24},{4,28},{8,16},{12,20},{16,8},{20,12},{24,0},{28,4},{1,25},{... | collective-permute-start | bytes 258056 | tf_op jit(solution)/shard_map/ppermute | solution.py:919
  90.1 9.3 %all_to_all.35.st = f32[8,8,128]{2,1,0:T(8,128)S(1)} all-to-all(f32[8,8,128]{2,1,0:T(8,128)S(1)} %add.14), channel_id=1, replica_groups=mesh['dp'=8,'chan'=4] {'dp'}, dimensions={0} | all-to-all | bytes 65536 | tf_op jit(solution)/shard_map/all_to_all | solution.py:886
  99.5 0.6 shard_map.284
  100.1 2.3 %shard_map.285 = (bf16[32,1664]{1,0:T(8,128)(2,1)S(1)}, bf16[35,16,128]{2,1,0:T(8,128)(2,1)S(1)}, bf16[8,3,16,128]{3,2,1,0:T(8,128)(2,1)S(1)}, bf16[4,3,16,128]{...) custom-call(s32[6]{0:T(128)S(1)} %copy-done.1, bf16[1920,128]{1,0:T(8,128)(2,1)S(1)} %get-tuple-element.187.d0, ...), custom_call_target="tpu_custom_call" | custom-call | flops 1000000 | bytes 10000 | tf_op jit(solution)/shard_map/pallas_call | solution.py:853
  102.4 1.8 %collective-permute-start.23 = (bf16[35,16,128]{2,1,0:T(8,128)(2,1)S(1)}, bf16[35,16,128]{2,1,0:T(8,128)(2,1)S(1)}, u32[]{:S(2)}, u32[]{:S(2)}) collective-permute-start(bf16[35,16,128]{2,1,0:T(8,128)(2,1)S(1)} %get-tuple-element.216), channel_id=1, source_target_pairs={{0,2},{1,3},{2,0},{3,1},{4,6},{5,7},{6,4},{7,5},{8,10},{9,11},{10,... | collective-permute-start | bytes 430088 | tf_op jit(solution)/shard_map/ppermute | solution.py:876
  104.1 0.5 collective-permute-start.19
  104.6 3.6 %collective-permute-done.19.refs_3_ = bf16[4,3,16,128]{3,2,1,0:T(8,128)(2,1)S(1)} collective-permute-done((bf16[4,3,16,128]{3,2,1,0:T(8,128)(2,1)S(1)}, bf16[4,3,16,128]{3,2,1,0:T(8,128)(2,1)S(1)}, u32[]{:S(2)}, u32[]{:S(2)}) %collective-permute-start.19) | collective-permute-done | bytes 49184 | tf_op jit(solution)/shard_map/ppermute | solution.py:913
  108.2 0.6 shard_map.286
  108.8 0.5 collective-permute-start.20
  109.3 0.9 collective-permute-start.21
  110.2 3.1 %collective-permute-start.22 = (bf16[21,16,128]{2,1,0:T(8,128)(2,1)S(1)}, bf16[21,16,128]{2,1,0:T(8,128)(2,1)S(1)}, u32[]{:S(2)}, u32[]{:S(2)}) collective-permute-start(bf16[21,16,128]{2,1,0:T(8,128)(2,1)S(1)} %get-tuple-element.214), channel_id=1, source_target_pairs={{0,24},{4,28},{8,16},{12,20},{16,8},{20,12},{24,0},{28,4},{1,25},{... | collective-permute-start | bytes 258056 | tf_op jit(solution)/shard_map/ppermute | solution.py:919
  113.3 0.1 collective-permute-done.20.refs_1_
  113.4 1.3 collective-permute-done.21.refs_2_
  114.7 2.2 %collective-permute-done.22.refs_3_ = bf16[21,16,128]{2,1,0:T(8,128)(2,1)S(1)} collective-permute-done((bf16[21,16,128]{2,1,0:T(8,128)(2,1)S(1)}, bf16[21,16,128]{2,1,0:T(8,128)(2,1)S(1)}, u32[]{:S(2)}, u32[]{:S(2)}) %collective-permute-start.22) | collective-permute-done | bytes 86048 | tf_op jit(solution)/shard_map/ppermute | solution.py:919
  116.9 0.6 shard_map.287
  117.5 0.9 collective-permute-start.27
  118.4 2.2 %collective-permute-start.26 = (bf16[34,16,128]{2,1,0:T(8,128)(2,1)S(1)}, bf16[34,16,128]{2,1,0:T(8,128)(2,1)S(1)}, u32[]{:S(2)}, u32[]{:S(2)}) collective-permute-start(bf16[34,16,128]{2,1,0:T(8,128)(2,1)S(1)} %shard_map.287), channel_id=1, source_target_pairs={{0,16},{1,24},{2,0},{3,8},{4,20},{5,28},{6,4},{7,12},{8,17},{9,25}... | collective-permute-start | bytes 417800 | tf_op jit(solution)/shard_map/ppermute | solution.py:900
  120.7 1.9 %collective-permute-start.25 = (bf16[34,16,128]{2,1,0:T(8,128)(2,1)S(1)}, bf16[34,16,128]{2,1,0:T(8,128)(2,1)S(1)}, u32[]{:S(2)}, u32[]{:S(2)}) collective-permute-start(bf16[34,16,128]{2,1,0:T(8,128)(2,1)S(1)} %shard_map.287), channel_id=1, source_target_pairs={{0,8},{1,0},{2,24},{3,16},{4,12},{5,4},{6,28},{7,20},{8,9},{9,1},{... | collective-permute-start | bytes 417800 | tf_op jit(solution)/shard_map/ppermute | solution.py:900
  122.5 3.9 %collective-permute-start.24 = (bf16[34,16,128]{2,1,0:T(8,128)(2,1)S(1)}, bf16[34,16,128]{2,1,0:T(8,128)(2,1)S(1)}, u32[]{:S(2)}, u32[]{:S(2)}) collective-permute-start(bf16[34,16,128]{2,1,0:T(8,128)(2,1)S(1)} %shard_map.287), channel_id=1, source_target_pairs={{0,0},{1,8},{2,16},{3,24},{4,4},{5,12},{6,20},{7,28},{8,1},{9,9},{... | collective-permute-start | bytes 417800 | tf_op jit(solution)/shard_map/ppermute | solution.py:900
  126.5 0.4 collective-permute-done.27.refs_3_
  126.9 1.1 collective-permute-start.31
  128.0 2.4 %collective-permute-done.26.refs_2_ = bf16[34,16,128]{2,1,0:T(8,128)(2,1)S(1)} collective-permute-done((bf16[34,16,128]{2,1,0:T(8,128)(2,1)S(1)}, bf16[34,16,128]{2,1,0:T(8,128)(2,1)S(1)}, u32[]{:S(2)}, u32[]{:S(2)}) %collective-permute-start.26) | collective-permute-done | bytes 139296 | tf_op jit(solution)/shard_map/ppermute | solution.py:900
  130.4 0.7 collective-permute-start.30
  131.1 0.6 collective-permute-done.25.refs_1_
  131.7 2.3 %collective-permute-start.29 = (bf16[34,16,128]{2,1,0:T(8,128)(2,1)S(1)}, bf16[34,16,128]{2,1,0:T(8,128)(2,1)S(1)}, u32[]{:S(2)}, u32[]{:S(2)}) collective-permute-start(bf16[34,16,128]{2,1,0:T(8,128)(2,1)S(1)} %collective-permute-done.25.refs_1_), channel_id=1, source_target_pairs={{0,4},{4,0},{8,12},{12,8},{16,20},{20,16},{24,28},{28,24},{1,5},{5... | collective-permute-start | bytes 417800 | tf_op jit(solution)/shard_map/ppermute | solution.py:913
  134.0 2.5 %collective-permute-done.24.refs_0_ = bf16[34,16,128]{2,1,0:T(8,128)(2,1)S(1)} collective-permute-done((bf16[34,16,128]{2,1,0:T(8,128)(2,1)S(1)}, bf16[34,16,128]{2,1,0:T(8,128)(2,1)S(1)}, u32[]{:S(2)}, u32[]{:S(2)}) %collective-permute-start.24) | collective-permute-done | bytes 139296 | tf_op jit(solution)/shard_map/ppermute | solution.py:900
  136.5 3.5 %shard_map.288 = (f32[3,4,9,32,128]{4,3,2,1,0:T(8,128)}, f32[3,20,128]{2,1,0:T(8,128)S(1)}, f32[3,20]{1,0:T(4,128)S(1)}, f32[5,3,32]{2,1,0:T(4,128)S(1)}, f32[32...) custom-call(s32[6]{0:T(128)S(1)} %copy-done.1, ...), custom_call_target="tpu_custom_call" | custom-call | flops 1000000 | bytes 10000 | tf_op jit(solution)/shard_map/pallas_call | solution.py:853
  140.0 1.3 shard_map.289
  141.3 1.3 shard_map.290
  142.7 2.3 %shard_map.291 = (f32[3,4,9,32,128]{4,3,2,1,0:T(8,128)}, f32[3,20,128]{2,1,0:T(8,128)}, f32[3,20]{1,0:T(4,128)}, f32[5,3,32]{2,1,0:T(4,128)}, f32[32,128]{1,0:T(...) custom-call(s32[6]{0:T(128)S(1)} %copy-done.1, ...), custom_call_target="tpu_custom_call", output_to_operand_aliasing={{0}: (5, {})} | custom-call | flops 1000000 | bytes 10000 | tf_op jit(solution)/shard_map/pallas_call | solution.py:853
  (33 shorter events, 0.2 us)
Async XLA Ops:
  1.8 6.8 %collective-permute-start.1 = (bf16[3,4,9,32,128]{4,3,2,1,0:T(8,128)(2,1)}, bf16[3,4,9,32,128]{4,3,2,1,0:T(8,128)(2,1)S(1)}, u32[]{:S(2)}, u32[]{:S(2)}) collective-permute-start(bf16[3,4,9,32,128]{4,3,2,1,0:T(8,128)(2,1)} %mine.3), channel_id=1, source_target_pairs={{0,1},{1,0},{2,3},{3,2},{4,5},{5,4},{6,7},{7,6},{8,9},{9,8},{10,11... | collective-permute-start | bytes 2654216 | tf_op jit(solution)/shard_map/ppermute | solution.py:882
  1.9 10.5 %collective-permute-start.2 = (bf16[32,2560]{1,0:T(8,128)(2,1)S(1)}, bf16[32,2560]{1,0:T(8,128)(2,1)S(1)}, u32[]{:S(2)}, u32[]{:S(2)}) collective-permute-start(bf16[32,2560]{1,0:T(8,128)(2,1)S(1)} %get-tuple-element.130.u0), channel_id=1, source_target_pairs={{0,1},{1,0},{2,3},{3,2},{4,5},{5,4},{6,7},{7,6},{8,9},{9,8},{10,11... | collective-permute-start | bytes 491528 | tf_op jit(solution)/shard_map/ppermute | solution.py:882
  2.4 6.2 %collective-permute-start = (bf16[32,2560]{1,0:T(8,128)(2,1)S(1)}, bf16[32,2560]{1,0:T(8,128)(2,1)S(1)}, u32[]{:S(2)}, u32[]{:S(2)}) collective-permute-start(bf16[32,2560]{1,0:T(8,128)(2,1)S(1)} %get-tuple-element.131), channel_id=1, source_target_pairs={{0,2},{1,3},{2,0},{3,1},{4,6},{5,7},{6,4},{7,5},{8,10},{9,11},{10,... | collective-permute-start | bytes 491528 | tf_op jit(solution)/shard_map/ppermute | solution.py:876
  3.7 8.8 %copy-start.1 = (s32[6]{0:T(128)S(1)}, s32[6]{0:T(128)}, u32[]{:S(2)}) copy-start(s32[6]{0:T(128)} %stack.23.meta) | copy-start | bytes 76
  3.7 23.4 %copy-start = (bf16[3,4,9,32,128]{4,3,2,1,0:T(8,128)(2,1)S(1)}, bf16[3,4,9,32,128]{4,3,2,1,0:T(8,128)(2,1)}, u32[]{:S(2)}) copy-start(bf16[3,4,9,32,128]{4,3,2,1,0:T(8,128)(2,1)} %mine.3) | copy-start | bytes 2654212
  8.6 3.8 %collective-permute-start.3 = (bf16[32,2560]{1,0:T(8,128)(2,1)S(1)}, bf16[32,2560]{1,0:T(8,128)(2,1)S(1)}, u32[]{:S(2)}, u32[]{:S(2)}) collective-permute-start(bf16[32,2560]{1,0:T(8,128)(2,1)S(1)} %collective-permute-done.u1), channel_id=1, source_target_pairs={{0,1},{1,0},{2,3},{3,2},{4,5},{5,4},{6,7},{7,6},{8,9},{9,8},{10,11... | collective-permute-start | bytes 491528 | tf_op jit(solution)/shard_map/ppermute | solution.py:882
  8.6 5.4 %collective-permute-start.4 = (bf16[17,32,128]{2,1,0:T(8,128)(2,1)S(1)}, bf16[17,32,128]{2,1,0:T(8,128)(2,1)S(1)}, u32[]{:S(2)}, u32[]{:S(2)}) collective-permute-start(bf16[17,32,128]{2,1,0:T(8,128)(2,1)S(1)} %get-tuple-element.138.k0), channel_id=1, source_target_pairs={{1,0},{3,2},{5,4},{7,6},{9,8},{11,10},{13,12},{15,14},{17,16},{19,... | collective-permute-start | bytes 417800 | tf_op jit(solution)/shard_map/ppermute | solution.py:882
  9.9 16.4 %collective-permute-start.5 = (bf16[18,32,128]{2,1,0:T(8,128)(2,1)S(1)}, bf16[18,32,128]{2,1,0:T(8,128)(2,1)S(1)}, u32[]{:S(2)}, u32[]{:S(2)}) collective-permute-start(bf16[18,32,128]{2,1,0:T(8,128)(2,1)S(1)} %get-tuple-element.144), channel_id=1, source_target_pairs={{0,2},{1,3},{2,0},{3,1},{4,6},{5,7},{6,4},{7,5},{8,10},{9,11},{10,... | collective-permute-start | bytes 442376 | tf_op jit(solution)/shard_map/ppermute | solution.py:876
  10.3 16.1 %collective-permute-start.6 = (bf16[18,32,128]{2,1,0:T(8,128)(2,1)S(1)}, bf16[18,32,128]{2,1,0:T(8,128)(2,1)S(1)}, u32[]{:S(2)}, u32[]{:S(2)}) collective-permute-start(bf16[18,32,128]{2,1,0:T(8,128)(2,1)S(1)} %get-tuple-element.146), channel_id=1, source_target_pairs={{0,3},{1,2},{2,1},{3,0},{4,7},{5,6},{6,5},{7,4},{8,11},{9,10},{10,... | collective-permute-start | bytes 442376 | tf_op jit(solution)/shard_map/ppermute | solution.py:879
  26.4 12.8 %collective-permute-start.8 = (bf16[35,32,128]{2,1,0:T(8,128)(2,1)S(1)}, bf16[35,32,128]{2,1,0:T(8,128)(2,1)S(1)}, u32[]{:S(2)}, u32[]{:S(2)}) collective-permute-start(bf16[35,32,128]{2,1,0:T(8,128)(2,1)S(1)} %get-tuple-element.155), channel_id=1, source_target_pairs={{0,3},{1,2},{2,1},{3,0},{4,7},{5,6},{6,5},{7,4},{8,11},{9,10},{10,... | collective-permute-start | bytes 860168 | tf_op jit(solution)/shard_map/ppermute | solution.py:879
  26.4 13.8 %collective-permute-start.7 = (bf16[35,32,128]{2,1,0:T(8,128)(2,1)S(1)}, bf16[35,32,128]{2,1,0:T(8,128)(2,1)S(1)}, u32[]{:S(2)}, u32[]{:S(2)}) collective-permute-start(bf16[35,32,128]{2,1,0:T(8,128)(2,1)S(1)} %get-tuple-element.153), channel_id=1, source_target_pairs={{0,2},{1,3},{2,0},{3,1},{4,6},{5,7},{6,4},{7,5},{8,10},{9,11},{10,... | collective-permute-start | bytes 860168 | tf_op jit(solution)/shard_map/ppermute | solution.py:876
  55.7 11.4 %collective-permute-start.9 = (bf16[32,1664]{1,0:T(8,128)(2,1)S(1)}, bf16[32,1664]{1,0:T(8,128)(2,1)S(1)}, u32[]{:S(2)}, u32[]{:S(2)}) collective-permute-start(bf16[32,1664]{1,0:T(8,128)(2,1)S(1)} %get-tuple-element.172), channel_id=1, source_target_pairs={{0,1},{1,0},{2,3},{3,2},{4,5},{5,4},{6,7},{7,6},{8,9},{9,8},{10,11... | collective-permute-start | bytes 319496 | tf_op jit(solution)/shard_map/ppermute | solution.py:882
  55.8 11.4 %collective-permute-start.10 = (bf16[32,1664]{1,0:T(8,128)(2,1)S(1)}, bf16[32,1664]{1,0:T(8,128)(2,1)S(1)}, u32[]{:S(2)}, u32[]{:S(2)}) collective-permute-start(bf16[32,1664]{1,0:T(8,128)(2,1)S(1)} %get-tuple-element.173), channel_id=1, source_target_pairs={{0,2},{1,3},{2,0},{3,1},{4,6},{5,7},{6,4},{7,5},{8,10},{9,11},{10,... | collective-permute-start | bytes 319496 | tf_op jit(solution)/shard_map/ppermute | solution.py:876
  58.0 9.1 %collective-permute-start.11 = (bf16[32,1664]{1,0:T(8,128)(2,1)S(1)}, bf16[32,1664]{1,0:T(8,128)(2,1)S(1)}, u32[]{:S(2)}, u32[]{:S(2)}) collective-permute-start(bf16[32,1664]{1,0:T(8,128)(2,1)S(1)} %get-tuple-element.174), channel_id=1, source_target_pairs={{0,3},{1,2},{2,1},{3,0},{4,7},{5,6},{6,5},{7,4},{8,11},{9,10},{10,... | collective-permute-start | bytes 319496 | tf_op jit(solution)/shard_map/ppermute | solution.py:879
  70.8 9.8 %collective-permute-start.12 = (bf16[4,21,16,128]{3,2,1,0:T(8,128)(2,1)S(1)}, bf16[4,21,16,128]{3,2,1,0:T(8,128)(2,1)S(1)}, u32[]{:S(2)}, u32[]{:S(2)}) collective-permute-start(bf16[4,21,16,128]{3,2,1,0:T(8,128)(2,1)S(1)} %get-tuple-element.181), channel_id=1, source_target_pairs={{0,4},{4,0},{8,12},{12,8},{16,20},{20,16},{24,28},{28,24},{1,5},{5... | collective-permute-start | bytes 1032200 | tf_op jit(solution)/shard_map/ppermute | solution.py:913
  84.2 5.9 %collective-permute-start.13 = (bf16[1920,128]{1,0:T(8,128)(2,1)S(1)}, bf16[1920,128]{1,0:T(8,128)(2,1)S(1)}, u32[]{:S(2)}, u32[]{:S(2)}) collective-permute-start(bf16[1920,128]{1,0:T(8,128)(2,1)S(1)} %get-tuple-element.187.d0), channel_id=1, source_target_pairs={{0,1},{1,0},{2,3},{3,2},{4,5},{5,4},{6,7},{7,6},{8,9},{9,8},{10,11... | collective-permute-start | bytes 1474568 | tf_op jit(solution)/shard_map/ppermute | solution.py:882
  84.3 15.2 %collective-permute-start.15 = (bf16[4,18,16,128]{3,2,1,0:T(8,128)(2,1)S(1)}, bf16[4,18,16,128]{3,2,1,0:T(8,128)(2,1)S(1)}, u32[]{:S(2)}, u32[]{:S(2)}) collective-permute-start(bf16[4,18,16,128]{3,2,1,0:T(8,128)(2,1)S(1)} %get-tuple-element.194), channel_id=1, source_target_pairs={{0,4},{4,0},{8,12},{12,8},{16,20},{20,16},{24,28},{28,24},{1,5},{5... | collective-permute-start | bytes 884744 | tf_op jit(solution)/shard_map/ppermute | solution.py:913
  84.9 2.2 %collective-permute-start.14 = (f32[8,8,128]{2,1,0:T(8,128)S(1)}, f32[8,8,128]{2,1,0:T(8,128)S(1)}, u32[]{:S(2)}, u32[]{:S(2)}) collective-permute-start(f32[8,8,128]{2,1,0:T(8,128)S(1)} %get-tuple-element.188), channel_id=1, source_target_pairs={{0,1},{1,0},{2,3},{3,2},{4,5},{5,4},{6,7},{7,6},{8,9},{9,8},{10,11... | collective-permute-start | bytes 98312 | tf_op jit(solution)/shard_map/ppermute | solution.py:882
  85.7 13.8 %collective-permute-start.16 = (bf16[21,16,128]{2,1,0:T(8,128)(2,1)S(1)}, bf16[21,16,128]{2,1,0:T(8,128)(2,1)S(1)}, u32[]{:S(2)}, u32[]{:S(2)}) collective-permute-start(bf16[21,16,128]{2,1,0:T(8,128)(2,1)S(1)} %get-tuple-element.195), channel_id=1, source_target_pairs={{0,8},{4,12},{8,0},{12,4},{16,24},{20,28},{24,16},{28,20},{1,9},{5... | collective-permute-start | bytes 258056 | tf_op jit(solution)/shard_map/ppermute | solution.py:919
  86.4 13.0 %collective-permute-start.17 = (bf16[21,16,128]{2,1,0:T(8,128)(2,1)S(1)}, bf16[21,16,128]{2,1,0:T(8,128)(2,1)S(1)}, u32[]{:S(2)}, u32[]{:S(2)}) collective-permute-start(bf16[21,16,128]{2,1,0:T(8,128)(2,1)S(1)} %get-tuple-element.196), channel_id=1, source_target_pairs={{0,16},{4,20},{8,24},{12,28},{16,0},{20,4},{24,8},{28,12},{1,17},{... | collective-permute-start | bytes 258056 | tf_op jit(solution)/shard_map/ppermute | solution.py:919
  87.1 12.4 %collective-permute-start.18 = (bf16[21,16,128]{2,1,0:T(8,128)(2,1)S(1)}, bf16[21,16,128]{2,1,0:T(8,128)(2,1)S(1)}, u32[]{:S(2)}, u32[]{:S(2)}) collective-permute-start(bf16[21,16,128]{2,1,0:T(8,128)(2,1)S(1)} %get-tuple-element.197), channel_id=1, source_target_pairs={{0,24},{4,28},{8,16},{12,20},{16,8},{20,12},{24,0},{28,4},{1,25},{... | collective-permute-start | bytes 258056 | tf_op jit(solution)/shard_map/ppermute | solution.py:919
  102.4 14.5 %collective-permute-start.23 = (bf16[35,16,128]{2,1,0:T(8,128)(2,1)S(1)}, bf16[35,16,128]{2,1,0:T(8,128)(2,1)S(1)}, u32[]{:S(2)}, u32[]{:S(2)}) collective-permute-start(bf16[35,16,128]{2,1,0:T(8,128)(2,1)S(1)} %get-tuple-element.216), channel_id=1, source_target_pairs={{0,2},{1,3},{2,0},{3,1},{4,6},{5,7},{6,4},{7,5},{8,10},{9,11},{10,... | collective-permute-start | bytes 430088 | tf_op jit(solution)/shard_map/ppermute | solution.py:876
  104.1 4.1 %collective-permute-start.19 = (bf16[4,3,16,128]{3,2,1,0:T(8,128)(2,1)S(1)}, bf16[4,3,16,128]{3,2,1,0:T(8,128)(2,1)S(1)}, u32[]{:S(2)}, u32[]{:S(2)}) collective-permute-start(bf16[4,3,16,128]{3,2,1,0:T(8,128)(2,1)S(1)} %get-tuple-element.210), channel_id=1, source_target_pairs={{0,4},{4,0},{8,12},{12,8},{16,20},{20,16},{24,28},{28,24},{1,5},{5... | collective-permute-start | bytes 147464 | tf_op jit(solution)/shard_map/ppermute | solution.py:913
  108.8 4.6 %collective-permute-start.20 = (bf16[21,16,128]{2,1,0:T(8,128)(2,1)S(1)}, bf16[21,16,128]{2,1,0:T(8,128)(2,1)S(1)}, u32[]{:S(2)}, u32[]{:S(2)}) collective-permute-start(bf16[21,16,128]{2,1,0:T(8,128)(2,1)S(1)} %get-tuple-element.212), channel_id=1, source_target_pairs={{0,8},{4,12},{8,0},{12,4},{16,24},{20,28},{24,16},{28,20},{1,9},{5... | collective-permute-start | bytes 258056 | tf_op jit(solution)/shard_map/ppermute | solution.py:919
  109.3 5.4 %collective-permute-start.21 = (bf16[21,16,128]{2,1,0:T(8,128)(2,1)S(1)}, bf16[21,16,128]{2,1,0:T(8,128)(2,1)S(1)}, u32[]{:S(2)}, u32[]{:S(2)}) collective-permute-start(bf16[21,16,128]{2,1,0:T(8,128)(2,1)S(1)} %get-tuple-element.213), channel_id=1, source_target_pairs={{0,16},{4,20},{8,24},{12,28},{16,0},{20,4},{24,8},{28,12},{1,17},{... | collective-permute-start | bytes 258056 | tf_op jit(solution)/shard_map/ppermute | solution.py:919
  110.2 6.7 %collective-permute-start.22 = (bf16[21,16,128]{2,1,0:T(8,128)(2,1)S(1)}, bf16[21,16,128]{2,1,0:T(8,128)(2,1)S(1)}, u32[]{:S(2)}, u32[]{:S(2)}) collective-permute-start(bf16[21,16,128]{2,1,0:T(8,128)(2,1)S(1)} %get-tuple-element.214), channel_id=1, source_target_pairs={{0,24},{4,28},{8,16},{12,20},{16,8},{20,12},{24,0},{28,4},{1,25},{... | collective-permute-start | bytes 258056 | tf_op jit(solution)/shard_map/ppermute | solution.py:919
  117.5 9.4 %collective-permute-start.27 = (bf16[34,16,128]{2,1,0:T(8,128)(2,1)S(1)}, bf16[34,16,128]{2,1,0:T(8,128)(2,1)S(1)}, u32[]{:S(2)}, u32[]{:S(2)}) collective-permute-start(bf16[34,16,128]{2,1,0:T(8,128)(2,1)S(1)} %shard_map.287), channel_id=1, source_target_pairs={{0,24},{1,16},{2,8},{3,0},{4,28},{5,20},{6,12},{7,4},{8,25},{9,17}... | collective-permute-start | bytes 417800 | tf_op jit(solution)/shard_map/ppermute | solution.py:900
  118.4 12.0 %collective-permute-start.26 = (bf16[34,16,128]{2,1,0:T(8,128)(2,1)S(1)}, bf16[34,16,128]{2,1,0:T(8,128)(2,1)S(1)}, u32[]{:S(2)}, u32[]{:S(2)}) collective-permute-start(bf16[34,16,128]{2,1,0:T(8,128)(2,1)S(1)} %shard_map.287), channel_id=1, source_target_pairs={{0,16},{1,24},{2,0},{3,8},{4,20},{5,28},{6,4},{7,12},{8,17},{9,25}... | collective-permute-start | bytes 417800 | tf_op jit(solution)/shard_map/ppermute | solution.py:900
  120.7 11.0 %collective-permute-start.25 = (bf16[34,16,128]{2,1,0:T(8,128)(2,1)S(1)}, bf16[34,16,128]{2,1,0:T(8,128)(2,1)S(1)}, u32[]{:S(2)}, u32[]{:S(2)}) collective-permute-start(bf16[34,16,128]{2,1,0:T(8,128)(2,1)S(1)} %shard_map.287), channel_id=1, source_target_pairs={{0,8},{1,0},{2,24},{3,16},{4,12},{5,4},{6,28},{7,20},{8,9},{9,1},{... | collective-permute-start | bytes 417800 | tf_op jit(solution)/shard_map/ppermute | solution.py:900
  122.5 14.0 %collective-permute-start.24 = (bf16[34,16,128]{2,1,0:T(8,128)(2,1)S(1)}, bf16[34,16,128]{2,1,0:T(8,128)(2,1)S(1)}, u32[]{:S(2)}, u32[]{:S(2)}) collective-permute-start(bf16[34,16,128]{2,1,0:T(8,128)(2,1)S(1)} %shard_map.287), channel_id=1, source_target_pairs={{0,0},{1,8},{2,16},{3,24},{4,4},{5,12},{6,20},{7,28},{8,1},{9,9},{... | collective-permute-start | bytes 417800 | tf_op jit(solution)/shard_map/ppermute | solution.py:900
  126.9 15.8 %collective-permute-start.31 = (bf16[34,16,128]{2,1,0:T(8,128)(2,1)S(1)}, bf16[34,16,128]{2,1,0:T(8,128)(2,1)S(1)}, u32[]{:S(2)}, u32[]{:S(2)}) collective-permute-start(bf16[34,16,128]{2,1,0:T(8,128)(2,1)S(1)} %collective-permute-done.27.refs_3_), channel_id=1, source_target_pairs={{0,4},{4,0},{8,12},{12,8},{16,20},{20,16},{24,28},{28,24},{1,5},{5... | collective-permute-start | bytes 417800 | tf_op jit(solution)/shard_map/ppermute | solution.py:913
  130.4 12.3 %collective-permute-start.30 = (bf16[34,16,128]{2,1,0:T(8,128)(2,1)S(1)}, bf16[34,16,128]{2,1,0:T(8,128)(2,1)S(1)}, u32[]{:S(2)}, u32[]{:S(2)}) collective-permute-start(bf16[34,16,128]{2,1,0:T(8,128)(2,1)S(1)} %collective-permute-done.26.refs_2_), channel_id=1, source_target_pairs={{0,4},{4,0},{8,12},{12,8},{16,20},{20,16},{24,28},{28,24},{1,5},{5... | collective-permute-start | bytes 417800 | tf_op jit(solution)/shard_map/ppermute | solution.py:913
  131.7 11.0 %collective-permute-start.29 = (bf16[34,16,128]{2,1,0:T(8,128)(2,1)S(1)}, bf16[34,16,128]{2,1,0:T(8,128)(2,1)S(1)}, u32[]{:S(2)}, u32[]{:S(2)}) collective-permute-start(bf16[34,16,128]{2,1,0:T(8,128)(2,1)S(1)} %collective-permute-done.25.refs_1_), channel_id=1, source_target_pairs={{0,4},{4,0},{8,12},{12,8},{16,20},{20,16},{24,28},{28,24},{1,5},{5... | collective-permute-start | bytes 417800 | tf_op jit(solution)/shard_map/ppermute | solution.py:913
  136.5 6.2 %collective-permute-start.28 = (bf16[34,16,128]{2,1,0:T(8,128)(2,1)S(1)}, bf16[34,16,128]{2,1,0:T(8,128)(2,1)S(1)}, u32[]{:S(2)}, u32[]{:S(2)}) collective-permute-start(bf16[34,16,128]{2,1,0:T(8,128)(2,1)S(1)} %collective-permute-done.24.refs_0_), channel_id=1, source_target_pairs={{0,4},{4,0},{8,12},{12,8},{16,20},{20,16},{24,28},{28,24},{1,5},{5... | collective-permute-start | bytes 417800 | tf_op jit(solution)/shard_map/ppermute | solution.py:913

commit v6 on v5

--- a/solution.py
+++ b/solution.py
@@ -26,6 +26,8 @@
 WIDE = PAR + 256
 CLS = CP // 128 + 4
 TAPS = 18
+LOW = (MID + 128) // 128
+SECOND = TAPS + LOW + 4
 SENT = 2 * (CP // 128) + 9
 VMEM = 12 * 2**20
 WHOLE = 56 * 2**20
@@ -280,12 +282,20 @@
 
     @pl.when(meta[1] == 0)
     def _():
-        for s, k, base in zip(slices_of(meta), (k0, k1, k2, k3), (0, TAPS, 0, TAPS)):
+        for s, k, sent in zip(slices_of(meta), (k0, k1, k2, k3), (False, True, False, True)):
             for i in range(pixels):
-                cot[at32(s), 128 * i : 128 * (i + 1)] = k[base + i]
+                if not sent or i < LOW:
+                    cot[at32(s), 128 * i : 128 * (i + 1)] = k[TAPS + i if sent else i]
             for slot in range(2):
                 for i in range(2):
-                    wp[slot, at32(s), 128 * i : 128 * (i + 1)] = k[base + pixels + 2 * slot + i]
+                    at = (TAPS + LOW if sent else pixels) + 2 * slot + i
+                    wp[slot, at32(s), 128 * i : 128 * (i + 1)] = k[at]
+
+    @pl.when((meta[1] == 0) & (meta[0] == 0))
+    def _():
+        for s, k in zip(slices_of(meta)[1::2], (k1, k3)):
+            for i in range(LOW, pixels):
+                cot[at32(s), 128 * i : 128 * (i + 1)] = k[9 + i - LOW]
 
     @pl.when(meta[1] == 1)
     def _():
@@ -468,8 +478,8 @@
     part_out(meta, wg, send)
 
 
-def final_kernel(meta, d0, d1, y, cst, st, sums1, sums2, u0, u1, u2, u3, extra, own, send, gs, gs_send, norm, *scratch):
-    sums, feat, stem, field, flat, dyt, gf, blocks, other = scratch
+def final_kernel(meta, d0, d1, y, cst, st, sums1, sums2, u0, u1, u2, u3, own, other, gs, gs_send, norm, *scratch):
+    sums, feat, stem, field, flat, dyt, gf, blocks = scratch
     load_inputs(meta, (u0, u1, u2, u3), feat, stem)
     grad_sums(meta, jnp.sum(st[...], axis=0), sums)
     for j in range(NCH):
@@ -510,10 +520,6 @@
                 at = pl.ds(pl.multiple_of(128 * s + 32 * i, 32), 32)
                 out[:, 1024 + 128 * i : 1152 + 128 * i] = gf[at, MID : MID + 128]
 
-    for i in range(CP // 128):
-        for h in range(2):
-            send[2 * i + h] = other[16 * h : 16 * (h + 1), 128 * i : 128 * (i + 1)]
-    send[2 * (CP // 128) : 2 * (CP // 128) + 9] = extra[...]
     for i in range(3):
         block = blocks[3 * meta[1] + i]
         for j in range(8):
@@ -538,6 +544,21 @@
             at += n
 
 
+def halve_kernel(meta, kept, got, own, send):
+    for k in range(4):
+        z = meta[4] ^ k
+        total = kept[2 * z + meta[5]].astype(F32) + got[z].astype(F32)
+        if k % 2:
+            send[k // 2] = total.astype(BF)
+        else:
+            own[k // 2] = total
+
+
+def again_kernel(meta, own, got, mine, send):
+    mine[...] = own[0] + got[0].astype(F32)
+    send[...] = (own[1] + got[1].astype(F32)).astype(BF)
+
+
 def summed(refs, begin, end):
     total = refs[0][begin:end].astype(F32)
     for r in refs[1:]:
@@ -546,22 +567,21 @@
 
 
 def sum_kernel(meta, *refs):
-    parts, (total, extra) = refs[:4], refs[4:]
+    parts, (total, extra) = refs[:-2], refs[-2:]
     total[0:9] = summed(parts, 0, 9)
     total[9:12] = summed(parts, 18, 21)
     extra[...] = summed(parts, 9, 18)
 
 
 def join_kernel(meta, *refs):
-    parts, (total, received, norm, out) = refs[:4], refs[4:]
+    parts, (total, extra, norm, out) = refs[:4], refs[4:]
     out[0:9] = summed(parts, 0, 9)
     out[9:18] = total[0:9]
     out[27:30] = total[9:12]
 
     @pl.when(meta[0] == 0)
     def _():
-        at = 2 * (CP // 128)
-        out[18:27] = received[at : at + 9]
+        out[18:27] = extra[...]
 
     @pl.when(meta[0] == 1)
     def _():
@@ -721,11 +741,7 @@
                     store(out, pair[group], pair[1 - group])
 
 
-def feature_out_kernel(meta, own, received, fine, mid, coarse, other):
-    for i in range(CP // 128):
-        for h in range(2):
-            other[16 * h : 16 * (h + 1), 128 * i : 128 * (i + 1)] = received[2 * i + h]
-
+def feature_out_kernel(meta, own, received, fine, mid, coarse):
     def store(a, b):
         n1, n2 = mid.shape[1], coarse.shape[0]
         fine[...] = a[:, 0 : fine.shape[1]]
@@ -736,11 +752,11 @@
 
     @pl.when(meta[0] == 0)
     def _():
-        store(own, other)
+        store(own, received)
 
     @pl.when(meta[0] == 1)
     def _():
-        store(other, own)
+        store(received, own)
 
 
 def pack_kernel(f0, f1, f2, s0, s1, s2, gains, shifts, box, own, send, small):
@@ -786,14 +802,15 @@
             out[:, PAR + 128 * i : PAR + 128 * (i + 1)] = block
 
 
-def pred_kernel(sizes, meta, ccot, cw, cb, bcot, bb, conv, own, box, first, first_cross, second, second_cross, room, sems):
+def pred_kernel(sizes, meta, ccot, cw, cb, bcot, bb, conv, own, box, first, first_cross, second, second_cross, room, spare, sems):
     n0, n1, n2 = sizes
     copies = []
     for layer, outs in enumerate(((first, first_cross), (second, second_cross))):
         for i, out in enumerate(outs):
             for slot in range(2):
                 taken = conv.at[1 - meta[0] + slot, 2 * (meta[1] ^ i) + layer]
-                copy = pltpu.make_async_copy(taken, out.at[pl.ds(9 * slot, 9)], sems.at[layer, i, slot])
+                to = spare.at[i] if layer == 1 and slot == 1 else out.at[pl.ds(9 * slot, 9)]
+                copy = pltpu.make_async_copy(taken, to, sems.at[layer, i, slot])
                 copy.start()
                 copies.append(copy)
     lane = lax.broadcasted_iota(jnp.int32, (32, 128), 1)
@@ -808,7 +825,7 @@
         v = jnp.where(lane == 0, high, jnp.where(lane == 1, mid, jnp.where(lane == 2, low, 0.0)))
         return v.astype(BF)
 
-    def fill(out, base, cot, b, fine, weights):
+    def fill(outs, cot, b, fine, weights, sent=False):
         n = cot.shape[0]
         room[...] = jnp.zeros((32, CP), BF)
         if fine:
@@ -816,30 +833,44 @@
         else:
             room[0:n, 0:n1] = cot[:, n0 : n0 + n1]
             room[0:n, MID : MID + n2] = cot[:, n0 + n1 : n0 + n1 + n2]
-        for i in range(CP // 128):
-            out[base + i] = room[:, 128 * i : 128 * (i + 1)]
-        for slot in range(2):
-            level = 0 if fine else 1 + slot
-            at = base + CP // 128 + 2 * slot
-            out[at] = jnp.zeros((32, 128), BF)
-            if weights:
-                out[at, 0:n] = cw[level]
-            out[at + 1] = biases(b, level)
+        base = CP // 128
+        if sent:
+            base = TAPS + LOW
+        for out in outs:
+            for i in range(CP // 128 if fine else LOW):
+                at = i
+                if sent:
+                    at = TAPS + i if i < LOW else 9 + i - LOW
+                out[at] = room[:, 128 * i : 128 * (i + 1)]
+            if not fine and not sent:
+                out[LOW : CP // 128] = jnp.zeros((CP // 128 - LOW, 32, 128), BF)
+            if fine and sent:
+                out[9 + CP // 128 - LOW] = jnp.zeros((32, 128), BF)
+            for slot in range(2):
+                level = 0 if fine else 1 + slot
+                out[base + 2 * slot] = jnp.zeros((32, 128), BF)
+                if weights:
+                    out[base + 2 * slot, 0:n] = cw[level]
+                out[base + 2 * slot + 1] = biases(b, level)
 
     for group in range(2):
 
         @pl.when(meta[0] == group)
         def _():
-            fill(own, 0, ccot, cb, group == 0, True)
-            fill(box, 0, bcot, bb, group == 0, False)
+            fill([own], ccot, cb, group == 0, True)
+            fill([box], bcot, bb, group == 0, False)
 
         @pl.when(meta[0] != group)
         def _():
-            fill(second, TAPS, ccot, cb, group == 0, True)
-            second_cross[TAPS:] = second[TAPS:]
+            fill([second, second_cross], ccot, cb, group == 0, True, True)
 
     for copy in copies:
         copy.wait()
+
+    @pl.when(meta[0] == 0)
+    def _():
+        second[9:18] = spare[0]
+        second_cross[9:18] = spare[1]
 
 
 def call(body, outs, scratch, args, last=False, limit=VMEM, in_place=(), aliases={}, flops=10**6):
@@ -931,8 +962,8 @@
     far_u = across(send)
     own_pred, box_pred, send1, send1_cross, send2, send2_cross = call(
         functools.partial(pred_kernel, (n0, n1, n2)),
-        [((CLS, 32, 128), BF)] * 2 + [((TAPS, 32, 128), BF)] * 2 + [((TAPS + CLS, 32, 128), BF)] * 2,
-        [((32, CP), BF), pltpu.SemaphoreType.DMA((2, 2, 2))],
+        [((CLS, 32, 128), BF)] * 2 + [((TAPS, 32, 128), BF)] * 2 + [((SECOND, 32, 128), BF)] * 2,
+        [((32, CP), BF), ((2, 9, 32, 128), BF), pltpu.SemaphoreType.DMA((2, 2, 2))],
         (meta, ccot[0], cw, cb, bcot[0], after(bb, own), conv),
         limit=WHOLE,
         in_place=(6,),
@@ -1006,17 +1037,19 @@
     d0_other, st_other = beside(d0), beside(st)
     st = st + st_other
     if direct:
-        parts2 = along_z([wg2], [after(got2, d0)])
-        st = after(st, d0_other, *parts2[:1])
-        (st,) = call(total_kernel, [((1, 8, 128), F32)], [], (exchange(st),))
-        st, got1, *parts2 = lax.optimization_barrier((st, got1, *parts2))
-        total, extra = call(sum_kernel, [((12, 16, 128), BF), ((9, 16, 128), BF)], [], (meta, *parts2))
+        pair = (2, 21, 16, 128)
+        own2, send2 = call(halve_kernel, [(pair, F32), (pair, BF)], [], (meta, wg2, after(got2, d0)))
+        got2 = lax.ppermute(send2, "dp", [(i, i ^ 2) for i in range(8)])
+        st = exchange(after(st, d0_other, own2))
+        (st,) = call(total_kernel, [((1, 8, 128), F32)], [], (st,))
+        st, got1, got2 = lax.optimization_barrier((st, got1, got2))
+        own2, send2 = call(again_kernel, [(pair[1:], F32), (pair[1:], BF)], [], (meta, own2, got2))
+        got2 = lax.ppermute(send2, "dp", [(i, i ^ 4) for i in range(8)])
     else:
         st = exchange(st)
-        extra = jnp.zeros((9, 16, 128), BF)
-    own, send, gs, gs_send, norm = call(
+    own, other, gs, gs_send, norm = call(
         final_kernel,
-        [((32, CP), BF), ((SENT, 16, 128), BF), ((8, 3, 16, 128), BF), ((4, 3, 16, 128), BF), ((1, 16, 128), BF)],
+        [((32, CP), BF), ((32, CP), BF), ((8, 3, 16, 128), BF), ((4, 3, 16, 128), BF), ((1, 16, 128), BF)],
         [
             ((8, 128), F32),
             ((512, CP), BF),
@@ -1026,14 +1059,18 @@
             ((128, CP), BF),
             ((512, CP), BF),
             ((6, 128, 128), BF),
-            ((32, CP), BF),
         ],
-        (meta, d0, d0_other, y0, cst0, st, sums1, sums2, *u, extra),
-    )
-    received = across(send)
+        (meta, d0, d0_other, y0, cst0, st, sums1, sums2, *u),
+    )
+    received = across(other)
     if direct:
         parts1 = along_z([wg1, gs], [got1, over_y(gs_send)])
-        (grads,) = call(join_kernel, [((34, 16, 128), BF)], [], (meta, *parts1, total, received, norm))
+        total, extra = call(
+            sum_kernel, [((12, 16, 128), BF), ((9, 16, 128), BF)], [], (meta, own2, after(got2, parts1[0]))
+        )
+        extra = lax.ppermute(extra, "chan", [(2, 0), (3, 1)])
+        extra, received = lax.optimization_barrier((extra, received))
+        (grads,) = call(join_kernel, [((34, 16, 128), BF)], [], (meta, *parts1, total, extra, norm))
     else:
         extra = lax.ppermute(got2[:, 9:18], "chan", [(2, 0), (3, 1)])
         third = jnp.where(fine, extra, got1[:, 9:18])
@@ -1059,7 +1096,7 @@
     grad_fine, grad_mid, grad_coarse = call(
         feature_out_kernel,
         [(f0.shape[1:], BF), (f1.shape[1:], BF), ((n2, f2.shape[1]), BF)],
-        [((32, CP), BF)],
+        [],
         (meta, own, received),
         True,
     )

time: 147 us -> 145 us (0.986)
  waiting for transfers between devices: 16.9 us -> 15.1 us
    ppermute x0 -> x3, starting transfers between devices: none -> 5.18 us  [the longest x1 3.84 us: shards(): extra = lax.ppermute(extra, 'chan', [(2, 0), (3, 1)])]
    ppermute x6 -> x3, starting transfers between devices: 8.9 us -> 4.45 us  [along_z(): lax.ppermute(v, 'dp', [(i, i ^ 2 * k + 2) for i in range(8)])]
    ppermute x6 -> x3, waiting for transfers between devices: 3.59 us -> 0.01 us  [along_z(): lax.ppermute(v, 'dp', [(i, i ^ 2 * k + 2) for i in range(8)])]
    ppermute x7, waiting for transfers between devices: 3.63 us -> 1.03 us  [over_y(): return lax.ppermute(v, 'dp', [(i, i ^ 1) for i in range(8)])]
    ppermute x4, waiting for transfers between devices: 5.96 us -> 8.15 us  [over_z(): parts.append(lax.ppermute(v, ('dp', 'chan'), pairs))]
    ppermute x0 -> x3, waiting for transfers between devices: none -> 1.99 us  [the longest x1 1.61 us: shards(): extra = lax.ppermute(extra, 'chan', [(2, 0), (3, 1)])]
    ppermute x4, starting transfers between devices: 9 us -> 7.09 us  [over_z(): parts.append(lax.ppermute(v, ('dp', 'chan'), pairs))]
    ppermute x7, starting transfers between devices: 5.62 us -> 7.14 us  [over_y(): return lax.ppermute(v, 'dp', [(i, i ^ 1) for i in range(8)])]
  transfers between devices with their start and end apart: 32 -> 32, of which waited for: 10 -> 8; matrix products, arithmetic and copies ran while one was open for 0% -> 0% of each run, Pallas kernels for 10% -> 11%
where the time goes in v6:
time: 145 us; the launch traced here: 144 us
  blocking collectives  58.9 us (41%)
  Pallas kernels  35.3 us (24%)
  starting transfers between devices  32.5 us (22%)
  waiting for transfers between devices  15.1 us (10%)
  between operations  1.7 us (1%)
    all_to_all x6, blocking collectives, exchange(): st = lax.all_to_all(st, 'dp', 0, 0, tiled=True)  58.9 us
    pallas_call x22, Pallas kernels, call(): pl.pallas_call(body, out_shape=[place(s, d) for s, d in outs], in_specs=[...  35.3 us
    ppermute x4, waiting for transfers between devices, over_z(): parts.append(lax.ppermute(v, ('dp', 'chan'), pairs))  8.15 us
    ppermute x7, starting transfers between devices, over_y(): return lax.ppermute(v, 'dp', [(i, i ^ 1) for i in range(8)])  7.14 us
    ppermute x4, starting transfers between devices, over_z(): parts.append(lax.ppermute(v, ('dp', 'chan'), pairs))  7.09 us
    ppermute x3, starting transfers between devices, along_z(): lax.ppermute(v, 'dp', [(i, i ^ 2 * k + 2) for i in range(8)])  4.45 us
    ppermute x5, starting transfers between devices, across(): return lax.ppermute(v, 'chan', [(i, i ^ 2) for i in range(4)])  4.07 us
    ppermute x1, starting transfers between devices, shards(): extra = lax.ppermute(extra, 'chan', [(2, 0), (3, 1)])  3.84 us
  transfers between devices with their start and end apart: 32, of which 8 were waited for; matrix products, arithmetic and copies ran while one was open for 0% of the time, Pallas kernels for 11%

profile of v6, /device:TPU:2, one launch (start us, length us, event | category | flops | bytes accessed | tf_op | source)
XLA Modules:
  0.0 144.1 jit_solution(7928775088180501275)
XLA Ops:
  0.6 1.2 shard_map.271
  1.8 0.1 collective-permute-start.1
  1.9 0.5 collective-permute-start.2
  2.4 0.0 collective-permute-start
  3.1 0.6 stack.23.meta
  3.7 2.2 %shard_map.272 = (bf16[17,32,128]{2,1,0:T(8,128)(2,1)S(1)}, bf16[17,32,128]{2,1,0:T(8,128)(2,1)S(1)}, bf16[18,32,128]{2,1,0:T(8,128)(2,1)S(1)}, bf16[18,32,128]{...) custom-call(s32[6]{0:T(128)} %stack.23.meta, bf16[20,2100]{1,0:T(8,128)(2,1)} %bitcast.32, ...), custom_call_target="tpu_custom_call" | custom-call | flops 2000000000 | bytes 10000 | tf_op jit(solution)/shard_map/pallas_call | solution.py:884
  5.9 2.7 %collective-permute-done.u1 = bf16[32,2560]{1,0:T(8,128)(2,1)S(1)} collective-permute-done((bf16[32,2560]{1,0:T(8,128)(2,1)S(1)}, bf16[32,2560]{1,0:T(8,128)(2,1)S(1)}, u32[]{:S(2)}, u32[]{:S(2)}) %collective-permute-start) | collective-permute-done | bytes 163872 | tf_op jit(solution)/shard_map/ppermute | solution.py:907
  8.6 1.3 collective-permute-start.4
  9.9 0.3 collective-permute-start.5
  10.3 2.2 %collective-permute-start.6 = (bf16[18,32,128]{2,1,0:T(8,128)(2,1)S(1)}, bf16[18,32,128]{2,1,0:T(8,128)(2,1)S(1)}, u32[]{:S(2)}, u32[]{:S(2)}) collective-permute-start(bf16[18,32,128]{2,1,0:T(8,128)(2,1)S(1)} %get-tuple-element.146), channel_id=1, source_target_pairs={{0,3},{1,2},{2,1},{3,0},{4,7},{5,6},{6,5},{7,4},{8,11},{9,10},{10,... | collective-permute-start | bytes 442376 | tf_op jit(solution)/shard_map/ppermute | solution.py:910
  12.5 1.6 %shard_map.273 = (f32[1920,128]{1,0:T(8,128)S(1)}, f32[8,8,128]{2,1,0:T(8,128)S(1)}, f32[8,128]{1,0:T(8,128)S(1)}, f32[64,128]{1,0:T(8,128)S(1)}) custom-call(s32[6]{0:T(128)S(1)} %copy-done.1, bf16[32,2560]{1,0:T(8,128)(2,1)S(1)} %get-tuple-element.130.u0, bf16[32,2560]{1,0:T(8,128)(2,1)S(1)} %collective-permute-done.u1, ...), custom_call_target="tpu_custom_call" | custom-call | flops 1000000 | bytes 10000 | tf_op jit(solution)/shard_map/pallas_call | solution.py:884
  14.0 12.3 %all_to_all.30.st = f32[8,8,128]{2,1,0:T(8,128)S(1)} all-to-all(f32[8,8,128]{2,1,0:T(8,128)S(1)} %get-tuple-element.139), channel_id=1, replica_groups=mesh['dp'=8,'chan'=4] {'dp'}, dimensions={0} | all-to-all | bytes 65536 | tf_op jit(solution)/shard_map/all_to_all | solution.py:917
  26.4 0.7 collective-permute-start.7
  27.1 0.7 shard_map.274
  27.9 2.2 %shard_map.275 = (bf16[1920,128]{1,0:T(8,128)(2,1)S(1)}, f32[1920,128]{1,0:T(8,128)S(1)}, f32[8,8,128]{2,1,0:T(8,128)S(1)}, f32[16,128]{1,0:T(8,128)S(1)}) custom-call(s32[6]{0:T(128)S(1)} %copy-done.1, f32[1920,128]{1,0:T(8,128)S(1)} %get-tuple-element.136.y.y_in, f32[8,8,128]{2,1,0:T(8,128)S(1)} %all_to_all.30.st, f32[8,128]{1,0:T(8,128)S(1)} %get-tuple-element.142.cnt, ...), custom_call_target="tpu_custom_call" | custom-call | flops 1000000 | bytes 10000 | tf_op jit(solution)/shard_map/pallas_call | solution.py:884
  30.0 9.1 %all_to_all.31.st = f32[8,8,128]{2,1,0:T(8,128)S(1)} all-to-all(f32[8,8,128]{2,1,0:T(8,128)S(1)} %get-tuple-element.152), channel_id=1, replica_groups=mesh['dp'=8,'chan'=4] {'dp'}, dimensions={0} | all-to-all | bytes 65536 | tf_op jit(solution)/shard_map/all_to_all | solution.py:917
  39.1 0.7 shard_map.276
  39.9 2.1 %shard_map.277 = (bf16[1920,128]{1,0:T(8,128)(2,1)S(1)}, f32[1920,128]{1,0:T(8,128)S(1)}, f32[8,8,128]{2,1,0:T(8,128)S(1)}, f32[16,128]{1,0:T(8,128)S(1)}) custom-call(s32[6]{0:T(128)S(1)} %copy-done.1, f32[1920,128]{1,0:T(8,128)S(1)} %get-tuple-element.151.y.y_in, f32[8,8,128]{2,1,0:T(8,128)S(1)} %all_to_all.31.st, f32[8,128]{1,0:T(8,128)S(1)} %get-tuple-element.142.cnt, ...), custom_call_target="tpu_custom_call" | custom-call | flops 1000000 | bytes 10000 | tf_op jit(solution)/shard_map/pallas_call | solution.py:884
  42.0 9.1 %all_to_all.32.st = f32[8,8,128]{2,1,0:T(8,128)S(1)} all-to-all(f32[8,8,128]{2,1,0:T(8,128)S(1)} %get-tuple-element.160), channel_id=1, replica_groups=mesh['dp'=8,'chan'=4] {'dp'}, dimensions={0} | all-to-all | bytes 65536 | tf_op jit(solution)/shard_map/all_to_all | solution.py:917
  51.1 2.3 %shard_map.278 = (f32[1920,128]{1,0:T(8,128)S(1)}, f32[8,8,128]{2,1,0:T(8,128)S(1)}, f32[16,128]{1,0:T(8,128)S(1)}, bf16[1664,256]{1,0:T(8,128)(2,1)S(1)}, bf16[...) custom-call(s32[6]{0:T(128)S(1)} %copy-done.1, f32[1920,128]{1,0:T(8,128)S(1)} %get-tuple-element.159.y, ...), custom_call_target="tpu_custom_call" | custom-call | flops 1000000 | bytes 10000 | tf_op jit(solution)/shard_map/pallas_call | solution.py:884
  53.4 1.3 shard_map.279
  54.7 0.1 collective-permute-start.9
  54.8 1.5 %collective-permute-start.10 = (bf16[32,1664]{1,0:T(8,128)(2,1)S(1)}, bf16[32,1664]{1,0:T(8,128)(2,1)S(1)}, u32[]{:S(2)}, u32[]{:S(2)}) collective-permute-start(bf16[32,1664]{1,0:T(8,128)(2,1)S(1)} %get-tuple-element.173), channel_id=1, source_target_pairs={{0,2},{1,3},{2,0},{3,1},{4,6},{5,7},{6,4},{7,5},{8,10},{9,11},{10,... | collective-permute-start | bytes 319496 | tf_op jit(solution)/shard_map/ppermute | solution.py:907
  56.3 0.3 collective-permute-start.11
  56.6 9.0 %all_to_all.33.st = f32[8,8,128]{2,1,0:T(8,128)S(1)} all-to-all(f32[8,8,128]{2,1,0:T(8,128)S(1)} %get-tuple-element.171), channel_id=1, replica_groups=mesh['dp'=8,'chan'=4] {'dp'}, dimensions={0} | all-to-all | bytes 65536 | tf_op jit(solution)/shard_map/all_to_all | solution.py:917
  65.7 3.7 %shard_map.280 = (f32[1920,128]{1,0:T(8,128)S(1)}, f32[8,8,128]{2,1,0:T(8,128)S(1)}, f32[8,128]{1,0:T(8,128)S(1)}, bf16[8,21,16,128]{3,2,1,0:T(8,128)(2,1)S(1)}, bf16[4,21,16,128]{3,2,1,0:T(8,128)(2,1)S(1)}) custom-call(s32[6]{0:T(128)S(1)} %copy-done.1, f32[1920,128]{1,0:T(8,128)S(1)} %get-tuple-element.167.dz, f32[1920,128]{1,0:T(8,128)S(1)} %get-tuple-element.159.y, ...), custom_call_target="tpu_custom_call" | custom-call | flops 1000000 | bytes 10000 | tf_op jit(solution)/shard_map/pallas_call | solution.py:884
  69.4 0.5 collective-permute-start.12
  70.0 9.3 %all_to_all.34.st = f32[8,8,128]{2,1,0:T(8,128)S(1)} all-to-all(f32[8,8,128]{2,1,0:T(8,128)S(1)} %get-tuple-element.182), channel_id=1, replica_groups=mesh['dp'=8,'chan'=4] {'dp'}, dimensions={0} | all-to-all | bytes 65536 | tf_op jit(solution)/shard_map/all_to_all | solution.py:917
  79.3 3.6 %shard_map.281 = (bf16[1920,128]{1,0:T(8,128)(2,1)S(1)}, f32[8,8,128]{2,1,0:T(8,128)S(1)}, f32[8,128]{1,0:T(8,128)S(1)}, bf16[8,18,16,128]{3,2,1,0:T(8,128)(2,1)S(1)}, bf16[4,18,16,128]{3,2,1,0:T(8,128)(2,1)S(1)}) custom-call(s32[6]{0:T(128)S(1)} %copy-done.1, f32[1920,128]{1,0:T(8,128)S(1)} %get-tuple-element.179.dz, ...), custom_call_target="tpu_custom_call" | custom-call | flops 1000000 | bytes 10000 | tf_op jit(solution)/shard_map/pallas_call | solution.py:884
  82.8 0.1 collective-permute-start.13
  82.9 0.6 collective-permute-start.15
  83.5 0.6 shard_map.282
  84.1 0.8 collective-permute-start.16
  84.9 1.2 collective-permute-done.14
  86.1 10.1 %all_to_all.35.st = f32[8,8,128]{2,1,0:T(8,128)S(1)} all-to-all(f32[8,8,128]{2,1,0:T(8,128)S(1)} %add.14), channel_id=1, replica_groups=mesh['dp'=8,'chan'=4] {'dp'}, dimensions={0} | all-to-all | bytes 65536 | tf_op jit(solution)/shard_map/all_to_all | solution.py:917
  96.2 2.3 %shard_map.284 = (bf16[32,1664]{1,0:T(8,128)(2,1)S(1)}, bf16[32,1664]{1,0:T(8,128)(2,1)S(1)}, bf16[8,3,16,128]{3,2,1,0:T(8,128)(2,1)S(1)}, bf16[4,3,16,128]{3,2,1,0:T(8,128)(2,1)S(1)}, bf16[1,16,128]{2,1,0:T(8,128)(2,1)S(1)}) custom-call(s32[6]{0:T(128)S(1)} %copy-done.1, bf16[1920,128]{1,0:T(8,128)(2,1)S(1)} %get-tuple-element.187.d0, ...), custom_call_target="tpu_custom_call" | custom-call | flops 1000000 | bytes 10000 | tf_op jit(solution)/shard_map/pallas_call | solution.py:884
  98.4 0.5 collective-permute-start.17
  99.0 0.6 shard_map.286
  99.6 0.6 collective-permute-start.21
  100.1 1.4 collective-permute-start.23
  101.6 1.0 collective-permute-done.17.refs_3_
  102.6 0.6 shard_map.285
  103.2 0.5 collective-permute-start.18
  103.7 1.7 %collective-permute-start.19 = (bf16[21,16,128]{2,1,0:T(8,128)(2,1)S(1)}, bf16[21,16,128]{2,1,0:T(8,128)(2,1)S(1)}, u32[]{:S(2)}, u32[]{:S(2)}) collective-permute-start(bf16[21,16,128]{2,1,0:T(8,128)(2,1)S(1)} %get-tuple-element.206), channel_id=1, source_target_pairs={{0,16},{4,20},{8,24},{12,28},{16,0},{20,4},{24,8},{28,12},{1,17},{... | collective-permute-start | bytes 258056 | tf_op jit(solution)/shard_map/ppermute | solution.py:950
  105.4 2.3 %collective-permute-start.20 = (bf16[21,16,128]{2,1,0:T(8,128)(2,1)S(1)}, bf16[21,16,128]{2,1,0:T(8,128)(2,1)S(1)}, u32[]{:S(2)}, u32[]{:S(2)}) collective-permute-start(bf16[21,16,128]{2,1,0:T(8,128)(2,1)S(1)} %get-tuple-element.207), channel_id=1, source_target_pairs={{0,24},{4,28},{8,16},{12,20},{16,8},{20,12},{24,0},{28,4},{1,25},{... | collective-permute-start | bytes 258056 | tf_op jit(solution)/shard_map/ppermute | solution.py:950
  107.7 0.4 collective-permute-done.21.refs_1_
  108.1 0.6 shard_map.287
  108.6 3.8 %collective-permute-start.22 = (bf16[9,16,128]{2,1,0:T(8,128)(2,1)S(1)}, bf16[9,16,128]{2,1,0:T(8,128)(2,1)S(1)}, u32[]{:S(2)}, u32[]{:S(2)}) collective-permute-start(bf16[9,16,128]{2,1,0:T(8,128)(2,1)S(1)} %get-tuple-element.213), channel_id=1, source_target_pairs={{2,0},{3,1},{6,4},{7,5},{10,8},{11,9},{14,12},{15,13},{18,16},{19,... | collective-permute-start | bytes 110600 | tf_op jit(solution)/shard_map/ppermute | solution.py:1071
  112.5 1.6 %collective-permute-done.22.refs_5_ = bf16[9,16,128]{2,1,0:T(8,128)(2,1)S(1)} collective-permute-done((bf16[9,16,128]{2,1,0:T(8,128)(2,1)S(1)}, bf16[9,16,128]{2,1,0:T(8,128)(2,1)S(1)}, u32[]{:S(2)}, u32[]{:S(2)}) %collective-permute-start.22) | collective-permute-done | bytes 36896 | tf_op jit(solution)/shard_map/ppermute | solution.py:1071
  114.1 0.6 shard_map.288
  114.7 0.7 collective-permute-start.27
  115.4 1.7 %collective-permute-start.26 = (bf16[34,16,128]{2,1,0:T(8,128)(2,1)S(1)}, bf16[34,16,128]{2,1,0:T(8,128)(2,1)S(1)}, u32[]{:S(2)}, u32[]{:S(2)}) collective-permute-start(bf16[34,16,128]{2,1,0:T(8,128)(2,1)S(1)} %shard_map.288), channel_id=1, source_target_pairs={{0,16},{1,24},{2,0},{3,8},{4,20},{5,28},{6,4},{7,12},{8,17},{9,25}... | collective-permute-start | bytes 417800 | tf_op jit(solution)/shard_map/ppermute | solution.py:931
  117.2 2.6 %collective-permute-start.25 = (bf16[34,16,128]{2,1,0:T(8,128)(2,1)S(1)}, bf16[34,16,128]{2,1,0:T(8,128)(2,1)S(1)}, u32[]{:S(2)}, u32[]{:S(2)}) collective-permute-start(bf16[34,16,128]{2,1,0:T(8,128)(2,1)S(1)} %shard_map.288), channel_id=1, source_target_pairs={{0,8},{1,0},{2,24},{3,16},{4,12},{5,4},{6,28},{7,20},{8,9},{9,1},{... | collective-permute-start | bytes 417800 | tf_op jit(solution)/shard_map/ppermute | solution.py:931
  119.8 2.0 %collective-permute-start.24 = (bf16[34,16,128]{2,1,0:T(8,128)(2,1)S(1)}, bf16[34,16,128]{2,1,0:T(8,128)(2,1)S(1)}, u32[]{:S(2)}, u32[]{:S(2)}) collective-permute-start(bf16[34,16,128]{2,1,0:T(8,128)(2,1)S(1)} %shard_map.288), channel_id=1, source_target_pairs={{0,0},{1,8},{2,16},{3,24},{4,4},{5,12},{6,20},{7,28},{8,1},{9,9},{... | collective-permute-start | bytes 417800 | tf_op jit(solution)/shard_map/ppermute | solution.py:931
  121.8 2.6 %collective-permute-done.27.refs_3_ = bf16[34,16,128]{2,1,0:T(8,128)(2,1)S(1)} collective-permute-done((bf16[34,16,128]{2,1,0:T(8,128)(2,1)S(1)}, bf16[34,16,128]{2,1,0:T(8,128)(2,1)S(1)}, u32[]{:S(2)}, u32[]{:S(2)}) %collective-permute-start.27) | collective-permute-done | bytes 139296 | tf_op jit(solution)/shard_map/ppermute | solution.py:931
  124.4 0.9 collective-permute-start.31
  125.3 1.9 %collective-permute-done.26.refs_2_ = bf16[34,16,128]{2,1,0:T(8,128)(2,1)S(1)} collective-permute-done((bf16[34,16,128]{2,1,0:T(8,128)(2,1)S(1)}, bf16[34,16,128]{2,1,0:T(8,128)(2,1)S(1)}, u32[]{:S(2)}, u32[]{:S(2)}) %collective-permute-start.26) | collective-permute-done | bytes 139296 | tf_op jit(solution)/shard_map/ppermute | solution.py:931
  127.2 3.6 %collective-permute-done.25.refs_1_ = bf16[34,16,128]{2,1,0:T(8,128)(2,1)S(1)} collective-permute-done((bf16[34,16,128]{2,1,0:T(8,128)(2,1)S(1)}, bf16[34,16,128]{2,1,0:T(8,128)(2,1)S(1)}, u32[]{:S(2)}, u32[]{:S(2)}) %collective-permute-start.25) | collective-permute-done | bytes 139296 | tf_op jit(solution)/shard_map/ppermute | solution.py:931
  130.8 2.8 %collective-permute-start.29 = (bf16[34,16,128]{2,1,0:T(8,128)(2,1)S(1)}, bf16[34,16,128]{2,1,0:T(8,128)(2,1)S(1)}, u32[]{:S(2)}, u32[]{:S(2)}) collective-permute-start(bf16[34,16,128]{2,1,0:T(8,128)(2,1)S(1)} %collective-permute-done.25.refs_1_), channel_id=1, source_target_pairs={{0,4},{4,0},{8,12},{12,8},{16,20},{20,16},{24,28},{28,24},{1,5},{5... | collective-permute-start | bytes 417800 | tf_op jit(solution)/shard_map/ppermute | solution.py:944
  133.6 1.8 %collective-permute-start.28 = (bf16[34,16,128]{2,1,0:T(8,128)(2,1)S(1)}, bf16[34,16,128]{2,1,0:T(8,128)(2,1)S(1)}, u32[]{:S(2)}, u32[]{:S(2)}) collective-permute-start(bf16[34,16,128]{2,1,0:T(8,128)(2,1)S(1)} %collective-permute-done.24.refs_0_), channel_id=1, source_target_pairs={{0,4},{4,0},{8,12},{12,8},{16,20},{20,16},{24,28},{28,24},{1,5},{5... | collective-permute-start | bytes 417800 | tf_op jit(solution)/shard_map/ppermute | solution.py:944
  135.5 3.5 %shard_map.289 = (f32[3,4,9,32,128]{4,3,2,1,0:T(8,128)}, f32[3,20,128]{2,1,0:T(8,128)S(1)}, f32[3,20]{1,0:T(4,128)S(1)}, f32[5,3,32]{2,1,0:T(4,128)S(1)}, f32[32...) custom-call(s32[6]{0:T(128)S(1)} %copy-done.1, ...), custom_call_target="tpu_custom_call" | custom-call | flops 1000000 | bytes 10000 | tf_op jit(solution)/shard_map/pallas_call | solution.py:884
  139.0 1.3 shard_map.291
  140.3 1.3 shard_map.290
  141.6 2.3 %shard_map.292 = (f32[3,4,9,32,128]{4,3,2,1,0:T(8,128)}, f32[3,20,128]{2,1,0:T(8,128)}, f32[3,20]{1,0:T(4,128)}, f32[5,3,32]{2,1,0:T(4,128)}, f32[32,128]{1,0:T(...) custom-call(s32[6]{0:T(128)S(1)} %copy-done.1, ...), custom_call_target="tpu_custom_call", output_to_operand_aliasing={{0}: (5, {})} | custom-call | flops 1000000 | bytes 10000 | tf_op jit(solution)/shard_map/pallas_call | solution.py:884
  (34 shorter events, 0.1 us)
Async XLA Ops:
  1.8 6.8 %collective-permute-start.1 = (bf16[3,4,9,32,128]{4,3,2,1,0:T(8,128)(2,1)}, bf16[3,4,9,32,128]{4,3,2,1,0:T(8,128)(2,1)S(1)}, u32[]{:S(2)}, u32[]{:S(2)}) collective-permute-start(bf16[3,4,9,32,128]{4,3,2,1,0:T(8,128)(2,1)} %mine.3), channel_id=1, source_target_pairs={{0,1},{1,0},{2,3},{3,2},{4,5},{5,4},{6,7},{7,6},{8,9},{9,8},{10,11... | collective-permute-start | bytes 2654216 | tf_op jit(solution)/shard_map/ppermute | solution.py:913
  1.9 10.5 %collective-permute-start.2 = (bf16[32,2560]{1,0:T(8,128)(2,1)S(1)}, bf16[32,2560]{1,0:T(8,128)(2,1)S(1)}, u32[]{:S(2)}, u32[]{:S(2)}) collective-permute-start(bf16[32,2560]{1,0:T(8,128)(2,1)S(1)} %get-tuple-element.130.u0), channel_id=1, source_target_pairs={{0,1},{1,0},{2,3},{3,2},{4,5},{5,4},{6,7},{7,6},{8,9},{9,8},{10,11... | collective-permute-start | bytes 491528 | tf_op jit(solution)/shard_map/ppermute | solution.py:913
  2.4 6.2 %collective-permute-start = (bf16[32,2560]{1,0:T(8,128)(2,1)S(1)}, bf16[32,2560]{1,0:T(8,128)(2,1)S(1)}, u32[]{:S(2)}, u32[]{:S(2)}) collective-permute-start(bf16[32,2560]{1,0:T(8,128)(2,1)S(1)} %get-tuple-element.131), channel_id=1, source_target_pairs={{0,2},{1,3},{2,0},{3,1},{4,6},{5,7},{6,4},{7,5},{8,10},{9,11},{10,... | collective-permute-start | bytes 491528 | tf_op jit(solution)/shard_map/ppermute | solution.py:907
  3.7 8.8 %copy-start.1 = (s32[6]{0:T(128)S(1)}, s32[6]{0:T(128)}, u32[]{:S(2)}) copy-start(s32[6]{0:T(128)} %stack.23.meta) | copy-start | bytes 76
  3.7 23.4 %copy-start = (bf16[3,4,9,32,128]{4,3,2,1,0:T(8,128)(2,1)S(1)}, bf16[3,4,9,32,128]{4,3,2,1,0:T(8,128)(2,1)}, u32[]{:S(2)}) copy-start(bf16[3,4,9,32,128]{4,3,2,1,0:T(8,128)(2,1)} %mine.3) | copy-start | bytes 2654212
  8.6 3.8 %collective-permute-start.3 = (bf16[32,2560]{1,0:T(8,128)(2,1)S(1)}, bf16[32,2560]{1,0:T(8,128)(2,1)S(1)}, u32[]{:S(2)}, u32[]{:S(2)}) collective-permute-start(bf16[32,2560]{1,0:T(8,128)(2,1)S(1)} %collective-permute-done.u1), channel_id=1, source_target_pairs={{0,1},{1,0},{2,3},{3,2},{4,5},{5,4},{6,7},{7,6},{8,9},{9,8},{10,11... | collective-permute-start | bytes 491528 | tf_op jit(solution)/shard_map/ppermute | solution.py:913
  8.6 5.4 %collective-permute-start.4 = (bf16[17,32,128]{2,1,0:T(8,128)(2,1)S(1)}, bf16[17,32,128]{2,1,0:T(8,128)(2,1)S(1)}, u32[]{:S(2)}, u32[]{:S(2)}) collective-permute-start(bf16[17,32,128]{2,1,0:T(8,128)(2,1)S(1)} %get-tuple-element.138.k0), channel_id=1, source_target_pairs={{1,0},{3,2},{5,4},{7,6},{9,8},{11,10},{13,12},{15,14},{17,16},{19,... | collective-permute-start | bytes 417800 | tf_op jit(solution)/shard_map/ppermute | solution.py:913
  9.9 16.4 %collective-permute-start.5 = (bf16[18,32,128]{2,1,0:T(8,128)(2,1)S(1)}, bf16[18,32,128]{2,1,0:T(8,128)(2,1)S(1)}, u32[]{:S(2)}, u32[]{:S(2)}) collective-permute-start(bf16[18,32,128]{2,1,0:T(8,128)(2,1)S(1)} %get-tuple-element.144), channel_id=1, source_target_pairs={{0,2},{1,3},{2,0},{3,1},{4,6},{5,7},{6,4},{7,5},{8,10},{9,11},{10,... | collective-permute-start | bytes 442376 | tf_op jit(solution)/shard_map/ppermute | solution.py:907
  10.3 16.1 %collective-permute-start.6 = (bf16[18,32,128]{2,1,0:T(8,128)(2,1)S(1)}, bf16[18,32,128]{2,1,0:T(8,128)(2,1)S(1)}, u32[]{:S(2)}, u32[]{:S(2)}) collective-permute-start(bf16[18,32,128]{2,1,0:T(8,128)(2,1)S(1)} %get-tuple-element.146), channel_id=1, source_target_pairs={{0,3},{1,2},{2,1},{3,0},{4,7},{5,6},{6,5},{7,4},{8,11},{9,10},{10,... | collective-permute-start | bytes 442376 | tf_op jit(solution)/shard_map/ppermute | solution.py:910
  26.4 12.8 %collective-permute-start.8 = (bf16[27,32,128]{2,1,0:T(8,128)(2,1)S(1)}, bf16[27,32,128]{2,1,0:T(8,128)(2,1)S(1)}, u32[]{:S(2)}, u32[]{:S(2)}) collective-permute-start(bf16[27,32,128]{2,1,0:T(8,128)(2,1)S(1)} %get-tuple-element.155), channel_id=1, source_target_pairs={{0,3},{1,2},{2,1},{3,0},{4,7},{5,6},{6,5},{7,4},{8,11},{9,10},{10,... | collective-permute-start | bytes 663560 | tf_op jit(solution)/shard_map/ppermute | solution.py:910
  26.4 12.8 %collective-permute-start.7 = (bf16[27,32,128]{2,1,0:T(8,128)(2,1)S(1)}, bf16[27,32,128]{2,1,0:T(8,128)(2,1)S(1)}, u32[]{:S(2)}, u32[]{:S(2)}) collective-permute-start(bf16[27,32,128]{2,1,0:T(8,128)(2,1)S(1)} %get-tuple-element.153), channel_id=1, source_target_pairs={{0,2},{1,3},{2,0},{3,1},{4,6},{5,7},{6,4},{7,5},{8,10},{9,11},{10,... | collective-permute-start | bytes 663560 | tf_op jit(solution)/shard_map/ppermute | solution.py:907
  54.7 11.0 %collective-permute-start.9 = (bf16[32,1664]{1,0:T(8,128)(2,1)S(1)}, bf16[32,1664]{1,0:T(8,128)(2,1)S(1)}, u32[]{:S(2)}, u32[]{:S(2)}) collective-permute-start(bf16[32,1664]{1,0:T(8,128)(2,1)S(1)} %get-tuple-element.172), channel_id=1, source_target_pairs={{0,1},{1,0},{2,3},{3,2},{4,5},{5,4},{6,7},{7,6},{8,9},{9,8},{10,11... | collective-permute-start | bytes 319496 | tf_op jit(solution)/shard_map/ppermute | solution.py:913
  54.8 10.9 %collective-permute-start.10 = (bf16[32,1664]{1,0:T(8,128)(2,1)S(1)}, bf16[32,1664]{1,0:T(8,128)(2,1)S(1)}, u32[]{:S(2)}, u32[]{:S(2)}) collective-permute-start(bf16[32,1664]{1,0:T(8,128)(2,1)S(1)} %get-tuple-element.173), channel_id=1, source_target_pairs={{0,2},{1,3},{2,0},{3,1},{4,6},{5,7},{6,4},{7,5},{8,10},{9,11},{10,... | collective-permute-start | bytes 319496 | tf_op jit(solution)/shard_map/ppermute | solution.py:907
  56.3 9.4 %collective-permute-start.11 = (bf16[32,1664]{1,0:T(8,128)(2,1)S(1)}, bf16[32,1664]{1,0:T(8,128)(2,1)S(1)}, u32[]{:S(2)}, u32[]{:S(2)}) collective-permute-start(bf16[32,1664]{1,0:T(8,128)(2,1)S(1)} %get-tuple-element.174), channel_id=1, source_target_pairs={{0,3},{1,2},{2,1},{3,0},{4,7},{5,6},{6,5},{7,4},{8,11},{9,10},{10,... | collective-permute-start | bytes 319496 | tf_op jit(solution)/shard_map/ppermute | solution.py:910
  69.4 9.8 %collective-permute-start.12 = (bf16[4,21,16,128]{3,2,1,0:T(8,128)(2,1)S(1)}, bf16[4,21,16,128]{3,2,1,0:T(8,128)(2,1)S(1)}, u32[]{:S(2)}, u32[]{:S(2)}) collective-permute-start(bf16[4,21,16,128]{3,2,1,0:T(8,128)(2,1)S(1)} %get-tuple-element.181), channel_id=1, source_target_pairs={{0,4},{4,0},{8,12},{12,8},{16,20},{20,16},{24,28},{28,24},{1,5},{5... | collective-permute-start | bytes 1032200 | tf_op jit(solution)/shard_map/ppermute | solution.py:944
  82.8 3.2 %collective-permute-start.13 = (bf16[1920,128]{1,0:T(8,128)(2,1)S(1)}, bf16[1920,128]{1,0:T(8,128)(2,1)S(1)}, u32[]{:S(2)}, u32[]{:S(2)}) collective-permute-start(bf16[1920,128]{1,0:T(8,128)(2,1)S(1)} %get-tuple-element.187.d0), channel_id=1, source_target_pairs={{0,1},{1,0},{2,3},{3,2},{4,5},{5,4},{6,7},{7,6},{8,9},{9,8},{10,11... | collective-permute-start | bytes 1474568 | tf_op jit(solution)/shard_map/ppermute | solution.py:913
  82.9 13.2 %collective-permute-start.15 = (bf16[4,18,16,128]{3,2,1,0:T(8,128)(2,1)S(1)}, bf16[4,18,16,128]{3,2,1,0:T(8,128)(2,1)S(1)}, u32[]{:S(2)}, u32[]{:S(2)}) collective-permute-start(bf16[4,18,16,128]{3,2,1,0:T(8,128)(2,1)S(1)} %get-tuple-element.194), channel_id=1, source_target_pairs={{0,4},{4,0},{8,12},{12,8},{16,20},{20,16},{24,28},{28,24},{1,5},{5... | collective-permute-start | bytes 884744 | tf_op jit(solution)/shard_map/ppermute | solution.py:944
  84.1 12.1 %collective-permute-start.16 = (bf16[2,21,16,128]{3,2,1,0:T(8,128)(2,1)S(1)}, bf16[2,21,16,128]{3,2,1,0:T(8,128)(2,1)S(1)}, u32[]{:S(2)}, u32[]{:S(2)}) collective-permute-start(bf16[2,21,16,128]{3,2,1,0:T(8,128)(2,1)S(1)} %get-tuple-element.195), channel_id=1, source_target_pairs={{0,8},{4,12},{8,0},{12,4},{16,24},{20,28},{24,16},{28,20},{1,9},{5... | collective-permute-start | bytes 516104 | tf_op jit(solution)/shard_map/ppermute | solution.py:1042
  84.9 1.2 collective-permute-start.14
  98.4 4.2 %collective-permute-start.17 = (bf16[4,3,16,128]{3,2,1,0:T(8,128)(2,1)S(1)}, bf16[4,3,16,128]{3,2,1,0:T(8,128)(2,1)S(1)}, u32[]{:S(2)}, u32[]{:S(2)}) collective-permute-start(bf16[4,3,16,128]{3,2,1,0:T(8,128)(2,1)S(1)} %get-tuple-element.203), channel_id=1, source_target_pairs={{0,4},{4,0},{8,12},{12,8},{16,20},{20,16},{24,28},{28,24},{1,5},{5... | collective-permute-start | bytes 147464 | tf_op jit(solution)/shard_map/ppermute | solution.py:944
  99.6 8.5 %collective-permute-start.21 = (bf16[21,16,128]{2,1,0:T(8,128)(2,1)S(1)}, bf16[21,16,128]{2,1,0:T(8,128)(2,1)S(1)}, u32[]{:S(2)}, u32[]{:S(2)}) collective-permute-start(bf16[21,16,128]{2,1,0:T(8,128)(2,1)S(1)} %get-tuple-element.210), channel_id=1, source_target_pairs={{0,16},{4,20},{8,24},{12,28},{16,0},{20,4},{24,8},{28,12},{1,17},{... | collective-permute-start | bytes 258056 | tf_op jit(solution)/shard_map/ppermute | solution.py:1047
  100.1 12.3 %collective-permute-start.23 = (bf16[32,1664]{1,0:T(8,128)(2,1)S(1)}, bf16[32,1664]{1,0:T(8,128)(2,1)S(1)}, u32[]{:S(2)}, u32[]{:S(2)}) collective-permute-start(bf16[32,1664]{1,0:T(8,128)(2,1)S(1)} %get-tuple-element.214), channel_id=1, source_target_pairs={{0,2},{1,3},{2,0},{3,1},{4,6},{5,7},{6,4},{7,5},{8,10},{9,11},{10,... | collective-permute-start | bytes 319496 | tf_op jit(solution)/shard_map/ppermute | solution.py:907
  103.2 10.9 %collective-permute-start.18 = (bf16[21,16,128]{2,1,0:T(8,128)(2,1)S(1)}, bf16[21,16,128]{2,1,0:T(8,128)(2,1)S(1)}, u32[]{:S(2)}, u32[]{:S(2)}) collective-permute-start(bf16[21,16,128]{2,1,0:T(8,128)(2,1)S(1)} %get-tuple-element.205), channel_id=1, source_target_pairs={{0,8},{4,12},{8,0},{12,4},{16,24},{20,28},{24,16},{28,20},{1,9},{5... | collective-permute-start | bytes 258056 | tf_op jit(solution)/shard_map/ppermute | solution.py:950
  103.7 10.4 %collective-permute-start.19 = (bf16[21,16,128]{2,1,0:T(8,128)(2,1)S(1)}, bf16[21,16,128]{2,1,0:T(8,128)(2,1)S(1)}, u32[]{:S(2)}, u32[]{:S(2)}) collective-permute-start(bf16[21,16,128]{2,1,0:T(8,128)(2,1)S(1)} %get-tuple-element.206), channel_id=1, source_target_pairs={{0,16},{4,20},{8,24},{12,28},{16,0},{20,4},{24,8},{28,12},{1,17},{... | collective-permute-start | bytes 258056 | tf_op jit(solution)/shard_map/ppermute | solution.py:950
  105.4 8.7 %collective-permute-start.20 = (bf16[21,16,128]{2,1,0:T(8,128)(2,1)S(1)}, bf16[21,16,128]{2,1,0:T(8,128)(2,1)S(1)}, u32[]{:S(2)}, u32[]{:S(2)}) collective-permute-start(bf16[21,16,128]{2,1,0:T(8,128)(2,1)S(1)} %get-tuple-element.207), channel_id=1, source_target_pairs={{0,24},{4,28},{8,16},{12,20},{16,8},{20,12},{24,0},{28,4},{1,25},{... | collective-permute-start | bytes 258056 | tf_op jit(solution)/shard_map/ppermute | solution.py:950
  108.6 5.5 %collective-permute-start.22 = (bf16[9,16,128]{2,1,0:T(8,128)(2,1)S(1)}, bf16[9,16,128]{2,1,0:T(8,128)(2,1)S(1)}, u32[]{:S(2)}, u32[]{:S(2)}) collective-permute-start(bf16[9,16,128]{2,1,0:T(8,128)(2,1)S(1)} %get-tuple-element.213), channel_id=1, source_target_pairs={{2,0},{3,1},{6,4},{7,5},{10,8},{11,9},{14,12},{15,13},{18,16},{19,... | collective-permute-start | bytes 110600 | tf_op jit(solution)/shard_map/ppermute | solution.py:1071
  114.7 9.7 %collective-permute-start.27 = (bf16[34,16,128]{2,1,0:T(8,128)(2,1)S(1)}, bf16[34,16,128]{2,1,0:T(8,128)(2,1)S(1)}, u32[]{:S(2)}, u32[]{:S(2)}) collective-permute-start(bf16[34,16,128]{2,1,0:T(8,128)(2,1)S(1)} %shard_map.288), channel_id=1, source_target_pairs={{0,24},{1,16},{2,8},{3,0},{4,28},{5,20},{6,12},{7,4},{8,25},{9,17}... | collective-permute-start | bytes 417800 | tf_op jit(solution)/shard_map/ppermute | solution.py:931
  115.4 11.8 %collective-permute-start.26 = (bf16[34,16,128]{2,1,0:T(8,128)(2,1)S(1)}, bf16[34,16,128]{2,1,0:T(8,128)(2,1)S(1)}, u32[]{:S(2)}, u32[]{:S(2)}) collective-permute-start(bf16[34,16,128]{2,1,0:T(8,128)(2,1)S(1)} %shard_map.288), channel_id=1, source_target_pairs={{0,16},{1,24},{2,0},{3,8},{4,20},{5,28},{6,4},{7,12},{8,17},{9,25}... | collective-permute-start | bytes 417800 | tf_op jit(solution)/shard_map/ppermute | solution.py:931
  117.2 13.7 %collective-permute-start.25 = (bf16[34,16,128]{2,1,0:T(8,128)(2,1)S(1)}, bf16[34,16,128]{2,1,0:T(8,128)(2,1)S(1)}, u32[]{:S(2)}, u32[]{:S(2)}) collective-permute-start(bf16[34,16,128]{2,1,0:T(8,128)(2,1)S(1)} %shard_map.288), channel_id=1, source_target_pairs={{0,8},{1,0},{2,24},{3,16},{4,12},{5,4},{6,28},{7,20},{8,9},{9,1},{... | collective-permute-start | bytes 417800 | tf_op jit(solution)/shard_map/ppermute | solution.py:931
  119.8 13.9 %collective-permute-start.24 = (bf16[34,16,128]{2,1,0:T(8,128)(2,1)S(1)}, bf16[34,16,128]{2,1,0:T(8,128)(2,1)S(1)}, u32[]{:S(2)}, u32[]{:S(2)}) collective-permute-start(bf16[34,16,128]{2,1,0:T(8,128)(2,1)S(1)} %shard_map.288), channel_id=1, source_target_pairs={{0,0},{1,8},{2,16},{3,24},{4,4},{5,12},{6,20},{7,28},{8,1},{9,9},{... | collective-permute-start | bytes 417800 | tf_op jit(solution)/shard_map/ppermute | solution.py:931
  124.4 17.2 %collective-permute-start.31 = (bf16[34,16,128]{2,1,0:T(8,128)(2,1)S(1)}, bf16[34,16,128]{2,1,0:T(8,128)(2,1)S(1)}, u32[]{:S(2)}, u32[]{:S(2)}) collective-permute-start(bf16[34,16,128]{2,1,0:T(8,128)(2,1)S(1)} %collective-permute-done.27.refs_3_), channel_id=1, source_target_pairs={{0,4},{4,0},{8,12},{12,8},{16,20},{20,16},{24,28},{28,24},{1,5},{5... | collective-permute-start | bytes 417800 | tf_op jit(solution)/shard_map/ppermute | solution.py:944
  127.2 14.4 %collective-permute-start.30 = (bf16[34,16,128]{2,1,0:T(8,128)(2,1)S(1)}, bf16[34,16,128]{2,1,0:T(8,128)(2,1)S(1)}, u32[]{:S(2)}, u32[]{:S(2)}) collective-permute-start(bf16[34,16,128]{2,1,0:T(8,128)(2,1)S(1)} %collective-permute-done.26.refs_2_), channel_id=1, source_target_pairs={{0,4},{4,0},{8,12},{12,8},{16,20},{20,16},{24,28},{28,24},{1,5},{5... | collective-permute-start | bytes 417800 | tf_op jit(solution)/shard_map/ppermute | solution.py:944
  130.8 10.8 %collective-permute-start.29 = (bf16[34,16,128]{2,1,0:T(8,128)(2,1)S(1)}, bf16[34,16,128]{2,1,0:T(8,128)(2,1)S(1)}, u32[]{:S(2)}, u32[]{:S(2)}) collective-permute-start(bf16[34,16,128]{2,1,0:T(8,128)(2,1)S(1)} %collective-permute-done.25.refs_1_), channel_id=1, source_target_pairs={{0,4},{4,0},{8,12},{12,8},{16,20},{20,16},{24,28},{28,24},{1,5},{5... | collective-permute-start | bytes 417800 | tf_op jit(solution)/shard_map/ppermute | solution.py:944
  133.6 8.0 %collective-permute-start.28 = (bf16[34,16,128]{2,1,0:T(8,128)(2,1)S(1)}, bf16[34,16,128]{2,1,0:T(8,128)(2,1)S(1)}, u32[]{:S(2)}, u32[]{:S(2)}) collective-permute-start(bf16[34,16,128]{2,1,0:T(8,128)(2,1)S(1)} %collective-permute-done.24.refs_0_), channel_id=1, source_target_pairs={{0,4},{4,0},{8,12},{12,8},{16,20},{20,16},{24,28},{28,24},{1,5},{5... | collective-permute-start | bytes 417800 | tf_op jit(solution)/shard_map/ppermute | solution.py:944

commit v7 on v6

--- a/solution.py
+++ b/solution.py
@@ -39,6 +39,12 @@
     return lax.dot_general(a, b, dims, preferred_element_type=F32)
 
 
+def position(units):
+    c = lax.axis_index("chan")
+    place = lax.axis_index("dp") if lax.axis_size("dp") == 8 else jnp.int32(0)
+    return c >> 1, c & 1, c, units[0:1, :], place >> 1, place & 1
+
+
 def limits(meta, slot):
     group, units = meta[0], meta[3]
     if slot == 0:
@@ -51,7 +57,7 @@
 
 
 def mask_of(meta, j):
-    row_end, col_end = limits(meta, SLOT[j])
+    row_end, col_end = (v.reshape(1, 1, 128) for v in limits(meta, SLOT[j]))
     row = lax.broadcasted_iota(jnp.int32, (CR, ST, 128), 0) + CR * j
     col = lax.broadcasted_iota(jnp.int32, (CR, ST, 128), 1)
     inside = (row < row_end) & (col < col_end)
@@ -430,6 +436,12 @@
     spread_out(st_out, total)
 
 
+def as_parts(st):
+    high = st.astype(BF).astype(F32)
+    mid = (st - high).astype(BF).astype(F32)
+    return jnp.concatenate([high, mid, st - high - mid, jnp.zeros((8, 128), F32)], axis=0).astype(BF)
+
+
 def weight_grad(meta, dyt, act, field, shifts, wg):
     for j in range(NCH):
         field[8 + CH * j : 8 + CH * (j + 1)] = act[CH * j : CH * (j + 1)].astype(F32)
@@ -474,6 +486,7 @@
     out_grad(meta, dz, y, cst, st, sums, field, dyt)
     fill_shifts(field, shifts)
     conv_back(meta, True, w, y_in, cst_in, shifts, grad, st_out)
+    grad[PX:] = as_parts(st_out[0])
     weight_grad(meta, dyt, act, field, shifts, wg)
     part_out(meta, wg, send)
 
@@ -527,6 +540,11 @@
     part_out(meta, gs, gs_send)
     rest = jnp.zeros((4, 128), F32)
     norm[0] = jnp.concatenate([sums[0:4], sums1[0:4], sums2[0:4], rest], axis=0).astype(BF)
+
+
+def both_kernel(st, other, out):
+    v = other[PX:].astype(F32)
+    out[...] = st[...] + (v[0:8] + v[8:16] + v[16:24])[None]
 
 
 def total_kernel(st, out):
@@ -876,16 +894,17 @@
 def call(body, outs, scratch, args, last=False, limit=VMEM, in_place=(), aliases={}, flops=10**6):
     place = jax.ShapeDtypeStruct if last else pltpu.VMEM
 
-    def space(i, dtype):
-        if i in in_place:
-            return pl.BlockSpec(memory_space=pl.ANY)
-        return pl.BlockSpec(memory_space=pltpu.SMEM if dtype == jnp.int32 else pltpu.VMEM)
+    def space(i):
+        return pl.BlockSpec(memory_space=pl.ANY if i in in_place else pltpu.VMEM)
+
+    def placed(units, *refs):
+        body(position(units), *refs)
 
     return pl.pallas_call(
-        body,
+        placed if args[0].dtype == jnp.int32 else body,
         out_shape=[place(s, d) for s, d in outs],
-        in_specs=[space(i, a.dtype) for i, a in enumerate(args)],
-        out_specs=[space(len(args) + i, d) for i, (_, d) in enumerate(outs)],
+        in_specs=[space(i) for i in range(len(args))],
+        out_specs=[space(len(args) + i) for i in range(len(outs))],
         scratch_shapes=[s if callable(getattr(s, "get_ref_aval", None)) else pltpu.VMEM(*s) for s in scratch],
         input_output_aliases=aliases,
         compiler_params=pltpu.CompilerParams(vmem_limit_bytes=limit),
@@ -899,8 +918,7 @@
     group, branch = c // 2, c % 2
     fine = group == 0
     direct = dp == 8
-    place = lax.axis_index("dp") if direct else 0
-    meta = jnp.stack([group, branch, c, units[0], place // 2, place % 2]).astype(jnp.int32)
+    meta = jnp.broadcast_to(units, (8, 128))
     n0, n1, n2 = f0.shape[2], f1.shape[2], f2.shape[2]
 
     def across(v):
@@ -1029,23 +1047,24 @@
     st, got2 = lax.optimization_barrier((exchange(after(st, send2)), got2))
     d0, st, sums1, wg1, send1 = call(
         first_back_kernel,
-        [(canvas, BF), (stat, F32), ((8, 128), F32), ((8, 18, 16, 128), BF), ((4, 18, 16, 128), BF)],
+        [((PX + 32, 128), BF), (stat, F32), ((8, 128), F32), ((8, 18, 16, 128), BF), ((4, 18, 16, 128), BF)],
         back_scratch,
         (meta, dz1, y1, cst1, st, w1_tall, act0, y0, cst0),
     )
     got1 = over_y(send1) if direct else reduce(wg1)
-    d0_other, st_other = beside(d0), beside(st)
-    st = st + st_other
+    d0_other = beside(d0)
     if direct:
         pair = (2, 21, 16, 128)
         own2, send2 = call(halve_kernel, [(pair, F32), (pair, BF)], [], (meta, wg2, after(got2, d0)))
         got2 = lax.ppermute(send2, "dp", [(i, i ^ 2) for i in range(8)])
-        st = exchange(after(st, d0_other, own2))
+        (st,) = call(both_kernel, [(stat, F32)], [], (after(st, own2), d0_other))
+        st = exchange(st)
         (st,) = call(total_kernel, [((1, 8, 128), F32)], [], (st,))
         st, got1, got2 = lax.optimization_barrier((st, got1, got2))
         own2, send2 = call(again_kernel, [(pair[1:], F32), (pair[1:], BF)], [], (meta, own2, got2))
         got2 = lax.ppermute(send2, "dp", [(i, i ^ 4) for i in range(8)])
     else:
+        (st,) = call(both_kernel, [(stat, F32)], [], (st, d0_other))
         st = exchange(st)
     own, other, gs, gs_send, norm = call(
         final_kernel,

time: 145 us -> 135 us (0.931)
  Pallas kernels: 35.3 us -> 24.9 us
    pallas_call x22 -> x23, Pallas kernels: 35.3 us -> 24.9 us  [call(): pl.pallas_call(placed if args[0].dtype == jnp.int32 else body, out_shape=...]
  transfers between devices with their start and end apart: 32 -> 31, of which waited for: 8 -> 8; matrix products, arithmetic and copies ran while one was open for 0% -> 0% of each run, Pallas kernels for 11% -> 7%
where the time goes in v7:
time: 135 us; the launch traced here: 134 us
  blocking collectives  58.5 us (43%)
  starting transfers between devices  32.7 us (24%)
  Pallas kernels  24.9 us (18%)
  waiting for transfers between devices  15.9 us (12%)
  between operations  1.69 us (1%)
    all_to_all x6, blocking collectives, exchange(): st = lax.all_to_all(st, 'dp', 0, 0, tiled=True)  58.5 us
    pallas_call x23, Pallas kernels, call(): pl.pallas_call(placed if args[0].dtype == jnp.int32 else body, out_shape=...  24.9 us
    ppermute x4, waiting for transfers between devices, over_z(): parts.append(lax.ppermute(v, ('dp', 'chan'), pairs))  8.41 us
    ppermute x7, starting transfers between devices, over_y(): return lax.ppermute(v, 'dp', [(i, i ^ 1) for i in range(8)])  7.74 us
    ppermute x4, starting transfers between devices, over_z(): parts.append(lax.ppermute(v, ('dp', 'chan'), pairs))  7.27 us
    ppermute x3, starting transfers between devices, along_z(): lax.ppermute(v, 'dp', [(i, i ^ 2 * k + 2) for i in range(8)])  4.45 us
    ppermute x5, starting transfers between devices, across(): return lax.ppermute(v, 'chan', [(i, i ^ 2) for i in range(4)])  4.04 us
    ppermute x1, starting transfers between devices, shards(): extra = lax.ppermute(extra, 'chan', [(2, 0), (3, 1)])  3.32 us
  transfers between devices with their start and end apart: 31, of which 8 were waited for; matrix products, arithmetic and copies ran while one was open for 0% of the time, Pallas kernels for 7%

profile of v7, /device:TPU:2, one launch (start us, length us, event | category | flops | bytes accessed | tf_op | source)
XLA Modules:
  0.0 134.2 jit_solution(13513982695129766256)
XLA Ops:
  0.6 1.2 shard_map.274
  1.8 0.1 collective-permute-start.1
  1.9 0.5 collective-permute-start.2
  3.1 0.6 broadcast_in_dim.20.units
  3.7 2.2 %shard_map.275 = (bf16[17,32,128]{2,1,0:T(8,128)(2,1)S(1)}, bf16[17,32,128]{2,1,0:T(8,128)(2,1)S(1)}, bf16[18,32,128]{2,1,0:T(8,128)(2,1)S(1)}, bf16[18,32,128]{...) custom-call(s32[8,128]{1,0:T(8,128)} %broadcast_in_dim.20.units, ...), custom_call_target="tpu_custom_call" | custom-call | flops 2000000000 | bytes 10000 | tf_op jit(solution)/shard_map/pallas_call | solution.py:903
  5.9 2.7 %collective-permute-done.refs_1_.refs_8_ = bf16[32,2560]{1,0:T(8,128)(2,1)S(1)} collective-permute-done((bf16[32,2560]{1,0:T(8,128)(2,1)S(1)}, bf16[32,2560]{1,0:T(8,128)(2,1)S(1)}, u32[]{:S(2)}, u32[]{:S(2)}) %collective-permute-start) | collective-permute-done | bytes 163872 | tf_op jit(solution)/shard_map/ppermute | solution.py:925
  8.6 0.0 collective-permute-done.1.refs_1_
  8.6 0.0 collective-permute-start.3
  8.6 1.3 collective-permute-start.4
  9.9 0.3 collective-permute-start.5
  10.3 2.2 %collective-permute-start.6 = (bf16[18,32,128]{2,1,0:T(8,128)(2,1)S(1)}, bf16[18,32,128]{2,1,0:T(8,128)(2,1)S(1)}, u32[]{:S(2)}, u32[]{:S(2)}) collective-permute-start(bf16[18,32,128]{2,1,0:T(8,128)(2,1)S(1)} %get-tuple-element.146), channel_id=1, source_target_pairs={{0,3},{1,2},{2,1},{3,0},{4,7},{5,6},{6,5},{7,4},{8,11},{9,10},{10,... | collective-permute-start | bytes 442376 | tf_op jit(solution)/shard_map/ppermute | solution.py:928
  12.5 0.0 collective-permute-done.2.refs_2_.refs_9_
  12.5 1.0 shard_map.276
  13.5 12.3 %all_to_all.30.refs_1_ = f32[8,8,128]{2,1,0:T(8,128)S(1)} all-to-all(f32[8,8,128]{2,1,0:T(8,128)S(1)} %get-tuple-element.139), channel_id=1, replica_groups=mesh['dp'=8,'chan'=4] {'dp'}, dimensions={0} | all-to-all | bytes 65536 | tf_op jit(solution)/shard_map/all_to_all | solution.py:935
  25.8 0.7 collective-permute-start.7
  26.5 0.2 shard_map.277
  26.7 1.6 %shard_map.278 = (bf16[1920,128]{1,0:T(8,128)(2,1)S(1)}, f32[1920,128]{1,0:T(8,128)S(1)}, f32[8,8,128]{2,1,0:T(8,128)S(1)}, f32[16,128]{1,0:T(8,128)S(1)}) custom-call(s32[8,128]{1,0:T(8,128)S(1)} %copy-done.1, f32[1920,128]{1,0:T(8,128)S(1)} %get-tuple-element.136.refs_0_.refs_6_.refs_2_, f32[8,8,128]{2,1,0:T(8,128)S(1)} %all_to_all.30.refs_1_, ...), custom_call_target="tpu_custom_call" | custom-call | flops 1000000 | bytes 10000 | tf_op jit(solution)/shard_map/pallas_call | solution.py:903
  28.4 9.1 %all_to_all.31.refs_1_ = f32[8,8,128]{2,1,0:T(8,128)S(1)} all-to-all(f32[8,8,128]{2,1,0:T(8,128)S(1)} %get-tuple-element.152), channel_id=1, replica_groups=mesh['dp'=8,'chan'=4] {'dp'}, dimensions={0} | all-to-all | bytes 65536 | tf_op jit(solution)/shard_map/all_to_all | solution.py:935
  37.5 0.2 shard_map.279
  37.7 1.6 %shard_map.280 = (bf16[1920,128]{1,0:T(8,128)(2,1)S(1)}, f32[1920,128]{1,0:T(8,128)S(1)}, f32[8,8,128]{2,1,0:T(8,128)S(1)}, f32[16,128]{1,0:T(8,128)S(1)}) custom-call(s32[8,128]{1,0:T(8,128)S(1)} %copy-done.1, f32[1920,128]{1,0:T(8,128)S(1)} %get-tuple-element.151.refs_0_.refs_6_.refs_1_, f32[8,8,128]{2,1,0:T(8,128)S(1)} %all_to_all.31.refs_1_, ...), custom_call_target="tpu_custom_call" | custom-call | flops 1000000 | bytes 10000 | tf_op jit(solution)/shard_map/pallas_call | solution.py:903
  39.4 9.1 %all_to_all.32.refs_1_ = f32[8,8,128]{2,1,0:T(8,128)S(1)} all-to-all(f32[8,8,128]{2,1,0:T(8,128)S(1)} %get-tuple-element.160), channel_id=1, replica_groups=mesh['dp'=8,'chan'=4] {'dp'}, dimensions={0} | all-to-all | bytes 65536 | tf_op jit(solution)/shard_map/all_to_all | solution.py:935
  48.4 1.7 %shard_map.281 = (f32[1920,128]{1,0:T(8,128)S(1)}, f32[8,8,128]{2,1,0:T(8,128)S(1)}, f32[16,128]{1,0:T(8,128)S(1)}, bf16[1664,256]{1,0:T(8,128)(2,1)S(1)}, bf16[...) custom-call(s32[8,128]{1,0:T(8,128)S(1)} %copy-done.1, f32[1920,128]{1,0:T(8,128)S(1)} %get-tuple-element.159.refs_0_.refs_1_, ...), custom_call_target="tpu_custom_call" | custom-call | flops 1000000 | bytes 10000 | tf_op jit(solution)/shard_map/pallas_call | solution.py:903
  50.1 0.7 shard_map.282
  50.9 0.1 collective-permute-start.9
  50.9 1.5 %collective-permute-start.10 = (bf16[32,1664]{1,0:T(8,128)(2,1)S(1)}, bf16[32,1664]{1,0:T(8,128)(2,1)S(1)}, u32[]{:S(2)}, u32[]{:S(2)}) collective-permute-start(bf16[32,1664]{1,0:T(8,128)(2,1)S(1)} %get-tuple-element.173), channel_id=1, source_target_pairs={{0,2},{1,3},{2,0},{3,1},{4,6},{5,7},{6,4},{7,5},{8,10},{9,11},{10,... | collective-permute-start | bytes 319496 | tf_op jit(solution)/shard_map/ppermute | solution.py:925
  52.5 0.3 collective-permute-start.11
  52.8 9.0 %all_to_all.33.refs_3_ = f32[8,8,128]{2,1,0:T(8,128)S(1)} all-to-all(f32[8,8,128]{2,1,0:T(8,128)S(1)} %get-tuple-element.171), channel_id=1, replica_groups=mesh['dp'=8,'chan'=4] {'dp'}, dimensions={0} | all-to-all | bytes 65536 | tf_op jit(solution)/shard_map/all_to_all | solution.py:935
  61.9 3.2 %shard_map.283 = (f32[1920,128]{1,0:T(8,128)S(1)}, f32[8,8,128]{2,1,0:T(8,128)S(1)}, f32[8,128]{1,0:T(8,128)S(1)}, bf16[8,21,16,128]{3,2,1,0:T(8,128)(2,1)S(1)}, bf16[4,21,16,128]{3,2,1,0:T(8,128)(2,1)S(1)}) custom-call(s32[8,128]{1,0:T(8,128)S(1)} %copy-done.1, f32[1920,128]{1,0:T(8,128)S(1)} %get-tuple-element.167.refs_0_, ...), custom_call_target="tpu_custom_call" | custom-call | flops 1000000 | bytes 10000 | tf_op jit(solution)/shard_map/pallas_call | solution.py:903
  65.1 0.5 collective-permute-start.12
  65.6 9.3 %all_to_all.34.refs_3_ = f32[8,8,128]{2,1,0:T(8,128)S(1)} all-to-all(f32[8,8,128]{2,1,0:T(8,128)S(1)} %get-tuple-element.182), channel_id=1, replica_groups=mesh['dp'=8,'chan'=4] {'dp'}, dimensions={0} | all-to-all | bytes 65536 | tf_op jit(solution)/shard_map/all_to_all | solution.py:935
  74.9 3.0 %shard_map.284 = (bf16[1952,128]{1,0:T(8,128)(2,1)S(1)}, f32[8,8,128]{2,1,0:T(8,128)S(1)}, f32[8,128]{1,0:T(8,128)S(1)}, bf16[8,18,16,128]{3,2,1,0:T(8,128)(2,1)S(1)}, bf16[4,18,16,128]{3,2,1,0:T(8,128)(2,1)S(1)}) custom-call(s32[8,128]{1,0:T(8,128)S(1)} %copy-done.1, f32[1920,128]{1,0:T(8,128)S(1)} %get-tuple-element.179.refs_0_, ...), custom_call_target="tpu_custom_call" | custom-call | flops 1000000 | bytes 10000 | tf_op jit(solution)/shard_map/pallas_call | solution.py:903
  77.9 0.1 collective-permute-start.13
  78.0 0.5 collective-permute-start.14
  78.5 0.1 shard_map.285
  78.6 0.8 collective-permute-start.15
  79.4 0.5 collective-permute-done.13.other.refs_1_
  79.8 9.6 %all_to_all.35.st = f32[8,8,128]{2,1,0:T(8,128)S(1)} all-to-all(f32[8,8,128]{2,1,0:T(8,128)S(1)} %shard_map.286), channel_id=1, replica_groups=mesh['dp'=8,'chan'=4] {'dp'}, dimensions={0} | all-to-all | bytes 65536 | tf_op jit(solution)/shard_map/all_to_all | solution.py:935
  89.5 1.7 %shard_map.288 = (bf16[32,1664]{1,0:T(8,128)(2,1)S(1)}, bf16[32,1664]{1,0:T(8,128)(2,1)S(1)}, bf16[8,3,16,128]{3,2,1,0:T(8,128)(2,1)S(1)}, bf16[4,3,16,128]{3,2,1,0:T(8,128)(2,1)S(1)}, bf16[1,16,128]{2,1,0:T(8,128)(2,1)S(1)}) custom-call(s32[8,128]{1,0:T(8,128)S(1)} %copy-done.1, bf16[1952,128]{1,0:T(8,128)(2,1)S(1)} %get-tuple-element.187.refs_0_, ...), custom_call_target="tpu_custom_call" | custom-call | flops 1000000 | bytes 10000 | tf_op jit(solution)/shard_map/pallas_call | solution.py:903
  91.2 0.5 collective-permute-start.16
  91.7 0.6 collective-permute-start.20
  92.3 1.4 %collective-permute-start.22 = (bf16[32,1664]{1,0:T(8,128)(2,1)S(1)}, bf16[32,1664]{1,0:T(8,128)(2,1)S(1)}, u32[]{:S(2)}, u32[]{:S(2)}) collective-permute-start(bf16[32,1664]{1,0:T(8,128)(2,1)S(1)} %get-tuple-element.214), channel_id=1, source_target_pairs={{0,2},{1,3},{2,0},{3,1},{4,6},{5,7},{6,4},{7,5},{8,10},{9,11},{10,... | collective-permute-start | bytes 319496 | tf_op jit(solution)/shard_map/ppermute | solution.py:925
  93.7 1.6 %collective-permute-done.16.refs_3_ = bf16[4,3,16,128]{3,2,1,0:T(8,128)(2,1)S(1)} collective-permute-done((bf16[4,3,16,128]{3,2,1,0:T(8,128)(2,1)S(1)}, bf16[4,3,16,128]{3,2,1,0:T(8,128)(2,1)S(1)}, u32[]{:S(2)}, u32[]{:S(2)}) %collective-permute-start.16) | collective-permute-done | bytes 49184 | tf_op jit(solution)/shard_map/ppermute | solution.py:962
  95.3 0.1 shard_map.289
  95.4 0.5 collective-permute-start.17
  95.8 1.2 collective-permute-start.18
  97.0 2.8 %collective-permute-start.19 = (bf16[21,16,128]{2,1,0:T(8,128)(2,1)S(1)}, bf16[21,16,128]{2,1,0:T(8,128)(2,1)S(1)}, u32[]{:S(2)}, u32[]{:S(2)}) collective-permute-start(bf16[21,16,128]{2,1,0:T(8,128)(2,1)S(1)} %get-tuple-element.207), channel_id=1, source_target_pairs={{0,24},{4,28},{8,16},{12,20},{16,8},{20,12},{24,0},{28,4},{1,25},{... | collective-permute-start | bytes 258056 | tf_op jit(solution)/shard_map/ppermute | solution.py:968
  99.8 1.0 collective-permute-done.20.refs_1_
  100.9 3.3 %collective-permute-start.21 = (bf16[9,16,128]{2,1,0:T(8,128)(2,1)S(1)}, bf16[9,16,128]{2,1,0:T(8,128)(2,1)S(1)}, u32[]{:S(2)}, u32[]{:S(2)}) collective-permute-start(bf16[9,16,128]{2,1,0:T(8,128)(2,1)S(1)} %get-tuple-element.213), channel_id=1, source_target_pairs={{2,0},{3,1},{6,4},{7,5},{10,8},{11,9},{14,12},{15,13},{18,16},{19,... | collective-permute-start | bytes 110600 | tf_op jit(solution)/shard_map/ppermute | solution.py:1090
  104.3 1.6 %collective-permute-done.21.refs_5_ = bf16[9,16,128]{2,1,0:T(8,128)(2,1)S(1)} collective-permute-done((bf16[9,16,128]{2,1,0:T(8,128)(2,1)S(1)}, bf16[9,16,128]{2,1,0:T(8,128)(2,1)S(1)}, u32[]{:S(2)}, u32[]{:S(2)}) %collective-permute-start.21) | collective-permute-done | bytes 36896 | tf_op jit(solution)/shard_map/ppermute | solution.py:1090
  105.9 0.1 shard_map.292
  105.9 1.1 collective-permute-start.26
  107.0 1.4 %collective-permute-start.25 = (bf16[34,16,128]{2,1,0:T(8,128)(2,1)S(1)}, bf16[34,16,128]{2,1,0:T(8,128)(2,1)S(1)}, u32[]{:S(2)}, u32[]{:S(2)}) collective-permute-start(bf16[34,16,128]{2,1,0:T(8,128)(2,1)S(1)} %shard_map.292), channel_id=1, source_target_pairs={{0,16},{1,24},{2,0},{3,8},{4,20},{5,28},{6,4},{7,12},{8,17},{9,25}... | collective-permute-start | bytes 417800 | tf_op jit(solution)/shard_map/ppermute | solution.py:949
  108.4 2.6 %collective-permute-start.24 = (bf16[34,16,128]{2,1,0:T(8,128)(2,1)S(1)}, bf16[34,16,128]{2,1,0:T(8,128)(2,1)S(1)}, u32[]{:S(2)}, u32[]{:S(2)}) collective-permute-start(bf16[34,16,128]{2,1,0:T(8,128)(2,1)S(1)} %shard_map.292), channel_id=1, source_target_pairs={{0,8},{1,0},{2,24},{3,16},{4,12},{5,4},{6,28},{7,20},{8,9},{9,1},{... | collective-permute-start | bytes 417800 | tf_op jit(solution)/shard_map/ppermute | solution.py:949
  111.0 2.2 %collective-permute-start.23 = (bf16[34,16,128]{2,1,0:T(8,128)(2,1)S(1)}, bf16[34,16,128]{2,1,0:T(8,128)(2,1)S(1)}, u32[]{:S(2)}, u32[]{:S(2)}) collective-permute-start(bf16[34,16,128]{2,1,0:T(8,128)(2,1)S(1)} %shard_map.292), channel_id=1, source_target_pairs={{0,0},{1,8},{2,16},{3,24},{4,4},{5,12},{6,20},{7,28},{8,1},{9,9},{... | collective-permute-start | bytes 417800 | tf_op jit(solution)/shard_map/ppermute | solution.py:949
  113.2 2.8 %collective-permute-done.26.refs_3_ = bf16[34,16,128]{2,1,0:T(8,128)(2,1)S(1)} collective-permute-done((bf16[34,16,128]{2,1,0:T(8,128)(2,1)S(1)}, bf16[34,16,128]{2,1,0:T(8,128)(2,1)S(1)}, u32[]{:S(2)}, u32[]{:S(2)}) %collective-permute-start.26) | collective-permute-done | bytes 139296 | tf_op jit(solution)/shard_map/ppermute | solution.py:949
  116.0 0.5 collective-permute-start.30
  116.5 2.3 %collective-permute-done.25.refs_2_ = bf16[34,16,128]{2,1,0:T(8,128)(2,1)S(1)} collective-permute-done((bf16[34,16,128]{2,1,0:T(8,128)(2,1)S(1)}, bf16[34,16,128]{2,1,0:T(8,128)(2,1)S(1)}, u32[]{:S(2)}, u32[]{:S(2)}) %collective-permute-start.25) | collective-permute-done | bytes 139296 | tf_op jit(solution)/shard_map/ppermute | solution.py:949
  118.9 3.3 %collective-permute-done.24.refs_1_ = bf16[34,16,128]{2,1,0:T(8,128)(2,1)S(1)} collective-permute-done((bf16[34,16,128]{2,1,0:T(8,128)(2,1)S(1)}, bf16[34,16,128]{2,1,0:T(8,128)(2,1)S(1)}, u32[]{:S(2)}, u32[]{:S(2)}) %collective-permute-start.24) | collective-permute-done | bytes 139296 | tf_op jit(solution)/shard_map/ppermute | solution.py:949
  122.1 3.2 %collective-permute-start.28 = (bf16[34,16,128]{2,1,0:T(8,128)(2,1)S(1)}, bf16[34,16,128]{2,1,0:T(8,128)(2,1)S(1)}, u32[]{:S(2)}, u32[]{:S(2)}) collective-permute-start(bf16[34,16,128]{2,1,0:T(8,128)(2,1)S(1)} %collective-permute-done.24.refs_1_), channel_id=1, source_target_pairs={{0,4},{4,0},{8,12},{12,8},{16,20},{20,16},{24,28},{28,24},{1,5},{5... | collective-permute-start | bytes 417800 | tf_op jit(solution)/shard_map/ppermute | solution.py:962
  125.3 2.4 %collective-permute-start.27 = (bf16[34,16,128]{2,1,0:T(8,128)(2,1)S(1)}, bf16[34,16,128]{2,1,0:T(8,128)(2,1)S(1)}, u32[]{:S(2)}, u32[]{:S(2)}) collective-permute-start(bf16[34,16,128]{2,1,0:T(8,128)(2,1)S(1)} %collective-permute-done.23.refs_0_), channel_id=1, source_target_pairs={{0,4},{4,0},{8,12},{12,8},{16,20},{20,16},{24,28},{28,24},{1,5},{5... | collective-permute-start | bytes 417800 | tf_op jit(solution)/shard_map/ppermute | solution.py:962
  127.7 3.0 %shard_map.293 = (f32[3,4,9,32,128]{4,3,2,1,0:T(8,128)}, f32[3,20,128]{2,1,0:T(8,128)S(1)}, f32[3,20]{1,0:T(4,128)S(1)}, f32[5,3,32]{2,1,0:T(4,128)S(1)}, f32[32...) custom-call(s32[8,128]{1,0:T(8,128)S(1)} %copy-done.1, ...), custom_call_target="tpu_custom_call" | custom-call | flops 1000000 | bytes 10000 | tf_op jit(solution)/shard_map/pallas_call | solution.py:903
  130.7 0.8 shard_map.295
  131.5 0.7 shard_map.294
  132.3 1.8 %shard_map.296 = (f32[3,4,9,32,128]{4,3,2,1,0:T(8,128)}, f32[3,20,128]{2,1,0:T(8,128)}, f32[3,20]{1,0:T(4,128)}, f32[5,3,32]{2,1,0:T(4,128)}, f32[32,128]{1,0:T(...) custom-call(s32[8,128]{1,0:T(8,128)S(1)} %copy-done.1, ...), custom_call_target="tpu_custom_call", output_to_operand_aliasing={{0}: (5, {})} | custom-call | flops 1000000 | bytes 10000 | tf_op jit(solution)/shard_map/pallas_call | solution.py:903
  (32 shorter events, 0.2 us)
Async XLA Ops:
  1.8 6.8 %collective-permute-start.1 = (bf16[3,4,9,32,128]{4,3,2,1,0:T(8,128)(2,1)}, bf16[3,4,9,32,128]{4,3,2,1,0:T(8,128)(2,1)S(1)}, u32[]{:S(2)}, u32[]{:S(2)}) collective-permute-start(bf16[3,4,9,32,128]{4,3,2,1,0:T(8,128)(2,1)} %refs_0_.3), channel_id=1, source_target_pairs={{0,1},{1,0},{2,3},{3,2},{4,5},{5,4},{6,7},{7,6},{8,9},{9,8},{10,11... | collective-permute-start | bytes 2654216 | tf_op jit(solution)/shard_map/ppermute | solution.py:931
  1.9 10.5 %collective-permute-start.2 = (bf16[32,2560]{1,0:T(8,128)(2,1)S(1)}, bf16[32,2560]{1,0:T(8,128)(2,1)S(1)}, u32[]{:S(2)}, u32[]{:S(2)}) collective-permute-start(bf16[32,2560]{1,0:T(8,128)(2,1)S(1)} %get-tuple-element.130.refs_0_.refs_7_), channel_id=1, source_target_pairs={{0,1},{1,0},{2,3},{3,2},{4,5},{5,4},{6,7},{7,6},{8,9},{9,8},{10,11... | collective-permute-start | bytes 491528 | tf_op jit(solution)/shard_map/ppermute | solution.py:931
  2.4 6.2 %collective-permute-start = (bf16[32,2560]{1,0:T(8,128)(2,1)S(1)}, bf16[32,2560]{1,0:T(8,128)(2,1)S(1)}, u32[]{:S(2)}, u32[]{:S(2)}) collective-permute-start(bf16[32,2560]{1,0:T(8,128)(2,1)S(1)} %get-tuple-element.131), channel_id=1, source_target_pairs={{0,2},{1,3},{2,0},{3,1},{4,6},{5,7},{6,4},{7,5},{8,10},{9,11},{10,... | collective-permute-start | bytes 491528 | tf_op jit(solution)/shard_map/ppermute | solution.py:925
  3.7 8.8 %copy-start.1 = (s32[8,128]{1,0:T(8,128)S(1)}, s32[8,128]{1,0:T(8,128)}, u32[]{:S(2)}) copy-start(s32[8,128]{1,0:T(8,128)} %broadcast_in_dim.20.units) | copy-start | bytes 12292
  3.7 22.9 %copy-start = (bf16[3,4,9,32,128]{4,3,2,1,0:T(8,128)(2,1)S(1)}, bf16[3,4,9,32,128]{4,3,2,1,0:T(8,128)(2,1)}, u32[]{:S(2)}) copy-start(bf16[3,4,9,32,128]{4,3,2,1,0:T(8,128)(2,1)} %refs_0_.3) | copy-start | bytes 2654212
  8.6 3.8 %collective-permute-start.3 = (bf16[32,2560]{1,0:T(8,128)(2,1)S(1)}, bf16[32,2560]{1,0:T(8,128)(2,1)S(1)}, u32[]{:S(2)}, u32[]{:S(2)}) collective-permute-start(bf16[32,2560]{1,0:T(8,128)(2,1)S(1)} %collective-permute-done.refs_1_.refs_8_), channel_id=1, source_target_pairs={{0,1},{1,0},{2,3},{3,2},{4,5},{5,4},{6,7},{7,6},{8,9},{9,8},{10,11... | collective-permute-start | bytes 491528 | tf_op jit(solution)/shard_map/ppermute | solution.py:931
  8.6 4.8 %collective-permute-start.4 = (bf16[17,32,128]{2,1,0:T(8,128)(2,1)S(1)}, bf16[17,32,128]{2,1,0:T(8,128)(2,1)S(1)}, u32[]{:S(2)}, u32[]{:S(2)}) collective-permute-start(bf16[17,32,128]{2,1,0:T(8,128)(2,1)S(1)} %get-tuple-element.138.refs_3_), channel_id=1, source_target_pairs={{1,0},{3,2},{5,4},{7,6},{9,8},{11,10},{13,12},{15,14},{17,16},{19,... | collective-permute-start | bytes 417800 | tf_op jit(solution)/shard_map/ppermute | solution.py:931
  9.9 15.9 %collective-permute-start.5 = (bf16[18,32,128]{2,1,0:T(8,128)(2,1)S(1)}, bf16[18,32,128]{2,1,0:T(8,128)(2,1)S(1)}, u32[]{:S(2)}, u32[]{:S(2)}) collective-permute-start(bf16[18,32,128]{2,1,0:T(8,128)(2,1)S(1)} %get-tuple-element.144), channel_id=1, source_target_pairs={{0,2},{1,3},{2,0},{3,1},{4,6},{5,7},{6,4},{7,5},{8,10},{9,11},{10,... | collective-permute-start | bytes 442376 | tf_op jit(solution)/shard_map/ppermute | solution.py:925
  10.3 15.5 %collective-permute-start.6 = (bf16[18,32,128]{2,1,0:T(8,128)(2,1)S(1)}, bf16[18,32,128]{2,1,0:T(8,128)(2,1)S(1)}, u32[]{:S(2)}, u32[]{:S(2)}) collective-permute-start(bf16[18,32,128]{2,1,0:T(8,128)(2,1)S(1)} %get-tuple-element.146), channel_id=1, source_target_pairs={{0,3},{1,2},{2,1},{3,0},{4,7},{5,6},{6,5},{7,4},{8,11},{9,10},{10,... | collective-permute-start | bytes 442376 | tf_op jit(solution)/shard_map/ppermute | solution.py:928
  25.8 11.7 %collective-permute-start.8 = (bf16[27,32,128]{2,1,0:T(8,128)(2,1)S(1)}, bf16[27,32,128]{2,1,0:T(8,128)(2,1)S(1)}, u32[]{:S(2)}, u32[]{:S(2)}) collective-permute-start(bf16[27,32,128]{2,1,0:T(8,128)(2,1)S(1)} %get-tuple-element.155), channel_id=1, source_target_pairs={{0,3},{1,2},{2,1},{3,0},{4,7},{5,6},{6,5},{7,4},{8,11},{9,10},{10,... | collective-permute-start | bytes 663560 | tf_op jit(solution)/shard_map/ppermute | solution.py:928
  25.8 11.7 %collective-permute-start.7 = (bf16[27,32,128]{2,1,0:T(8,128)(2,1)S(1)}, bf16[27,32,128]{2,1,0:T(8,128)(2,1)S(1)}, u32[]{:S(2)}, u32[]{:S(2)}) collective-permute-start(bf16[27,32,128]{2,1,0:T(8,128)(2,1)S(1)} %get-tuple-element.153), channel_id=1, source_target_pairs={{0,2},{1,3},{2,0},{3,1},{4,6},{5,7},{6,4},{7,5},{8,10},{9,11},{10,... | collective-permute-start | bytes 663560 | tf_op jit(solution)/shard_map/ppermute | solution.py:925
  50.9 11.0 %collective-permute-start.9 = (bf16[32,1664]{1,0:T(8,128)(2,1)S(1)}, bf16[32,1664]{1,0:T(8,128)(2,1)S(1)}, u32[]{:S(2)}, u32[]{:S(2)}) collective-permute-start(bf16[32,1664]{1,0:T(8,128)(2,1)S(1)} %get-tuple-element.172), channel_id=1, source_target_pairs={{0,1},{1,0},{2,3},{3,2},{4,5},{5,4},{6,7},{7,6},{8,9},{9,8},{10,11... | collective-permute-start | bytes 319496 | tf_op jit(solution)/shard_map/ppermute | solution.py:931
  50.9 10.9 %collective-permute-start.10 = (bf16[32,1664]{1,0:T(8,128)(2,1)S(1)}, bf16[32,1664]{1,0:T(8,128)(2,1)S(1)}, u32[]{:S(2)}, u32[]{:S(2)}) collective-permute-start(bf16[32,1664]{1,0:T(8,128)(2,1)S(1)} %get-tuple-element.173), channel_id=1, source_target_pairs={{0,2},{1,3},{2,0},{3,1},{4,6},{5,7},{6,4},{7,5},{8,10},{9,11},{10,... | collective-permute-start | bytes 319496 | tf_op jit(solution)/shard_map/ppermute | solution.py:925
  52.5 9.4 %collective-permute-start.11 = (bf16[32,1664]{1,0:T(8,128)(2,1)S(1)}, bf16[32,1664]{1,0:T(8,128)(2,1)S(1)}, u32[]{:S(2)}, u32[]{:S(2)}) collective-permute-start(bf16[32,1664]{1,0:T(8,128)(2,1)S(1)} %get-tuple-element.174), channel_id=1, source_target_pairs={{0,3},{1,2},{2,1},{3,0},{4,7},{5,6},{6,5},{7,4},{8,11},{9,10},{10,... | collective-permute-start | bytes 319496 | tf_op jit(solution)/shard_map/ppermute | solution.py:928
  65.1 9.8 %collective-permute-start.12 = (bf16[4,21,16,128]{3,2,1,0:T(8,128)(2,1)S(1)}, bf16[4,21,16,128]{3,2,1,0:T(8,128)(2,1)S(1)}, u32[]{:S(2)}, u32[]{:S(2)}) collective-permute-start(bf16[4,21,16,128]{3,2,1,0:T(8,128)(2,1)S(1)} %get-tuple-element.181), channel_id=1, source_target_pairs={{0,4},{4,0},{8,12},{12,8},{16,20},{20,16},{24,28},{28,24},{1,5},{5... | collective-permute-start | bytes 1032200 | tf_op jit(solution)/shard_map/ppermute | solution.py:962
  77.9 1.9 %collective-permute-start.13 = (bf16[1952,128]{1,0:T(8,128)(2,1)S(1)}, bf16[1952,128]{1,0:T(8,128)(2,1)S(1)}, u32[]{:S(2)}, u32[]{:S(2)}) collective-permute-start(bf16[1952,128]{1,0:T(8,128)(2,1)S(1)} %get-tuple-element.187.refs_0_), channel_id=1, source_target_pairs={{0,1},{1,0},{2,3},{3,2},{4,5},{5,4},{6,7},{7,6},{8,9},{9,8},{10,11... | collective-permute-start | bytes 1499144 | tf_op jit(solution)/shard_map/ppermute | solution.py:931
  78.0 11.5 %collective-permute-start.14 = (bf16[4,18,16,128]{3,2,1,0:T(8,128)(2,1)S(1)}, bf16[4,18,16,128]{3,2,1,0:T(8,128)(2,1)S(1)}, u32[]{:S(2)}, u32[]{:S(2)}) collective-permute-start(bf16[4,18,16,128]{3,2,1,0:T(8,128)(2,1)S(1)} %get-tuple-element.194), channel_id=1, source_target_pairs={{0,4},{4,0},{8,12},{12,8},{16,20},{20,16},{24,28},{28,24},{1,5},{5... | collective-permute-start | bytes 884744 | tf_op jit(solution)/shard_map/ppermute | solution.py:962
  78.6 10.9 %collective-permute-start.15 = (bf16[2,21,16,128]{3,2,1,0:T(8,128)(2,1)S(1)}, bf16[2,21,16,128]{3,2,1,0:T(8,128)(2,1)S(1)}, u32[]{:S(2)}, u32[]{:S(2)}) collective-permute-start(bf16[2,21,16,128]{3,2,1,0:T(8,128)(2,1)S(1)} %get-tuple-element.195), channel_id=1, source_target_pairs={{0,8},{4,12},{8,0},{12,4},{16,24},{20,28},{24,16},{28,20},{1,9},{5... | collective-permute-start | bytes 516104 | tf_op jit(solution)/shard_map/ppermute | solution.py:1059
  91.2 4.2 %collective-permute-start.16 = (bf16[4,3,16,128]{3,2,1,0:T(8,128)(2,1)S(1)}, bf16[4,3,16,128]{3,2,1,0:T(8,128)(2,1)S(1)}, u32[]{:S(2)}, u32[]{:S(2)}) collective-permute-start(bf16[4,3,16,128]{3,2,1,0:T(8,128)(2,1)S(1)} %get-tuple-element.203), channel_id=1, source_target_pairs={{0,4},{4,0},{8,12},{12,8},{16,20},{20,16},{24,28},{28,24},{1,5},{5... | collective-permute-start | bytes 147464 | tf_op jit(solution)/shard_map/ppermute | solution.py:962
  91.7 9.1 %collective-permute-start.20 = (bf16[21,16,128]{2,1,0:T(8,128)(2,1)S(1)}, bf16[21,16,128]{2,1,0:T(8,128)(2,1)S(1)}, u32[]{:S(2)}, u32[]{:S(2)}) collective-permute-start(bf16[21,16,128]{2,1,0:T(8,128)(2,1)S(1)} %get-tuple-element.210), channel_id=1, source_target_pairs={{0,16},{4,20},{8,24},{12,28},{16,0},{20,4},{24,8},{28,12},{1,17},{... | collective-permute-start | bytes 258056 | tf_op jit(solution)/shard_map/ppermute | solution.py:1065
  92.3 11.9 %collective-permute-start.22 = (bf16[32,1664]{1,0:T(8,128)(2,1)S(1)}, bf16[32,1664]{1,0:T(8,128)(2,1)S(1)}, u32[]{:S(2)}, u32[]{:S(2)}) collective-permute-start(bf16[32,1664]{1,0:T(8,128)(2,1)S(1)} %get-tuple-element.214), channel_id=1, source_target_pairs={{0,2},{1,3},{2,0},{3,1},{4,6},{5,7},{6,4},{7,5},{8,10},{9,11},{10,... | collective-permute-start | bytes 319496 | tf_op jit(solution)/shard_map/ppermute | solution.py:925
  95.4 10.5 %collective-permute-start.17 = (bf16[21,16,128]{2,1,0:T(8,128)(2,1)S(1)}, bf16[21,16,128]{2,1,0:T(8,128)(2,1)S(1)}, u32[]{:S(2)}, u32[]{:S(2)}) collective-permute-start(bf16[21,16,128]{2,1,0:T(8,128)(2,1)S(1)} %get-tuple-element.205), channel_id=1, source_target_pairs={{0,8},{4,12},{8,0},{12,4},{16,24},{20,28},{24,16},{28,20},{1,9},{5... | collective-permute-start | bytes 258056 | tf_op jit(solution)/shard_map/ppermute | solution.py:968
  95.8 10.0 %collective-permute-start.18 = (bf16[21,16,128]{2,1,0:T(8,128)(2,1)S(1)}, bf16[21,16,128]{2,1,0:T(8,128)(2,1)S(1)}, u32[]{:S(2)}, u32[]{:S(2)}) collective-permute-start(bf16[21,16,128]{2,1,0:T(8,128)(2,1)S(1)} %get-tuple-element.206), channel_id=1, source_target_pairs={{0,16},{4,20},{8,24},{12,28},{16,0},{20,4},{24,8},{28,12},{1,17},{... | collective-permute-start | bytes 258056 | tf_op jit(solution)/shard_map/ppermute | solution.py:968
  97.0 8.9 %collective-permute-start.19 = (bf16[21,16,128]{2,1,0:T(8,128)(2,1)S(1)}, bf16[21,16,128]{2,1,0:T(8,128)(2,1)S(1)}, u32[]{:S(2)}, u32[]{:S(2)}) collective-permute-start(bf16[21,16,128]{2,1,0:T(8,128)(2,1)S(1)} %get-tuple-element.207), channel_id=1, source_target_pairs={{0,24},{4,28},{8,16},{12,20},{16,8},{20,12},{24,0},{28,4},{1,25},{... | collective-permute-start | bytes 258056 | tf_op jit(solution)/shard_map/ppermute | solution.py:968
  100.9 4.9 %collective-permute-start.21 = (bf16[9,16,128]{2,1,0:T(8,128)(2,1)S(1)}, bf16[9,16,128]{2,1,0:T(8,128)(2,1)S(1)}, u32[]{:S(2)}, u32[]{:S(2)}) collective-permute-start(bf16[9,16,128]{2,1,0:T(8,128)(2,1)S(1)} %get-tuple-element.213), channel_id=1, source_target_pairs={{2,0},{3,1},{6,4},{7,5},{10,8},{11,9},{14,12},{15,13},{18,16},{19,... | collective-permute-start | bytes 110600 | tf_op jit(solution)/shard_map/ppermute | solution.py:1090
  105.9 10.1 %collective-permute-start.26 = (bf16[34,16,128]{2,1,0:T(8,128)(2,1)S(1)}, bf16[34,16,128]{2,1,0:T(8,128)(2,1)S(1)}, u32[]{:S(2)}, u32[]{:S(2)}) collective-permute-start(bf16[34,16,128]{2,1,0:T(8,128)(2,1)S(1)} %shard_map.292), channel_id=1, source_target_pairs={{0,24},{1,16},{2,8},{3,0},{4,28},{5,20},{6,12},{7,4},{8,25},{9,17}... | collective-permute-start | bytes 417800 | tf_op jit(solution)/shard_map/ppermute | solution.py:949
  107.0 11.8 %collective-permute-start.25 = (bf16[34,16,128]{2,1,0:T(8,128)(2,1)S(1)}, bf16[34,16,128]{2,1,0:T(8,128)(2,1)S(1)}, u32[]{:S(2)}, u32[]{:S(2)}) collective-permute-start(bf16[34,16,128]{2,1,0:T(8,128)(2,1)S(1)} %shard_map.292), channel_id=1, source_target_pairs={{0,16},{1,24},{2,0},{3,8},{4,20},{5,28},{6,4},{7,12},{8,17},{9,25}... | collective-permute-start | bytes 417800 | tf_op jit(solution)/shard_map/ppermute | solution.py:949
  108.4 13.7 %collective-permute-start.24 = (bf16[34,16,128]{2,1,0:T(8,128)(2,1)S(1)}, bf16[34,16,128]{2,1,0:T(8,128)(2,1)S(1)}, u32[]{:S(2)}, u32[]{:S(2)}) collective-permute-start(bf16[34,16,128]{2,1,0:T(8,128)(2,1)S(1)} %shard_map.292), channel_id=1, source_target_pairs={{0,8},{1,0},{2,24},{3,16},{4,12},{5,4},{6,28},{7,20},{8,9},{9,1},{... | collective-permute-start | bytes 417800 | tf_op jit(solution)/shard_map/ppermute | solution.py:949
  111.0 14.3 %collective-permute-start.23 = (bf16[34,16,128]{2,1,0:T(8,128)(2,1)S(1)}, bf16[34,16,128]{2,1,0:T(8,128)(2,1)S(1)}, u32[]{:S(2)}, u32[]{:S(2)}) collective-permute-start(bf16[34,16,128]{2,1,0:T(8,128)(2,1)S(1)} %shard_map.292), channel_id=1, source_target_pairs={{0,0},{1,8},{2,16},{3,24},{4,4},{5,12},{6,20},{7,28},{8,1},{9,9},{... | collective-permute-start | bytes 417800 | tf_op jit(solution)/shard_map/ppermute | solution.py:949
  116.0 16.3 %collective-permute-start.30 = (bf16[34,16,128]{2,1,0:T(8,128)(2,1)S(1)}, bf16[34,16,128]{2,1,0:T(8,128)(2,1)S(1)}, u32[]{:S(2)}, u32[]{:S(2)}) collective-permute-start(bf16[34,16,128]{2,1,0:T(8,128)(2,1)S(1)} %collective-permute-done.26.refs_3_), channel_id=1, source_target_pairs={{0,4},{4,0},{8,12},{12,8},{16,20},{20,16},{24,28},{28,24},{1,5},{5... | collective-permute-start | bytes 417800 | tf_op jit(solution)/shard_map/ppermute | solution.py:962
  118.9 13.4 %collective-permute-start.29 = (bf16[34,16,128]{2,1,0:T(8,128)(2,1)S(1)}, bf16[34,16,128]{2,1,0:T(8,128)(2,1)S(1)}, u32[]{:S(2)}, u32[]{:S(2)}) collective-permute-start(bf16[34,16,128]{2,1,0:T(8,128)(2,1)S(1)} %collective-permute-done.25.refs_2_), channel_id=1, source_target_pairs={{0,4},{4,0},{8,12},{12,8},{16,20},{20,16},{24,28},{28,24},{1,5},{5... | collective-permute-start | bytes 417800 | tf_op jit(solution)/shard_map/ppermute | solution.py:962
  122.1 10.1 %collective-permute-start.28 = (bf16[34,16,128]{2,1,0:T(8,128)(2,1)S(1)}, bf16[34,16,128]{2,1,0:T(8,128)(2,1)S(1)}, u32[]{:S(2)}, u32[]{:S(2)}) collective-permute-start(bf16[34,16,128]{2,1,0:T(8,128)(2,1)S(1)} %collective-permute-done.24.refs_1_), channel_id=1, source_target_pairs={{0,4},{4,0},{8,12},{12,8},{16,20},{20,16},{24,28},{28,24},{1,5},{5... | collective-permute-start | bytes 417800 | tf_op jit(solution)/shard_map/ppermute | solution.py:962
  125.3 7.0 %collective-permute-start.27 = (bf16[34,16,128]{2,1,0:T(8,128)(2,1)S(1)}, bf16[34,16,128]{2,1,0:T(8,128)(2,1)S(1)}, u32[]{:S(2)}, u32[]{:S(2)}) collective-permute-start(bf16[34,16,128]{2,1,0:T(8,128)(2,1)S(1)} %collective-permute-done.23.refs_0_), channel_id=1, source_target_pairs={{0,4},{4,0},{8,12},{12,8},{16,20},{20,16},{24,28},{28,24},{1,5},{5... | collective-permute-start | bytes 417800 | tf_op jit(solution)/shard_map/ppermute | solution.py:962

commit v8 on v7

--- a/solution.py
+++ b/solution.py
@@ -892,7 +892,7 @@
 
 
 def call(body, outs, scratch, args, last=False, limit=VMEM, in_place=(), aliases={}, flops=10**6):
-    place = jax.ShapeDtypeStruct if last else pltpu.VMEM
+    final = range(len(outs)) if last is True else last or ()
 
     def space(i):
         return pl.BlockSpec(memory_space=pl.ANY if i in in_place else pltpu.VMEM)
@@ -902,7 +902,7 @@
 
     return pl.pallas_call(
         placed if args[0].dtype == jnp.int32 else body,
-        out_shape=[place(s, d) for s, d in outs],
+        out_shape=[(jax.ShapeDtypeStruct if i in final else pltpu.VMEM)(*o) for i, o in enumerate(outs)],
         in_specs=[space(i) for i in range(len(args))],
         out_specs=[space(len(args) + i) for i in range(len(outs))],
         scratch_shapes=[s if callable(getattr(s, "get_ref_aval", None)) else pltpu.VMEM(*s) for s in scratch],
@@ -1081,9 +1081,11 @@
         ],
         (meta, d0, d0_other, y0, cst0, st, sums1, sums2, *u),
     )
-    received = across(other)
+    if not direct:
+        received = across(other)
     if direct:
         parts1 = along_z([wg1, gs], [got1, over_y(gs_send)])
+        received = across(after(other, parts1[0]))
         total, extra = call(
             sum_kernel, [((12, 16, 128), BF), ((9, 16, 128), BF)], [], (meta, own2, after(got2, parts1[0]))
         )
@@ -1101,7 +1103,7 @@
     rows = [(cw.shape, F32), (cb.shape, F32), ((5, 3, 32), F32), (s0.shape, F32), (s1.shape, F32), (s2.shape, F32)]
     wholes = [(bb.shape, F32), ((5, 3, 32), F32), ((5, 3, 32), F32)]
     grad_conv, *half, grad_bb, grad_gains, grad_shifts = call(
-        near_out_kernel, [(conv.shape, F32)] + rows + wholes, room, (meta, *grads[:4]), True, in_place=(5,)
+        near_out_kernel, [(conv.shape, F32)] + rows + wholes, room, (meta, *grads[:4]), (0, 7, 8, 9), in_place=(5,)
     )
     mine, own = after((mine, own), *half)
     box_rows, class_rows = bcot.shape[1], ccot.shape[1]

time: 135 us -> 133 us (0.985)
  waiting for transfers between devices: 15.9 us -> 14.4 us
    ppermute x4, waiting for transfers between devices: 8.41 us -> 6.5 us  [over_z(): parts.append(lax.ppermute(v, ('dp', 'chan'), pairs))]
    ppermute x7, waiting for transfers between devices: 1.58 us -> 3 us  [over_y(): return lax.ppermute(v, 'dp', [(i, i ^ 1) for i in range(8)])]
where the time goes in v8:
time: 133 us
  blocking collectives  58.5 us (44%)
  starting transfers between devices  32.6 us (25%)
  Pallas kernels  24.9 us (19%)
  waiting for transfers between devices  14.4 us (11%)
  between operations  1.69 us (1%)
    all_to_all x6, blocking collectives, exchange(): st = lax.all_to_all(st, 'dp', 0, 0, tiled=True)  58.5 us
    pallas_call x23, Pallas kernels, call(): pl.pallas_call(placed if args[0].dtype == jnp.int32 else body, out_shape=...  24.9 us
    ppermute x7, starting transfers between devices, over_y(): return lax.ppermute(v, 'dp', [(i, i ^ 1) for i in range(8)])  8.18 us
    ppermute x4, starting transfers between devices, over_z(): parts.append(lax.ppermute(v, ('dp', 'chan'), pairs))  7.25 us
    ppermute x4, waiting for transfers between devices, over_z(): parts.append(lax.ppermute(v, ('dp', 'chan'), pairs))  6.5 us
    ppermute x3, starting transfers between devices, along_z(): lax.ppermute(v, 'dp', [(i, i ^ 2 * k + 2) for i in range(8)])  4.39 us
    ppermute x5, starting transfers between devices, across(): return lax.ppermute(v, 'chan', [(i, i ^ 2) for i in range(4)])  4.11 us
    ppermute x7, waiting for transfers between devices, over_y(): return lax.ppermute(v, 'dp', [(i, i ^ 1) for i in range(8)])  3 us
  transfers between devices with their start and end apart: 31, of which 8 were waited for; matrix products, arithmetic and copies ran while one was open for 0% of the time, Pallas kernels for 7%

profile of v8, /device:TPU:2, one launch (start us, length us, event | category | flops | bytes accessed | tf_op | source)
XLA Modules:
  0.0 132.6 jit_solution(343985827170728422)
XLA Ops:
  0.6 1.2 shard_map.274
  1.8 0.1 collective-permute-start.1
  1.9 0.5 collective-permute-start.2
  3.1 0.6 broadcast_in_dim.20.units
  3.7 2.2 %shard_map.275 = (bf16[17,32,128]{2,1,0:T(8,128)(2,1)S(1)}, bf16[17,32,128]{2,1,0:T(8,128)(2,1)S(1)}, bf16[18,32,128]{2,1,0:T(8,128)(2,1)S(1)}, bf16[18,32,128]{...) custom-call(s32[8,128]{1,0:T(8,128)} %broadcast_in_dim.20.units, ...), custom_call_target="tpu_custom_call" | custom-call | flops 2000000000 | bytes 10000 | tf_op jit(solution)/shard_map/pallas_call | solution.py:903
  5.9 2.7 %collective-permute-done.refs_1_.refs_8_ = bf16[32,2560]{1,0:T(8,128)(2,1)S(1)} collective-permute-done((bf16[32,2560]{1,0:T(8,128)(2,1)S(1)}, bf16[32,2560]{1,0:T(8,128)(2,1)S(1)}, u32[]{:S(2)}, u32[]{:S(2)}) %collective-permute-start) | collective-permute-done | bytes 163872 | tf_op jit(solution)/shard_map/ppermute | solution.py:925
  8.6 0.0 collective-permute-done.1.refs_1_
  8.6 0.0 collective-permute-start.3
  8.6 1.3 collective-permute-start.4
  9.9 0.3 collective-permute-start.5
  10.3 2.2 %collective-permute-start.6 = (bf16[18,32,128]{2,1,0:T(8,128)(2,1)S(1)}, bf16[18,32,128]{2,1,0:T(8,128)(2,1)S(1)}, u32[]{:S(2)}, u32[]{:S(2)}) collective-permute-start(bf16[18,32,128]{2,1,0:T(8,128)(2,1)S(1)} %get-tuple-element.147), channel_id=1, source_target_pairs={{0,3},{1,2},{2,1},{3,0},{4,7},{5,6},{6,5},{7,4},{8,11},{9,10},{10,... | collective-permute-start | bytes 442376 | tf_op jit(solution)/shard_map/ppermute | solution.py:928
  12.5 1.0 shard_map.276
  13.5 12.3 %all_to_all.30.refs_1_ = f32[8,8,128]{2,1,0:T(8,128)S(1)} all-to-all(f32[8,8,128]{2,1,0:T(8,128)S(1)} %get-tuple-element.140), channel_id=1, replica_groups=mesh['dp'=8,'chan'=4] {'dp'}, dimensions={0} | all-to-all | bytes 65536 | tf_op jit(solution)/shard_map/all_to_all | solution.py:935
  25.8 0.7 collective-permute-start.7
  26.5 0.2 shard_map.277
  26.7 1.6 %shard_map.278 = (bf16[1920,128]{1,0:T(8,128)(2,1)S(1)}, f32[1920,128]{1,0:T(8,128)S(1)}, f32[8,8,128]{2,1,0:T(8,128)S(1)}, f32[16,128]{1,0:T(8,128)S(1)}) custom-call(s32[8,128]{1,0:T(8,128)S(1)} %copy-done.1, f32[1920,128]{1,0:T(8,128)S(1)} %get-tuple-element.137.refs_0_.refs_6_.refs_2_, f32[8,8,128]{2,1,0:T(8,128)S(1)} %all_to_all.30.refs_1_, ...), custom_call_target="tpu_custom_call" | custom-call | flops 1000000 | bytes 10000 | tf_op jit(solution)/shard_map/pallas_call | solution.py:903
  28.4 9.1 %all_to_all.31.refs_1_ = f32[8,8,128]{2,1,0:T(8,128)S(1)} all-to-all(f32[8,8,128]{2,1,0:T(8,128)S(1)} %get-tuple-element.153), channel_id=1, replica_groups=mesh['dp'=8,'chan'=4] {'dp'}, dimensions={0} | all-to-all | bytes 65536 | tf_op jit(solution)/shard_map/all_to_all | solution.py:935
  37.5 0.2 shard_map.279
  37.7 1.6 %shard_map.280 = (bf16[1920,128]{1,0:T(8,128)(2,1)S(1)}, f32[1920,128]{1,0:T(8,128)S(1)}, f32[8,8,128]{2,1,0:T(8,128)S(1)}, f32[16,128]{1,0:T(8,128)S(1)}) custom-call(s32[8,128]{1,0:T(8,128)S(1)} %copy-done.1, f32[1920,128]{1,0:T(8,128)S(1)} %get-tuple-element.152.refs_0_.refs_6_.refs_1_, f32[8,8,128]{2,1,0:T(8,128)S(1)} %all_to_all.31.refs_1_, ...), custom_call_target="tpu_custom_call" | custom-call | flops 1000000 | bytes 10000 | tf_op jit(solution)/shard_map/pallas_call | solution.py:903
  39.4 9.1 %all_to_all.32.refs_1_ = f32[8,8,128]{2,1,0:T(8,128)S(1)} all-to-all(f32[8,8,128]{2,1,0:T(8,128)S(1)} %get-tuple-element.161), channel_id=1, replica_groups=mesh['dp'=8,'chan'=4] {'dp'}, dimensions={0} | all-to-all | bytes 65536 | tf_op jit(solution)/shard_map/all_to_all | solution.py:935
  48.4 1.7 %shard_map.281 = (f32[1920,128]{1,0:T(8,128)S(1)}, f32[8,8,128]{2,1,0:T(8,128)S(1)}, f32[16,128]{1,0:T(8,128)S(1)}, bf16[1664,256]{1,0:T(8,128)(2,1)S(1)}, bf16[...) custom-call(s32[8,128]{1,0:T(8,128)S(1)} %copy-done.1, f32[1920,128]{1,0:T(8,128)S(1)} %get-tuple-element.160.refs_0_.refs_1_, ...), custom_call_target="tpu_custom_call" | custom-call | flops 1000000 | bytes 10000 | tf_op jit(solution)/shard_map/pallas_call | solution.py:903
  50.1 0.7 shard_map.282
  50.9 0.1 collective-permute-start.9
  50.9 1.5 %collective-permute-start.10 = (bf16[32,1664]{1,0:T(8,128)(2,1)S(1)}, bf16[32,1664]{1,0:T(8,128)(2,1)S(1)}, u32[]{:S(2)}, u32[]{:S(2)}) collective-permute-start(bf16[32,1664]{1,0:T(8,128)(2,1)S(1)} %get-tuple-element.174), channel_id=1, source_target_pairs={{0,2},{1,3},{2,0},{3,1},{4,6},{5,7},{6,4},{7,5},{8,10},{9,11},{10,... | collective-permute-start | bytes 319496 | tf_op jit(solution)/shard_map/ppermute | solution.py:925
  52.5 0.3 collective-permute-start.11
  52.8 9.0 %all_to_all.33.refs_3_ = f32[8,8,128]{2,1,0:T(8,128)S(1)} all-to-all(f32[8,8,128]{2,1,0:T(8,128)S(1)} %get-tuple-element.172), channel_id=1, replica_groups=mesh['dp'=8,'chan'=4] {'dp'}, dimensions={0} | all-to-all | bytes 65536 | tf_op jit(solution)/shard_map/all_to_all | solution.py:935
  61.9 3.2 %shard_map.283 = (f32[1920,128]{1,0:T(8,128)S(1)}, f32[8,8,128]{2,1,0:T(8,128)S(1)}, f32[8,128]{1,0:T(8,128)S(1)}, bf16[8,21,16,128]{3,2,1,0:T(8,128)(2,1)S(1)}, bf16[4,21,16,128]{3,2,1,0:T(8,128)(2,1)S(1)}) custom-call(s32[8,128]{1,0:T(8,128)S(1)} %copy-done.1, f32[1920,128]{1,0:T(8,128)S(1)} %get-tuple-element.168.refs_0_, ...), custom_call_target="tpu_custom_call" | custom-call | flops 1000000 | bytes 10000 | tf_op jit(solution)/shard_map/pallas_call | solution.py:903
  65.1 0.5 collective-permute-start.12
  65.6 9.3 %all_to_all.34.refs_3_ = f32[8,8,128]{2,1,0:T(8,128)S(1)} all-to-all(f32[8,8,128]{2,1,0:T(8,128)S(1)} %get-tuple-element.183), channel_id=1, replica_groups=mesh['dp'=8,'chan'=4] {'dp'}, dimensions={0} | all-to-all | bytes 65536 | tf_op jit(solution)/shard_map/all_to_all | solution.py:935
  74.9 3.0 %shard_map.284 = (bf16[1952,128]{1,0:T(8,128)(2,1)S(1)}, f32[8,8,128]{2,1,0:T(8,128)S(1)}, f32[8,128]{1,0:T(8,128)S(1)}, bf16[8,18,16,128]{3,2,1,0:T(8,128)(2,1)S(1)}, bf16[4,18,16,128]{3,2,1,0:T(8,128)(2,1)S(1)}) custom-call(s32[8,128]{1,0:T(8,128)S(1)} %copy-done.1, f32[1920,128]{1,0:T(8,128)S(1)} %get-tuple-element.180.refs_0_, ...), custom_call_target="tpu_custom_call" | custom-call | flops 1000000 | bytes 10000 | tf_op jit(solution)/shard_map/pallas_call | solution.py:903
  77.9 0.1 collective-permute-start.13
  78.0 0.5 collective-permute-start.14
  78.5 0.1 shard_map.285
  78.6 0.8 collective-permute-start.15
  79.4 0.5 collective-permute-done.13.other.refs_1_
  79.8 9.6 %all_to_all.35.st = f32[8,8,128]{2,1,0:T(8,128)S(1)} all-to-all(f32[8,8,128]{2,1,0:T(8,128)S(1)} %shard_map.286), channel_id=1, replica_groups=mesh['dp'=8,'chan'=4] {'dp'}, dimensions={0} | all-to-all | bytes 65536 | tf_op jit(solution)/shard_map/all_to_all | solution.py:935
  89.5 1.7 %shard_map.288 = (bf16[32,1664]{1,0:T(8,128)(2,1)S(1)}, bf16[32,1664]{1,0:T(8,128)(2,1)S(1)}, bf16[8,3,16,128]{3,2,1,0:T(8,128)(2,1)S(1)}, bf16[4,3,16,128]{3,2,1,0:T(8,128)(2,1)S(1)}, bf16[1,16,128]{2,1,0:T(8,128)(2,1)S(1)}) custom-call(s32[8,128]{1,0:T(8,128)S(1)} %copy-done.1, bf16[1952,128]{1,0:T(8,128)(2,1)S(1)} %get-tuple-element.188.refs_0_, ...), custom_call_target="tpu_custom_call" | custom-call | flops 1000000 | bytes 10000 | tf_op jit(solution)/shard_map/pallas_call | solution.py:903
  91.2 0.5 collective-permute-start.16
  91.7 0.6 collective-permute-start.20
  92.3 3.0 %collective-permute-done.16.refs_3_ = bf16[4,3,16,128]{3,2,1,0:T(8,128)(2,1)S(1)} collective-permute-done((bf16[4,3,16,128]{3,2,1,0:T(8,128)(2,1)S(1)}, bf16[4,3,16,128]{3,2,1,0:T(8,128)(2,1)S(1)}, u32[]{:S(2)}, u32[]{:S(2)}) %collective-permute-start.16) | collective-permute-done | bytes 49184 | tf_op jit(solution)/shard_map/ppermute | solution.py:962
  95.3 0.1 shard_map.289
  95.4 1.5 %collective-permute-start.22 = (bf16[32,1664]{1,0:T(8,128)(2,1)S(1)}, bf16[32,1664]{1,0:T(8,128)(2,1)S(1)}, u32[]{:S(2)}, u32[]{:S(2)}) collective-permute-start(bf16[32,1664]{1,0:T(8,128)(2,1)S(1)} %get-tuple-element.216), channel_id=1, source_target_pairs={{0,2},{1,3},{2,0},{3,1},{4,6},{5,7},{6,4},{7,5},{8,10},{9,11},{10,... | collective-permute-start | bytes 319496 | tf_op jit(solution)/shard_map/ppermute | solution.py:925
  96.9 0.4 collective-permute-start.17
  97.3 0.7 collective-permute-start.18
  98.0 3.3 %collective-permute-start.19 = (bf16[21,16,128]{2,1,0:T(8,128)(2,1)S(1)}, bf16[21,16,128]{2,1,0:T(8,128)(2,1)S(1)}, u32[]{:S(2)}, u32[]{:S(2)}) collective-permute-start(bf16[21,16,128]{2,1,0:T(8,128)(2,1)S(1)} %get-tuple-element.208), channel_id=1, source_target_pairs={{0,24},{4,28},{8,16},{12,20},{16,8},{20,12},{24,0},{28,4},{1,25},{... | collective-permute-start | bytes 258056 | tf_op jit(solution)/shard_map/ppermute | solution.py:968
  101.3 2.8 %collective-permute-start.21 = (bf16[9,16,128]{2,1,0:T(8,128)(2,1)S(1)}, bf16[9,16,128]{2,1,0:T(8,128)(2,1)S(1)}, u32[]{:S(2)}, u32[]{:S(2)}) collective-permute-start(bf16[9,16,128]{2,1,0:T(8,128)(2,1)S(1)} %get-tuple-element.214), channel_id=1, source_target_pairs={{2,0},{3,1},{6,4},{7,5},{10,8},{11,9},{14,12},{15,13},{18,16},{19,... | collective-permute-start | bytes 110600 | tf_op jit(solution)/shard_map/ppermute | solution.py:1092
  104.1 1.6 %collective-permute-done.21.refs_5_ = bf16[9,16,128]{2,1,0:T(8,128)(2,1)S(1)} collective-permute-done((bf16[9,16,128]{2,1,0:T(8,128)(2,1)S(1)}, bf16[9,16,128]{2,1,0:T(8,128)(2,1)S(1)}, u32[]{:S(2)}, u32[]{:S(2)}) %collective-permute-start.21) | collective-permute-done | bytes 36896 | tf_op jit(solution)/shard_map/ppermute | solution.py:1092
  105.7 0.1 shard_map.292
  105.8 1.2 collective-permute-start.26
  107.0 1.4 %collective-permute-start.25 = (bf16[34,16,128]{2,1,0:T(8,128)(2,1)S(1)}, bf16[34,16,128]{2,1,0:T(8,128)(2,1)S(1)}, u32[]{:S(2)}, u32[]{:S(2)}) collective-permute-start(bf16[34,16,128]{2,1,0:T(8,128)(2,1)S(1)} %shard_map.292), channel_id=1, source_target_pairs={{0,16},{1,24},{2,0},{3,8},{4,20},{5,28},{6,4},{7,12},{8,17},{9,25}... | collective-permute-start | bytes 417800 | tf_op jit(solution)/shard_map/ppermute | solution.py:949
  108.4 2.4 %collective-permute-start.24 = (bf16[34,16,128]{2,1,0:T(8,128)(2,1)S(1)}, bf16[34,16,128]{2,1,0:T(8,128)(2,1)S(1)}, u32[]{:S(2)}, u32[]{:S(2)}) collective-permute-start(bf16[34,16,128]{2,1,0:T(8,128)(2,1)S(1)} %shard_map.292), channel_id=1, source_target_pairs={{0,8},{1,0},{2,24},{3,16},{4,12},{5,4},{6,28},{7,20},{8,9},{9,1},{... | collective-permute-start | bytes 417800 | tf_op jit(solution)/shard_map/ppermute | solution.py:949
  110.9 2.2 %collective-permute-start.23 = (bf16[34,16,128]{2,1,0:T(8,128)(2,1)S(1)}, bf16[34,16,128]{2,1,0:T(8,128)(2,1)S(1)}, u32[]{:S(2)}, u32[]{:S(2)}) collective-permute-start(bf16[34,16,128]{2,1,0:T(8,128)(2,1)S(1)} %shard_map.292), channel_id=1, source_target_pairs={{0,0},{1,8},{2,16},{3,24},{4,4},{5,12},{6,20},{7,28},{8,1},{9,9},{... | collective-permute-start | bytes 417800 | tf_op jit(solution)/shard_map/ppermute | solution.py:949
  113.0 2.1 %collective-permute-done.26.refs_3_ = bf16[34,16,128]{2,1,0:T(8,128)(2,1)S(1)} collective-permute-done((bf16[34,16,128]{2,1,0:T(8,128)(2,1)S(1)}, bf16[34,16,128]{2,1,0:T(8,128)(2,1)S(1)}, u32[]{:S(2)}, u32[]{:S(2)}) %collective-permute-start.26) | collective-permute-done | bytes 139296 | tf_op jit(solution)/shard_map/ppermute | solution.py:949
  115.2 1.5 %collective-permute-start.30 = (bf16[34,16,128]{2,1,0:T(8,128)(2,1)S(1)}, bf16[34,16,128]{2,1,0:T(8,128)(2,1)S(1)}, u32[]{:S(2)}, u32[]{:S(2)}) collective-permute-start(bf16[34,16,128]{2,1,0:T(8,128)(2,1)S(1)} %collective-permute-done.26.refs_3_), channel_id=1, source_target_pairs={{0,4},{4,0},{8,12},{12,8},{16,20},{20,16},{24,28},{28,24},{1,5},{5... | collective-permute-start | bytes 417800 | tf_op jit(solution)/shard_map/ppermute | solution.py:962
  116.7 1.5 %collective-permute-done.25.refs_2_ = bf16[34,16,128]{2,1,0:T(8,128)(2,1)S(1)} collective-permute-done((bf16[34,16,128]{2,1,0:T(8,128)(2,1)S(1)}, bf16[34,16,128]{2,1,0:T(8,128)(2,1)S(1)}, u32[]{:S(2)}, u32[]{:S(2)}) %collective-permute-start.25) | collective-permute-done | bytes 139296 | tf_op jit(solution)/shard_map/ppermute | solution.py:949
  118.2 1.6 %collective-permute-start.29 = (bf16[34,16,128]{2,1,0:T(8,128)(2,1)S(1)}, bf16[34,16,128]{2,1,0:T(8,128)(2,1)S(1)}, u32[]{:S(2)}, u32[]{:S(2)}) collective-permute-start(bf16[34,16,128]{2,1,0:T(8,128)(2,1)S(1)} %collective-permute-done.25.refs_2_), channel_id=1, source_target_pairs={{0,4},{4,0},{8,12},{12,8},{16,20},{20,16},{24,28},{28,24},{1,5},{5... | collective-permute-start | bytes 417800 | tf_op jit(solution)/shard_map/ppermute | solution.py:962
  119.7 2.4 %collective-permute-done.24.refs_1_ = bf16[34,16,128]{2,1,0:T(8,128)(2,1)S(1)} collective-permute-done((bf16[34,16,128]{2,1,0:T(8,128)(2,1)S(1)}, bf16[34,16,128]{2,1,0:T(8,128)(2,1)S(1)}, u32[]{:S(2)}, u32[]{:S(2)}) %collective-permute-start.24) | collective-permute-done | bytes 139296 | tf_op jit(solution)/shard_map/ppermute | solution.py:949
  122.1 1.5 %collective-permute-start.28 = (bf16[34,16,128]{2,1,0:T(8,128)(2,1)S(1)}, bf16[34,16,128]{2,1,0:T(8,128)(2,1)S(1)}, u32[]{:S(2)}, u32[]{:S(2)}) collective-permute-start(bf16[34,16,128]{2,1,0:T(8,128)(2,1)S(1)} %collective-permute-done.24.refs_1_), channel_id=1, source_target_pairs={{0,4},{4,0},{8,12},{12,8},{16,20},{20,16},{24,28},{28,24},{1,5},{5... | collective-permute-start | bytes 417800 | tf_op jit(solution)/shard_map/ppermute | solution.py:962
  123.6 0.5 collective-permute-done.23.refs_0_
  124.1 2.0 %collective-permute-start.27 = (bf16[34,16,128]{2,1,0:T(8,128)(2,1)S(1)}, bf16[34,16,128]{2,1,0:T(8,128)(2,1)S(1)}, u32[]{:S(2)}, u32[]{:S(2)}) collective-permute-start(bf16[34,16,128]{2,1,0:T(8,128)(2,1)S(1)} %collective-permute-done.23.refs_0_), channel_id=1, source_target_pairs={{0,4},{4,0},{8,12},{12,8},{16,20},{20,16},{24,28},{28,24},{1,5},{5... | collective-permute-start | bytes 417800 | tf_op jit(solution)/shard_map/ppermute | solution.py:962
  126.1 3.0 %shard_map.293 = (f32[3,4,9,32,128]{4,3,2,1,0:T(8,128)}, f32[3,20,128]{2,1,0:T(8,128)S(1)}, f32[3,20]{1,0:T(4,128)S(1)}, f32[5,3,32]{2,1,0:T(4,128)S(1)}, f32[32...) custom-call(s32[8,128]{1,0:T(8,128)S(1)} %copy-done.1, ...), custom_call_target="tpu_custom_call" | custom-call | flops 1000000 | bytes 10000 | tf_op jit(solution)/shard_map/pallas_call | solution.py:903
  129.1 0.8 shard_map.295
  129.9 0.7 shard_map.294
  130.6 1.8 %shard_map.296 = (f32[3,4,9,32,128]{4,3,2,1,0:T(8,128)}, f32[3,20,128]{2,1,0:T(8,128)}, f32[3,20]{1,0:T(4,128)}, f32[5,3,32]{2,1,0:T(4,128)}, f32[32,128]{1,0:T(...) custom-call(s32[8,128]{1,0:T(8,128)S(1)} %copy-done.1, ...), custom_call_target="tpu_custom_call", output_to_operand_aliasing={{0}: (5, {})} | custom-call | flops 1000000 | bytes 10000 | tf_op jit(solution)/shard_map/pallas_call | solution.py:903
  (32 shorter events, 0.2 us)
Async XLA Ops:
  1.8 6.8 %collective-permute-start.1 = (bf16[3,4,9,32,128]{4,3,2,1,0:T(8,128)(2,1)}, bf16[3,4,9,32,128]{4,3,2,1,0:T(8,128)(2,1)S(1)}, u32[]{:S(2)}, u32[]{:S(2)}) collective-permute-start(bf16[3,4,9,32,128]{4,3,2,1,0:T(8,128)(2,1)} %refs_0_.3), channel_id=1, source_target_pairs={{0,1},{1,0},{2,3},{3,2},{4,5},{5,4},{6,7},{7,6},{8,9},{9,8},{10,11... | collective-permute-start | bytes 2654216 | tf_op jit(solution)/shard_map/ppermute | solution.py:931
  1.9 10.5 %collective-permute-start.2 = (bf16[32,2560]{1,0:T(8,128)(2,1)S(1)}, bf16[32,2560]{1,0:T(8,128)(2,1)S(1)}, u32[]{:S(2)}, u32[]{:S(2)}) collective-permute-start(bf16[32,2560]{1,0:T(8,128)(2,1)S(1)} %get-tuple-element.131.refs_0_.refs_7_), channel_id=1, source_target_pairs={{0,1},{1,0},{2,3},{3,2},{4,5},{5,4},{6,7},{7,6},{8,9},{9,8},{10,11... | collective-permute-start | bytes 491528 | tf_op jit(solution)/shard_map/ppermute | solution.py:931
  2.4 6.2 %collective-permute-start = (bf16[32,2560]{1,0:T(8,128)(2,1)S(1)}, bf16[32,2560]{1,0:T(8,128)(2,1)S(1)}, u32[]{:S(2)}, u32[]{:S(2)}) collective-permute-start(bf16[32,2560]{1,0:T(8,128)(2,1)S(1)} %get-tuple-element.132), channel_id=1, source_target_pairs={{0,2},{1,3},{2,0},{3,1},{4,6},{5,7},{6,4},{7,5},{8,10},{9,11},{10,... | collective-permute-start | bytes 491528 | tf_op jit(solution)/shard_map/ppermute | solution.py:925
  3.7 8.8 %copy-start.1 = (s32[8,128]{1,0:T(8,128)S(1)}, s32[8,128]{1,0:T(8,128)}, u32[]{:S(2)}) copy-start(s32[8,128]{1,0:T(8,128)} %broadcast_in_dim.20.units) | copy-start | bytes 12292
  3.7 22.9 %copy-start = (bf16[3,4,9,32,128]{4,3,2,1,0:T(8,128)(2,1)S(1)}, bf16[3,4,9,32,128]{4,3,2,1,0:T(8,128)(2,1)}, u32[]{:S(2)}) copy-start(bf16[3,4,9,32,128]{4,3,2,1,0:T(8,128)(2,1)} %refs_0_.3) | copy-start | bytes 2654212
  8.6 3.8 %collective-permute-start.3 = (bf16[32,2560]{1,0:T(8,128)(2,1)S(1)}, bf16[32,2560]{1,0:T(8,128)(2,1)S(1)}, u32[]{:S(2)}, u32[]{:S(2)}) collective-permute-start(bf16[32,2560]{1,0:T(8,128)(2,1)S(1)} %collective-permute-done.refs_1_.refs_8_), channel_id=1, source_target_pairs={{0,1},{1,0},{2,3},{3,2},{4,5},{5,4},{6,7},{7,6},{8,9},{9,8},{10,11... | collective-permute-start | bytes 491528 | tf_op jit(solution)/shard_map/ppermute | solution.py:931
  8.6 4.8 %collective-permute-start.4 = (bf16[17,32,128]{2,1,0:T(8,128)(2,1)S(1)}, bf16[17,32,128]{2,1,0:T(8,128)(2,1)S(1)}, u32[]{:S(2)}, u32[]{:S(2)}) collective-permute-start(bf16[17,32,128]{2,1,0:T(8,128)(2,1)S(1)} %get-tuple-element.139.refs_3_), channel_id=1, source_target_pairs={{1,0},{3,2},{5,4},{7,6},{9,8},{11,10},{13,12},{15,14},{17,16},{19,... | collective-permute-start | bytes 417800 | tf_op jit(solution)/shard_map/ppermute | solution.py:931
  9.9 15.9 %collective-permute-start.5 = (bf16[18,32,128]{2,1,0:T(8,128)(2,1)S(1)}, bf16[18,32,128]{2,1,0:T(8,128)(2,1)S(1)}, u32[]{:S(2)}, u32[]{:S(2)}) collective-permute-start(bf16[18,32,128]{2,1,0:T(8,128)(2,1)S(1)} %get-tuple-element.145), channel_id=1, source_target_pairs={{0,2},{1,3},{2,0},{3,1},{4,6},{5,7},{6,4},{7,5},{8,10},{9,11},{10,... | collective-permute-start | bytes 442376 | tf_op jit(solution)/shard_map/ppermute | solution.py:925
  10.3 15.5 %collective-permute-start.6 = (bf16[18,32,128]{2,1,0:T(8,128)(2,1)S(1)}, bf16[18,32,128]{2,1,0:T(8,128)(2,1)S(1)}, u32[]{:S(2)}, u32[]{:S(2)}) collective-permute-start(bf16[18,32,128]{2,1,0:T(8,128)(2,1)S(1)} %get-tuple-element.147), channel_id=1, source_target_pairs={{0,3},{1,2},{2,1},{3,0},{4,7},{5,6},{6,5},{7,4},{8,11},{9,10},{10,... | collective-permute-start | bytes 442376 | tf_op jit(solution)/shard_map/ppermute | solution.py:928
  25.8 11.7 %collective-permute-start.8 = (bf16[27,32,128]{2,1,0:T(8,128)(2,1)S(1)}, bf16[27,32,128]{2,1,0:T(8,128)(2,1)S(1)}, u32[]{:S(2)}, u32[]{:S(2)}) collective-permute-start(bf16[27,32,128]{2,1,0:T(8,128)(2,1)S(1)} %get-tuple-element.156), channel_id=1, source_target_pairs={{0,3},{1,2},{2,1},{3,0},{4,7},{5,6},{6,5},{7,4},{8,11},{9,10},{10,... | collective-permute-start | bytes 663560 | tf_op jit(solution)/shard_map/ppermute | solution.py:928
  25.8 11.7 %collective-permute-start.7 = (bf16[27,32,128]{2,1,0:T(8,128)(2,1)S(1)}, bf16[27,32,128]{2,1,0:T(8,128)(2,1)S(1)}, u32[]{:S(2)}, u32[]{:S(2)}) collective-permute-start(bf16[27,32,128]{2,1,0:T(8,128)(2,1)S(1)} %get-tuple-element.154), channel_id=1, source_target_pairs={{0,2},{1,3},{2,0},{3,1},{4,6},{5,7},{6,4},{7,5},{8,10},{9,11},{10,... | collective-permute-start | bytes 663560 | tf_op jit(solution)/shard_map/ppermute | solution.py:925
  50.9 11.0 %collective-permute-start.9 = (bf16[32,1664]{1,0:T(8,128)(2,1)S(1)}, bf16[32,1664]{1,0:T(8,128)(2,1)S(1)}, u32[]{:S(2)}, u32[]{:S(2)}) collective-permute-start(bf16[32,1664]{1,0:T(8,128)(2,1)S(1)} %get-tuple-element.173), channel_id=1, source_target_pairs={{0,1},{1,0},{2,3},{3,2},{4,5},{5,4},{6,7},{7,6},{8,9},{9,8},{10,11... | collective-permute-start | bytes 319496 | tf_op jit(solution)/shard_map/ppermute | solution.py:931
  50.9 10.9 %collective-permute-start.10 = (bf16[32,1664]{1,0:T(8,128)(2,1)S(1)}, bf16[32,1664]{1,0:T(8,128)(2,1)S(1)}, u32[]{:S(2)}, u32[]{:S(2)}) collective-permute-start(bf16[32,1664]{1,0:T(8,128)(2,1)S(1)} %get-tuple-element.174), channel_id=1, source_target_pairs={{0,2},{1,3},{2,0},{3,1},{4,6},{5,7},{6,4},{7,5},{8,10},{9,11},{10,... | collective-permute-start | bytes 319496 | tf_op jit(solution)/shard_map/ppermute | solution.py:925
  52.5 9.4 %collective-permute-start.11 = (bf16[32,1664]{1,0:T(8,128)(2,1)S(1)}, bf16[32,1664]{1,0:T(8,128)(2,1)S(1)}, u32[]{:S(2)}, u32[]{:S(2)}) collective-permute-start(bf16[32,1664]{1,0:T(8,128)(2,1)S(1)} %get-tuple-element.175), channel_id=1, source_target_pairs={{0,3},{1,2},{2,1},{3,0},{4,7},{5,6},{6,5},{7,4},{8,11},{9,10},{10,... | collective-permute-start | bytes 319496 | tf_op jit(solution)/shard_map/ppermute | solution.py:928
  65.1 9.8 %collective-permute-start.12 = (bf16[4,21,16,128]{3,2,1,0:T(8,128)(2,1)S(1)}, bf16[4,21,16,128]{3,2,1,0:T(8,128)(2,1)S(1)}, u32[]{:S(2)}, u32[]{:S(2)}) collective-permute-start(bf16[4,21,16,128]{3,2,1,0:T(8,128)(2,1)S(1)} %get-tuple-element.182), channel_id=1, source_target_pairs={{0,4},{4,0},{8,12},{12,8},{16,20},{20,16},{24,28},{28,24},{1,5},{5... | collective-permute-start | bytes 1032200 | tf_op jit(solution)/shard_map/ppermute | solution.py:962
  77.9 1.9 %collective-permute-start.13 = (bf16[1952,128]{1,0:T(8,128)(2,1)S(1)}, bf16[1952,128]{1,0:T(8,128)(2,1)S(1)}, u32[]{:S(2)}, u32[]{:S(2)}) collective-permute-start(bf16[1952,128]{1,0:T(8,128)(2,1)S(1)} %get-tuple-element.188.refs_0_), channel_id=1, source_target_pairs={{0,1},{1,0},{2,3},{3,2},{4,5},{5,4},{6,7},{7,6},{8,9},{9,8},{10,11... | collective-permute-start | bytes 1499144 | tf_op jit(solution)/shard_map/ppermute | solution.py:931
  78.0 11.5 %collective-permute-start.14 = (bf16[4,18,16,128]{3,2,1,0:T(8,128)(2,1)S(1)}, bf16[4,18,16,128]{3,2,1,0:T(8,128)(2,1)S(1)}, u32[]{:S(2)}, u32[]{:S(2)}) collective-permute-start(bf16[4,18,16,128]{3,2,1,0:T(8,128)(2,1)S(1)} %get-tuple-element.195), channel_id=1, source_target_pairs={{0,4},{4,0},{8,12},{12,8},{16,20},{20,16},{24,28},{28,24},{1,5},{5... | collective-permute-start | bytes 884744 | tf_op jit(solution)/shard_map/ppermute | solution.py:962
  78.6 10.9 %collective-permute-start.15 = (bf16[2,21,16,128]{3,2,1,0:T(8,128)(2,1)S(1)}, bf16[2,21,16,128]{3,2,1,0:T(8,128)(2,1)S(1)}, u32[]{:S(2)}, u32[]{:S(2)}) collective-permute-start(bf16[2,21,16,128]{3,2,1,0:T(8,128)(2,1)S(1)} %get-tuple-element.196), channel_id=1, source_target_pairs={{0,8},{4,12},{8,0},{12,4},{16,24},{20,28},{24,16},{28,20},{1,9},{5... | collective-permute-start | bytes 516104 | tf_op jit(solution)/shard_map/ppermute | solution.py:1059
  91.2 4.2 %collective-permute-start.16 = (bf16[4,3,16,128]{3,2,1,0:T(8,128)(2,1)S(1)}, bf16[4,3,16,128]{3,2,1,0:T(8,128)(2,1)S(1)}, u32[]{:S(2)}, u32[]{:S(2)}) collective-permute-start(bf16[4,3,16,128]{3,2,1,0:T(8,128)(2,1)S(1)} %get-tuple-element.204), channel_id=1, source_target_pairs={{0,4},{4,0},{8,12},{12,8},{16,20},{20,16},{24,28},{28,24},{1,5},{5... | collective-permute-start | bytes 147464 | tf_op jit(solution)/shard_map/ppermute | solution.py:962
  91.7 9.5 %collective-permute-start.20 = (bf16[21,16,128]{2,1,0:T(8,128)(2,1)S(1)}, bf16[21,16,128]{2,1,0:T(8,128)(2,1)S(1)}, u32[]{:S(2)}, u32[]{:S(2)}) collective-permute-start(bf16[21,16,128]{2,1,0:T(8,128)(2,1)S(1)} %get-tuple-element.211), channel_id=1, source_target_pairs={{0,16},{4,20},{8,24},{12,28},{16,0},{20,4},{24,8},{28,12},{1,17},{... | collective-permute-start | bytes 258056 | tf_op jit(solution)/shard_map/ppermute | solution.py:1065
  95.4 10.3 %collective-permute-start.22 = (bf16[32,1664]{1,0:T(8,128)(2,1)S(1)}, bf16[32,1664]{1,0:T(8,128)(2,1)S(1)}, u32[]{:S(2)}, u32[]{:S(2)}) collective-permute-start(bf16[32,1664]{1,0:T(8,128)(2,1)S(1)} %get-tuple-element.216), channel_id=1, source_target_pairs={{0,2},{1,3},{2,0},{3,1},{4,6},{5,7},{6,4},{7,5},{8,10},{9,11},{10,... | collective-permute-start | bytes 319496 | tf_op jit(solution)/shard_map/ppermute | solution.py:925
  96.9 8.8 %collective-permute-start.17 = (bf16[21,16,128]{2,1,0:T(8,128)(2,1)S(1)}, bf16[21,16,128]{2,1,0:T(8,128)(2,1)S(1)}, u32[]{:S(2)}, u32[]{:S(2)}) collective-permute-start(bf16[21,16,128]{2,1,0:T(8,128)(2,1)S(1)} %get-tuple-element.206), channel_id=1, source_target_pairs={{0,8},{4,12},{8,0},{12,4},{16,24},{20,28},{24,16},{28,20},{1,9},{5... | collective-permute-start | bytes 258056 | tf_op jit(solution)/shard_map/ppermute | solution.py:968
  97.3 8.5 %collective-permute-start.18 = (bf16[21,16,128]{2,1,0:T(8,128)(2,1)S(1)}, bf16[21,16,128]{2,1,0:T(8,128)(2,1)S(1)}, u32[]{:S(2)}, u32[]{:S(2)}) collective-permute-start(bf16[21,16,128]{2,1,0:T(8,128)(2,1)S(1)} %get-tuple-element.207), channel_id=1, source_target_pairs={{0,16},{4,20},{8,24},{12,28},{16,0},{20,4},{24,8},{28,12},{1,17},{... | collective-permute-start | bytes 258056 | tf_op jit(solution)/shard_map/ppermute | solution.py:968
  98.0 7.7 %collective-permute-start.19 = (bf16[21,16,128]{2,1,0:T(8,128)(2,1)S(1)}, bf16[21,16,128]{2,1,0:T(8,128)(2,1)S(1)}, u32[]{:S(2)}, u32[]{:S(2)}) collective-permute-start(bf16[21,16,128]{2,1,0:T(8,128)(2,1)S(1)} %get-tuple-element.208), channel_id=1, source_target_pairs={{0,24},{4,28},{8,16},{12,20},{16,8},{20,12},{24,0},{28,4},{1,25},{... | collective-permute-start | bytes 258056 | tf_op jit(solution)/shard_map/ppermute | solution.py:968
  101.3 4.4 %collective-permute-start.21 = (bf16[9,16,128]{2,1,0:T(8,128)(2,1)S(1)}, bf16[9,16,128]{2,1,0:T(8,128)(2,1)S(1)}, u32[]{:S(2)}, u32[]{:S(2)}) collective-permute-start(bf16[9,16,128]{2,1,0:T(8,128)(2,1)S(1)} %get-tuple-element.214), channel_id=1, source_target_pairs={{2,0},{3,1},{6,4},{7,5},{10,8},{11,9},{14,12},{15,13},{18,16},{19,... | collective-permute-start | bytes 110600 | tf_op jit(solution)/shard_map/ppermute | solution.py:1092
  105.8 9.4 %collective-permute-start.26 = (bf16[34,16,128]{2,1,0:T(8,128)(2,1)S(1)}, bf16[34,16,128]{2,1,0:T(8,128)(2,1)S(1)}, u32[]{:S(2)}, u32[]{:S(2)}) collective-permute-start(bf16[34,16,128]{2,1,0:T(8,128)(2,1)S(1)} %shard_map.292), channel_id=1, source_target_pairs={{0,24},{1,16},{2,8},{3,0},{4,28},{5,20},{6,12},{7,4},{8,25},{9,17}... | collective-permute-start | bytes 417800 | tf_op jit(solution)/shard_map/ppermute | solution.py:949
  107.0 11.2 %collective-permute-start.25 = (bf16[34,16,128]{2,1,0:T(8,128)(2,1)S(1)}, bf16[34,16,128]{2,1,0:T(8,128)(2,1)S(1)}, u32[]{:S(2)}, u32[]{:S(2)}) collective-permute-start(bf16[34,16,128]{2,1,0:T(8,128)(2,1)S(1)} %shard_map.292), channel_id=1, source_target_pairs={{0,16},{1,24},{2,0},{3,8},{4,20},{5,28},{6,4},{7,12},{8,17},{9,25}... | collective-permute-start | bytes 417800 | tf_op jit(solution)/shard_map/ppermute | solution.py:949
  108.4 13.7 %collective-permute-start.24 = (bf16[34,16,128]{2,1,0:T(8,128)(2,1)S(1)}, bf16[34,16,128]{2,1,0:T(8,128)(2,1)S(1)}, u32[]{:S(2)}, u32[]{:S(2)}) collective-permute-start(bf16[34,16,128]{2,1,0:T(8,128)(2,1)S(1)} %shard_map.292), channel_id=1, source_target_pairs={{0,8},{1,0},{2,24},{3,16},{4,12},{5,4},{6,28},{7,20},{8,9},{9,1},{... | collective-permute-start | bytes 417800 | tf_op jit(solution)/shard_map/ppermute | solution.py:949
  110.9 13.3 %collective-permute-start.23 = (bf16[34,16,128]{2,1,0:T(8,128)(2,1)S(1)}, bf16[34,16,128]{2,1,0:T(8,128)(2,1)S(1)}, u32[]{:S(2)}, u32[]{:S(2)}) collective-permute-start(bf16[34,16,128]{2,1,0:T(8,128)(2,1)S(1)} %shard_map.292), channel_id=1, source_target_pairs={{0,0},{1,8},{2,16},{3,24},{4,4},{5,12},{6,20},{7,28},{8,1},{9,9},{... | collective-permute-start | bytes 417800 | tf_op jit(solution)/shard_map/ppermute | solution.py:949
  115.2 15.4 %collective-permute-start.30 = (bf16[34,16,128]{2,1,0:T(8,128)(2,1)S(1)}, bf16[34,16,128]{2,1,0:T(8,128)(2,1)S(1)}, u32[]{:S(2)}, u32[]{:S(2)}) collective-permute-start(bf16[34,16,128]{2,1,0:T(8,128)(2,1)S(1)} %collective-permute-done.26.refs_3_), channel_id=1, source_target_pairs={{0,4},{4,0},{8,12},{12,8},{16,20},{20,16},{24,28},{28,24},{1,5},{5... | collective-permute-start | bytes 417800 | tf_op jit(solution)/shard_map/ppermute | solution.py:962
  118.2 12.5 %collective-permute-start.29 = (bf16[34,16,128]{2,1,0:T(8,128)(2,1)S(1)}, bf16[34,16,128]{2,1,0:T(8,128)(2,1)S(1)}, u32[]{:S(2)}, u32[]{:S(2)}) collective-permute-start(bf16[34,16,128]{2,1,0:T(8,128)(2,1)S(1)} %collective-permute-done.25.refs_2_), channel_id=1, source_target_pairs={{0,4},{4,0},{8,12},{12,8},{16,20},{20,16},{24,28},{28,24},{1,5},{5... | collective-permute-start | bytes 417800 | tf_op jit(solution)/shard_map/ppermute | solution.py:962
  122.1 8.5 %collective-permute-start.28 = (bf16[34,16,128]{2,1,0:T(8,128)(2,1)S(1)}, bf16[34,16,128]{2,1,0:T(8,128)(2,1)S(1)}, u32[]{:S(2)}, u32[]{:S(2)}) collective-permute-start(bf16[34,16,128]{2,1,0:T(8,128)(2,1)S(1)} %collective-permute-done.24.refs_1_), channel_id=1, source_target_pairs={{0,4},{4,0},{8,12},{12,8},{16,20},{20,16},{24,28},{28,24},{1,5},{5... | collective-permute-start | bytes 417800 | tf_op jit(solution)/shard_map/ppermute | solution.py:962
  124.1 6.5 %collective-permute-start.27 = (bf16[34,16,128]{2,1,0:T(8,128)(2,1)S(1)}, bf16[34,16,128]{2,1,0:T(8,128)(2,1)S(1)}, u32[]{:S(2)}, u32[]{:S(2)}) collective-permute-start(bf16[34,16,128]{2,1,0:T(8,128)(2,1)S(1)} %collective-permute-done.23.refs_0_), channel_id=1, source_target_pairs={{0,4},{4,0},{8,12},{12,8},{16,20},{20,16},{24,28},{28,24},{1,5},{5... | collective-permute-start | bytes 417800 | tf_op jit(solution)/shard_map/ppermute | solution.py:962

commit v9 on v8

--- a/solution.py
+++ b/solution.py
@@ -587,26 +587,36 @@
 def sum_kernel(meta, *refs):
     parts, (total, extra) = refs[:-2], refs[-2:]
     total[0:9] = summed(parts, 0, 9)
-    total[9:12] = summed(parts, 18, 21)
-    extra[...] = summed(parts, 9, 18)
+    total[9:10] = summed(parts, 18, 19)
+    total[10:11] = summed(parts, 20, 21)
+    extra[0:9] = summed(parts, 9, 18)
+    extra[9:10] = summed(parts, 19, 20)
 
 
 def join_kernel(meta, *refs):
     parts, (total, extra, norm, out) = refs[:4], refs[4:]
     out[0:9] = summed(parts, 0, 9)
     out[9:18] = total[0:9]
-    out[27:30] = total[9:12]
+    out[27:28] = total[9:10]
+    out[28:31] = summed(parts, 18, 21)
 
     @pl.when(meta[0] == 0)
     def _():
-        out[18:27] = extra[...]
+        out[18:27] = extra[0:9]
+        out[29:30] = extra[9:10]
 
     @pl.when(meta[0] == 1)
     def _():
         out[18:27] = summed(parts, 9, 18)
 
-    out[30:33] = summed(parts, 18, 21)
-    out[33:34] = norm[...]
+    bias = total[10].astype(F32)
+    turned = jnp.concatenate([bias.T[0:2], jnp.zeros((2, 112), F32)], axis=1)
+    row = lax.broadcasted_iota(jnp.int32, (16, 128), 0)
+    block = norm[0].astype(F32)
+    for i in range(2):
+        line = jnp.where(meta[1] == 0, turned[i : i + 1], bias[0:1])
+        block = jnp.where(row == 12 + i, line, block)
+    out[31] = block.astype(BF)
 
 
 def source(meta, k):
@@ -618,95 +628,91 @@
     return pl.ds(pl.multiple_of(16 * h, 16), 16)
 
 
-def conv_out(meta, half, parts, out, room, sems):
-    for k in range(4):
-        group, branch, _ = source(meta, k)
-        r = parts[k]
+def conv_out(meta, half, first, parts, out, room, sems):
+    h = meta[5] ^ half
+    copies = []
+    for j, r in enumerate(parts):
+        group, branch, _ = source(meta, first + j)
         for i in range(3):
             layer = i if i < 2 else 1 - group
             level = group if i < 2 else 2
             for t in range(9):
-                room[layer, level, branch, t] = r[9 * i + t].astype(F32)
-
+                room[j, i, t] = r[9 * i + t].astype(F32)
+            to = out.at[level, 2 * branch + layer, :, at16(h), :]
+            copy = pltpu.make_async_copy(room.at[j, i], to, sems.at[j, i])
+            copy.start()
+            copies.append(copy)
+    return copies
+
+
+def row_outs(meta, half, first, parts, gcw, gcb, gbw, s0, s1, s2):
     h = meta[5] ^ half
-    copies = []
-    for layer in range(2):
-        for level in range(3):
-            for branch in range(2):
-                to = out.at[level, 2 * branch + layer, :, at16(h), :]
-                copy = pltpu.make_async_copy(room.at[layer, level, branch], to, sems.at[layer, level, branch])
-                copy.start()
-                copies.append(copy)
-    return copies
-
-
-def row_outs(meta, half, parts, gcw, gcb, gbw, s0, s1, s2):
-    h = meta[5] ^ half
-    for k in range(4):
-        group, branch, _ = source(meta, k)
-        r = parts[k]
+    for j, r in enumerate(parts):
+        group, branch, _ = source(meta, first + j)
         for group_id in range(2):
-            slots = range(1 + group_id)
+            heads = ((27, 0), (29, 2)) if group_id == 0 else ((27, 1),)
+            biases = ((12, 0),) if group_id == 0 else ((12, 1), (13, 2))
 
             @pl.when((group == group_id) & (branch == 0))
             def _():
-                turned = r[29].astype(F32).T
+                rows = r[31].astype(F32)
                 for half_id in range(2):
                     size = (16, 4)[half_id]
+                    at = 16 * half_id
 
                     @pl.when(h == half_id)
                     def _():
-                        for slot in slots:
-                            level = group_id + slot
-                            gcw[level, 16 * half_id : 16 * half_id + size, :] = r[27 + slot].astype(F32)[0:size]
-                            gcb[level : level + 1, 16 * half_id : 16 * half_id + size] = turned[slot : slot + 1, 0:size]
+                        for block, level in heads:
+                            gcw[level, at : at + size, :] = r[block].astype(F32)[0:size]
+                        for row, level in biases:
+                            gcb[level : level + 1, at : at + size] = rows[row : row + 1, 0:size]
 
             @pl.when((group == group_id) & (branch == 1))
             def _():
-                for slot in slots:
-                    turned = r[27 + slot].astype(F32).T
+                for block, level in heads:
+                    turned = r[block].astype(F32).T
                     for half_id in range(2):
 
                         @pl.when(h == half_id)
                         def _():
                             for i in range(5):
                                 at = 16 * half_id
-                                gbw[i, group_id + slot : group_id + slot + 1, at : at + 16] = turned[i : i + 1, 0:16]
+                                gbw[i, level : level + 1, at : at + 16] = turned[i : i + 1, 0:16]
 
         @pl.when((group == 0) & (branch == 0))
         def _():
-            s0[at16(h), :] = r[30].astype(F32)
+            s0[at16(h), :] = r[28].astype(F32)
 
         @pl.when((group == 1) & (branch == 0))
         def _():
             for i in range(2):
-                s1[at16(h), 128 * i : 128 * (i + 1)] = r[30 + i].astype(F32)
-            s2[at16(h), 0:128] = r[32].astype(F32)
+                s1[at16(h), 128 * i : 128 * (i + 1)] = r[28 + i].astype(F32)
+            s2[at16(h), 0:128] = r[30].astype(F32)
 
         @pl.when((group == 1) & (branch == 1))
         def _():
             for i in range(3):
-                s2[at16(h), 128 * (i + 1) : 128 * (i + 2)] = r[30 + i].astype(F32)
+                s2[at16(h), 128 * (i + 1) : 128 * (i + 2)] = r[28 + i].astype(F32)
 
 
 def near_out_kernel(meta, *refs):
     parts, (out, gcw, gcb, gbw, s0, s1, s2, gbb, gains, shifts, room, sems) = refs[:4], refs[4:]
-    copies = conv_out(meta, 0, parts, out, room, sems)
-    row_outs(meta, 0, parts, gcw, gcb, gbw, s0, s1, s2)
+    copies = conv_out(meta, 0, 0, parts, out, room, sems)
+    row_outs(meta, 0, 0, parts, gcw, gcb, gbw, s0, s1, s2)
     c = meta[2]
     for k in range(4):
         group, branch, _ = source(meta, k)
-        r = parts[k]
-        for group_id in range(2):
-
-            @pl.when((group == group_id) & (branch == 1))
-            def _():
-                bias = r[29].astype(F32)
-                for slot in range(1 + group_id):
-                    level = group_id + slot
-                    gbb[level : level + 1, :] = bias[0:1, 2 + 5 * slot : 7 + 5 * slot]
-
-        v = r[33].astype(F32)
+        v = parts[k][31].astype(F32)
+
+        @pl.when((group == 0) & (branch == 1))
+        def _():
+            gbb[0:1, :] = v[12:13, 2:7]
+
+        @pl.when((group == 1) & (branch == 1))
+        def _():
+            gbb[1:2, :] = v[12:13, 2:7]
+            gbb[2:3, :] = v[12:13, 7:12]
+
         mine = v[:, 0:32]
         for i in range(1, 4):
             mine = jnp.where(c == i, v[:, 32 * i : 32 * (i + 1)], mine)
@@ -730,11 +736,11 @@
 
 def far_out_kernel(meta, *refs):
     parts, earlier, (out, gcw, gcb, gbw, s0, s1, s2, room, sems) = refs[:4], refs[5:11], refs[11:]
-    copies = conv_out(meta, 1, parts, out, room, sems)
+    copies = conv_out(meta, 1, 0, parts, out, room, sems)
     outs = (gcw, gcb, gbw, s0, s1, s2)
     for old, new in zip(earlier, outs):
         new[...] = old[...]
-    row_outs(meta, 1, parts, *outs)
+    row_outs(meta, 1, 0, parts, *outs)
     for copy in copies:
         copy.wait()
 
@@ -1087,19 +1093,24 @@
         parts1 = along_z([wg1, gs], [got1, over_y(gs_send)])
         received = across(after(other, parts1[0]))
         total, extra = call(
-            sum_kernel, [((12, 16, 128), BF), ((9, 16, 128), BF)], [], (meta, own2, after(got2, parts1[0]))
+            sum_kernel, [((11, 16, 128), BF), ((10, 16, 128), BF)], [], (meta, own2, after(got2, parts1[0]))
         )
         extra = lax.ppermute(extra, "chan", [(2, 0), (3, 1)])
         extra, received = lax.optimization_barrier((extra, received))
-        (grads,) = call(join_kernel, [((34, 16, 128), BF)], [], (meta, *parts1, total, extra, norm))
+        (grads,) = call(join_kernel, [((32, 16, 128), BF)], [], (meta, *parts1, total, extra, norm))
     else:
-        extra = lax.ppermute(got2[:, 9:18], "chan", [(2, 0), (3, 1)])
-        third = jnp.where(fine, extra, got1[:, 9:18])
-        norm = jnp.broadcast_to(norm[None], (8, *norm.shape))
-        grads = joined(got1[:, :9], got2[:, :9], third, got2[:, 18:21], reduce(gs), norm)
+        gs = reduce(gs)
+        extra = lax.ppermute(got2[:, 9:20], "chan", [(2, 0), (3, 1)])
+        third = jnp.where(fine, extra[:, :9], got1[:, 9:18])
+        stems = jnp.where(fine, joined(gs[:, :1], extra[:, 10:], gs[:, 2:]), gs)
+        bias = got2[:, 20]
+        turned = jnp.pad(bias[:, :, :2].transpose(0, 2, 1), ((0, 0), (0, 0), (0, 112)))
+        biases = jnp.where(branch == 0, turned, jnp.broadcast_to(bias[:, :1], turned.shape))
+        norm = jnp.broadcast_to(norm, (8, 16, 128)).at[:, 12:14].set(biases)[:, None]
+        grads = joined(got1[:, :9], got2[:, :9], third, got2[:, 18:19], stems, norm)
     grads = everywhere(over_z(grads))
 
-    room = [((2, 3, 2, conv.shape[2], 16, 128), F32), pltpu.SemaphoreType.DMA((2, 3, 2))]
+    room = [((4, 3, conv.shape[2], 16, 128), F32), pltpu.SemaphoreType.DMA((4, 3))]
     rows = [(cw.shape, F32), (cb.shape, F32), ((5, 3, 32), F32), (s0.shape, F32), (s1.shape, F32), (s2.shape, F32)]
     wholes = [(bb.shape, F32), ((5, 3, 32), F32), ((5, 3, 32), F32)]
     grad_conv, *half, grad_bb, grad_gains, grad_shifts = call(

time: 133 us -> 132 us (level)
  no operation moved by 1% of the time
where the time goes in v9:
time: 132 us
  blocking collectives  58.5 us (44%)
  starting transfers between devices  32.5 us (25%)
  Pallas kernels  24.9 us (19%)
  waiting for transfers between devices  13.7 us (10%)
  between operations  1.69 us (1%)
    all_to_all x6, blocking collectives, exchange(): st = lax.all_to_all(st, 'dp', 0, 0, tiled=True)  58.5 us
    pallas_call x23, Pallas kernels, call(): pl.pallas_call(placed if args[0].dtype == jnp.int32 else body, out_shape=...  24.9 us
    ppermute x7, starting transfers between devices, over_y(): return lax.ppermute(v, 'dp', [(i, i ^ 1) for i in range(8)])  8.15 us
    ppermute x4, starting transfers between devices, over_z(): parts.append(lax.ppermute(v, ('dp', 'chan'), pairs))  7.19 us
    ppermute x4, waiting for transfers between devices, over_z(): parts.append(lax.ppermute(v, ('dp', 'chan'), pairs))  5.82 us
    ppermute x3, starting transfers between devices, along_z(): lax.ppermute(v, 'dp', [(i, i ^ 2 * k + 2) for i in range(8)])  4.39 us
    ppermute x5, starting transfers between devices, across(): return lax.ppermute(v, 'chan', [(i, i ^ 2) for i in range(4)])  4.12 us
    ppermute x7, waiting for transfers between devices, over_y(): return lax.ppermute(v, 'dp', [(i, i ^ 1) for i in range(8)])  3 us
  transfers between devices with their start and end apart: 31, of which 8 were waited for; matrix products, arithmetic and copies ran while one was open for 0% of the time, Pallas kernels for 7%

profile of v9, /device:TPU:2, one launch (start us, length us, event | category | flops | bytes accessed | tf_op | source)
XLA Modules:
  0.0 131.8 jit_solution(16296513145683773455)
XLA Ops:
  0.6 1.2 shard_map.274
  1.8 0.1 collective-permute-start.1
  1.9 0.5 collective-permute-start.2
  3.1 0.6 broadcast_in_dim.20.units
  3.7 2.2 %shard_map.275 = (bf16[17,32,128]{2,1,0:T(8,128)(2,1)S(1)}, bf16[17,32,128]{2,1,0:T(8,128)(2,1)S(1)}, bf16[18,32,128]{2,1,0:T(8,128)(2,1)S(1)}, bf16[18,32,128]{...) custom-call(s32[8,128]{1,0:T(8,128)} %broadcast_in_dim.20.units, ...), custom_call_target="tpu_custom_call" | custom-call | flops 2000000000 | bytes 10000 | tf_op jit(solution)/shard_map/pallas_call | solution.py:909
  5.9 2.7 %collective-permute-done.refs_1_.refs_8_ = bf16[32,2560]{1,0:T(8,128)(2,1)S(1)} collective-permute-done((bf16[32,2560]{1,0:T(8,128)(2,1)S(1)}, bf16[32,2560]{1,0:T(8,128)(2,1)S(1)}, u32[]{:S(2)}, u32[]{:S(2)}) %collective-permute-start) | collective-permute-done | bytes 163872 | tf_op jit(solution)/shard_map/ppermute | solution.py:931
  8.6 0.0 collective-permute-done.1.refs_1_
  8.6 0.0 collective-permute-start.3
  8.6 1.3 collective-permute-start.4
  9.9 0.3 collective-permute-start.5
  10.3 2.2 %collective-permute-start.6 = (bf16[18,32,128]{2,1,0:T(8,128)(2,1)S(1)}, bf16[18,32,128]{2,1,0:T(8,128)(2,1)S(1)}, u32[]{:S(2)}, u32[]{:S(2)}) collective-permute-start(bf16[18,32,128]{2,1,0:T(8,128)(2,1)S(1)} %get-tuple-element.147), channel_id=1, source_target_pairs={{0,3},{1,2},{2,1},{3,0},{4,7},{5,6},{6,5},{7,4},{8,11},{9,10},{10,... | collective-permute-start | bytes 442376 | tf_op jit(solution)/shard_map/ppermute | solution.py:934
  12.5 1.0 shard_map.276
  13.5 12.3 %all_to_all.30.refs_1_ = f32[8,8,128]{2,1,0:T(8,128)S(1)} all-to-all(f32[8,8,128]{2,1,0:T(8,128)S(1)} %get-tuple-element.140), channel_id=1, replica_groups=mesh['dp'=8,'chan'=4] {'dp'}, dimensions={0} | all-to-all | bytes 65536 | tf_op jit(solution)/shard_map/all_to_all | solution.py:941
  25.8 0.7 collective-permute-start.7
  26.5 0.2 shard_map.277
  26.7 1.6 %shard_map.278 = (bf16[1920,128]{1,0:T(8,128)(2,1)S(1)}, f32[1920,128]{1,0:T(8,128)S(1)}, f32[8,8,128]{2,1,0:T(8,128)S(1)}, f32[16,128]{1,0:T(8,128)S(1)}) custom-call(s32[8,128]{1,0:T(8,128)S(1)} %copy-done.1, f32[1920,128]{1,0:T(8,128)S(1)} %get-tuple-element.137.refs_0_.refs_6_.refs_2_, f32[8,8,128]{2,1,0:T(8,128)S(1)} %all_to_all.30.refs_1_, ...), custom_call_target="tpu_custom_call" | custom-call | flops 1000000 | bytes 10000 | tf_op jit(solution)/shard_map/pallas_call | solution.py:909
  28.4 9.1 %all_to_all.31.refs_1_ = f32[8,8,128]{2,1,0:T(8,128)S(1)} all-to-all(f32[8,8,128]{2,1,0:T(8,128)S(1)} %get-tuple-element.153), channel_id=1, replica_groups=mesh['dp'=8,'chan'=4] {'dp'}, dimensions={0} | all-to-all | bytes 65536 | tf_op jit(solution)/shard_map/all_to_all | solution.py:941
  37.5 0.2 shard_map.279
  37.7 1.6 %shard_map.280 = (bf16[1920,128]{1,0:T(8,128)(2,1)S(1)}, f32[1920,128]{1,0:T(8,128)S(1)}, f32[8,8,128]{2,1,0:T(8,128)S(1)}, f32[16,128]{1,0:T(8,128)S(1)}) custom-call(s32[8,128]{1,0:T(8,128)S(1)} %copy-done.1, f32[1920,128]{1,0:T(8,128)S(1)} %get-tuple-element.152.refs_0_.refs_6_.refs_1_, f32[8,8,128]{2,1,0:T(8,128)S(1)} %all_to_all.31.refs_1_, ...), custom_call_target="tpu_custom_call" | custom-call | flops 1000000 | bytes 10000 | tf_op jit(solution)/shard_map/pallas_call | solution.py:909
  39.4 9.1 %all_to_all.32.refs_1_ = f32[8,8,128]{2,1,0:T(8,128)S(1)} all-to-all(f32[8,8,128]{2,1,0:T(8,128)S(1)} %get-tuple-element.161), channel_id=1, replica_groups=mesh['dp'=8,'chan'=4] {'dp'}, dimensions={0} | all-to-all | bytes 65536 | tf_op jit(solution)/shard_map/all_to_all | solution.py:941
  48.4 1.7 %shard_map.281 = (f32[1920,128]{1,0:T(8,128)S(1)}, f32[8,8,128]{2,1,0:T(8,128)S(1)}, f32[16,128]{1,0:T(8,128)S(1)}, bf16[1664,256]{1,0:T(8,128)(2,1)S(1)}, bf16[...) custom-call(s32[8,128]{1,0:T(8,128)S(1)} %copy-done.1, f32[1920,128]{1,0:T(8,128)S(1)} %get-tuple-element.160.refs_0_.refs_1_, ...), custom_call_target="tpu_custom_call" | custom-call | flops 1000000 | bytes 10000 | tf_op jit(solution)/shard_map/pallas_call | solution.py:909
  50.1 0.7 shard_map.282
  50.9 0.1 collective-permute-start.9
  50.9 1.5 %collective-permute-start.10 = (bf16[32,1664]{1,0:T(8,128)(2,1)S(1)}, bf16[32,1664]{1,0:T(8,128)(2,1)S(1)}, u32[]{:S(2)}, u32[]{:S(2)}) collective-permute-start(bf16[32,1664]{1,0:T(8,128)(2,1)S(1)} %get-tuple-element.174), channel_id=1, source_target_pairs={{0,2},{1,3},{2,0},{3,1},{4,6},{5,7},{6,4},{7,5},{8,10},{9,11},{10,... | collective-permute-start | bytes 319496 | tf_op jit(solution)/shard_map/ppermute | solution.py:931
  52.5 0.3 collective-permute-start.11
  52.8 9.0 %all_to_all.33.refs_3_ = f32[8,8,128]{2,1,0:T(8,128)S(1)} all-to-all(f32[8,8,128]{2,1,0:T(8,128)S(1)} %get-tuple-element.172), channel_id=1, replica_groups=mesh['dp'=8,'chan'=4] {'dp'}, dimensions={0} | all-to-all | bytes 65536 | tf_op jit(solution)/shard_map/all_to_all | solution.py:941
  61.9 3.2 %shard_map.283 = (f32[1920,128]{1,0:T(8,128)S(1)}, f32[8,8,128]{2,1,0:T(8,128)S(1)}, f32[8,128]{1,0:T(8,128)S(1)}, bf16[8,21,16,128]{3,2,1,0:T(8,128)(2,1)S(1)}, bf16[4,21,16,128]{3,2,1,0:T(8,128)(2,1)S(1)}) custom-call(s32[8,128]{1,0:T(8,128)S(1)} %copy-done.1, f32[1920,128]{1,0:T(8,128)S(1)} %get-tuple-element.168.refs_0_, ...), custom_call_target="tpu_custom_call" | custom-call | flops 1000000 | bytes 10000 | tf_op jit(solution)/shard_map/pallas_call | solution.py:909
  65.1 0.5 collective-permute-start.12
  65.6 9.3 %all_to_all.34.refs_3_ = f32[8,8,128]{2,1,0:T(8,128)S(1)} all-to-all(f32[8,8,128]{2,1,0:T(8,128)S(1)} %get-tuple-element.183), channel_id=1, replica_groups=mesh['dp'=8,'chan'=4] {'dp'}, dimensions={0} | all-to-all | bytes 65536 | tf_op jit(solution)/shard_map/all_to_all | solution.py:941
  74.9 3.0 %shard_map.284 = (bf16[1952,128]{1,0:T(8,128)(2,1)S(1)}, f32[8,8,128]{2,1,0:T(8,128)S(1)}, f32[8,128]{1,0:T(8,128)S(1)}, bf16[8,18,16,128]{3,2,1,0:T(8,128)(2,1)S(1)}, bf16[4,18,16,128]{3,2,1,0:T(8,128)(2,1)S(1)}) custom-call(s32[8,128]{1,0:T(8,128)S(1)} %copy-done.1, f32[1920,128]{1,0:T(8,128)S(1)} %get-tuple-element.180.refs_0_, ...), custom_call_target="tpu_custom_call" | custom-call | flops 1000000 | bytes 10000 | tf_op jit(solution)/shard_map/pallas_call | solution.py:909
  77.9 0.1 collective-permute-start.13
  78.0 0.5 collective-permute-start.14
  78.5 0.1 shard_map.285
  78.6 0.8 collective-permute-start.15
  79.4 0.5 collective-permute-done.13.other.refs_1_
  79.9 9.6 %all_to_all.35.st = f32[8,8,128]{2,1,0:T(8,128)S(1)} all-to-all(f32[8,8,128]{2,1,0:T(8,128)S(1)} %shard_map.286), channel_id=1, replica_groups=mesh['dp'=8,'chan'=4] {'dp'}, dimensions={0} | all-to-all | bytes 65536 | tf_op jit(solution)/shard_map/all_to_all | solution.py:941
  89.5 1.7 %shard_map.288 = (bf16[32,1664]{1,0:T(8,128)(2,1)S(1)}, bf16[32,1664]{1,0:T(8,128)(2,1)S(1)}, bf16[8,3,16,128]{3,2,1,0:T(8,128)(2,1)S(1)}, bf16[4,3,16,128]{3,2,1,0:T(8,128)(2,1)S(1)}, bf16[1,16,128]{2,1,0:T(8,128)(2,1)S(1)}) custom-call(s32[8,128]{1,0:T(8,128)S(1)} %copy-done.1, bf16[1952,128]{1,0:T(8,128)(2,1)S(1)} %get-tuple-element.188.refs_0_, ...), custom_call_target="tpu_custom_call" | custom-call | flops 1000000 | bytes 10000 | tf_op jit(solution)/shard_map/pallas_call | solution.py:909
  91.2 0.5 collective-permute-start.16
  91.8 0.6 collective-permute-start.20
  92.3 3.0 %collective-permute-done.16.refs_3_ = bf16[4,3,16,128]{3,2,1,0:T(8,128)(2,1)S(1)} collective-permute-done((bf16[4,3,16,128]{3,2,1,0:T(8,128)(2,1)S(1)}, bf16[4,3,16,128]{3,2,1,0:T(8,128)(2,1)S(1)}, u32[]{:S(2)}, u32[]{:S(2)}) %collective-permute-start.16) | collective-permute-done | bytes 49184 | tf_op jit(solution)/shard_map/ppermute | solution.py:968
  95.3 0.1 shard_map.289
  95.4 1.5 %collective-permute-start.22 = (bf16[32,1664]{1,0:T(8,128)(2,1)S(1)}, bf16[32,1664]{1,0:T(8,128)(2,1)S(1)}, u32[]{:S(2)}, u32[]{:S(2)}) collective-permute-start(bf16[32,1664]{1,0:T(8,128)(2,1)S(1)} %get-tuple-element.216), channel_id=1, source_target_pairs={{0,2},{1,3},{2,0},{3,1},{4,6},{5,7},{6,4},{7,5},{8,10},{9,11},{10,... | collective-permute-start | bytes 319496 | tf_op jit(solution)/shard_map/ppermute | solution.py:931
  96.9 0.4 collective-permute-start.17
  97.3 0.7 collective-permute-start.18
  98.0 3.3 %collective-permute-start.19 = (bf16[21,16,128]{2,1,0:T(8,128)(2,1)S(1)}, bf16[21,16,128]{2,1,0:T(8,128)(2,1)S(1)}, u32[]{:S(2)}, u32[]{:S(2)}) collective-permute-start(bf16[21,16,128]{2,1,0:T(8,128)(2,1)S(1)} %get-tuple-element.208), channel_id=1, source_target_pairs={{0,24},{4,28},{8,16},{12,20},{16,8},{20,12},{24,0},{28,4},{1,25},{... | collective-permute-start | bytes 258056 | tf_op jit(solution)/shard_map/ppermute | solution.py:974
  101.3 2.8 %collective-permute-start.21 = (bf16[10,16,128]{2,1,0:T(8,128)(2,1)S(1)}, bf16[10,16,128]{2,1,0:T(8,128)(2,1)S(1)}, u32[]{:S(2)}, u32[]{:S(2)}) collective-permute-start(bf16[10,16,128]{2,1,0:T(8,128)(2,1)S(1)} %get-tuple-element.214), channel_id=1, source_target_pairs={{2,0},{3,1},{6,4},{7,5},{10,8},{11,9},{14,12},{15,13},{18,16},{19,... | collective-permute-start | bytes 122888 | tf_op jit(solution)/shard_map/ppermute | solution.py:1098
  104.1 1.7 %collective-permute-done.21.refs_5_ = bf16[10,16,128]{2,1,0:T(8,128)(2,1)S(1)} collective-permute-done((bf16[10,16,128]{2,1,0:T(8,128)(2,1)S(1)}, bf16[10,16,128]{2,1,0:T(8,128)(2,1)S(1)}, u32[]{:S(2)}, u32[]{:S(2)}) %collective-permute-start.21) | collective-permute-done | bytes 40992 | tf_op jit(solution)/shard_map/ppermute | solution.py:1098
  105.8 0.1 shard_map.292
  105.9 1.1 collective-permute-start.26
  107.0 1.5 %collective-permute-start.25 = (bf16[32,16,128]{2,1,0:T(8,128)(2,1)S(1)}, bf16[32,16,128]{2,1,0:T(8,128)(2,1)S(1)}, u32[]{:S(2)}, u32[]{:S(2)}) collective-permute-start(bf16[32,16,128]{2,1,0:T(8,128)(2,1)S(1)} %shard_map.292), channel_id=1, source_target_pairs={{0,16},{1,24},{2,0},{3,8},{4,20},{5,28},{6,4},{7,12},{8,17},{9,25}... | collective-permute-start | bytes 393224 | tf_op jit(solution)/shard_map/ppermute | solution.py:955
  108.5 2.4 %collective-permute-start.24 = (bf16[32,16,128]{2,1,0:T(8,128)(2,1)S(1)}, bf16[32,16,128]{2,1,0:T(8,128)(2,1)S(1)}, u32[]{:S(2)}, u32[]{:S(2)}) collective-permute-start(bf16[32,16,128]{2,1,0:T(8,128)(2,1)S(1)} %shard_map.292), channel_id=1, source_target_pairs={{0,8},{1,0},{2,24},{3,16},{4,12},{5,4},{6,28},{7,20},{8,9},{9,1},{... | collective-permute-start | bytes 393224 | tf_op jit(solution)/shard_map/ppermute | solution.py:955
  110.9 2.2 %collective-permute-start.23 = (bf16[32,16,128]{2,1,0:T(8,128)(2,1)S(1)}, bf16[32,16,128]{2,1,0:T(8,128)(2,1)S(1)}, u32[]{:S(2)}, u32[]{:S(2)}) collective-permute-start(bf16[32,16,128]{2,1,0:T(8,128)(2,1)S(1)} %shard_map.292), channel_id=1, source_target_pairs={{0,0},{1,8},{2,16},{3,24},{4,4},{5,12},{6,20},{7,28},{8,1},{9,9},{... | collective-permute-start | bytes 393224 | tf_op jit(solution)/shard_map/ppermute | solution.py:955
  113.1 0.3 collective-permute-done.26.refs_3_
  113.4 1.6 %collective-permute-start.30 = (bf16[32,16,128]{2,1,0:T(8,128)(2,1)S(1)}, bf16[32,16,128]{2,1,0:T(8,128)(2,1)S(1)}, u32[]{:S(2)}, u32[]{:S(2)}) collective-permute-start(bf16[32,16,128]{2,1,0:T(8,128)(2,1)S(1)} %collective-permute-done.26.refs_3_), channel_id=1, source_target_pairs={{0,4},{4,0},{8,12},{12,8},{16,20},{20,16},{24,28},{28,24},{1,5},{5... | collective-permute-start | bytes 393224 | tf_op jit(solution)/shard_map/ppermute | solution.py:968
  114.9 2.7 %collective-permute-done.25.refs_2_ = bf16[32,16,128]{2,1,0:T(8,128)(2,1)S(1)} collective-permute-done((bf16[32,16,128]{2,1,0:T(8,128)(2,1)S(1)}, bf16[32,16,128]{2,1,0:T(8,128)(2,1)S(1)}, u32[]{:S(2)}, u32[]{:S(2)}) %collective-permute-start.25) | collective-permute-done | bytes 131104 | tf_op jit(solution)/shard_map/ppermute | solution.py:955
  117.7 1.5 %collective-permute-start.29 = (bf16[32,16,128]{2,1,0:T(8,128)(2,1)S(1)}, bf16[32,16,128]{2,1,0:T(8,128)(2,1)S(1)}, u32[]{:S(2)}, u32[]{:S(2)}) collective-permute-start(bf16[32,16,128]{2,1,0:T(8,128)(2,1)S(1)} %collective-permute-done.25.refs_2_), channel_id=1, source_target_pairs={{0,4},{4,0},{8,12},{12,8},{16,20},{20,16},{24,28},{28,24},{1,5},{5... | collective-permute-start | bytes 393224 | tf_op jit(solution)/shard_map/ppermute | solution.py:968
  119.1 2.5 %collective-permute-done.24.refs_1_ = bf16[32,16,128]{2,1,0:T(8,128)(2,1)S(1)} collective-permute-done((bf16[32,16,128]{2,1,0:T(8,128)(2,1)S(1)}, bf16[32,16,128]{2,1,0:T(8,128)(2,1)S(1)}, u32[]{:S(2)}, u32[]{:S(2)}) %collective-permute-start.24) | collective-permute-done | bytes 131104 | tf_op jit(solution)/shard_map/ppermute | solution.py:955
  121.7 1.5 %collective-permute-start.28 = (bf16[32,16,128]{2,1,0:T(8,128)(2,1)S(1)}, bf16[32,16,128]{2,1,0:T(8,128)(2,1)S(1)}, u32[]{:S(2)}, u32[]{:S(2)}) collective-permute-start(bf16[32,16,128]{2,1,0:T(8,128)(2,1)S(1)} %collective-permute-done.24.refs_1_), channel_id=1, source_target_pairs={{0,4},{4,0},{8,12},{12,8},{16,20},{20,16},{24,28},{28,24},{1,5},{5... | collective-permute-start | bytes 393224 | tf_op jit(solution)/shard_map/ppermute | solution.py:968
  123.2 0.3 collective-permute-done.23.refs_0_
  123.5 2.0 %collective-permute-start.27 = (bf16[32,16,128]{2,1,0:T(8,128)(2,1)S(1)}, bf16[32,16,128]{2,1,0:T(8,128)(2,1)S(1)}, u32[]{:S(2)}, u32[]{:S(2)}) collective-permute-start(bf16[32,16,128]{2,1,0:T(8,128)(2,1)S(1)} %collective-permute-done.23.refs_0_), channel_id=1, source_target_pairs={{0,4},{4,0},{8,12},{12,8},{16,20},{20,16},{24,28},{28,24},{1,5},{5... | collective-permute-start | bytes 393224 | tf_op jit(solution)/shard_map/ppermute | solution.py:968
  125.5 2.9 %shard_map.293 = (f32[3,4,9,32,128]{4,3,2,1,0:T(8,128)}, f32[3,20,128]{2,1,0:T(8,128)S(1)}, f32[3,20]{1,0:T(4,128)S(1)}, f32[5,3,32]{2,1,0:T(4,128)S(1)}, f32[32...) custom-call(s32[8,128]{1,0:T(8,128)S(1)} %copy-done.1, ...), custom_call_target="tpu_custom_call" | custom-call | flops 1000000 | bytes 10000 | tf_op jit(solution)/shard_map/pallas_call | solution.py:909
  128.4 0.8 shard_map.295
  129.2 0.7 shard_map.294
  129.9 1.7 %shard_map.296 = (f32[3,4,9,32,128]{4,3,2,1,0:T(8,128)}, f32[3,20,128]{2,1,0:T(8,128)}, f32[3,20]{1,0:T(4,128)}, f32[5,3,32]{2,1,0:T(4,128)}, f32[32,128]{1,0:T(...) custom-call(s32[8,128]{1,0:T(8,128)S(1)} %copy-done.1, ...), custom_call_target="tpu_custom_call", output_to_operand_aliasing={{0}: (5, {})} | custom-call | flops 1000000 | bytes 10000 | tf_op jit(solution)/shard_map/pallas_call | solution.py:909
  (32 shorter events, 0.2 us)
Async XLA Ops:
  1.8 6.8 %collective-permute-start.1 = (bf16[3,4,9,32,128]{4,3,2,1,0:T(8,128)(2,1)}, bf16[3,4,9,32,128]{4,3,2,1,0:T(8,128)(2,1)S(1)}, u32[]{:S(2)}, u32[]{:S(2)}) collective-permute-start(bf16[3,4,9,32,128]{4,3,2,1,0:T(8,128)(2,1)} %refs_0_.3), channel_id=1, source_target_pairs={{0,1},{1,0},{2,3},{3,2},{4,5},{5,4},{6,7},{7,6},{8,9},{9,8},{10,11... | collective-permute-start | bytes 2654216 | tf_op jit(solution)/shard_map/ppermute | solution.py:937
  1.9 10.5 %collective-permute-start.2 = (bf16[32,2560]{1,0:T(8,128)(2,1)S(1)}, bf16[32,2560]{1,0:T(8,128)(2,1)S(1)}, u32[]{:S(2)}, u32[]{:S(2)}) collective-permute-start(bf16[32,2560]{1,0:T(8,128)(2,1)S(1)} %get-tuple-element.131.refs_0_.refs_7_), channel_id=1, source_target_pairs={{0,1},{1,0},{2,3},{3,2},{4,5},{5,4},{6,7},{7,6},{8,9},{9,8},{10,11... | collective-permute-start | bytes 491528 | tf_op jit(solution)/shard_map/ppermute | solution.py:937
  2.4 6.2 %collective-permute-start = (bf16[32,2560]{1,0:T(8,128)(2,1)S(1)}, bf16[32,2560]{1,0:T(8,128)(2,1)S(1)}, u32[]{:S(2)}, u32[]{:S(2)}) collective-permute-start(bf16[32,2560]{1,0:T(8,128)(2,1)S(1)} %get-tuple-element.132), channel_id=1, source_target_pairs={{0,2},{1,3},{2,0},{3,1},{4,6},{5,7},{6,4},{7,5},{8,10},{9,11},{10,... | collective-permute-start | bytes 491528 | tf_op jit(solution)/shard_map/ppermute | solution.py:931
  3.7 8.8 %copy-start.1 = (s32[8,128]{1,0:T(8,128)S(1)}, s32[8,128]{1,0:T(8,128)}, u32[]{:S(2)}) copy-start(s32[8,128]{1,0:T(8,128)} %broadcast_in_dim.20.units) | copy-start | bytes 12292
  3.7 22.9 %copy-start = (bf16[3,4,9,32,128]{4,3,2,1,0:T(8,128)(2,1)S(1)}, bf16[3,4,9,32,128]{4,3,2,1,0:T(8,128)(2,1)}, u32[]{:S(2)}) copy-start(bf16[3,4,9,32,128]{4,3,2,1,0:T(8,128)(2,1)} %refs_0_.3) | copy-start | bytes 2654212
  8.6 3.8 %collective-permute-start.3 = (bf16[32,2560]{1,0:T(8,128)(2,1)S(1)}, bf16[32,2560]{1,0:T(8,128)(2,1)S(1)}, u32[]{:S(2)}, u32[]{:S(2)}) collective-permute-start(bf16[32,2560]{1,0:T(8,128)(2,1)S(1)} %collective-permute-done.refs_1_.refs_8_), channel_id=1, source_target_pairs={{0,1},{1,0},{2,3},{3,2},{4,5},{5,4},{6,7},{7,6},{8,9},{9,8},{10,11... | collective-permute-start | bytes 491528 | tf_op jit(solution)/shard_map/ppermute | solution.py:937
  8.6 4.8 %collective-permute-start.4 = (bf16[17,32,128]{2,1,0:T(8,128)(2,1)S(1)}, bf16[17,32,128]{2,1,0:T(8,128)(2,1)S(1)}, u32[]{:S(2)}, u32[]{:S(2)}) collective-permute-start(bf16[17,32,128]{2,1,0:T(8,128)(2,1)S(1)} %get-tuple-element.139.refs_3_), channel_id=1, source_target_pairs={{1,0},{3,2},{5,4},{7,6},{9,8},{11,10},{13,12},{15,14},{17,16},{19,... | collective-permute-start | bytes 417800 | tf_op jit(solution)/shard_map/ppermute | solution.py:937
  9.9 15.9 %collective-permute-start.5 = (bf16[18,32,128]{2,1,0:T(8,128)(2,1)S(1)}, bf16[18,32,128]{2,1,0:T(8,128)(2,1)S(1)}, u32[]{:S(2)}, u32[]{:S(2)}) collective-permute-start(bf16[18,32,128]{2,1,0:T(8,128)(2,1)S(1)} %get-tuple-element.145), channel_id=1, source_target_pairs={{0,2},{1,3},{2,0},{3,1},{4,6},{5,7},{6,4},{7,5},{8,10},{9,11},{10,... | collective-permute-start | bytes 442376 | tf_op jit(solution)/shard_map/ppermute | solution.py:931
  10.3 15.5 %collective-permute-start.6 = (bf16[18,32,128]{2,1,0:T(8,128)(2,1)S(1)}, bf16[18,32,128]{2,1,0:T(8,128)(2,1)S(1)}, u32[]{:S(2)}, u32[]{:S(2)}) collective-permute-start(bf16[18,32,128]{2,1,0:T(8,128)(2,1)S(1)} %get-tuple-element.147), channel_id=1, source_target_pairs={{0,3},{1,2},{2,1},{3,0},{4,7},{5,6},{6,5},{7,4},{8,11},{9,10},{10,... | collective-permute-start | bytes 442376 | tf_op jit(solution)/shard_map/ppermute | solution.py:934
  25.8 11.7 %collective-permute-start.8 = (bf16[27,32,128]{2,1,0:T(8,128)(2,1)S(1)}, bf16[27,32,128]{2,1,0:T(8,128)(2,1)S(1)}, u32[]{:S(2)}, u32[]{:S(2)}) collective-permute-start(bf16[27,32,128]{2,1,0:T(8,128)(2,1)S(1)} %get-tuple-element.156), channel_id=1, source_target_pairs={{0,3},{1,2},{2,1},{3,0},{4,7},{5,6},{6,5},{7,4},{8,11},{9,10},{10,... | collective-permute-start | bytes 663560 | tf_op jit(solution)/shard_map/ppermute | solution.py:934
  25.8 11.7 %collective-permute-start.7 = (bf16[27,32,128]{2,1,0:T(8,128)(2,1)S(1)}, bf16[27,32,128]{2,1,0:T(8,128)(2,1)S(1)}, u32[]{:S(2)}, u32[]{:S(2)}) collective-permute-start(bf16[27,32,128]{2,1,0:T(8,128)(2,1)S(1)} %get-tuple-element.154), channel_id=1, source_target_pairs={{0,2},{1,3},{2,0},{3,1},{4,6},{5,7},{6,4},{7,5},{8,10},{9,11},{10,... | collective-permute-start | bytes 663560 | tf_op jit(solution)/shard_map/ppermute | solution.py:931
  50.9 11.0 %collective-permute-start.9 = (bf16[32,1664]{1,0:T(8,128)(2,1)S(1)}, bf16[32,1664]{1,0:T(8,128)(2,1)S(1)}, u32[]{:S(2)}, u32[]{:S(2)}) collective-permute-start(bf16[32,1664]{1,0:T(8,128)(2,1)S(1)} %get-tuple-element.173), channel_id=1, source_target_pairs={{0,1},{1,0},{2,3},{3,2},{4,5},{5,4},{6,7},{7,6},{8,9},{9,8},{10,11... | collective-permute-start | bytes 319496 | tf_op jit(solution)/shard_map/ppermute | solution.py:937
  50.9 10.9 %collective-permute-start.10 = (bf16[32,1664]{1,0:T(8,128)(2,1)S(1)}, bf16[32,1664]{1,0:T(8,128)(2,1)S(1)}, u32[]{:S(2)}, u32[]{:S(2)}) collective-permute-start(bf16[32,1664]{1,0:T(8,128)(2,1)S(1)} %get-tuple-element.174), channel_id=1, source_target_pairs={{0,2},{1,3},{2,0},{3,1},{4,6},{5,7},{6,4},{7,5},{8,10},{9,11},{10,... | collective-permute-start | bytes 319496 | tf_op jit(solution)/shard_map/ppermute | solution.py:931
  52.5 9.4 %collective-permute-start.11 = (bf16[32,1664]{1,0:T(8,128)(2,1)S(1)}, bf16[32,1664]{1,0:T(8,128)(2,1)S(1)}, u32[]{:S(2)}, u32[]{:S(2)}) collective-permute-start(bf16[32,1664]{1,0:T(8,128)(2,1)S(1)} %get-tuple-element.175), channel_id=1, source_target_pairs={{0,3},{1,2},{2,1},{3,0},{4,7},{5,6},{6,5},{7,4},{8,11},{9,10},{10,... | collective-permute-start | bytes 319496 | tf_op jit(solution)/shard_map/ppermute | solution.py:934
  65.1 9.8 %collective-permute-start.12 = (bf16[4,21,16,128]{3,2,1,0:T(8,128)(2,1)S(1)}, bf16[4,21,16,128]{3,2,1,0:T(8,128)(2,1)S(1)}, u32[]{:S(2)}, u32[]{:S(2)}) collective-permute-start(bf16[4,21,16,128]{3,2,1,0:T(8,128)(2,1)S(1)} %get-tuple-element.182), channel_id=1, source_target_pairs={{0,4},{4,0},{8,12},{12,8},{16,20},{20,16},{24,28},{28,24},{1,5},{5... | collective-permute-start | bytes 1032200 | tf_op jit(solution)/shard_map/ppermute | solution.py:968
  77.9 1.9 %collective-permute-start.13 = (bf16[1952,128]{1,0:T(8,128)(2,1)S(1)}, bf16[1952,128]{1,0:T(8,128)(2,1)S(1)}, u32[]{:S(2)}, u32[]{:S(2)}) collective-permute-start(bf16[1952,128]{1,0:T(8,128)(2,1)S(1)} %get-tuple-element.188.refs_0_), channel_id=1, source_target_pairs={{0,1},{1,0},{2,3},{3,2},{4,5},{5,4},{6,7},{7,6},{8,9},{9,8},{10,11... | collective-permute-start | bytes 1499144 | tf_op jit(solution)/shard_map/ppermute | solution.py:937
  78.0 11.5 %collective-permute-start.14 = (bf16[4,18,16,128]{3,2,1,0:T(8,128)(2,1)S(1)}, bf16[4,18,16,128]{3,2,1,0:T(8,128)(2,1)S(1)}, u32[]{:S(2)}, u32[]{:S(2)}) collective-permute-start(bf16[4,18,16,128]{3,2,1,0:T(8,128)(2,1)S(1)} %get-tuple-element.195), channel_id=1, source_target_pairs={{0,4},{4,0},{8,12},{12,8},{16,20},{20,16},{24,28},{28,24},{1,5},{5... | collective-permute-start | bytes 884744 | tf_op jit(solution)/shard_map/ppermute | solution.py:968
  78.6 10.9 %collective-permute-start.15 = (bf16[2,21,16,128]{3,2,1,0:T(8,128)(2,1)S(1)}, bf16[2,21,16,128]{3,2,1,0:T(8,128)(2,1)S(1)}, u32[]{:S(2)}, u32[]{:S(2)}) collective-permute-start(bf16[2,21,16,128]{3,2,1,0:T(8,128)(2,1)S(1)} %get-tuple-element.196), channel_id=1, source_target_pairs={{0,8},{4,12},{8,0},{12,4},{16,24},{20,28},{24,16},{28,20},{1,9},{5... | collective-permute-start | bytes 516104 | tf_op jit(solution)/shard_map/ppermute | solution.py:1065
  91.2 4.2 %collective-permute-start.16 = (bf16[4,3,16,128]{3,2,1,0:T(8,128)(2,1)S(1)}, bf16[4,3,16,128]{3,2,1,0:T(8,128)(2,1)S(1)}, u32[]{:S(2)}, u32[]{:S(2)}) collective-permute-start(bf16[4,3,16,128]{3,2,1,0:T(8,128)(2,1)S(1)} %get-tuple-element.204), channel_id=1, source_target_pairs={{0,4},{4,0},{8,12},{12,8},{16,20},{20,16},{24,28},{28,24},{1,5},{5... | collective-permute-start | bytes 147464 | tf_op jit(solution)/shard_map/ppermute | solution.py:968
  91.8 9.5 %collective-permute-start.20 = (bf16[21,16,128]{2,1,0:T(8,128)(2,1)S(1)}, bf16[21,16,128]{2,1,0:T(8,128)(2,1)S(1)}, u32[]{:S(2)}, u32[]{:S(2)}) collective-permute-start(bf16[21,16,128]{2,1,0:T(8,128)(2,1)S(1)} %get-tuple-element.211), channel_id=1, source_target_pairs={{0,16},{4,20},{8,24},{12,28},{16,0},{20,4},{24,8},{28,12},{1,17},{... | collective-permute-start | bytes 258056 | tf_op jit(solution)/shard_map/ppermute | solution.py:1071
  95.4 10.3 %collective-permute-start.22 = (bf16[32,1664]{1,0:T(8,128)(2,1)S(1)}, bf16[32,1664]{1,0:T(8,128)(2,1)S(1)}, u32[]{:S(2)}, u32[]{:S(2)}) collective-permute-start(bf16[32,1664]{1,0:T(8,128)(2,1)S(1)} %get-tuple-element.216), channel_id=1, source_target_pairs={{0,2},{1,3},{2,0},{3,1},{4,6},{5,7},{6,4},{7,5},{8,10},{9,11},{10,... | collective-permute-start | bytes 319496 | tf_op jit(solution)/shard_map/ppermute | solution.py:931
  96.9 8.9 %collective-permute-start.17 = (bf16[21,16,128]{2,1,0:T(8,128)(2,1)S(1)}, bf16[21,16,128]{2,1,0:T(8,128)(2,1)S(1)}, u32[]{:S(2)}, u32[]{:S(2)}) collective-permute-start(bf16[21,16,128]{2,1,0:T(8,128)(2,1)S(1)} %get-tuple-element.206), channel_id=1, source_target_pairs={{0,8},{4,12},{8,0},{12,4},{16,24},{20,28},{24,16},{28,20},{1,9},{5... | collective-permute-start | bytes 258056 | tf_op jit(solution)/shard_map/ppermute | solution.py:974
  97.3 8.5 %collective-permute-start.18 = (bf16[21,16,128]{2,1,0:T(8,128)(2,1)S(1)}, bf16[21,16,128]{2,1,0:T(8,128)(2,1)S(1)}, u32[]{:S(2)}, u32[]{:S(2)}) collective-permute-start(bf16[21,16,128]{2,1,0:T(8,128)(2,1)S(1)} %get-tuple-element.207), channel_id=1, source_target_pairs={{0,16},{4,20},{8,24},{12,28},{16,0},{20,4},{24,8},{28,12},{1,17},{... | collective-permute-start | bytes 258056 | tf_op jit(solution)/shard_map/ppermute | solution.py:974
  98.0 7.7 %collective-permute-start.19 = (bf16[21,16,128]{2,1,0:T(8,128)(2,1)S(1)}, bf16[21,16,128]{2,1,0:T(8,128)(2,1)S(1)}, u32[]{:S(2)}, u32[]{:S(2)}) collective-permute-start(bf16[21,16,128]{2,1,0:T(8,128)(2,1)S(1)} %get-tuple-element.208), channel_id=1, source_target_pairs={{0,24},{4,28},{8,16},{12,20},{16,8},{20,12},{24,0},{28,4},{1,25},{... | collective-permute-start | bytes 258056 | tf_op jit(solution)/shard_map/ppermute | solution.py:974
  101.3 4.4 %collective-permute-start.21 = (bf16[10,16,128]{2,1,0:T(8,128)(2,1)S(1)}, bf16[10,16,128]{2,1,0:T(8,128)(2,1)S(1)}, u32[]{:S(2)}, u32[]{:S(2)}) collective-permute-start(bf16[10,16,128]{2,1,0:T(8,128)(2,1)S(1)} %get-tuple-element.214), channel_id=1, source_target_pairs={{2,0},{3,1},{6,4},{7,5},{10,8},{11,9},{14,12},{15,13},{18,16},{19,... | collective-permute-start | bytes 122888 | tf_op jit(solution)/shard_map/ppermute | solution.py:1098
  105.9 7.5 %collective-permute-start.26 = (bf16[32,16,128]{2,1,0:T(8,128)(2,1)S(1)}, bf16[32,16,128]{2,1,0:T(8,128)(2,1)S(1)}, u32[]{:S(2)}, u32[]{:S(2)}) collective-permute-start(bf16[32,16,128]{2,1,0:T(8,128)(2,1)S(1)} %shard_map.292), channel_id=1, source_target_pairs={{0,24},{1,16},{2,8},{3,0},{4,28},{5,20},{6,12},{7,4},{8,25},{9,17}... | collective-permute-start | bytes 393224 | tf_op jit(solution)/shard_map/ppermute | solution.py:955
  107.0 10.6 %collective-permute-start.25 = (bf16[32,16,128]{2,1,0:T(8,128)(2,1)S(1)}, bf16[32,16,128]{2,1,0:T(8,128)(2,1)S(1)}, u32[]{:S(2)}, u32[]{:S(2)}) collective-permute-start(bf16[32,16,128]{2,1,0:T(8,128)(2,1)S(1)} %shard_map.292), channel_id=1, source_target_pairs={{0,16},{1,24},{2,0},{3,8},{4,20},{5,28},{6,4},{7,12},{8,17},{9,25}... | collective-permute-start | bytes 393224 | tf_op jit(solution)/shard_map/ppermute | solution.py:955
  108.5 13.1 %collective-permute-start.24 = (bf16[32,16,128]{2,1,0:T(8,128)(2,1)S(1)}, bf16[32,16,128]{2,1,0:T(8,128)(2,1)S(1)}, u32[]{:S(2)}, u32[]{:S(2)}) collective-permute-start(bf16[32,16,128]{2,1,0:T(8,128)(2,1)S(1)} %shard_map.292), channel_id=1, source_target_pairs={{0,8},{1,0},{2,24},{3,16},{4,12},{5,4},{6,28},{7,20},{8,9},{9,1},{... | collective-permute-start | bytes 393224 | tf_op jit(solution)/shard_map/ppermute | solution.py:955
  110.9 12.6 %collective-permute-start.23 = (bf16[32,16,128]{2,1,0:T(8,128)(2,1)S(1)}, bf16[32,16,128]{2,1,0:T(8,128)(2,1)S(1)}, u32[]{:S(2)}, u32[]{:S(2)}) collective-permute-start(bf16[32,16,128]{2,1,0:T(8,128)(2,1)S(1)} %shard_map.292), channel_id=1, source_target_pairs={{0,0},{1,8},{2,16},{3,24},{4,4},{5,12},{6,20},{7,28},{8,1},{9,9},{... | collective-permute-start | bytes 393224 | tf_op jit(solution)/shard_map/ppermute | solution.py:955
  113.4 16.6 %collective-permute-start.30 = (bf16[32,16,128]{2,1,0:T(8,128)(2,1)S(1)}, bf16[32,16,128]{2,1,0:T(8,128)(2,1)S(1)}, u32[]{:S(2)}, u32[]{:S(2)}) collective-permute-start(bf16[32,16,128]{2,1,0:T(8,128)(2,1)S(1)} %collective-permute-done.26.refs_3_), channel_id=1, source_target_pairs={{0,4},{4,0},{8,12},{12,8},{16,20},{20,16},{24,28},{28,24},{1,5},{5... | collective-permute-start | bytes 393224 | tf_op jit(solution)/shard_map/ppermute | solution.py:968
  117.7 12.3 %collective-permute-start.29 = (bf16[32,16,128]{2,1,0:T(8,128)(2,1)S(1)}, bf16[32,16,128]{2,1,0:T(8,128)(2,1)S(1)}, u32[]{:S(2)}, u32[]{:S(2)}) collective-permute-start(bf16[32,16,128]{2,1,0:T(8,128)(2,1)S(1)} %collective-permute-done.25.refs_2_), channel_id=1, source_target_pairs={{0,4},{4,0},{8,12},{12,8},{16,20},{20,16},{24,28},{28,24},{1,5},{5... | collective-permute-start | bytes 393224 | tf_op jit(solution)/shard_map/ppermute | solution.py:968
  121.7 8.3 %collective-permute-start.28 = (bf16[32,16,128]{2,1,0:T(8,128)(2,1)S(1)}, bf16[32,16,128]{2,1,0:T(8,128)(2,1)S(1)}, u32[]{:S(2)}, u32[]{:S(2)}) collective-permute-start(bf16[32,16,128]{2,1,0:T(8,128)(2,1)S(1)} %collective-permute-done.24.refs_1_), channel_id=1, source_target_pairs={{0,4},{4,0},{8,12},{12,8},{16,20},{20,16},{24,28},{28,24},{1,5},{5... | collective-permute-start | bytes 393224 | tf_op jit(solution)/shard_map/ppermute | solution.py:968
  123.5 6.5 %collective-permute-start.27 = (bf16[32,16,128]{2,1,0:T(8,128)(2,1)S(1)}, bf16[32,16,128]{2,1,0:T(8,128)(2,1)S(1)}, u32[]{:S(2)}, u32[]{:S(2)}) collective-permute-start(bf16[32,16,128]{2,1,0:T(8,128)(2,1)S(1)} %collective-permute-done.23.refs_0_), channel_id=1, source_target_pairs={{0,4},{4,0},{8,12},{12,8},{16,20},{20,16},{24,28},{28,24},{1,5},{5... | collective-permute-start | bytes 393224 | tf_op jit(solution)/shard_map/ppermute | solution.py:968

commit v10 on v9

--- a/solution.py
+++ b/solution.py
@@ -620,7 +620,7 @@
 
 
 def source(meta, k):
-    c = meta[4] ^ (k % 4)
+    c = (meta[4] - (k % 4)) & 3
     return c >> 1, c & 1, meta[5] ^ (k // 4)
 
 
@@ -950,7 +950,7 @@
         parts = []
         for k in range(4):
             pairs = [
-                (8 * z + 4 * y + i, 8 * (i ^ k) + 4 * y + z) for z in range(4) for y in range(2) for i in range(4)
+                (8 * z + 4 * y + i, 8 * ((i + k) % 4) + 4 * y + z) for z in range(4) for y in range(2) for i in range(4)
             ]
             parts.append(lax.ppermute(v, ("dp", "chan"), pairs))
         return parts
@@ -959,7 +959,7 @@
         if direct:
             return parts + [over_y(p) for p in parts]
         v = lax.all_to_all(parts.reshape(4, 2, *parts.shape[1:]), "chan", 0, 0, tiled=True)
-        return [v[k % 4, k // 4] for k in range(8)]
+        return [v[-k % 4, k // 4] for k in range(8)]
 
     def joined(*parts):
         return jnp.concatenate(parts, axis=-3)

time: 132 us -> 131 us (level); the launches traced: 132 us -> 129 us
  waiting for transfers between devices: 13.7 us -> 11.5 us
    ppermute x4, waiting for transfers between devices: 5.82 us -> 3.59 us  [over_z(): parts.append(lax.ppermute(v, ('dp', 'chan'), pairs))]
    ppermute x7, starting transfers between devices: 8.15 us -> 6.72 us  [over_y(): return lax.ppermute(v, 'dp', [(i, i ^ 1) for i in range(8)])]
  transfers between devices with their start and end apart: 31 -> 31, of which waited for: 8 -> 5; matrix products, arithmetic and copies ran while one was open for 0% -> 0% of each run, Pallas kernels for 7% -> 8%
where the time goes in v10:
time: 131 us; the launch traced here: 129 us
  blocking collectives  58.5 us (45%)
  starting transfers between devices  32 us (24%)
  Pallas kernels  24.9 us (19%)
  waiting for transfers between devices  11.5 us (9%)
  between operations  1.69 us (1%)
    all_to_all x6, blocking collectives, exchange(): st = lax.all_to_all(st, 'dp', 0, 0, tiled=True)  58.5 us
    pallas_call x23, Pallas kernels, call(): pl.pallas_call(placed if args[0].dtype == jnp.int32 else body, out_shape=...  24.9 us
    ppermute x4, starting transfers between devices, over_z(): parts.append(lax.ppermute(v, ('dp', 'chan'), pairs))  8.14 us
    ppermute x7, starting transfers between devices, over_y(): return lax.ppermute(v, 'dp', [(i, i ^ 1) for i in range(8)])  6.72 us
    ppermute x3, starting transfers between devices, along_z(): lax.ppermute(v, 'dp', [(i, i ^ 2 * k + 2) for i in range(8)])  4.39 us
    ppermute x5, starting transfers between devices, across(): return lax.ppermute(v, 'chan', [(i, i ^ 2) for i in range(4)])  4.12 us
    ppermute x4, waiting for transfers between devices, over_z(): parts.append(lax.ppermute(v, ('dp', 'chan'), pairs))  3.59 us
    ppermute x7, waiting for transfers between devices, over_y(): return lax.ppermute(v, 'dp', [(i, i ^ 1) for i in range(8)])  3 us
  transfers between devices with their start and end apart: 31, of which 5 were waited for; matrix products, arithmetic and copies ran while one was open for 0% of the time, Pallas kernels for 8%

profile of v10, /device:TPU:2, one launch (start us, length us, event | category | flops | bytes accessed | tf_op | source)
XLA Modules:
  0.0 129.1 jit_solution(11978949653289113327)
XLA Ops:
  0.6 1.2 shard_map.274
  1.8 0.1 collective-permute-start.1
  1.9 0.5 collective-permute-start.2
  2.4 0.0 collective-permute-start
  3.1 0.6 broadcast_in_dim.20.units
  3.7 2.2 %shard_map.275 = (bf16[17,32,128]{2,1,0:T(8,128)(2,1)S(1)}, bf16[17,32,128]{2,1,0:T(8,128)(2,1)S(1)}, bf16[18,32,128]{2,1,0:T(8,128)(2,1)S(1)}, bf16[18,32,128]{...) custom-call(s32[8,128]{1,0:T(8,128)} %broadcast_in_dim.20.units, ...), custom_call_target="tpu_custom_call" | custom-call | flops 2000000000 | bytes 10000 | tf_op jit(solution)/shard_map/pallas_call | solution.py:909
  5.9 2.7 %collective-permute-done.refs_1_.refs_8_ = bf16[32,2560]{1,0:T(8,128)(2,1)S(1)} collective-permute-done((bf16[32,2560]{1,0:T(8,128)(2,1)S(1)}, bf16[32,2560]{1,0:T(8,128)(2,1)S(1)}, u32[]{:S(2)}, u32[]{:S(2)}) %collective-permute-start) | collective-permute-done | bytes 163872 | tf_op jit(solution)/shard_map/ppermute | solution.py:931
  8.6 0.0 collective-permute-start.3
  8.6 1.3 collective-permute-start.4
  9.9 0.3 collective-permute-start.5
  10.3 2.2 %collective-permute-start.6 = (bf16[18,32,128]{2,1,0:T(8,128)(2,1)S(1)}, bf16[18,32,128]{2,1,0:T(8,128)(2,1)S(1)}, u32[]{:S(2)}, u32[]{:S(2)}) collective-permute-start(bf16[18,32,128]{2,1,0:T(8,128)(2,1)S(1)} %get-tuple-element.147), channel_id=1, source_target_pairs={{0,3},{1,2},{2,1},{3,0},{4,7},{5,6},{6,5},{7,4},{8,11},{9,10},{10,... | collective-permute-start | bytes 442376 | tf_op jit(solution)/shard_map/ppermute | solution.py:934
  12.5 0.0 collective-permute-done.2.refs_2_.refs_9_
  12.5 0.0 collective-permute-done.3.refs_3_.refs_10_
  12.5 1.0 shard_map.276
  13.5 0.0 collective-permute-done.4.refs_5_
  13.5 12.3 %all_to_all.30.refs_1_ = f32[8,8,128]{2,1,0:T(8,128)S(1)} all-to-all(f32[8,8,128]{2,1,0:T(8,128)S(1)} %get-tuple-element.140), channel_id=1, replica_groups=mesh['dp'=8,'chan'=4] {'dp'}, dimensions={0} | all-to-all | bytes 65536 | tf_op jit(solution)/shard_map/all_to_all | solution.py:941
  25.8 0.0 collective-permute-done.5.refs_2_
  25.8 0.7 collective-permute-start.7
  26.5 0.2 shard_map.277
  26.7 1.6 %shard_map.278 = (bf16[1920,128]{1,0:T(8,128)(2,1)S(1)}, f32[1920,128]{1,0:T(8,128)S(1)}, f32[8,8,128]{2,1,0:T(8,128)S(1)}, f32[16,128]{1,0:T(8,128)S(1)}) custom-call(s32[8,128]{1,0:T(8,128)S(1)} %copy-done.1, f32[1920,128]{1,0:T(8,128)S(1)} %get-tuple-element.137.refs_0_.refs_6_.refs_2_, f32[8,8,128]{2,1,0:T(8,128)S(1)} %all_to_all.30.refs_1_, ...), custom_call_target="tpu_custom_call" | custom-call | flops 1000000 | bytes 10000 | tf_op jit(solution)/shard_map/pallas_call | solution.py:909
  28.4 9.1 %all_to_all.31.refs_1_ = f32[8,8,128]{2,1,0:T(8,128)S(1)} all-to-all(f32[8,8,128]{2,1,0:T(8,128)S(1)} %get-tuple-element.153), channel_id=1, replica_groups=mesh['dp'=8,'chan'=4] {'dp'}, dimensions={0} | all-to-all | bytes 65536 | tf_op jit(solution)/shard_map/all_to_all | solution.py:941
  37.5 0.2 shard_map.279
  37.7 1.6 %shard_map.280 = (bf16[1920,128]{1,0:T(8,128)(2,1)S(1)}, f32[1920,128]{1,0:T(8,128)S(1)}, f32[8,8,128]{2,1,0:T(8,128)S(1)}, f32[16,128]{1,0:T(8,128)S(1)}) custom-call(s32[8,128]{1,0:T(8,128)S(1)} %copy-done.1, f32[1920,128]{1,0:T(8,128)S(1)} %get-tuple-element.152.refs_0_.refs_6_.refs_1_, f32[8,8,128]{2,1,0:T(8,128)S(1)} %all_to_all.31.refs_1_, ...), custom_call_target="tpu_custom_call" | custom-call | flops 1000000 | bytes 10000 | tf_op jit(solution)/shard_map/pallas_call | solution.py:909
  39.4 9.1 %all_to_all.32.refs_1_ = f32[8,8,128]{2,1,0:T(8,128)S(1)} all-to-all(f32[8,8,128]{2,1,0:T(8,128)S(1)} %get-tuple-element.161), channel_id=1, replica_groups=mesh['dp'=8,'chan'=4] {'dp'}, dimensions={0} | all-to-all | bytes 65536 | tf_op jit(solution)/shard_map/all_to_all | solution.py:941
  48.4 1.7 %shard_map.281 = (f32[1920,128]{1,0:T(8,128)S(1)}, f32[8,8,128]{2,1,0:T(8,128)S(1)}, f32[16,128]{1,0:T(8,128)S(1)}, bf16[1664,256]{1,0:T(8,128)(2,1)S(1)}, bf16[...) custom-call(s32[8,128]{1,0:T(8,128)S(1)} %copy-done.1, f32[1920,128]{1,0:T(8,128)S(1)} %get-tuple-element.160.refs_0_.refs_1_, ...), custom_call_target="tpu_custom_call" | custom-call | flops 1000000 | bytes 10000 | tf_op jit(solution)/shard_map/pallas_call | solution.py:909
  50.1 0.7 shard_map.282
  50.9 0.1 collective-permute-start.9
  50.9 1.5 %collective-permute-start.10 = (bf16[32,1664]{1,0:T(8,128)(2,1)S(1)}, bf16[32,1664]{1,0:T(8,128)(2,1)S(1)}, u32[]{:S(2)}, u32[]{:S(2)}) collective-permute-start(bf16[32,1664]{1,0:T(8,128)(2,1)S(1)} %get-tuple-element.174), channel_id=1, source_target_pairs={{0,2},{1,3},{2,0},{3,1},{4,6},{5,7},{6,4},{7,5},{8,10},{9,11},{10,... | collective-permute-start | bytes 319496 | tf_op jit(solution)/shard_map/ppermute | solution.py:931
  52.5 0.3 collective-permute-start.11
  52.8 9.0 %all_to_all.33.refs_3_ = f32[8,8,128]{2,1,0:T(8,128)S(1)} all-to-all(f32[8,8,128]{2,1,0:T(8,128)S(1)} %get-tuple-element.172), channel_id=1, replica_groups=mesh['dp'=8,'chan'=4] {'dp'}, dimensions={0} | all-to-all | bytes 65536 | tf_op jit(solution)/shard_map/all_to_all | solution.py:941
  61.9 3.2 %shard_map.283 = (f32[1920,128]{1,0:T(8,128)S(1)}, f32[8,8,128]{2,1,0:T(8,128)S(1)}, f32[8,128]{1,0:T(8,128)S(1)}, bf16[8,21,16,128]{3,2,1,0:T(8,128)(2,1)S(1)}, bf16[4,21,16,128]{3,2,1,0:T(8,128)(2,1)S(1)}) custom-call(s32[8,128]{1,0:T(8,128)S(1)} %copy-done.1, f32[1920,128]{1,0:T(8,128)S(1)} %get-tuple-element.168.refs_0_, ...), custom_call_target="tpu_custom_call" | custom-call | flops 1000000 | bytes 10000 | tf_op jit(solution)/shard_map/pallas_call | solution.py:909
  65.1 0.5 collective-permute-start.12
  65.6 9.3 %all_to_all.34.refs_3_ = f32[8,8,128]{2,1,0:T(8,128)S(1)} all-to-all(f32[8,8,128]{2,1,0:T(8,128)S(1)} %get-tuple-element.183), channel_id=1, replica_groups=mesh['dp'=8,'chan'=4] {'dp'}, dimensions={0} | all-to-all | bytes 65536 | tf_op jit(solution)/shard_map/all_to_all | solution.py:941
  74.9 3.0 %shard_map.284 = (bf16[1952,128]{1,0:T(8,128)(2,1)S(1)}, f32[8,8,128]{2,1,0:T(8,128)S(1)}, f32[8,128]{1,0:T(8,128)S(1)}, bf16[8,18,16,128]{3,2,1,0:T(8,128)(2,1)S(1)}, bf16[4,18,16,128]{3,2,1,0:T(8,128)(2,1)S(1)}) custom-call(s32[8,128]{1,0:T(8,128)S(1)} %copy-done.1, f32[1920,128]{1,0:T(8,128)S(1)} %get-tuple-element.180.refs_0_, ...), custom_call_target="tpu_custom_call" | custom-call | flops 1000000 | bytes 10000 | tf_op jit(solution)/shard_map/pallas_call | solution.py:909
  77.9 0.1 collective-permute-start.13
  78.0 0.5 collective-permute-start.14
  78.5 0.1 shard_map.285
  78.6 0.8 collective-permute-start.15
  79.4 0.5 collective-permute-done.13.other.refs_1_
  79.9 9.6 %all_to_all.35.st = f32[8,8,128]{2,1,0:T(8,128)S(1)} all-to-all(f32[8,8,128]{2,1,0:T(8,128)S(1)} %shard_map.286), channel_id=1, replica_groups=mesh['dp'=8,'chan'=4] {'dp'}, dimensions={0} | all-to-all | bytes 65536 | tf_op jit(solution)/shard_map/all_to_all | solution.py:941
  89.5 1.7 %shard_map.288 = (bf16[32,1664]{1,0:T(8,128)(2,1)S(1)}, bf16[32,1664]{1,0:T(8,128)(2,1)S(1)}, bf16[8,3,16,128]{3,2,1,0:T(8,128)(2,1)S(1)}, bf16[4,3,16,128]{3,2,1,0:T(8,128)(2,1)S(1)}, bf16[1,16,128]{2,1,0:T(8,128)(2,1)S(1)}) custom-call(s32[8,128]{1,0:T(8,128)S(1)} %copy-done.1, bf16[1952,128]{1,0:T(8,128)(2,1)S(1)} %get-tuple-element.188.refs_0_, ...), custom_call_target="tpu_custom_call" | custom-call | flops 1000000 | bytes 10000 | tf_op jit(solution)/shard_map/pallas_call | solution.py:909
  91.2 0.5 collective-permute-start.16
  91.8 0.6 collective-permute-start.20
  92.3 3.0 %collective-permute-done.16.refs_3_ = bf16[4,3,16,128]{3,2,1,0:T(8,128)(2,1)S(1)} collective-permute-done((bf16[4,3,16,128]{3,2,1,0:T(8,128)(2,1)S(1)}, bf16[4,3,16,128]{3,2,1,0:T(8,128)(2,1)S(1)}, u32[]{:S(2)}, u32[]{:S(2)}) %collective-permute-start.16) | collective-permute-done | bytes 49184 | tf_op jit(solution)/shard_map/ppermute | solution.py:968
  95.3 0.1 shard_map.289
  95.4 1.5 %collective-permute-start.22 = (bf16[32,1664]{1,0:T(8,128)(2,1)S(1)}, bf16[32,1664]{1,0:T(8,128)(2,1)S(1)}, u32[]{:S(2)}, u32[]{:S(2)}) collective-permute-start(bf16[32,1664]{1,0:T(8,128)(2,1)S(1)} %get-tuple-element.216), channel_id=1, source_target_pairs={{0,2},{1,3},{2,0},{3,1},{4,6},{5,7},{6,4},{7,5},{8,10},{9,11},{10,... | collective-permute-start | bytes 319496 | tf_op jit(solution)/shard_map/ppermute | solution.py:931
  96.9 0.4 collective-permute-start.17
  97.3 0.7 collective-permute-start.18
  98.0 3.3 %collective-permute-start.19 = (bf16[21,16,128]{2,1,0:T(8,128)(2,1)S(1)}, bf16[21,16,128]{2,1,0:T(8,128)(2,1)S(1)}, u32[]{:S(2)}, u32[]{:S(2)}) collective-permute-start(bf16[21,16,128]{2,1,0:T(8,128)(2,1)S(1)} %get-tuple-element.208), channel_id=1, source_target_pairs={{0,24},{4,28},{8,16},{12,20},{16,8},{20,12},{24,0},{28,4},{1,25},{... | collective-permute-start | bytes 258056 | tf_op jit(solution)/shard_map/ppermute | solution.py:974
  101.3 2.8 %collective-permute-start.21 = (bf16[10,16,128]{2,1,0:T(8,128)(2,1)S(1)}, bf16[10,16,128]{2,1,0:T(8,128)(2,1)S(1)}, u32[]{:S(2)}, u32[]{:S(2)}) collective-permute-start(bf16[10,16,128]{2,1,0:T(8,128)(2,1)S(1)} %get-tuple-element.214), channel_id=1, source_target_pairs={{2,0},{3,1},{6,4},{7,5},{10,8},{11,9},{14,12},{15,13},{18,16},{19,... | collective-permute-start | bytes 122888 | tf_op jit(solution)/shard_map/ppermute | solution.py:1098
  104.1 1.7 %collective-permute-done.21.refs_5_ = bf16[10,16,128]{2,1,0:T(8,128)(2,1)S(1)} collective-permute-done((bf16[10,16,128]{2,1,0:T(8,128)(2,1)S(1)}, bf16[10,16,128]{2,1,0:T(8,128)(2,1)S(1)}, u32[]{:S(2)}, u32[]{:S(2)}) %collective-permute-start.21) | collective-permute-done | bytes 40992 | tf_op jit(solution)/shard_map/ppermute | solution.py:1098
  105.8 0.1 shard_map.292
  105.9 1.1 collective-permute-start.26
  107.0 1.5 %collective-permute-start.25 = (bf16[32,16,128]{2,1,0:T(8,128)(2,1)S(1)}, bf16[32,16,128]{2,1,0:T(8,128)(2,1)S(1)}, u32[]{:S(2)}, u32[]{:S(2)}) collective-permute-start(bf16[32,16,128]{2,1,0:T(8,128)(2,1)S(1)} %shard_map.292), channel_id=1, source_target_pairs={{0,16},{1,24},{2,0},{3,8},{4,20},{5,28},{6,4},{7,12},{8,17},{9,25}... | collective-permute-start | bytes 393224 | tf_op jit(solution)/shard_map/ppermute | solution.py:955
  108.5 5.5 %collective-permute-start.23 = (bf16[32,16,128]{2,1,0:T(8,128)(2,1)S(1)}, bf16[32,16,128]{2,1,0:T(8,128)(2,1)S(1)}, u32[]{:S(2)}, u32[]{:S(2)}) collective-permute-start(bf16[32,16,128]{2,1,0:T(8,128)(2,1)S(1)} %shard_map.292), channel_id=1, source_target_pairs={{0,0},{1,8},{2,16},{3,24},{4,4},{5,12},{6,20},{7,28},{8,1},{9,9},{... | collective-permute-start | bytes 393224 | tf_op jit(solution)/shard_map/ppermute | solution.py:955
  114.1 1.7 %collective-permute-start.30 = (bf16[32,16,128]{2,1,0:T(8,128)(2,1)S(1)}, bf16[32,16,128]{2,1,0:T(8,128)(2,1)S(1)}, u32[]{:S(2)}, u32[]{:S(2)}) collective-permute-start(bf16[32,16,128]{2,1,0:T(8,128)(2,1)S(1)} %collective-permute-done.26.refs_3_), channel_id=1, source_target_pairs={{0,4},{4,0},{8,12},{12,8},{16,20},{20,16},{24,28},{28,24},{1,5},{5... | collective-permute-start | bytes 393224 | tf_op jit(solution)/shard_map/ppermute | solution.py:968
  115.8 3.6 %collective-permute-done.25.refs_2_ = bf16[32,16,128]{2,1,0:T(8,128)(2,1)S(1)} collective-permute-done((bf16[32,16,128]{2,1,0:T(8,128)(2,1)S(1)}, bf16[32,16,128]{2,1,0:T(8,128)(2,1)S(1)}, u32[]{:S(2)}, u32[]{:S(2)}) %collective-permute-start.25) | collective-permute-done | bytes 131104 | tf_op jit(solution)/shard_map/ppermute | solution.py:955
  119.4 1.3 %collective-permute-start.29 = (bf16[32,16,128]{2,1,0:T(8,128)(2,1)S(1)}, bf16[32,16,128]{2,1,0:T(8,128)(2,1)S(1)}, u32[]{:S(2)}, u32[]{:S(2)}) collective-permute-start(bf16[32,16,128]{2,1,0:T(8,128)(2,1)S(1)} %collective-permute-done.25.refs_2_), channel_id=1, source_target_pairs={{0,4},{4,0},{8,12},{12,8},{16,20},{20,16},{24,28},{28,24},{1,5},{5... | collective-permute-start | bytes 393224 | tf_op jit(solution)/shard_map/ppermute | solution.py:968
  120.7 0.7 collective-permute-start.28
  121.4 1.3 %collective-permute-start.27 = (bf16[32,16,128]{2,1,0:T(8,128)(2,1)S(1)}, bf16[32,16,128]{2,1,0:T(8,128)(2,1)S(1)}, u32[]{:S(2)}, u32[]{:S(2)}) collective-permute-start(bf16[32,16,128]{2,1,0:T(8,128)(2,1)S(1)} %collective-permute-done.23.refs_0_), channel_id=1, source_target_pairs={{0,4},{4,0},{8,12},{12,8},{16,20},{20,16},{24,28},{28,24},{1,5},{5... | collective-permute-start | bytes 393224 | tf_op jit(solution)/shard_map/ppermute | solution.py:968
  122.8 2.9 %shard_map.293 = (f32[3,4,9,32,128]{4,3,2,1,0:T(8,128)}, f32[3,20,128]{2,1,0:T(8,128)S(1)}, f32[3,20]{1,0:T(4,128)S(1)}, f32[5,3,32]{2,1,0:T(4,128)S(1)}, f32[32...) custom-call(s32[8,128]{1,0:T(8,128)S(1)} %copy-done.1, ...), custom_call_target="tpu_custom_call" | custom-call | flops 1000000 | bytes 10000 | tf_op jit(solution)/shard_map/pallas_call | solution.py:909
  125.7 0.8 shard_map.295
  126.5 0.7 shard_map.294
  127.2 1.7 %shard_map.296 = (f32[3,4,9,32,128]{4,3,2,1,0:T(8,128)}, f32[3,20,128]{2,1,0:T(8,128)}, f32[3,20]{1,0:T(4,128)}, f32[5,3,32]{2,1,0:T(4,128)}, f32[32,128]{1,0:T(...) custom-call(s32[8,128]{1,0:T(8,128)S(1)} %copy-done.1, ...), custom_call_target="tpu_custom_call", output_to_operand_aliasing={{0}: (5, {})} | custom-call | flops 1000000 | bytes 10000 | tf_op jit(solution)/shard_map/pallas_call | solution.py:909
  (32 shorter events, 0.2 us)
Async XLA Ops:
  1.8 6.8 %collective-permute-start.1 = (bf16[3,4,9,32,128]{4,3,2,1,0:T(8,128)(2,1)}, bf16[3,4,9,32,128]{4,3,2,1,0:T(8,128)(2,1)S(1)}, u32[]{:S(2)}, u32[]{:S(2)}) collective-permute-start(bf16[3,4,9,32,128]{4,3,2,1,0:T(8,128)(2,1)} %refs_0_.3), channel_id=1, source_target_pairs={{0,1},{1,0},{2,3},{3,2},{4,5},{5,4},{6,7},{7,6},{8,9},{9,8},{10,11... | collective-permute-start | bytes 2654216 | tf_op jit(solution)/shard_map/ppermute | solution.py:937
  1.9 10.5 %collective-permute-start.2 = (bf16[32,2560]{1,0:T(8,128)(2,1)S(1)}, bf16[32,2560]{1,0:T(8,128)(2,1)S(1)}, u32[]{:S(2)}, u32[]{:S(2)}) collective-permute-start(bf16[32,2560]{1,0:T(8,128)(2,1)S(1)} %get-tuple-element.131.refs_0_.refs_7_), channel_id=1, source_target_pairs={{0,1},{1,0},{2,3},{3,2},{4,5},{5,4},{6,7},{7,6},{8,9},{9,8},{10,11... | collective-permute-start | bytes 491528 | tf_op jit(solution)/shard_map/ppermute | solution.py:937
  2.4 6.2 %collective-permute-start = (bf16[32,2560]{1,0:T(8,128)(2,1)S(1)}, bf16[32,2560]{1,0:T(8,128)(2,1)S(1)}, u32[]{:S(2)}, u32[]{:S(2)}) collective-permute-start(bf16[32,2560]{1,0:T(8,128)(2,1)S(1)} %get-tuple-element.132), channel_id=1, source_target_pairs={{0,2},{1,3},{2,0},{3,1},{4,6},{5,7},{6,4},{7,5},{8,10},{9,11},{10,... | collective-permute-start | bytes 491528 | tf_op jit(solution)/shard_map/ppermute | solution.py:931
  3.7 8.8 %copy-start.1 = (s32[8,128]{1,0:T(8,128)S(1)}, s32[8,128]{1,0:T(8,128)}, u32[]{:S(2)}) copy-start(s32[8,128]{1,0:T(8,128)} %broadcast_in_dim.20.units) | copy-start | bytes 12292
  3.7 22.9 %copy-start = (bf16[3,4,9,32,128]{4,3,2,1,0:T(8,128)(2,1)S(1)}, bf16[3,4,9,32,128]{4,3,2,1,0:T(8,128)(2,1)}, u32[]{:S(2)}) copy-start(bf16[3,4,9,32,128]{4,3,2,1,0:T(8,128)(2,1)} %refs_0_.3) | copy-start | bytes 2654212
  8.6 3.8 %collective-permute-start.3 = (bf16[32,2560]{1,0:T(8,128)(2,1)S(1)}, bf16[32,2560]{1,0:T(8,128)(2,1)S(1)}, u32[]{:S(2)}, u32[]{:S(2)}) collective-permute-start(bf16[32,2560]{1,0:T(8,128)(2,1)S(1)} %collective-permute-done.refs_1_.refs_8_), channel_id=1, source_target_pairs={{0,1},{1,0},{2,3},{3,2},{4,5},{5,4},{6,7},{7,6},{8,9},{9,8},{10,11... | collective-permute-start | bytes 491528 | tf_op jit(solution)/shard_map/ppermute | solution.py:937
  8.6 4.8 %collective-permute-start.4 = (bf16[17,32,128]{2,1,0:T(8,128)(2,1)S(1)}, bf16[17,32,128]{2,1,0:T(8,128)(2,1)S(1)}, u32[]{:S(2)}, u32[]{:S(2)}) collective-permute-start(bf16[17,32,128]{2,1,0:T(8,128)(2,1)S(1)} %get-tuple-element.139.refs_3_), channel_id=1, source_target_pairs={{1,0},{3,2},{5,4},{7,6},{9,8},{11,10},{13,12},{15,14},{17,16},{19,... | collective-permute-start | bytes 417800 | tf_op jit(solution)/shard_map/ppermute | solution.py:937
  9.9 15.9 %collective-permute-start.5 = (bf16[18,32,128]{2,1,0:T(8,128)(2,1)S(1)}, bf16[18,32,128]{2,1,0:T(8,128)(2,1)S(1)}, u32[]{:S(2)}, u32[]{:S(2)}) collective-permute-start(bf16[18,32,128]{2,1,0:T(8,128)(2,1)S(1)} %get-tuple-element.145), channel_id=1, source_target_pairs={{0,2},{1,3},{2,0},{3,1},{4,6},{5,7},{6,4},{7,5},{8,10},{9,11},{10,... | collective-permute-start | bytes 442376 | tf_op jit(solution)/shard_map/ppermute | solution.py:931
  10.3 15.5 %collective-permute-start.6 = (bf16[18,32,128]{2,1,0:T(8,128)(2,1)S(1)}, bf16[18,32,128]{2,1,0:T(8,128)(2,1)S(1)}, u32[]{:S(2)}, u32[]{:S(2)}) collective-permute-start(bf16[18,32,128]{2,1,0:T(8,128)(2,1)S(1)} %get-tuple-element.147), channel_id=1, source_target_pairs={{0,3},{1,2},{2,1},{3,0},{4,7},{5,6},{6,5},{7,4},{8,11},{9,10},{10,... | collective-permute-start | bytes 442376 | tf_op jit(solution)/shard_map/ppermute | solution.py:934
  25.8 11.7 %collective-permute-start.8 = (bf16[27,32,128]{2,1,0:T(8,128)(2,1)S(1)}, bf16[27,32,128]{2,1,0:T(8,128)(2,1)S(1)}, u32[]{:S(2)}, u32[]{:S(2)}) collective-permute-start(bf16[27,32,128]{2,1,0:T(8,128)(2,1)S(1)} %get-tuple-element.156), channel_id=1, source_target_pairs={{0,3},{1,2},{2,1},{3,0},{4,7},{5,6},{6,5},{7,4},{8,11},{9,10},{10,... | collective-permute-start | bytes 663560 | tf_op jit(solution)/shard_map/ppermute | solution.py:934
  25.8 11.7 %collective-permute-start.7 = (bf16[27,32,128]{2,1,0:T(8,128)(2,1)S(1)}, bf16[27,32,128]{2,1,0:T(8,128)(2,1)S(1)}, u32[]{:S(2)}, u32[]{:S(2)}) collective-permute-start(bf16[27,32,128]{2,1,0:T(8,128)(2,1)S(1)} %get-tuple-element.154), channel_id=1, source_target_pairs={{0,2},{1,3},{2,0},{3,1},{4,6},{5,7},{6,4},{7,5},{8,10},{9,11},{10,... | collective-permute-start | bytes 663560 | tf_op jit(solution)/shard_map/ppermute | solution.py:931
  50.9 11.0 %collective-permute-start.9 = (bf16[32,1664]{1,0:T(8,128)(2,1)S(1)}, bf16[32,1664]{1,0:T(8,128)(2,1)S(1)}, u32[]{:S(2)}, u32[]{:S(2)}) collective-permute-start(bf16[32,1664]{1,0:T(8,128)(2,1)S(1)} %get-tuple-element.173), channel_id=1, source_target_pairs={{0,1},{1,0},{2,3},{3,2},{4,5},{5,4},{6,7},{7,6},{8,9},{9,8},{10,11... | collective-permute-start | bytes 319496 | tf_op jit(solution)/shard_map/ppermute | solution.py:937
  50.9 10.9 %collective-permute-start.10 = (bf16[32,1664]{1,0:T(8,128)(2,1)S(1)}, bf16[32,1664]{1,0:T(8,128)(2,1)S(1)}, u32[]{:S(2)}, u32[]{:S(2)}) collective-permute-start(bf16[32,1664]{1,0:T(8,128)(2,1)S(1)} %get-tuple-element.174), channel_id=1, source_target_pairs={{0,2},{1,3},{2,0},{3,1},{4,6},{5,7},{6,4},{7,5},{8,10},{9,11},{10,... | collective-permute-start | bytes 319496 | tf_op jit(solution)/shard_map/ppermute | solution.py:931
  52.5 9.4 %collective-permute-start.11 = (bf16[32,1664]{1,0:T(8,128)(2,1)S(1)}, bf16[32,1664]{1,0:T(8,128)(2,1)S(1)}, u32[]{:S(2)}, u32[]{:S(2)}) collective-permute-start(bf16[32,1664]{1,0:T(8,128)(2,1)S(1)} %get-tuple-element.175), channel_id=1, source_target_pairs={{0,3},{1,2},{2,1},{3,0},{4,7},{5,6},{6,5},{7,4},{8,11},{9,10},{10,... | collective-permute-start | bytes 319496 | tf_op jit(solution)/shard_map/ppermute | solution.py:934
  65.1 9.8 %collective-permute-start.12 = (bf16[4,21,16,128]{3,2,1,0:T(8,128)(2,1)S(1)}, bf16[4,21,16,128]{3,2,1,0:T(8,128)(2,1)S(1)}, u32[]{:S(2)}, u32[]{:S(2)}) collective-permute-start(bf16[4,21,16,128]{3,2,1,0:T(8,128)(2,1)S(1)} %get-tuple-element.182), channel_id=1, source_target_pairs={{0,4},{4,0},{8,12},{12,8},{16,20},{20,16},{24,28},{28,24},{1,5},{5... | collective-permute-start | bytes 1032200 | tf_op jit(solution)/shard_map/ppermute | solution.py:968
  77.9 1.9 %collective-permute-start.13 = (bf16[1952,128]{1,0:T(8,128)(2,1)S(1)}, bf16[1952,128]{1,0:T(8,128)(2,1)S(1)}, u32[]{:S(2)}, u32[]{:S(2)}) collective-permute-start(bf16[1952,128]{1,0:T(8,128)(2,1)S(1)} %get-tuple-element.188.refs_0_), channel_id=1, source_target_pairs={{0,1},{1,0},{2,3},{3,2},{4,5},{5,4},{6,7},{7,6},{8,9},{9,8},{10,11... | collective-permute-start | bytes 1499144 | tf_op jit(solution)/shard_map/ppermute | solution.py:937
  78.0 11.5 %collective-permute-start.14 = (bf16[4,18,16,128]{3,2,1,0:T(8,128)(2,1)S(1)}, bf16[4,18,16,128]{3,2,1,0:T(8,128)(2,1)S(1)}, u32[]{:S(2)}, u32[]{:S(2)}) collective-permute-start(bf16[4,18,16,128]{3,2,1,0:T(8,128)(2,1)S(1)} %get-tuple-element.195), channel_id=1, source_target_pairs={{0,4},{4,0},{8,12},{12,8},{16,20},{20,16},{24,28},{28,24},{1,5},{5... | collective-permute-start | bytes 884744 | tf_op jit(solution)/shard_map/ppermute | solution.py:968
  78.6 10.9 %collective-permute-start.15 = (bf16[2,21,16,128]{3,2,1,0:T(8,128)(2,1)S(1)}, bf16[2,21,16,128]{3,2,1,0:T(8,128)(2,1)S(1)}, u32[]{:S(2)}, u32[]{:S(2)}) collective-permute-start(bf16[2,21,16,128]{3,2,1,0:T(8,128)(2,1)S(1)} %get-tuple-element.196), channel_id=1, source_target_pairs={{0,8},{4,12},{8,0},{12,4},{16,24},{20,28},{24,16},{28,20},{1,9},{5... | collective-permute-start | bytes 516104 | tf_op jit(solution)/shard_map/ppermute | solution.py:1065
  91.2 4.2 %collective-permute-start.16 = (bf16[4,3,16,128]{3,2,1,0:T(8,128)(2,1)S(1)}, bf16[4,3,16,128]{3,2,1,0:T(8,128)(2,1)S(1)}, u32[]{:S(2)}, u32[]{:S(2)}) collective-permute-start(bf16[4,3,16,128]{3,2,1,0:T(8,128)(2,1)S(1)} %get-tuple-element.204), channel_id=1, source_target_pairs={{0,4},{4,0},{8,12},{12,8},{16,20},{20,16},{24,28},{28,24},{1,5},{5... | collective-permute-start | bytes 147464 | tf_op jit(solution)/shard_map/ppermute | solution.py:968
  91.8 9.5 %collective-permute-start.20 = (bf16[21,16,128]{2,1,0:T(8,128)(2,1)S(1)}, bf16[21,16,128]{2,1,0:T(8,128)(2,1)S(1)}, u32[]{:S(2)}, u32[]{:S(2)}) collective-permute-start(bf16[21,16,128]{2,1,0:T(8,128)(2,1)S(1)} %get-tuple-element.211), channel_id=1, source_target_pairs={{0,16},{4,20},{8,24},{12,28},{16,0},{20,4},{24,8},{28,12},{1,17},{... | collective-permute-start | bytes 258056 | tf_op jit(solution)/shard_map/ppermute | solution.py:1071
  95.4 10.3 %collective-permute-start.22 = (bf16[32,1664]{1,0:T(8,128)(2,1)S(1)}, bf16[32,1664]{1,0:T(8,128)(2,1)S(1)}, u32[]{:S(2)}, u32[]{:S(2)}) collective-permute-start(bf16[32,1664]{1,0:T(8,128)(2,1)S(1)} %get-tuple-element.216), channel_id=1, source_target_pairs={{0,2},{1,3},{2,0},{3,1},{4,6},{5,7},{6,4},{7,5},{8,10},{9,11},{10,... | collective-permute-start | bytes 319496 | tf_op jit(solution)/shard_map/ppermute | solution.py:931
  96.9 8.9 %collective-permute-start.17 = (bf16[21,16,128]{2,1,0:T(8,128)(2,1)S(1)}, bf16[21,16,128]{2,1,0:T(8,128)(2,1)S(1)}, u32[]{:S(2)}, u32[]{:S(2)}) collective-permute-start(bf16[21,16,128]{2,1,0:T(8,128)(2,1)S(1)} %get-tuple-element.206), channel_id=1, source_target_pairs={{0,8},{4,12},{8,0},{12,4},{16,24},{20,28},{24,16},{28,20},{1,9},{5... | collective-permute-start | bytes 258056 | tf_op jit(solution)/shard_map/ppermute | solution.py:974
  97.3 8.5 %collective-permute-start.18 = (bf16[21,16,128]{2,1,0:T(8,128)(2,1)S(1)}, bf16[21,16,128]{2,1,0:T(8,128)(2,1)S(1)}, u32[]{:S(2)}, u32[]{:S(2)}) collective-permute-start(bf16[21,16,128]{2,1,0:T(8,128)(2,1)S(1)} %get-tuple-element.207), channel_id=1, source_target_pairs={{0,16},{4,20},{8,24},{12,28},{16,0},{20,4},{24,8},{28,12},{1,17},{... | collective-permute-start | bytes 258056 | tf_op jit(solution)/shard_map/ppermute | solution.py:974
  98.0 7.7 %collective-permute-start.19 = (bf16[21,16,128]{2,1,0:T(8,128)(2,1)S(1)}, bf16[21,16,128]{2,1,0:T(8,128)(2,1)S(1)}, u32[]{:S(2)}, u32[]{:S(2)}) collective-permute-start(bf16[21,16,128]{2,1,0:T(8,128)(2,1)S(1)} %get-tuple-element.208), channel_id=1, source_target_pairs={{0,24},{4,28},{8,16},{12,20},{16,8},{20,12},{24,0},{28,4},{1,25},{... | collective-permute-start | bytes 258056 | tf_op jit(solution)/shard_map/ppermute | solution.py:974
  101.3 4.4 %collective-permute-start.21 = (bf16[10,16,128]{2,1,0:T(8,128)(2,1)S(1)}, bf16[10,16,128]{2,1,0:T(8,128)(2,1)S(1)}, u32[]{:S(2)}, u32[]{:S(2)}) collective-permute-start(bf16[10,16,128]{2,1,0:T(8,128)(2,1)S(1)} %get-tuple-element.214), channel_id=1, source_target_pairs={{2,0},{3,1},{6,4},{7,5},{10,8},{11,9},{14,12},{15,13},{18,16},{19,... | collective-permute-start | bytes 122888 | tf_op jit(solution)/shard_map/ppermute | solution.py:1098
  105.9 8.2 %collective-permute-start.26 = (bf16[32,16,128]{2,1,0:T(8,128)(2,1)S(1)}, bf16[32,16,128]{2,1,0:T(8,128)(2,1)S(1)}, u32[]{:S(2)}, u32[]{:S(2)}) collective-permute-start(bf16[32,16,128]{2,1,0:T(8,128)(2,1)S(1)} %shard_map.292), channel_id=1, source_target_pairs={{0,24},{1,0},{2,8},{3,16},{4,28},{5,4},{6,12},{7,20},{8,25},{9,1},... | collective-permute-start | bytes 393224 | tf_op jit(solution)/shard_map/ppermute | solution.py:955
  107.0 12.4 %collective-permute-start.25 = (bf16[32,16,128]{2,1,0:T(8,128)(2,1)S(1)}, bf16[32,16,128]{2,1,0:T(8,128)(2,1)S(1)}, u32[]{:S(2)}, u32[]{:S(2)}) collective-permute-start(bf16[32,16,128]{2,1,0:T(8,128)(2,1)S(1)} %shard_map.292), channel_id=1, source_target_pairs={{0,16},{1,24},{2,0},{3,8},{4,20},{5,28},{6,4},{7,12},{8,17},{9,25}... | collective-permute-start | bytes 393224 | tf_op jit(solution)/shard_map/ppermute | solution.py:955
  108.5 12.2 %collective-permute-start.24 = (bf16[32,16,128]{2,1,0:T(8,128)(2,1)S(1)}, bf16[32,16,128]{2,1,0:T(8,128)(2,1)S(1)}, u32[]{:S(2)}, u32[]{:S(2)}) collective-permute-start(bf16[32,16,128]{2,1,0:T(8,128)(2,1)S(1)} %shard_map.292), channel_id=1, source_target_pairs={{0,8},{1,16},{2,24},{3,0},{4,12},{5,20},{6,28},{7,4},{8,9},{9,17},... | collective-permute-start | bytes 393224 | tf_op jit(solution)/shard_map/ppermute | solution.py:955
  108.5 12.9 %collective-permute-start.23 = (bf16[32,16,128]{2,1,0:T(8,128)(2,1)S(1)}, bf16[32,16,128]{2,1,0:T(8,128)(2,1)S(1)}, u32[]{:S(2)}, u32[]{:S(2)}) collective-permute-start(bf16[32,16,128]{2,1,0:T(8,128)(2,1)S(1)} %shard_map.292), channel_id=1, source_target_pairs={{0,0},{1,8},{2,16},{3,24},{4,4},{5,12},{6,20},{7,28},{8,1},{9,9},{... | collective-permute-start | bytes 393224 | tf_op jit(solution)/shard_map/ppermute | solution.py:955
  114.1 13.2 %collective-permute-start.30 = (bf16[32,16,128]{2,1,0:T(8,128)(2,1)S(1)}, bf16[32,16,128]{2,1,0:T(8,128)(2,1)S(1)}, u32[]{:S(2)}, u32[]{:S(2)}) collective-permute-start(bf16[32,16,128]{2,1,0:T(8,128)(2,1)S(1)} %collective-permute-done.26.refs_3_), channel_id=1, source_target_pairs={{0,4},{4,0},{8,12},{12,8},{16,20},{20,16},{24,28},{28,24},{1,5},{5... | collective-permute-start | bytes 393224 | tf_op jit(solution)/shard_map/ppermute | solution.py:968
  119.4 7.8 %collective-permute-start.29 = (bf16[32,16,128]{2,1,0:T(8,128)(2,1)S(1)}, bf16[32,16,128]{2,1,0:T(8,128)(2,1)S(1)}, u32[]{:S(2)}, u32[]{:S(2)}) collective-permute-start(bf16[32,16,128]{2,1,0:T(8,128)(2,1)S(1)} %collective-permute-done.25.refs_2_), channel_id=1, source_target_pairs={{0,4},{4,0},{8,12},{12,8},{16,20},{20,16},{24,28},{28,24},{1,5},{5... | collective-permute-start | bytes 393224 | tf_op jit(solution)/shard_map/ppermute | solution.py:968
  120.7 6.5 %collective-permute-start.28 = (bf16[32,16,128]{2,1,0:T(8,128)(2,1)S(1)}, bf16[32,16,128]{2,1,0:T(8,128)(2,1)S(1)}, u32[]{:S(2)}, u32[]{:S(2)}) collective-permute-start(bf16[32,16,128]{2,1,0:T(8,128)(2,1)S(1)} %collective-permute-done.24.refs_1_), channel_id=1, source_target_pairs={{0,4},{4,0},{8,12},{12,8},{16,20},{20,16},{24,28},{28,24},{1,5},{5... | collective-permute-start | bytes 393224 | tf_op jit(solution)/shard_map/ppermute | solution.py:968
  121.4 5.8 %collective-permute-start.27 = (bf16[32,16,128]{2,1,0:T(8,128)(2,1)S(1)}, bf16[32,16,128]{2,1,0:T(8,128)(2,1)S(1)}, u32[]{:S(2)}, u32[]{:S(2)}) collective-permute-start(bf16[32,16,128]{2,1,0:T(8,128)(2,1)S(1)} %collective-permute-done.23.refs_0_), channel_id=1, source_target_pairs={{0,4},{4,0},{8,12},{12,8},{16,20},{20,16},{24,28},{28,24},{1,5},{5... | collective-permute-start | bytes 393224 | tf_op jit(solution)/shard_map/ppermute | solution.py:968
